TPU v7x, 512 devices: a whole 4x8x8 slice. The times are simulated.
512 devices in a mesh: col: 64 (over y, z_lo, core), row: 8 (over x, z_hi).
Axes of the slice: x: 4, y: 8, z: 8 (z_hi: 2, z_lo: 4; z = z_hi * 4 + z_lo), core: 2. Of those that a mesh axis runs over, the one named last changes fastest.
Arguments:
- field: bfloat16 [128, 1024, 128], P('row', 'col'), may hold values from -6 to 6
- cotangent: bfloat16 [128, 1024, 128], P('row', 'col'), may hold values from -6 to 6
- w_first: bfloat16 [3, 3, 128, 128], replicated, may hold values from -0.1875 to 0.1875
- w_down: bfloat16 [3, 3, 128, 256], replicated, may hold values from -0.1875 to 0.1875
- w_up: bfloat16 [2, 2, 256, 128], replicated, may hold values from -0.375 to 0.375
- offsets: int32 [8, 64, 2], replicated, may hold values from -8 to 8
- blend_table: int32 [32, 32], replicated, may hold values from 1 to 16
Outputs:
- blended: bfloat16 [128, 1024, 128], P('row', 'col')
- field_grad: float32 [128, 1024, 128], P('row', 'col')
- grad_first: float32 [3, 3, 128, 128], replicated
- grad_down: float32 [3, 3, 128, 256], replicated
- grad_up: float32 [2, 2, 256, 128], replicated
Inputs may be any that keep to these rules, and one draw needn't show every extreme that they name: `offsets`: A patch's first cell lies 8 cells minus its offset before its tile's first cell on each axis.
All inputs are finite; a program needn't handle non-finite values.
Results may differ from a plain program's by a relative error of at most 0.015.
Values may be sent and summed in bfloat16 or wider, within the bound.
No kernel may reach another device: no remote copies, remote signals or barrier semaphores. Data moves between devices by JAX's collectives and lax.ppermute only.
A program may use at most 64 MiB of HBM per device.

v0:
```python
import math

import jax
import jax.numpy as jnp
from jax import lax
from jax.sharding import PartitionSpec as P

MARGIN = 8


def passed_along(block, axis, distance):
    devices = range(lax.axis_size(axis))
    route = [(i - distance, i) for i in devices if i - distance in devices]
    return lax.ppermute(block, axis, route)


def extended(x, sides, width):
    for axis, dim in sides:
        size, length = (lax.axis_size(axis), x.shape[dim])
        up = [(i, (i + 1) % size) for i in range(size - 1)]
        down = [(j, i) for i, j in up]
        last = lax.slice_in_dim(x, length - width, length, axis=dim)
        leading = lax.slice_in_dim(x, 0, width, axis=dim)
        before = lax.ppermute(last, axis, up)
        after = lax.ppermute(leading, axis, down)
        x = jnp.concatenate([before, x, after], axis=dim)
    return x


def conv_same(inputs, kernel):
    rows, cols, chans = inputs.shape
    padded = jnp.pad(inputs, ((1, 1), (1, 1), (0, 0)))
    total = jnp.zeros((rows * cols, kernel.shape[3]), jnp.float32)
    for row_tap in range(3):
        for col_tap in range(3):
            window = padded[row_tap : row_tap + rows, col_tap : col_tap + cols].reshape(
                rows * cols, chans
            )
            total = total + jnp.dot(
                window, kernel[row_tap, col_tap], preferred_element_type=jnp.float32
            )
    return total.reshape(rows, cols, kernel.shape[3])


def conv_down(inputs, kernel):
    rows, cols, chans = inputs.shape
    padded = jnp.pad(inputs, ((1, 1), (1, 1), (0, 0)))
    half_r = rows // 2
    half_c = cols // 2
    total = jnp.zeros((half_r * half_c, kernel.shape[3]), jnp.float32)
    for row_tap in range(3):
        for col_tap in range(3):
            window = padded[row_tap : row_tap + rows : 2, col_tap : col_tap + cols : 2].reshape(
                half_r * half_c, chans
            )
            total = total + jnp.dot(
                window, kernel[row_tap, col_tap], preferred_element_type=jnp.float32
            )
    return total.reshape(half_r, half_c, kernel.shape[3])


def conv_up(inputs, kernel):
    rows, cols, chans = inputs.shape
    flat = inputs.reshape(rows * cols, chans)
    lines = []
    for row_tap in range(2):
        pieces = []
        for col_tap in range(2):
            pieces.append(
                jnp.dot(flat, kernel[row_tap, col_tap], preferred_element_type=jnp.float32).reshape(
                    rows, cols, kernel.shape[3]
                )
            )
        lines.append(jnp.stack(pieces, axis=2))
    return jnp.stack(lines, axis=1).reshape(2 * rows, 2 * cols, kernel.shape[3])


def patch_net(patch, w_first, w_down, w_up):
    hidden = jax.nn.silu(conv_same(patch, w_first)).astype(jnp.bfloat16)
    lower = jax.nn.silu(conv_down(hidden, w_down)).astype(jnp.bfloat16)
    return hidden.astype(jnp.float32) + conv_up(lower, w_up)


def return_margins(canvas, tile_h, tile_w, edge):
    summed = canvas
    for heading in (1, -1):
        strip = canvas[tile_h + edge :] if heading == 1 else canvas[:edge]
        arrived = passed_along(strip.astype(jnp.bfloat16), "row", heading).astype(strip.dtype)
        if heading == 1:
            summed = summed.at[edge : 2 * edge].add(arrived)
        else:
            summed = summed.at[tile_h : tile_h + edge].add(arrived)
    middle = summed[edge : tile_h + edge]
    result = middle
    for heading in (1, -1):
        strip = middle[:, tile_w + edge :] if heading == 1 else middle[:, :edge]
        arrived = passed_along(strip.astype(jnp.bfloat16), "col", heading).astype(strip.dtype)
        if heading == 1:
            result = result.at[:, edge : 2 * edge].add(arrived)
        else:
            result = result.at[:, tile_w : tile_w + edge].add(arrived)
    return result[:, edge : tile_w + edge]


def weight_total(offsets, table_f, row_at, col_at, rows_n, cols_n, tile_h, tile_w, lead, reach):
    patch_h, patch_w = table_f.shape
    total = jnp.zeros((tile_h + 2 * lead, tile_w + 2 * lead), jnp.float32)
    for row_step in range(-reach, reach + 1):
        for col_step in range(-reach, reach + 1):
            near_row = row_at + row_step
            near_col = col_at + col_step
            inside = (
                (near_row >= 0) & (near_row < rows_n) & (near_col >= 0) & (near_col < cols_n)
            ).astype(jnp.float32)
            shift_pair = offsets[
                jnp.clip(near_row, 0, rows_n - 1), jnp.clip(near_col, 0, cols_n - 1)
            ]
            top = row_step * tile_h - MARGIN + shift_pair[0] + lead
            left = col_step * tile_w - MARGIN + shift_pair[1] + lead
            pick_rows = (
                jnp.arange(tile_h + 2 * lead)[:, None] - top == jnp.arange(patch_h)[None, :]
            ).astype(jnp.float32)
            pick_cols = (
                jnp.arange(tile_w + 2 * lead)[:, None] - left == jnp.arange(patch_w)[None, :]
            ).astype(jnp.float32)
            placed = jnp.dot(
                jnp.dot(pick_rows, table_f, precision=lax.Precision.HIGHEST),
                pick_cols.T,
                precision=lax.Precision.HIGHEST,
            )
            total = total + inside * placed
    return total


def per_device(field, cotangent, w_first, w_down, w_up, offsets, blend_table):
    tile_h, tile_w, chans = field.shape
    patch_h, patch_w = blend_table.shape
    edge = 2 * MARGIN
    rows_n = lax.axis_size("row")
    cols_n = lax.axis_size("col")
    row_at = lax.axis_index("row")
    col_at = lax.axis_index("col")
    table_f = blend_table.astype(jnp.float32)
    grown = extended(field, (("row", 0), ("col", 1)), edge)
    own_shift = offsets[row_at, col_at]
    start_r = MARGIN + own_shift[0]
    start_c = MARGIN + own_shift[1]
    zero = jnp.int32(0)
    patch = lax.dynamic_slice(grown, (start_r, start_c, zero), (patch_h, patch_w, chans))
    out_patch, back = jax.vjp(patch_net, patch, w_first, w_down, w_up)
    empty = jnp.zeros((tile_h + 2 * edge, tile_w + 2 * edge, chans), jnp.float32)
    canvas = lax.dynamic_update_slice(
        empty, table_f[:, :, None] * out_patch, (start_r, start_c, zero)
    )
    numer = return_margins(canvas, tile_h, tile_w, edge)
    weight_sum = weight_total(
        offsets, table_f, row_at, col_at, rows_n, cols_n, tile_h, tile_w, 0, 1
    )
    ratio = cotangent.astype(jnp.float32) / weight_sum[:, :, None]
    ratio_grown = extended(ratio.astype(jnp.bfloat16), (("row", 0), ("col", 1)), edge).astype(
        ratio.dtype
    )
    blended = (numer / weight_sum[:, :, None]).astype(jnp.bfloat16)
    out_grad = table_f[:, :, None] * lax.dynamic_slice(
        ratio_grown, (start_r, start_c, zero), (patch_h, patch_w, chans)
    )
    d_patch, d_first, d_down, d_up = back(out_grad)
    d_canvas = lax.dynamic_update_slice(
        empty, d_patch.astype(jnp.float32), (start_r, start_c, zero)
    )
    field_grad = return_margins(d_canvas, tile_h, tile_w, edge)
    g_first, g_down, g_up = lax.psum(
        (d_first.astype(jnp.float32), d_down.astype(jnp.float32), d_up.astype(jnp.float32)),
        ("col", "row"),
    )
    scale = 1.0 / math.sqrt(tile_h * rows_n * tile_w * cols_n)
    return (blended, field_grad, g_first * scale, g_down * scale, g_up * scale)


def solution(mesh):
    return jax.shard_map(
        per_device,
        mesh=mesh,
        in_specs=(P("row", "col", None), P("row", "col", None), P(), P(), P(), P(), P()),
        out_specs=(P("row", "col", None), P("row", "col", None), P(), P(), P()),
        check_vma=False,
    )
```

profile of v0, /device:TPU:1, one launch (start us, length us, event | category | flops | bytes accessed | tf_op | source)
XLA Modules:
  0.0 497.3 jit_solution(4310469566527345241)
XLA Ops:
  7.2 11.5 %collective-permute-start = (bf16[16,16,128]{2,1,0:T(8,128)(2,1)}, bf16[16,16,128]{2,1,0:T(8,128)(2,1)S(1)}, u32[]{:S(2)}, u32[]{:S(2)}) collective-permute-start(bf16[16,16,128]{2,1,0:T(8,128)(2,1)} %param.23), channel_id=1, source_target_pairs={{0,1},{1,2},{2,3},{3,4},{4,5},{5,6},{6,7},{8,9},{9,10},{10,11},{11... | collective-permute-start | bytes 196616 | tf_op jit(solution)/shard_map/ppermute | solution.py:24
  18.7 1.3 collective-permute-start.1
  20.0 1.0 constant_dynamic-slice_fusion
  24.2 0.9 fusion.167
  25.1 0.9 fusion.168
  27.4 0.9 fusion.169
  30.2 0.9 fusion.170
  32.5 0.9 fusion.171
  35.3 0.9 fusion.172
  37.6 0.9 fusion.173
  40.4 0.9 fusion.174
  42.7 0.9 fusion.175
  46.2 3.9 collective-permute-start.2
  50.1 1.9 collective-permute-start.3
  52.2 8.1 %collective-permute-start.8 = (bf16[16,16,128]{2,1,0:T(8,128)(2,1)S(1)}, bf16[16,16,128]{2,1,0:T(8,128)(2,1)S(1)}, u32[]{:S(2)}, u32[]{:S(2)}) collective-permute-start(bf16[16,16,128]{2,1,0:T(8,128)(2,1)S(1)} %divide_convert_fusion), channel_id=1, source_target_pairs={{0,1},{1,2},{2,3},{3,4},{4,5},{5,6},{6,7},{8,9},{9,10},{10,11},{11... | collective-permute-start | bytes 196616 | tf_op jit(solution)/shard_map/ppermute | solution.py:24
  60.3 1.3 collective-permute-start.9
  64.3 5.5 %collective-permute-done.9 = bf16[16,16,128]{2,1,0:T(8,128)(2,1)S(1)} collective-permute-done((bf16[16,16,128]{2,1,0:T(8,128)(2,1)S(1)}, bf16[16,16,128]{2,1,0:T(8,128)(2,1)S(1)}, u32[]{:S(2)}, u32[]{:S(2)}) %collective-permute-start.9) | collective-permute-done | bytes 65568 | tf_op jit(solution)/shard_map/ppermute | solution.py:25
  70.5 5.2 %collective-permute-start.10 = (bf16[48,16,128]{2,1,0:T(8,128)(2,1)}, bf16[48,16,128]{2,1,0:T(8,128)(2,1)}, u32[]{:S(2)}, u32[]{:S(2)}) collective-permute-start(bf16[48,16,128]{2,1,0:T(8,128)(2,1)} %pad_maximum_fusion.1), channel_id=1, source_target_pairs={{0,8},{8,16},{16,24},{24,32},{32,40},{40,48},{48,56},{56,64},{64,7... | collective-permute-start | bytes 589832 | tf_op jit(solution)/shard_map/ppermute | solution.py:24
  75.7 1.9 collective-permute-start.11
  88.5 2.3 convert_multiply_fusion.2
  107.3 5.6 %pad.156 = bf16[34,34,128]{2,1,0:T(8,128)(2,1)S(1)} pad(bf16[16,16,128]{2,1,0:T(8,128)(2,1)} %bitcast.505, bf16[]{:T(256)} %constant.241.clone.1), padding=2_1_1x0_3_1x0_0_0 | pad | bytes 361474 | tf_op jit(solution)/shard_map/transpose(jvp())/pad | solution.py:53
  112.9 8.5 %pad.345 = bf16[33,33,128]{2,1,0:T(8,128)(2,1)} pad(bf16[16,16,128]{2,1,0:T(8,128)(2,1)} %bitcast.504, bf16[]{:T(256)} %constant.241.clone.1), padding=0_2_1x0_2_1x0_0_0 | pad | bytes 344322
  121.4 8.5 %pad.348 = bf16[32,33,128]{2,1,0:T(8,128)(2,1)} pad(bf16[16,16,128]{2,1,0:T(8,128)(2,1)} %bitcast.511, bf16[]{:T(256)} %constant.241.clone.1), padding=0_1_1x0_2_1x0_0_0 | pad | bytes 335874
  129.9 8.4 %pad.346 = bf16[33,32,128]{2,1,0:T(8,128)(2,1)} pad(bf16[16,16,128]{2,1,0:T(8,128)(2,1)} %bitcast.510, bf16[]{:T(256)} %constant.241.clone.1), padding=0_2_1x0_1_1x0_0_0 | pad | bytes 335874
  138.3 8.4 %pad.347 = bf16[33,32,128]{2,1,0:T(8,128)(2,1)} pad(bf16[16,16,128]{2,1,0:T(8,128)(2,1)} %bitcast.509, bf16[]{:T(256)} %constant.241.clone.1), padding=0_2_1x1_0_1x0_0_0 | pad | bytes 335874
  146.7 8.4 %pad.214 = bf16[32,32,128]{2,1,0:T(8,128)(2,1)} pad(bf16[16,16,128]{2,1,0:T(8,128)(2,1)} %bitcast.503, bf16[]{:T(256)} %constant.241.clone.1), padding=0_1_1x1_0_1x0_0_0 | pad | bytes 327682 | tf_op jit(solution)/shard_map/transpose(jvp(jit(_pad)))/pad | solution.py:47
  155.1 5.6 %pad.215 = bf16[32,32,128]{2,1,0:T(8,128)(2,1)} pad(bf16[16,16,128]{2,1,0:T(8,128)(2,1)S(1)} %bitcast.502, bf16[]{:T(256)} %constant.241.clone.1), padding=0_1_1x0_1_1x0_0_0 | pad | bytes 327682 | tf_op jit(solution)/shard_map/transpose(jvp(jit(_pad)))/pad | solution.py:47
  161.9 1.7 fusion.52
  164.4 0.9 fusion.38
  166.2 0.9 fusion.40
  167.1 0.9 fusion.41
  172.7 1.3 dynamic_update_slice.7
  174.8 4.5 collective-permute-start.12
  179.3 1.3 collective-permute-start.13
  180.7 1.3 dynamic_update_slice.6
  182.9 8.6 %collective-permute-start.4 = (bf16[16,48,128]{2,1,0:T(8,128)(2,1)}, bf16[16,48,128]{2,1,0:T(8,128)(2,1)}, u32[]{:S(2)}, u32[]{:S(2)}) collective-permute-start(bf16[16,48,128]{2,1,0:T(8,128)(2,1)} %get-tuple-element.110), channel_id=1, source_target_pairs={{0,1},{1,2},{2,3},{3,4},{4,5},{5,6},{6,7},{8,9},{9,10},{10,11},{11... | collective-permute-start | bytes 589832 | tf_op jit(solution)/shard_map/ppermute | solution.py:14
  191.5 1.3 collective-permute-start.5
  194.8 1.2 add_convert_fusion
  196.0 11.6 %collective-permute-done.5 = bf16[16,48,128]{2,1,0:T(8,128)(2,1)} collective-permute-done((bf16[16,48,128]{2,1,0:T(8,128)(2,1)S(1)}, bf16[16,48,128]{2,1,0:T(8,128)(2,1)}, u32[]{:S(2)}, u32[]{:S(2)}) %collective-permute-start.5) | collective-permute-done | bytes 196640 | tf_op jit(solution)/shard_map/ppermute | solution.py:14
  207.6 1.1 fusion.205
  208.7 13.8 %collective-permute-start.6 = (bf16[16,16,128]{2,1,0:T(8,128)(2,1)S(1)}, bf16[16,16,128]{2,1,0:T(8,128)(2,1)S(1)}, u32[]{:S(2)}, u32[]{:S(2)}) collective-permute-start(bf16[16,16,128]{2,1,0:T(8,128)(2,1)S(1)} %get-tuple-element.128), channel_id=1, source_target_pairs={{0,8},{8,16},{16,24},{24,32},{32,40},{40,48},{48,56},{56,64},{64,7... | collective-permute-start | bytes 196616 | tf_op jit(solution)/shard_map/ppermute | solution.py:14
  222.6 1.9 collective-permute-start.7
  224.5 1.1 fusion.203
  225.6 3.6 collective-permute-start.14
  229.3 1.9 collective-permute-start.15
  232.0 3.4 collective-permute-done.15
  236.1 249.8 %all-reduce.45.cloned.1.call-done = (f32[3,3,128,128]{3,2,1,0:T(8,128)}, f32[3,3,128,256]{3,2,1,0:T(8,128)}, f32[2,2,256,128]{3,2,1,0:T(8,128)}) async-done(((f32[3,3,128,128]{3,2,1,0:T(8,128)}, f32[3,3,128,256]{3,2,1,0:T(8,128)}, f32[2,2,256,128]{3,2,1,0:T(8,128)}), (f32[3,3,128,128]{3,2,1,0:T(8,128)}, f32[3,3,128,256]{3,2,1,0:T(8,128)}, f32[2,2,256,128]{3,2,1,0:T(8,128)})) %all-reduce.45.cloned.1.call-update) | async-done | bytes 2293776 | tf_op jit(solution)/shard_map/psum | solution.py:172
  485.9 2.4 broadcast_multiply_fusion
  (244 shorter events, 47.3 us)
Async XLA Ops:
  7.2 39.0 %copy-start.35 = (bf16[16,16,128]{2,1,0:T(8,128)(2,1)S(1)}, bf16[16,16,128]{2,1,0:T(8,128)(2,1)}, u32[]{:S(2)}) copy-start(bf16[16,16,128]{2,1,0:T(8,128)(2,1)} %param.23) | copy-start | bytes 196612
  7.2 57.0 %copy-start.43 = (s32[32,32]{1,0:T(8,128)S(1)}, s32[32,32]{1,0:T(8,128)}, u32[]{:S(2)}) copy-start(s32[32,32]{1,0:T(8,128)} %param.29) | copy-start | bytes 12292
  7.2 44.9 %copy-start.36 = (bf16[16,16,128]{2,1,0:T(8,128)(2,1)S(1)}, bf16[16,16,128]{2,1,0:T(8,128)(2,1)}, u32[]{:S(2)}) copy-start(bf16[16,16,128]{2,1,0:T(8,128)(2,1)} %param.24) | copy-start | bytes 196612
  7.2 478.7 %all-reduce.45.cloned.1.call-start = ((), (), s32[]{:S(2)}) async-start(), calls=%async_computation | async-start | bytes 4587520 | tf_op jit(solution)/shard_map/psum | solution.py:172
  7.2 38.9 %collective-permute-start = (bf16[16,16,128]{2,1,0:T(8,128)(2,1)}, bf16[16,16,128]{2,1,0:T(8,128)(2,1)S(1)}, u32[]{:S(2)}, u32[]{:S(2)}) collective-permute-start(bf16[16,16,128]{2,1,0:T(8,128)(2,1)} %param.23), channel_id=1, source_target_pairs={{0,1},{1,2},{2,3},{3,4},{4,5},{5,6},{6,7},{8,9},{9,10},{10,11},{11... | collective-permute-start | bytes 196616 | tf_op jit(solution)/shard_map/ppermute | solution.py:24
  18.7 27.5 %collective-permute-start.1 = (bf16[16,16,128]{2,1,0:T(8,128)(2,1)}, bf16[16,16,128]{2,1,0:T(8,128)(2,1)S(1)}, u32[]{:S(2)}, u32[]{:S(2)}) collective-permute-start(bf16[16,16,128]{2,1,0:T(8,128)(2,1)} %param.23), channel_id=1, source_target_pairs={{1,0},{2,1},{3,2},{4,3},{5,4},{6,5},{7,6},{9,8},{10,9},{11,10},{12... | collective-permute-start | bytes 196616 | tf_op jit(solution)/shard_map/ppermute | solution.py:25
  46.2 31.4 %collective-permute-start.2 = (bf16[48,16,128]{2,1,0:T(8,128)(2,1)S(1)}, bf16[48,16,128]{2,1,0:T(8,128)(2,1)S(1)}, u32[]{:S(2)}, u32[]{:S(2)}) collective-permute-start(bf16[48,16,128]{2,1,0:T(8,128)(2,1)S(1)} %constant_dynamic-update-slice_fusion), channel_id=1, source_target_pairs={{0,8},{8,16},{16,24},{24,32},{32,40},{40,48},{48,56},{56,64},{64,7... | collective-permute-start | bytes 589832 | tf_op jit(solution)/shard_map/ppermute | solution.py:24
  50.1 27.5 %collective-permute-start.3 = (bf16[48,16,128]{2,1,0:T(8,128)(2,1)S(1)}, bf16[48,16,128]{2,1,0:T(8,128)(2,1)S(1)}, u32[]{:S(2)}, u32[]{:S(2)}) collective-permute-start(bf16[48,16,128]{2,1,0:T(8,128)(2,1)S(1)} %constant_dynamic-update-slice_fusion), channel_id=1, source_target_pairs={{8,0},{16,8},{24,16},{32,24},{40,32},{48,40},{56,48},{64,56},{72,6... | collective-permute-start | bytes 589832 | tf_op jit(solution)/shard_map/ppermute | solution.py:25
  52.2 12.0 %collective-permute-start.8 = (bf16[16,16,128]{2,1,0:T(8,128)(2,1)S(1)}, bf16[16,16,128]{2,1,0:T(8,128)(2,1)S(1)}, u32[]{:S(2)}, u32[]{:S(2)}) collective-permute-start(bf16[16,16,128]{2,1,0:T(8,128)(2,1)S(1)} %divide_convert_fusion), channel_id=1, source_target_pairs={{0,1},{1,2},{2,3},{3,4},{4,5},{5,6},{6,7},{8,9},{9,10},{10,11},{11... | collective-permute-start | bytes 196616 | tf_op jit(solution)/shard_map/ppermute | solution.py:24
  60.3 9.5 %collective-permute-start.9 = (bf16[16,16,128]{2,1,0:T(8,128)(2,1)S(1)}, bf16[16,16,128]{2,1,0:T(8,128)(2,1)S(1)}, u32[]{:S(2)}, u32[]{:S(2)}) collective-permute-start(bf16[16,16,128]{2,1,0:T(8,128)(2,1)S(1)} %divide_convert_fusion), channel_id=1, source_target_pairs={{1,0},{2,1},{3,2},{4,3},{5,4},{6,5},{7,6},{9,8},{10,9},{11,10},{12... | collective-permute-start | bytes 196616 | tf_op jit(solution)/shard_map/ppermute | solution.py:25
  64.3 14.0 %copy-start.29 = (bf16[16,16,128]{2,1,0:T(8,128)(2,1)}, bf16[16,16,128]{2,1,0:T(8,128)(2,1)S(1)}, u32[]{:S(2)}) copy-start(bf16[16,16,128]{2,1,0:T(8,128)(2,1)S(1)} %collective-permute-done.8) | copy-start | bytes 196612
  69.8 8.5 %copy-start.31 = (bf16[16,16,128]{2,1,0:T(8,128)(2,1)}, bf16[16,16,128]{2,1,0:T(8,128)(2,1)S(1)}, u32[]{:S(2)}) copy-start(bf16[16,16,128]{2,1,0:T(8,128)(2,1)S(1)} %collective-permute-done.9) | copy-start | bytes 196612
  70.5 17.6 %collective-permute-start.10 = (bf16[48,16,128]{2,1,0:T(8,128)(2,1)}, bf16[48,16,128]{2,1,0:T(8,128)(2,1)}, u32[]{:S(2)}, u32[]{:S(2)}) collective-permute-start(bf16[48,16,128]{2,1,0:T(8,128)(2,1)} %pad_maximum_fusion.1), channel_id=1, source_target_pairs={{0,8},{8,16},{16,24},{24,32},{32,40},{40,48},{48,56},{56,64},{64,7... | collective-permute-start | bytes 589832 | tf_op jit(solution)/shard_map/ppermute | solution.py:24
  75.7 12.4 %collective-permute-start.11 = (bf16[48,16,128]{2,1,0:T(8,128)(2,1)}, bf16[48,16,128]{2,1,0:T(8,128)(2,1)}, u32[]{:S(2)}, u32[]{:S(2)}) collective-permute-start(bf16[48,16,128]{2,1,0:T(8,128)(2,1)} %pad_maximum_fusion.1), channel_id=1, source_target_pairs={{8,0},{16,8},{24,16},{32,24},{40,32},{48,40},{56,48},{64,56},{72,6... | collective-permute-start | bytes 589832 | tf_op jit(solution)/shard_map/ppermute | solution.py:25
  80.8 4.0 copy-start
  81.7 3.7 copy-start.16
  83.2 2.3 copy-start.8
  83.6 2.1 copy-start.10
  84.0 1.9 copy-start.12
  95.3 2.5 copy-start.13
  95.3 3.3 copy-start.11
  95.5 3.9 copy-start.9
  174.8 49.7 %collective-permute-start.12 = (bf16[16,48,128]{2,1,0:T(8,128)(2,1)}, bf16[16,48,128]{2,1,0:T(8,128)(2,1)}, u32[]{:S(2)}, u32[]{:S(2)}) collective-permute-start(bf16[16,48,128]{2,1,0:T(8,128)(2,1)} %get-tuple-element.108), channel_id=1, source_target_pairs={{0,1},{1,2},{2,3},{3,4},{4,5},{5,6},{6,7},{8,9},{9,10},{10,11},{11... | collective-permute-start | bytes 589832 | tf_op jit(solution)/shard_map/ppermute | solution.py:14
  179.3 45.2 %collective-permute-start.13 = (bf16[16,48,128]{2,1,0:T(8,128)(2,1)S(1)}, bf16[16,48,128]{2,1,0:T(8,128)(2,1)}, u32[]{:S(2)}, u32[]{:S(2)}) collective-permute-start(bf16[16,48,128]{2,1,0:T(8,128)(2,1)S(1)} %get-tuple-element.109), channel_id=1, source_target_pairs={{1,0},{2,1},{3,2},{4,3},{5,4},{6,5},{7,6},{9,8},{10,9},{11,10},{12... | collective-permute-start | bytes 589832 | tf_op jit(solution)/shard_map/ppermute | solution.py:14
  181.9 10.8 %copy-start.25 = (bf16[1,1,256,128]{3,2,1,0:T(8,128)(2,1)S(1)}, bf16[1,1,256,128]{3,2,1,0:T(8,128)(2,1)}, u32[]{:S(2)}) copy-start(bf16[1,1,256,128]{3,2,1,0:T(8,128)(2,1)} %fusion.14) | copy-start | bytes 196612
  181.9 10.8 %copy-start.26 = (bf16[1,1,256,128]{3,2,1,0:T(8,128)(2,1)S(1)}, bf16[1,1,256,128]{3,2,1,0:T(8,128)(2,1)}, u32[]{:S(2)}) copy-start(bf16[1,1,256,128]{3,2,1,0:T(8,128)(2,1)} %fusion.13) | copy-start | bytes 196612
  182.0 10.8 %copy-start.27 = (bf16[1,1,256,128]{3,2,1,0:T(8,128)(2,1)S(1)}, bf16[1,1,256,128]{3,2,1,0:T(8,128)(2,1)}, u32[]{:S(2)}) copy-start(bf16[1,1,256,128]{3,2,1,0:T(8,128)(2,1)} %fusion.15) | copy-start | bytes 196612
  182.0 10.8 %copy-start.28 = (bf16[1,1,256,128]{3,2,1,0:T(8,128)(2,1)S(1)}, bf16[1,1,256,128]{3,2,1,0:T(8,128)(2,1)}, u32[]{:S(2)}) copy-start(bf16[1,1,256,128]{3,2,1,0:T(8,128)(2,1)} %fusion.16) | copy-start | bytes 196612
  182.1 11.6 %copy-start.37 = (bf16[1,1,128,128]{3,2,1,0:T(8,128)(2,1)S(1)}, bf16[1,1,128,128]{3,2,1,0:T(8,128)(2,1)}, u32[]{:S(2)}) copy-start(bf16[1,1,128,128]{3,2,1,0:T(8,128)(2,1)} %fusion.38) | copy-start | bytes 98308
  182.1 11.6 %copy-start.38 = (bf16[1,1,128,128]{3,2,1,0:T(8,128)(2,1)S(1)}, bf16[1,1,128,128]{3,2,1,0:T(8,128)(2,1)}, u32[]{:S(2)}) copy-start(bf16[1,1,128,128]{3,2,1,0:T(8,128)(2,1)} %fusion.39) | copy-start | bytes 98308
  182.1 11.6 %copy-start.39 = (bf16[1,1,128,128]{3,2,1,0:T(8,128)(2,1)S(1)}, bf16[1,1,128,128]{3,2,1,0:T(8,128)(2,1)}, u32[]{:S(2)}) copy-start(bf16[1,1,128,128]{3,2,1,0:T(8,128)(2,1)} %fusion.40) | copy-start | bytes 98308
  182.1 11.5 %copy-start.40 = (bf16[1,1,128,128]{3,2,1,0:T(8,128)(2,1)S(1)}, bf16[1,1,128,128]{3,2,1,0:T(8,128)(2,1)}, u32[]{:S(2)}) copy-start(bf16[1,1,128,128]{3,2,1,0:T(8,128)(2,1)} %fusion.41) | copy-start | bytes 98308
  182.1 11.5 %copy-start.41 = (bf16[1,1,128,128]{3,2,1,0:T(8,128)(2,1)S(1)}, bf16[1,1,128,128]{3,2,1,0:T(8,128)(2,1)}, u32[]{:S(2)}) copy-start(bf16[1,1,128,128]{3,2,1,0:T(8,128)(2,1)} %fusion.42) | copy-start | bytes 98308
  182.1 11.5 %copy-start.42 = (bf16[1,1,128,128]{3,2,1,0:T(8,128)(2,1)S(1)}, bf16[1,1,128,128]{3,2,1,0:T(8,128)(2,1)}, u32[]{:S(2)}) copy-start(bf16[1,1,128,128]{3,2,1,0:T(8,128)(2,1)} %fusion.43) | copy-start | bytes 98308
  182.1 12.4 %copy-start.17 = (bf16[16,16,128]{2,1,0:T(8,128)(2,1)S(1)}, bf16[16,16,128]{2,1,0:T(8,128)(2,1)}, u32[]{:S(2)}) copy-start(bf16[16,16,128]{2,1,0:T(8,128)(2,1)} %copy-done.16) | copy-start | bytes 196612
  182.1 12.6 %copy-start.19 = (bf16[1,1,128,256]{3,2,1,0:T(8,128)(2,1)S(1)}, bf16[1,1,128,256]{3,2,1,0:T(8,128)(2,1)}, u32[]{:S(2)}) copy-start(bf16[1,1,128,256]{3,2,1,0:T(8,128)(2,1)} %fusion.25) | copy-start | bytes 196612
  182.2 12.6 %copy-start.20 = (bf16[1,1,128,256]{3,2,1,0:T(8,128)(2,1)S(1)}, bf16[1,1,128,256]{3,2,1,0:T(8,128)(2,1)}, u32[]{:S(2)}) copy-start(bf16[1,1,128,256]{3,2,1,0:T(8,128)(2,1)} %fusion.24) | copy-start | bytes 196612
  182.2 12.6 %copy-start.21 = (bf16[1,1,128,256]{3,2,1,0:T(8,128)(2,1)S(1)}, bf16[1,1,128,256]{3,2,1,0:T(8,128)(2,1)}, u32[]{:S(2)}) copy-start(bf16[1,1,128,256]{3,2,1,0:T(8,128)(2,1)} %fusion.23) | copy-start | bytes 196612
  182.2 12.6 %copy-start.22 = (bf16[1,1,128,256]{3,2,1,0:T(8,128)(2,1)S(1)}, bf16[1,1,128,256]{3,2,1,0:T(8,128)(2,1)}, u32[]{:S(2)}) copy-start(bf16[1,1,128,256]{3,2,1,0:T(8,128)(2,1)} %fusion.22) | copy-start | bytes 196612
  182.2 12.6 %copy-start.23 = (bf16[1,1,128,256]{3,2,1,0:T(8,128)(2,1)S(1)}, bf16[1,1,128,256]{3,2,1,0:T(8,128)(2,1)}, u32[]{:S(2)}) copy-start(bf16[1,1,128,256]{3,2,1,0:T(8,128)(2,1)} %fusion.21) | copy-start | bytes 196612
  182.2 12.6 %copy-start.24 = (bf16[1,1,128,256]{3,2,1,0:T(8,128)(2,1)S(1)}, bf16[1,1,128,256]{3,2,1,0:T(8,128)(2,1)}, u32[]{:S(2)}) copy-start(bf16[1,1,128,256]{3,2,1,0:T(8,128)(2,1)} %fusion.20) | copy-start | bytes 196612
  182.9 13.1 %collective-permute-start.4 = (bf16[16,48,128]{2,1,0:T(8,128)(2,1)}, bf16[16,48,128]{2,1,0:T(8,128)(2,1)}, u32[]{:S(2)}, u32[]{:S(2)}) collective-permute-start(bf16[16,48,128]{2,1,0:T(8,128)(2,1)} %get-tuple-element.110), channel_id=1, source_target_pairs={{0,1},{1,2},{2,3},{3,4},{4,5},{5,6},{6,7},{8,9},{9,10},{10,11},{11... | collective-permute-start | bytes 589832 | tf_op jit(solution)/shard_map/ppermute | solution.py:14
  191.5 16.2 %collective-permute-start.5 = (bf16[16,48,128]{2,1,0:T(8,128)(2,1)S(1)}, bf16[16,48,128]{2,1,0:T(8,128)(2,1)}, u32[]{:S(2)}, u32[]{:S(2)}) collective-permute-start(bf16[16,48,128]{2,1,0:T(8,128)(2,1)S(1)} %get-tuple-element.111), channel_id=1, source_target_pairs={{1,0},{2,1},{3,2},{4,3},{5,4},{6,5},{7,6},{9,8},{10,9},{11,10},{12... | collective-permute-start | bytes 589832 | tf_op jit(solution)/shard_map/ppermute | solution.py:14
  208.7 22.5 %collective-permute-start.6 = (bf16[16,16,128]{2,1,0:T(8,128)(2,1)S(1)}, bf16[16,16,128]{2,1,0:T(8,128)(2,1)S(1)}, u32[]{:S(2)}, u32[]{:S(2)}) collective-permute-start(bf16[16,16,128]{2,1,0:T(8,128)(2,1)S(1)} %get-tuple-element.128), channel_id=1, source_target_pairs={{0,8},{8,16},{16,24},{24,32},{32,40},{40,48},{48,56},{56,64},{64,7... | collective-permute-start | bytes 196616 | tf_op jit(solution)/shard_map/ppermute | solution.py:14
  222.6 8.7 %collective-permute-start.7 = (bf16[16,16,128]{2,1,0:T(8,128)(2,1)S(1)}, bf16[16,16,128]{2,1,0:T(8,128)(2,1)S(1)}, u32[]{:S(2)}, u32[]{:S(2)}) collective-permute-start(bf16[16,16,128]{2,1,0:T(8,128)(2,1)S(1)} %get-tuple-element.129), channel_id=1, source_target_pairs={{8,0},{16,8},{24,16},{32,24},{40,32},{48,40},{56,48},{64,56},{72,6... | collective-permute-start | bytes 196616 | tf_op jit(solution)/shard_map/ppermute | solution.py:14
  225.6 6.3 %collective-permute-start.14 = (bf16[16,16,128]{2,1,0:T(8,128)(2,1)S(1)}, bf16[16,16,128]{2,1,0:T(8,128)(2,1)S(1)}, u32[]{:S(2)}, u32[]{:S(2)}) collective-permute-start(bf16[16,16,128]{2,1,0:T(8,128)(2,1)S(1)} %get-tuple-element.126), channel_id=1, source_target_pairs={{0,8},{8,16},{16,24},{24,32},{32,40},{40,48},{48,56},{56,64},{64,7... | collective-permute-start | bytes 196616 | tf_op jit(solution)/shard_map/ppermute | solution.py:14
  229.3 6.1 %collective-permute-start.15 = (bf16[16,16,128]{2,1,0:T(8,128)(2,1)S(1)}, bf16[16,16,128]{2,1,0:T(8,128)(2,1)S(1)}, u32[]{:S(2)}, u32[]{:S(2)}) collective-permute-start(bf16[16,16,128]{2,1,0:T(8,128)(2,1)S(1)} %get-tuple-element.127), channel_id=1, source_target_pairs={{8,0},{16,8},{24,16},{32,24},{40,32},{48,40},{56,48},{64,56},{72,6... | collective-permute-start | bytes 196616 | tf_op jit(solution)/shard_map/ppermute | solution.py:14
  485.9 2.5 copy-start.7
  (13 other events, 15.0 us)
Sparse Core Ops, SparseCore 0:
  196.1 289.7 all-reduce.44
where the time goes:
time: 502 us; the launch traced here: 497 us
  waiting for transfers between devices  270 us (54%)
  starting transfers between devices  72.1 us (14%)
  local copies, waits for them, and re-layouts  70.1 us (14%)
  matrix products  37.5 us (7%)
  between operations  30.1 us (6%)
  other arithmetic  17.2 us (3%)
    psum x1, waiting for transfers between devices, per_device(): lax.psum((d_first.astype(jnp.float32), d_down.astype(jnp.float32), d_up.a...  250 us
    unnamed x94, local copies, waits for them, and re-layouts  37.2 us
    ppermute x8, starting transfers between devices, passed_along(): return lax.ppermute(block, axis, route)  36.9 us
    ppermute x4, starting transfers between devices, extended(): before = lax.ppermute(last, axis, up)  28.7 us
    ppermute x8, waiting for transfers between devices, passed_along(): return lax.ppermute(block, axis, route)  15.1 us
    pad x3, local copies, waits for them, and re-layouts, conv_down(): padded = jnp.pad(inputs, ((1, 1), (1, 1), (0, 0)))  14.1 us
    dot_general x27, matrix products, conv_down(): jnp.dot(window, kernel[row_tap, col_tap], preferred_element_type=jnp.floa...  12.5 us
    dot_general x27, matrix products, conv_same(): jnp.dot(window, kernel[row_tap, col_tap], preferred_element_type=jnp.floa...  10.1 us
  transfers between devices with their start and end apart: 17, of which 4 were waited for; matrix products, arithmetic and copies ran while one was open for 7% of the time, Pallas kernels for 0%

commit v1 on v0

--- a/solution.py
+++ b/solution.py
@@ -3,9 +3,11 @@
 import jax
 import jax.numpy as jnp
 from jax import lax
-from jax.sharding import PartitionSpec as P
+from jax.sharding import Mesh, PartitionSpec as P
 
 MARGIN = 8
+ROW = ("x", "zh")
+COL = ("y", "zl", "core")
 
 
 def passed_along(block, axis, distance):
@@ -85,7 +87,7 @@
     summed = canvas
     for heading in (1, -1):
         strip = canvas[tile_h + edge :] if heading == 1 else canvas[:edge]
-        arrived = passed_along(strip.astype(jnp.bfloat16), "row", heading).astype(strip.dtype)
+        arrived = passed_along(strip.astype(jnp.bfloat16), ROW, heading).astype(strip.dtype)
         if heading == 1:
             summed = summed.at[edge : 2 * edge].add(arrived)
         else:
@@ -94,7 +96,7 @@
     result = middle
     for heading in (1, -1):
         strip = middle[:, tile_w + edge :] if heading == 1 else middle[:, :edge]
-        arrived = passed_along(strip.astype(jnp.bfloat16), "col", heading).astype(strip.dtype)
+        arrived = passed_along(strip.astype(jnp.bfloat16), COL, heading).astype(strip.dtype)
         if heading == 1:
             result = result.at[:, edge : 2 * edge].add(arrived)
         else:
@@ -132,16 +134,41 @@
     return total
 
 
+def scattered(x, axes):
+    size = lax.axis_size(axes)
+    parts = x.reshape(size, x.shape[0] // size, x.shape[1])
+    got = lax.all_to_all(parts, axes, 0, 0, tiled=True)
+    return got.astype(jnp.float32).sum(0).astype(jnp.bfloat16)
+
+
+def gathered(x, axes):
+    size = lax.axis_size(axes)
+    parts = jnp.broadcast_to(x[None], (size,) + x.shape)
+    return lax.all_to_all(parts, axes, 0, 0, tiled=True)
+
+
+def summed_over_mesh(flat):
+    rows = flat.shape[0]
+    part = jnp.pad(flat, ((0, -rows % 512), (0, 0)))
+    part = scattered(part, "core")
+    part = scattered(part, "x")
+    part = scattered(part, "y")
+    part = gathered(part, ("zl", "zh")).astype(jnp.float32).sum(0).astype(jnp.bfloat16)
+    for axis in ("y", "x", "core"):
+        part = gathered(part, axis).reshape(-1, part.shape[1])
+    return part
+
+
 def per_device(field, cotangent, w_first, w_down, w_up, offsets, blend_table):
     tile_h, tile_w, chans = field.shape
     patch_h, patch_w = blend_table.shape
     edge = 2 * MARGIN
-    rows_n = lax.axis_size("row")
-    cols_n = lax.axis_size("col")
-    row_at = lax.axis_index("row")
-    col_at = lax.axis_index("col")
+    rows_n = lax.axis_size(ROW)
+    cols_n = lax.axis_size(COL)
+    row_at = lax.axis_index(ROW)
+    col_at = lax.axis_index(COL)
     table_f = blend_table.astype(jnp.float32)
-    grown = extended(field, (("row", 0), ("col", 1)), edge)
+    grown = extended(field, ((ROW, 0), (COL, 1)), edge)
     own_shift = offsets[row_at, col_at]
     start_r = MARGIN + own_shift[0]
     start_c = MARGIN + own_shift[1]
@@ -157,7 +184,7 @@
         offsets, table_f, row_at, col_at, rows_n, cols_n, tile_h, tile_w, 0, 1
     )
     ratio = cotangent.astype(jnp.float32) / weight_sum[:, :, None]
-    ratio_grown = extended(ratio.astype(jnp.bfloat16), (("row", 0), ("col", 1)), edge).astype(
+    ratio_grown = extended(ratio.astype(jnp.bfloat16), ((ROW, 0), (COL, 1)), edge).astype(
         ratio.dtype
     )
     blended = (numer / weight_sum[:, :, None]).astype(jnp.bfloat16)
@@ -169,19 +196,26 @@
         empty, d_patch.astype(jnp.float32), (start_r, start_c, zero)
     )
     field_grad = return_margins(d_canvas, tile_h, tile_w, edge)
-    g_first, g_down, g_up = lax.psum(
-        (d_first.astype(jnp.float32), d_down.astype(jnp.float32), d_up.astype(jnp.float32)),
-        ("col", "row"),
-    )
+    flat = jnp.concatenate(
+        [d_first.reshape(-1, 128), d_down.reshape(-1, 128), d_up.reshape(-1, 128)], axis=0
+    )
+    total = summed_over_mesh(flat)
+    n_first, n_down = d_first.size // 128, d_down.size // 128
+    g_first = total[:n_first].reshape(d_first.shape).astype(jnp.float32)
+    g_down = total[n_first : n_first + n_down].reshape(d_down.shape).astype(jnp.float32)
+    g_up = total[n_first + n_down : n_first + n_down + d_up.size // 128]
+    g_up = g_up.reshape(d_up.shape).astype(jnp.float32)
     scale = 1.0 / math.sqrt(tile_h * rows_n * tile_w * cols_n)
     return (blended, field_grad, g_first * scale, g_down * scale, g_up * scale)
 
 
 def solution(mesh):
+    fine = Mesh(mesh.devices.reshape(8, 4, 2, 4, 2), ("y", "zl", "core", "x", "zh"))
+    tiles = P(ROW, COL, None)
     return jax.shard_map(
         per_device,
-        mesh=mesh,
-        in_specs=(P("row", "col", None), P("row", "col", None), P(), P(), P(), P(), P()),
-        out_specs=(P("row", "col", None), P("row", "col", None), P(), P(), P()),
+        mesh=fine,
+        in_specs=(tiles, tiles, P(), P(), P(), P(), P()),
+        out_specs=(tiles, tiles, P(), P(), P()),
         check_vma=False,
     )

time: 502 us -> 274 us (0.55)
  waiting for transfers between devices: 270 us -> 19.1 us
  starting transfers between devices: 72.1 us -> 105 us
  between operations: 30.1 us -> 16.9 us
  blocking collectives: 0 us -> 12.9 us
    psum x1 -> x0, waiting for transfers between devices: 250 us -> none  [per_device(): lax.psum((d_first.astype(jnp.float32), d_down.astype(jnp.float32), d_up.a...]
    all_to_all x0 -> x5, starting transfers between devices: none -> 37.1 us  [the longest x3 18.7 us: gathered(): return lax.all_to_all(parts, axes, 0, 0, tiled=True)]
    ppermute x8, waiting for transfers between devices: 15.1 us -> 0.02 us  [passed_along(): return lax.ppermute(block, axis, route)]
    all_to_all x0 -> x5, waiting for transfers between devices: none -> 13.5 us  [the longest x3 7.3 us: gathered(): return lax.all_to_all(parts, axes, 0, 0, tiled=True)]
    all_to_all x0 -> x2, blocking collectives: none -> 12.9 us  [the longest x1 8.43 us: gathered(): return lax.all_to_all(parts, axes, 0, 0, tiled=True)]
    unnamed x94 -> x102, local copies, waits for them, and re-layouts: 37.2 us -> 35.2 us
  transfers between devices with their start and end apart: 17 -> 21, of which waited for: 4 -> 4; matrix products, arithmetic and copies ran while one was open for 7% -> 13% of each run, Pallas kernels for 0% -> 0%
where the time goes in v1:
time: 274 us; the launch traced here: 270 us
  starting transfers between devices  105 us (38%)
  local copies, waits for them, and re-layouts  68.9 us (25%)
  matrix products  34.5 us (13%)
  waiting for transfers between devices  19.1 us (7%)
  between operations  16.9 us (6%)
  blocking collectives  12.9 us (5%)
  other arithmetic  12.6 us (5%)
    unnamed x102, local copies, waits for them, and re-layouts  35.2 us
    ppermute x8, starting transfers between devices, passed_along(): return lax.ppermute(block, axis, route)  32.8 us
    ppermute x4, starting transfers between devices, extended(): before = lax.ppermute(last, axis, up)  28.8 us
    all_to_all x3, starting transfers between devices, gathered(): return lax.all_to_all(parts, axes, 0, 0, tiled=True)  18.7 us
    all_to_all x2, starting transfers between devices, scattered(): got = lax.all_to_all(parts, axes, 0, 0, tiled=True)  18.3 us
    dot_general x27, matrix products, conv_same(): jnp.dot(window, kernel[row_tap, col_tap], preferred_element_type=jnp.floa...  12.1 us
    pad x3, local copies, waits for them, and re-layouts, conv_down(): padded = jnp.pad(inputs, ((1, 1), (1, 1), (0, 0)))  11.2 us
    dot_general x27, matrix products, conv_down(): jnp.dot(window, kernel[row_tap, col_tap], preferred_element_type=jnp.floa...  9.38 us
  transfers between devices with their start and end apart: 21, of which 4 were waited for; matrix products, arithmetic and copies ran while one was open for 13% of the time, Pallas kernels for 0%

profile of v1, /device:TPU:1, one launch (start us, length us, event | category | flops | bytes accessed | tf_op | source)
XLA Modules:
  0.0 270.0 jit_solution(7700945318492553286)
XLA Ops:
  0.7 11.6 %collective-permute-start = (bf16[16,16,128]{2,1,0:T(8,128)(2,1)}, bf16[16,16,128]{2,1,0:T(8,128)(2,1)S(1)}, u32[]{:S(2)}, u32[]{:S(2)}) collective-permute-start(bf16[16,16,128]{2,1,0:T(8,128)(2,1)} %param.23), channel_id=1, source_target_pairs={{0,1},{1,2},{2,3},{3,4},{4,5},{5,6},{6,7},{8,9},{9,10},{10,11},{11... | collective-permute-start | bytes 196616 | tf_op jit(solution)/shard_map/ppermute | solution.py:26
  12.3 1.3 collective-permute-start.1
  13.6 1.0 constant_dynamic-slice_fusion
  39.8 3.9 %collective-permute-start.2 = (bf16[48,16,128]{2,1,0:T(8,128)(2,1)S(1)}, bf16[48,16,128]{2,1,0:T(8,128)(2,1)S(1)}, u32[]{:S(2)}, u32[]{:S(2)}) collective-permute-start(bf16[48,16,128]{2,1,0:T(8,128)(2,1)S(1)} %constant_dynamic-update-slice_fusion), channel_id=1, source_target_pairs={{0,8},{8,16},{16,24},{24,32},{32,40},{40,48},{48,56},{56,64},{64,7... | collective-permute-start | bytes 589832 | tf_op jit(solution)/shard_map/ppermute | solution.py:26
  43.7 1.9 collective-permute-start.3
  45.8 8.1 %collective-permute-start.8 = (bf16[16,16,128]{2,1,0:T(8,128)(2,1)S(1)}, bf16[16,16,128]{2,1,0:T(8,128)(2,1)S(1)}, u32[]{:S(2)}, u32[]{:S(2)}) collective-permute-start(bf16[16,16,128]{2,1,0:T(8,128)(2,1)S(1)} %divide_convert_fusion), channel_id=1, source_target_pairs={{0,1},{1,2},{2,3},{3,4},{4,5},{5,6},{6,7},{8,9},{9,10},{10,11},{11... | collective-permute-start | bytes 196616 | tf_op jit(solution)/shard_map/ppermute | solution.py:26
  53.9 1.3 collective-permute-start.9
  57.8 5.6 %collective-permute-done.9 = bf16[16,16,128]{2,1,0:T(8,128)(2,1)S(1)} collective-permute-done((bf16[16,16,128]{2,1,0:T(8,128)(2,1)S(1)}, bf16[16,16,128]{2,1,0:T(8,128)(2,1)S(1)}, u32[]{:S(2)}, u32[]{:S(2)}) %collective-permute-start.9) | collective-permute-done | bytes 65568 | tf_op jit(solution)/shard_map/ppermute | solution.py:27
  63.4 5.2 %collective-permute-start.10 = (bf16[48,16,128]{2,1,0:T(8,128)(2,1)S(1)}, bf16[48,16,128]{2,1,0:T(8,128)(2,1)S(1)}, u32[]{:S(2)}, u32[]{:S(2)}) collective-permute-start(bf16[48,16,128]{2,1,0:T(8,128)(2,1)S(1)} %pad_maximum_fusion.1), channel_id=1, source_target_pairs={{0,8},{8,16},{16,24},{24,32},{32,40},{40,48},{48,56},{56,64},{64,7... | collective-permute-start | bytes 589832 | tf_op jit(solution)/shard_map/ppermute | solution.py:26
  68.6 1.9 collective-permute-start.11
  80.9 1.4 convert_multiply_fusion.5
  90.8 5.6 %pad.160 = bf16[34,34,128]{2,1,0:T(8,128)(2,1)S(1)} pad(bf16[16,16,128]{2,1,0:T(8,128)(2,1)} %bitcast.527, bf16[]{:T(256)} %constant.259.clone.1), padding=2_1_1x0_3_1x0_0_0 | pad | bytes 361474 | tf_op jit(solution)/shard_map/transpose(jvp())/pad | solution.py:55
  96.5 8.5 %pad.359 = bf16[33,33,128]{2,1,0:T(8,128)(2,1)} pad(bf16[16,16,128]{2,1,0:T(8,128)(2,1)} %bitcast.526, bf16[]{:T(256)} %constant.259.clone.1), padding=0_2_1x0_2_1x0_0_0 | pad | bytes 344322
  104.9 8.5 %pad.362 = bf16[32,33,128]{2,1,0:T(8,128)(2,1)} pad(bf16[16,16,128]{2,1,0:T(8,128)(2,1)} %bitcast.533, bf16[]{:T(256)} %constant.259.clone.1), padding=0_1_1x0_2_1x0_0_0 | pad | bytes 335874
  113.4 8.4 %pad.360 = bf16[33,32,128]{2,1,0:T(8,128)(2,1)} pad(bf16[16,16,128]{2,1,0:T(8,128)(2,1)} %bitcast.532, bf16[]{:T(256)} %constant.259.clone.1), padding=0_2_1x0_1_1x0_0_0 | pad | bytes 335874
  121.8 5.6 %pad.361 = bf16[33,32,128]{2,1,0:T(8,128)(2,1)} pad(bf16[16,16,128]{2,1,0:T(8,128)(2,1)S(1)} %bitcast.531, bf16[]{:T(256)} %constant.259.clone.1), padding=0_2_1x1_0_1x0_0_0 | pad | bytes 335874
  127.4 5.6 %pad.222 = bf16[32,32,128]{2,1,0:T(8,128)(2,1)} pad(bf16[16,16,128]{2,1,0:T(8,128)(2,1)S(1)} %bitcast.525, bf16[]{:T(256)} %constant.259.clone.1), padding=0_1_1x1_0_1x0_0_0 | pad | bytes 327682 | tf_op jit(solution)/shard_map/transpose(jvp(jit(_pad)))/pad | solution.py:49
  133.0 5.6 %pad.223 = bf16[32,32,128]{2,1,0:T(8,128)(2,1)} pad(bf16[16,16,128]{2,1,0:T(8,128)(2,1)S(1)} %bitcast.524, bf16[]{:T(256)} %constant.259.clone.1), padding=0_1_1x0_1_1x0_0_0 | pad | bytes 327682 | tf_op jit(solution)/shard_map/transpose(jvp(jit(_pad)))/pad | solution.py:49
  139.8 1.7 fusion.57
  147.4 0.9 convolution_convert_fusion.8
  148.3 0.9 convolution_convert_fusion.7
  149.3 1.0 convolution_convert_fusion.6
  153.0 0.9 convolution_convert_fusion.3
  154.0 0.9 convolution_convert_fusion.2
  155.4 4.5 %all_to_all.35 = bf16[2,2304,128]{2,1,0:T(8,128)(2,1)S(1)} all-to-all(bf16[2,2304,128]{2,1,0:T(8,128)(2,1)S(1)} %bitcast.476), channel_id=1, replica_groups=mesh['y'=8,'zl'=4,'core'=2,'x'=4,'zh'=2] {'core'}, dimensions={0} | all-to-all | bytes 2359296 | tf_op jit(solution)/shard_map/all_to_all | solution.py:140
  159.9 1.2 reduce_sum.48
  161.1 3.5 %all-to-all-start.1 = ((bf16[4,576,128]{2,1,0:T(8,128)(2,1)}), bf16[4,576,128]{2,1,0:T(8,128)(2,1)S(1)}, u32[]{:S(2)}, u32[]{:S(2)}) async-start(bf16[4,576,128]{2,1,0:T(8,128)(2,1)} %bitcast.146), calls=%async_computation.1 | async-start | bytes 1179648 | tf_op jit(solution)/shard_map/all_to_all | solution.py:140
  164.7 1.3 dynamic_update_slice.6
  168.1 6.2 %all-to-all-done.1 = bf16[4,576,128]{2,1,0:T(8,128)(2,1)S(1)} async-done(((bf16[4,576,128]{2,1,0:T(8,128)(2,1)}), bf16[4,576,128]{2,1,0:T(8,128)(2,1)S(1)}, u32[]{:S(2)}, u32[]{:S(2)}) %all-to-all-start.1) | async-done | bytes 589856 | tf_op jit(solution)/shard_map/all_to_all | solution.py:140
  175.1 14.9 %all-to-all-start.2 = ((bf16[8,72,128]{2,1,0:T(8,128)(2,1)}), bf16[8,72,128]{2,1,0:T(8,128)(2,1)S(1)}, u32[]{:S(2)}, u32[]{:S(2)}) async-start(bf16[8,72,128]{2,1,0:T(8,128)(2,1)} %bitcast.147), calls=%async_computation.2 | async-start | bytes 294912 | tf_op jit(solution)/shard_map/all_to_all | solution.py:140
  190.7 1.3 dynamic_update_slice.7
  192.1 4.5 %collective-permute-start.4 = (bf16[16,48,128]{2,1,0:T(8,128)(2,1)}, bf16[16,48,128]{2,1,0:T(8,128)(2,1)S(1)}, u32[]{:S(2)}, u32[]{:S(2)}) collective-permute-start(bf16[16,48,128]{2,1,0:T(8,128)(2,1)} %get-tuple-element.107), channel_id=1, source_target_pairs={{0,1},{1,2},{2,3},{3,4},{4,5},{5,6},{6,7},{8,9},{9,10},{10,11},{11... | collective-permute-start | bytes 589832 | tf_op jit(solution)/shard_map/ppermute | solution.py:16
  196.6 1.3 collective-permute-start.5
  198.6 8.6 %collective-permute-start.12 = (bf16[16,48,128]{2,1,0:T(8,128)(2,1)}, bf16[16,48,128]{2,1,0:T(8,128)(2,1)}, u32[]{:S(2)}, u32[]{:S(2)}) collective-permute-start(bf16[16,48,128]{2,1,0:T(8,128)(2,1)} %get-tuple-element.105), channel_id=1, source_target_pairs={{0,1},{1,2},{2,3},{3,4},{4,5},{5,6},{6,7},{8,9},{9,10},{10,11},{11... | collective-permute-start | bytes 589832 | tf_op jit(solution)/shard_map/ppermute | solution.py:16
  207.2 1.3 collective-permute-start.13
  209.2 7.3 %all-to-all-start.3 = ((bf16[8,72,128]{2,1,0:T(8,128)(2,1)}), bf16[8,72,128]{2,1,0:T(8,128)(2,1)S(1)}, u32[]{:S(2)}, u32[]{:S(2)}) async-start(bf16[8,72,128]{2,1,0:T(8,128)(2,1)} %broadcast_in_dim.158), calls=%async_computation.3 | async-start | bytes 294912 | tf_op jit(solution)/shard_map/all_to_all | solution.py:147
  217.2 1.1 fusion.210
  218.3 6.7 %collective-permute-start.6 = (bf16[16,16,128]{2,1,0:T(8,128)(2,1)S(1)}, bf16[16,16,128]{2,1,0:T(8,128)(2,1)S(1)}, u32[]{:S(2)}, u32[]{:S(2)}) collective-permute-start(bf16[16,16,128]{2,1,0:T(8,128)(2,1)S(1)} %get-tuple-element.125), channel_id=1, source_target_pairs={{0,8},{8,16},{16,24},{24,32},{32,40},{40,48},{48,56},{56,64},{64,7... | collective-permute-start | bytes 196616 | tf_op jit(solution)/shard_map/ppermute | solution.py:16
  225.0 1.9 collective-permute-start.7
  226.9 1.4 all-to-all-done.3
  229.1 6.9 %all-to-all-start.4 = ((bf16[8,72,128]{2,1,0:T(8,128)(2,1)}), bf16[8,72,128]{2,1,0:T(8,128)(2,1)S(1)}, u32[]{:S(2)}, u32[]{:S(2)}) async-start(bf16[8,72,128]{2,1,0:T(8,128)(2,1)} %broadcast_in_dim.159), calls=%async_computation.4 | async-start | bytes 294912 | tf_op jit(solution)/shard_map/all_to_all | solution.py:147
  236.0 1.1 fusion.208
  237.1 6.5 %collective-permute-start.14 = (bf16[16,16,128]{2,1,0:T(8,128)(2,1)S(1)}, bf16[16,16,128]{2,1,0:T(8,128)(2,1)S(1)}, u32[]{:S(2)}, u32[]{:S(2)}) collective-permute-start(bf16[16,16,128]{2,1,0:T(8,128)(2,1)S(1)} %get-tuple-element.123), channel_id=1, source_target_pairs={{0,8},{8,16},{16,24},{24,32},{32,40},{40,48},{48,56},{56,64},{64,7... | collective-permute-start | bytes 196616 | tf_op jit(solution)/shard_map/ppermute | solution.py:16
  243.7 1.9 collective-permute-start.15
  246.5 4.5 %all-to-all-start.5 = ((bf16[4,576,128]{2,1,0:T(8,128)(2,1)}), bf16[4,576,128]{2,1,0:T(8,128)(2,1)S(1)}, u32[]{:S(2)}, u32[]{:S(2)}) async-start(bf16[4,576,128]{2,1,0:T(8,128)(2,1)} %broadcast_in_dim.161), calls=%async_computation.5 | async-start | bytes 1179648 | tf_op jit(solution)/shard_map/all_to_all | solution.py:147
  252.5 5.9 %all-to-all-done.5 = bf16[4,576,128]{2,1,0:T(8,128)(2,1)S(1)} async-done(((bf16[4,576,128]{2,1,0:T(8,128)(2,1)}), bf16[4,576,128]{2,1,0:T(8,128)(2,1)S(1)}, u32[]{:S(2)}, u32[]{:S(2)}) %all-to-all-start.5) | async-done | bytes 589856 | tf_op jit(solution)/shard_map/all_to_all | solution.py:147
  258.4 8.4 %all_to_all.36 = bf16[2,2304,128]{2,1,0:T(8,128)(2,1)S(1)} all-to-all(bf16[2,2304,128]{2,1,0:T(8,128)(2,1)S(1)} %broadcast_in_dim.163), channel_id=1, replica_groups=mesh['y'=8,'zl'=4,'core'=2,'x'=4,'zh'=2] {'core'}, dimensions={0} | all-to-all | bytes 2359296 | tf_op jit(solution)/shard_map/all_to_all | solution.py:147
  268.6 1.3 mul.200
  (272 shorter events, 52.3 us)
Async XLA Ops:
  0.6 39.1 %copy-start.45 = (bf16[16,16,128]{2,1,0:T(8,128)(2,1)S(1)}, bf16[16,16,128]{2,1,0:T(8,128)(2,1)}, u32[]{:S(2)}) copy-start(bf16[16,16,128]{2,1,0:T(8,128)(2,1)} %param.23) | copy-start | bytes 196612
  0.6 57.1 %copy-start.47 = (s32[32,32]{1,0:T(8,128)S(1)}, s32[32,32]{1,0:T(8,128)}, u32[]{:S(2)}) copy-start(s32[32,32]{1,0:T(8,128)} %param.29) | copy-start | bytes 12292
  0.7 45.0 %copy-start.46 = (bf16[16,16,128]{2,1,0:T(8,128)(2,1)S(1)}, bf16[16,16,128]{2,1,0:T(8,128)(2,1)}, u32[]{:S(2)}) copy-start(bf16[16,16,128]{2,1,0:T(8,128)(2,1)} %param.24) | copy-start | bytes 196612
  0.7 39.0 %collective-permute-start = (bf16[16,16,128]{2,1,0:T(8,128)(2,1)}, bf16[16,16,128]{2,1,0:T(8,128)(2,1)S(1)}, u32[]{:S(2)}, u32[]{:S(2)}) collective-permute-start(bf16[16,16,128]{2,1,0:T(8,128)(2,1)} %param.23), channel_id=1, source_target_pairs={{0,1},{1,2},{2,3},{3,4},{4,5},{5,6},{6,7},{8,9},{9,10},{10,11},{11... | collective-permute-start | bytes 196616 | tf_op jit(solution)/shard_map/ppermute | solution.py:26
  12.3 27.5 %collective-permute-start.1 = (bf16[16,16,128]{2,1,0:T(8,128)(2,1)}, bf16[16,16,128]{2,1,0:T(8,128)(2,1)S(1)}, u32[]{:S(2)}, u32[]{:S(2)}) collective-permute-start(bf16[16,16,128]{2,1,0:T(8,128)(2,1)} %param.23), channel_id=1, source_target_pairs={{1,0},{2,1},{3,2},{4,3},{5,4},{6,5},{7,6},{9,8},{10,9},{11,10},{12... | collective-permute-start | bytes 196616 | tf_op jit(solution)/shard_map/ppermute | solution.py:27
  39.8 30.8 %collective-permute-start.2 = (bf16[48,16,128]{2,1,0:T(8,128)(2,1)S(1)}, bf16[48,16,128]{2,1,0:T(8,128)(2,1)S(1)}, u32[]{:S(2)}, u32[]{:S(2)}) collective-permute-start(bf16[48,16,128]{2,1,0:T(8,128)(2,1)S(1)} %constant_dynamic-update-slice_fusion), channel_id=1, source_target_pairs={{0,8},{8,16},{16,24},{24,32},{32,40},{40,48},{48,56},{56,64},{64,7... | collective-permute-start | bytes 589832 | tf_op jit(solution)/shard_map/ppermute | solution.py:26
  43.7 26.8 %collective-permute-start.3 = (bf16[48,16,128]{2,1,0:T(8,128)(2,1)S(1)}, bf16[48,16,128]{2,1,0:T(8,128)(2,1)S(1)}, u32[]{:S(2)}, u32[]{:S(2)}) collective-permute-start(bf16[48,16,128]{2,1,0:T(8,128)(2,1)S(1)} %constant_dynamic-update-slice_fusion), channel_id=1, source_target_pairs={{8,0},{16,8},{24,16},{32,24},{40,32},{48,40},{56,48},{64,56},{72,6... | collective-permute-start | bytes 589832 | tf_op jit(solution)/shard_map/ppermute | solution.py:27
  45.8 12.0 %collective-permute-start.8 = (bf16[16,16,128]{2,1,0:T(8,128)(2,1)S(1)}, bf16[16,16,128]{2,1,0:T(8,128)(2,1)S(1)}, u32[]{:S(2)}, u32[]{:S(2)}) collective-permute-start(bf16[16,16,128]{2,1,0:T(8,128)(2,1)S(1)} %divide_convert_fusion), channel_id=1, source_target_pairs={{0,1},{1,2},{2,3},{3,4},{4,5},{5,6},{6,7},{8,9},{9,10},{10,11},{11... | collective-permute-start | bytes 196616 | tf_op jit(solution)/shard_map/ppermute | solution.py:26
  53.9 9.5 %collective-permute-start.9 = (bf16[16,16,128]{2,1,0:T(8,128)(2,1)S(1)}, bf16[16,16,128]{2,1,0:T(8,128)(2,1)S(1)}, u32[]{:S(2)}, u32[]{:S(2)}) collective-permute-start(bf16[16,16,128]{2,1,0:T(8,128)(2,1)S(1)} %divide_convert_fusion), channel_id=1, source_target_pairs={{1,0},{2,1},{3,2},{4,3},{5,4},{6,5},{7,6},{9,8},{10,9},{11,10},{12... | collective-permute-start | bytes 196616 | tf_op jit(solution)/shard_map/ppermute | solution.py:27
  63.4 17.5 %collective-permute-start.10 = (bf16[48,16,128]{2,1,0:T(8,128)(2,1)S(1)}, bf16[48,16,128]{2,1,0:T(8,128)(2,1)S(1)}, u32[]{:S(2)}, u32[]{:S(2)}) collective-permute-start(bf16[48,16,128]{2,1,0:T(8,128)(2,1)S(1)} %pad_maximum_fusion.1), channel_id=1, source_target_pairs={{0,8},{8,16},{16,24},{24,32},{32,40},{40,48},{48,56},{56,64},{64,7... | collective-permute-start | bytes 589832 | tf_op jit(solution)/shard_map/ppermute | solution.py:26
  68.6 12.3 %collective-permute-start.11 = (bf16[48,16,128]{2,1,0:T(8,128)(2,1)S(1)}, bf16[48,16,128]{2,1,0:T(8,128)(2,1)S(1)}, u32[]{:S(2)}, u32[]{:S(2)}) collective-permute-start(bf16[48,16,128]{2,1,0:T(8,128)(2,1)S(1)} %pad_maximum_fusion.1), channel_id=1, source_target_pairs={{8,0},{16,8},{24,16},{32,24},{40,32},{48,40},{56,48},{64,56},{72,6... | collective-permute-start | bytes 589832 | tf_op jit(solution)/shard_map/ppermute | solution.py:27
  73.7 3.8 %copy-start = (bf16[3,3,128,256]{3,2,1,0:T(8,128)(2,1)S(1)}, bf16[3,3,128,256]{3,2,1,0:T(8,128)(2,1)}, u32[]{:S(2)}) copy-start(bf16[3,3,128,256]{3,2,1,0:T(8,128)(2,1)} %param.26) | copy-start | bytes 1769476
  74.4 3.7 %copy-start.32 = (bf16[16,16,128]{2,1,0:T(8,128)(2,1)}, bf16[16,16,128]{2,1,0:T(8,128)(2,1)S(1)}, u32[]{:S(2)}) copy-start(bf16[16,16,128]{2,1,0:T(8,128)(2,1)S(1)} %slice.456) | copy-start | bytes 196612
  74.8 3.4 %copy-start.18 = (bf16[16,16,128]{2,1,0:T(8,128)(2,1)}, bf16[16,16,128]{2,1,0:T(8,128)(2,1)S(1)}, u32[]{:S(2)}) copy-start(bf16[16,16,128]{2,1,0:T(8,128)(2,1)S(1)} %slice.458) | copy-start | bytes 196612
  75.2 3.0 %copy-start.20 = (bf16[16,16,128]{2,1,0:T(8,128)(2,1)}, bf16[16,16,128]{2,1,0:T(8,128)(2,1)S(1)}, u32[]{:S(2)}) copy-start(bf16[16,16,128]{2,1,0:T(8,128)(2,1)S(1)} %slice.460) | copy-start | bytes 196612
  75.5 2.6 copy-start.22
  75.9 2.4 copy-start.24
  76.4 2.2 copy-start.26
  76.7 2.0 copy-start.28
  77.1 1.8 copy-start.30
  77.5 1.5 copy-start.41
  79.3 4.1 %copy-start.36 = (f32[256,256]{1,0:T(8,128)}, f32[256,256]{1,0:T(8,128)S(1)}, u32[]{:S(2)}) copy-start(f32[256,256]{1,0:T(8,128)S(1)} %get-tuple-element.160) | copy-start | bytes 786436
  82.6 1.8 copy-start.1
  90.4 31.4 %copy-start.43 = (bf16[256,128]{1,0:T(8,128)(2,1)S(1)}, bf16[256,128]{1,0:T(8,128)(2,1)}, u32[]{:S(2)}) copy-start(bf16[256,128]{1,0:T(8,128)(2,1)} %convolution_convert_fusion.19) | copy-start | bytes 196612
  90.6 36.8 %copy-start.40 = (bf16[256,128]{1,0:T(8,128)(2,1)S(1)}, bf16[256,128]{1,0:T(8,128)(2,1)}, u32[]{:S(2)}) copy-start(bf16[256,128]{1,0:T(8,128)(2,1)} %convolution_convert_fusion.22) | copy-start | bytes 196612
  90.8 42.1 %copy-start.39 = (bf16[256,128]{1,0:T(8,128)(2,1)S(1)}, bf16[256,128]{1,0:T(8,128)(2,1)}, u32[]{:S(2)}) copy-start(bf16[256,128]{1,0:T(8,128)(2,1)} %convolution_convert_fusion.21) | copy-start | bytes 196612
  143.7 1.5 copy-start.27
  143.7 1.7 copy-start.25
  144.0 1.6 copy-start.23
  144.0 1.8 copy-start.21
  144.4 1.6 copy-start.19
  144.5 1.7 copy-start.33
  144.8 1.9 copy-start.2
  145.4 1.7 copy-start.35
  145.6 1.8 copy-start.4
  161.1 13.2 %all-to-all-start.1 = ((bf16[4,576,128]{2,1,0:T(8,128)(2,1)}), bf16[4,576,128]{2,1,0:T(8,128)(2,1)S(1)}, u32[]{:S(2)}, u32[]{:S(2)}) async-start(bf16[4,576,128]{2,1,0:T(8,128)(2,1)} %bitcast.146), calls=%async_computation.1 | async-start | bytes 1179648 | tf_op jit(solution)/shard_map/all_to_all | solution.py:140
  175.1 33.4 %all-to-all-start.2 = ((bf16[8,72,128]{2,1,0:T(8,128)(2,1)}), bf16[8,72,128]{2,1,0:T(8,128)(2,1)S(1)}, u32[]{:S(2)}, u32[]{:S(2)}) async-start(bf16[8,72,128]{2,1,0:T(8,128)(2,1)} %bitcast.147), calls=%async_computation.2 | async-start | bytes 294912 | tf_op jit(solution)/shard_map/all_to_all | solution.py:140
  192.1 24.4 %collective-permute-start.4 = (bf16[16,48,128]{2,1,0:T(8,128)(2,1)}, bf16[16,48,128]{2,1,0:T(8,128)(2,1)S(1)}, u32[]{:S(2)}, u32[]{:S(2)}) collective-permute-start(bf16[16,48,128]{2,1,0:T(8,128)(2,1)} %get-tuple-element.107), channel_id=1, source_target_pairs={{0,1},{1,2},{2,3},{3,4},{4,5},{5,6},{6,7},{8,9},{9,10},{10,11},{11... | collective-permute-start | bytes 589832 | tf_op jit(solution)/shard_map/ppermute | solution.py:16
  196.6 20.5 %collective-permute-start.5 = (bf16[16,48,128]{2,1,0:T(8,128)(2,1)S(1)}, bf16[16,48,128]{2,1,0:T(8,128)(2,1)}, u32[]{:S(2)}, u32[]{:S(2)}) collective-permute-start(bf16[16,48,128]{2,1,0:T(8,128)(2,1)S(1)} %get-tuple-element.108), channel_id=1, source_target_pairs={{1,0},{2,1},{3,2},{4,3},{5,4},{6,5},{7,6},{9,8},{10,9},{11,10},{12... | collective-permute-start | bytes 589832 | tf_op jit(solution)/shard_map/ppermute | solution.py:16
  198.6 37.4 %collective-permute-start.12 = (bf16[16,48,128]{2,1,0:T(8,128)(2,1)}, bf16[16,48,128]{2,1,0:T(8,128)(2,1)}, u32[]{:S(2)}, u32[]{:S(2)}) collective-permute-start(bf16[16,48,128]{2,1,0:T(8,128)(2,1)} %get-tuple-element.105), channel_id=1, source_target_pairs={{0,1},{1,2},{2,3},{3,4},{4,5},{5,6},{6,7},{8,9},{9,10},{10,11},{11... | collective-permute-start | bytes 589832 | tf_op jit(solution)/shard_map/ppermute | solution.py:16
  207.2 28.8 %collective-permute-start.13 = (bf16[16,48,128]{2,1,0:T(8,128)(2,1)S(1)}, bf16[16,48,128]{2,1,0:T(8,128)(2,1)}, u32[]{:S(2)}, u32[]{:S(2)}) collective-permute-start(bf16[16,48,128]{2,1,0:T(8,128)(2,1)S(1)} %get-tuple-element.106), channel_id=1, source_target_pairs={{1,0},{2,1},{3,2},{4,3},{5,4},{6,5},{7,6},{9,8},{10,9},{11,10},{12... | collective-permute-start | bytes 589832 | tf_op jit(solution)/shard_map/ppermute | solution.py:16
  209.2 19.2 %all-to-all-start.3 = ((bf16[8,72,128]{2,1,0:T(8,128)(2,1)}), bf16[8,72,128]{2,1,0:T(8,128)(2,1)S(1)}, u32[]{:S(2)}, u32[]{:S(2)}) async-start(bf16[8,72,128]{2,1,0:T(8,128)(2,1)} %broadcast_in_dim.158), calls=%async_computation.3 | async-start | bytes 294912 | tf_op jit(solution)/shard_map/all_to_all | solution.py:147
  218.3 32.8 %collective-permute-start.6 = (bf16[16,16,128]{2,1,0:T(8,128)(2,1)S(1)}, bf16[16,16,128]{2,1,0:T(8,128)(2,1)S(1)}, u32[]{:S(2)}, u32[]{:S(2)}) collective-permute-start(bf16[16,16,128]{2,1,0:T(8,128)(2,1)S(1)} %get-tuple-element.125), channel_id=1, source_target_pairs={{0,8},{8,16},{16,24},{24,32},{32,40},{40,48},{48,56},{56,64},{64,7... | collective-permute-start | bytes 196616 | tf_op jit(solution)/shard_map/ppermute | solution.py:16
  225.0 26.1 %collective-permute-start.7 = (bf16[16,16,128]{2,1,0:T(8,128)(2,1)S(1)}, bf16[16,16,128]{2,1,0:T(8,128)(2,1)S(1)}, u32[]{:S(2)}, u32[]{:S(2)}) collective-permute-start(bf16[16,16,128]{2,1,0:T(8,128)(2,1)S(1)} %get-tuple-element.126), channel_id=1, source_target_pairs={{8,0},{16,8},{24,16},{32,24},{40,32},{48,40},{56,48},{64,56},{72,6... | collective-permute-start | bytes 196616 | tf_op jit(solution)/shard_map/ppermute | solution.py:16
  229.1 16.5 %all-to-all-start.4 = ((bf16[8,72,128]{2,1,0:T(8,128)(2,1)}), bf16[8,72,128]{2,1,0:T(8,128)(2,1)S(1)}, u32[]{:S(2)}, u32[]{:S(2)}) async-start(bf16[8,72,128]{2,1,0:T(8,128)(2,1)} %broadcast_in_dim.159), calls=%async_computation.4 | async-start | bytes 294912 | tf_op jit(solution)/shard_map/all_to_all | solution.py:147
  237.1 14.7 %collective-permute-start.14 = (bf16[16,16,128]{2,1,0:T(8,128)(2,1)S(1)}, bf16[16,16,128]{2,1,0:T(8,128)(2,1)S(1)}, u32[]{:S(2)}, u32[]{:S(2)}) collective-permute-start(bf16[16,16,128]{2,1,0:T(8,128)(2,1)S(1)} %get-tuple-element.123), channel_id=1, source_target_pairs={{0,8},{8,16},{16,24},{24,32},{32,40},{40,48},{48,56},{56,64},{64,7... | collective-permute-start | bytes 196616 | tf_op jit(solution)/shard_map/ppermute | solution.py:16
  243.7 8.1 %collective-permute-start.15 = (bf16[16,16,128]{2,1,0:T(8,128)(2,1)S(1)}, bf16[16,16,128]{2,1,0:T(8,128)(2,1)S(1)}, u32[]{:S(2)}, u32[]{:S(2)}) collective-permute-start(bf16[16,16,128]{2,1,0:T(8,128)(2,1)S(1)} %get-tuple-element.124), channel_id=1, source_target_pairs={{8,0},{16,8},{24,16},{32,24},{40,32},{48,40},{56,48},{64,56},{72,6... | collective-permute-start | bytes 196616 | tf_op jit(solution)/shard_map/ppermute | solution.py:16
  246.5 11.8 %all-to-all-start.5 = ((bf16[4,576,128]{2,1,0:T(8,128)(2,1)}), bf16[4,576,128]{2,1,0:T(8,128)(2,1)S(1)}, u32[]{:S(2)}, u32[]{:S(2)}) async-start(bf16[4,576,128]{2,1,0:T(8,128)(2,1)} %broadcast_in_dim.161), calls=%async_computation.5 | async-start | bytes 1179648 | tf_op jit(solution)/shard_map/all_to_all | solution.py:147
  (21 other events, 24.3 us)

commit v2 on v1

v2 whole, which is shorter than its diff:
```python
import math

import jax
import jax.numpy as jnp
from jax import lax
from jax.experimental import pallas as pl
from jax.experimental.pallas import tpu as pltpu
from jax.sharding import Mesh, PartitionSpec as P

MARGIN = 8
ROW = ("x", "zh")
COL = ("y", "zl", "core")
F32 = jnp.float32
BF16 = jnp.bfloat16
REACH = 2
FAR = 1000
TILE = 16
C1 = 128
C2 = 256
FIRST_ROWS = 9 * C1
DOWN_ROWS = 18 * C1
UP_ROWS = 4 * C2
FLAT_ROWS = 4608


def dot(a, b):
    return lax.dot_general(a, b, (((1,), (0,)), ((), ())), preferred_element_type=F32)


def dot_nt(a, b):
    return lax.dot_general(a, b, (((1,), (1,)), ((), ())), preferred_element_type=F32)


def prepare_kernel(where, offsets, table, w_first, w_down, w_up, fb, rf, rft, rdt, ru):
    row_at, col_at = where[0], where[1]
    rows_n, cols_n = offsets.shape[0], offsets.shape[1] // 2
    sub = lax.broadcasted_iota(jnp.int32, (32, 32), 0)
    lane = lax.broadcasted_iota(jnp.int32, (32, 32), 1)
    column = jnp.where(sub < 16, 2 * sub, 2 * (sub - 16) + 1)
    table_t = table[...].astype(F32).T.astype(BF16)
    own_r = offsets[row_at, 2 * col_at]
    own_c = offsets[row_at, 2 * col_at + 1]
    total = jnp.zeros((32, 32), F32)
    own = jnp.zeros((32, 32), F32)
    for row_step in range(-REACH, REACH + 1):
        for col_step in range(-REACH, REACH + 1):
            near_r, near_c = row_at + row_step, col_at + col_step
            inside = (near_r >= 0) & (near_r < rows_n) & (near_c >= 0) & (near_c < cols_n)
            at_r = jnp.clip(near_r, 0, rows_n - 1)
            at_c = jnp.clip(near_c, 0, cols_n - 1)
            down_by = row_step * TILE + offsets[at_r, 2 * at_c] - own_r
            right_by = col_step * TILE + offsets[at_r, 2 * at_c + 1] - own_c
            down_by = jnp.where(inside, down_by, FAR)
            pick_c = (column - right_by == lane).astype(F32).astype(BF16)
            pick_r = (lane - down_by == sub).astype(F32).astype(BF16)
            placed = dot(pick_c, table_t)
            if row_step == 0 and col_step == 0:
                own = placed
            total = total + dot(placed.astype(BF16), pick_r)
    share = own / total
    for r in range(32):
        fb[r % 2, r // 2, :, :C1] = jnp.broadcast_to(share[:16, r : r + 1], (16, C1))
        fb[r % 2, r // 2, :, C1:] = jnp.broadcast_to(share[16:, r : r + 1], (16, C1))
    none = jnp.zeros((C1, C1), BF16)
    for t in range(3):
        for v in range(4):
            for b in range(2):
                rows, cols = pl.ds(v * C1, C1), pl.ds(b * C1, C1)
                held = 0 <= v - b <= 2
                rf[t, rows, cols] = w_first[t, v - b] if held else none
                rft[t, cols, rows] = w_first[2 - t, 2 - v + b] if held else none
        rdt[t, :C1, :C2] = w_down[t, 1]
        rdt[t, :C1, C2:] = jnp.zeros((C1, C2), BF16)
        rdt[t, C1:, :C2] = w_down[t, 2]
        rdt[t, C1:, C2:] = w_down[t, 0]
    for a in range(2):
        for b in range(2):
            ru[a, :, pl.ds(b * C1, C1)] = w_up[a, b]


def shifted(x, by):
    j = lax.broadcasted_iota(jnp.int32, x.shape, 0) % 16
    moved = pltpu.roll(x, by % x.shape[0], 0)
    return jnp.where(j == (0 if by > 0 else 15), 0.0, moved)


def spread(x):
    return jnp.concatenate(
        [shifted(x[:, C1:], 1).astype(BF16), x.astype(BF16), shifted(x[:, :C1], -1).astype(BF16)], axis=1
    )


def window(ref, a, t):
    part = ref[(a + t) % 2, (a + t) // 2 : (a + t) // 2 + 16]
    return part.reshape(256, part.shape[-1])


def net_kernel(
    start, left, middle, right, fb, rf, rft, wd, rdt, ru,
    up_o, mid_o, down_o, flat,
    fs, cs, xv, hv, gv, g4, gs, bs, can_b, can_g,
):
    start_r, start_c = start[0], start[1]
    for ref in (xv, hv, gv):
        edge = jnp.zeros((16, ref.shape[-1]), BF16)
        ref[0, 0] = edge
        ref[1, 16] = edge
    g4[16] = jnp.zeros((16, 2 * C2), BF16)

    def stage(r, carry):
        for k, ref in enumerate((left, middle, right)):
            cells = ref[start_r + r].astype(F32)
            fs[r, 8 + 16 * k : 24 + 16 * k, :] = cells[:, :C1]
            cs[r, 8 + 16 * k : 24 + 16 * k, :] = cells[:, C1:]
        return carry

    lax.fori_loop(0, 32, stage, 0, unroll=4)
    j = lax.broadcasted_iota(jnp.int32, (16, C1), 0)

    def load(i, carry):
        for a in range(2):
            r = 2 * i + a
            at = start_c + 8
            before = jnp.where(j == 0, 0.0, fs[r, pl.ds(at - 1, 16, 2), :])
            even = fs[r, pl.ds(at, 16, 2), :]
            odd = fs[r, pl.ds(at + 1, 16, 2), :]
            after = jnp.where(j == 15, 0.0, fs[r, pl.ds(at + 2, 16, 2), :])
            xv[1 - a, i + a] = jnp.concatenate([before, even, odd, after], axis=1).astype(BF16)
            gs[a, i, :, :C1] = cs[r, pl.ds(at, 16, 2), :] * fb[a, i, :, :C1]
            gs[a, i, :, C1:] = cs[r, pl.ds(at + 1, 16, 2), :] * fb[a, i, :, C1:]
        return carry

    lax.fori_loop(0, 16, load, 0, unroll=2)

    h, slope_h = [], []
    for a in range(2):
        pre = dot(window(xv, a, 0), rf[0]) + dot(window(xv, a, 1), rf[1]) + dot(window(xv, a, 2), rf[2])
        sig = lax.logistic(pre)
        value = pre * sig
        slope_h.append(sig + value * (1.0 - sig))
        h.append(value.astype(BF16))
        hv[1 - a, a : a + 16] = jnp.concatenate(
            [shifted(value[:, C1:], 1).astype(BF16), h[a]], axis=1
        ).reshape(16, 16, 3 * C1)
    pre = dot(window(hv, 0, 0), wd[0]) + dot(window(hv, 0, 1), wd[1]) + dot(window(hv, 0, 2), wd[2])
    sig = lax.logistic(pre)
    value = pre * sig
    slope_d = sig + value * (1.0 - sig)
    d = value.astype(BF16)
    d_t = value.T.astype(BF16)
    g_d = jnp.zeros((256, C2), F32)
    for a in range(2):
        out = h[a].astype(F32) + dot(d, ru[a])
        bs[a] = (fb[a].reshape(256, 2 * C1) * out).reshape(16, 16, 2 * C1)
        g = gs[a].reshape(256, 2 * C1).astype(BF16)
        g_d = g_d + dot_nt(g, ru[a])
        g_up = dot(d_t, g).astype(BF16)
        base = FIRST_ROWS + DOWN_ROWS + 2 * a * C2
        flat[base : base + C2] = g_up[:, :C1]
        flat[base + C2 : base + 2 * C2] = g_up[:, C1:]
    g_pre = g_d.astype(BF16).astype(F32) * slope_d
    g4[0:16] = jnp.concatenate([g_pre.astype(BF16), shifted(g_pre, -1).astype(BF16)], axis=1).reshape(
        16, 16, 2 * C2
    )
    g_pre_t = g_pre.T.astype(BF16)
    for t in range(3):
        g_down = dot(g_pre_t, window(hv, 0, t)).T.astype(BF16)
        base = FIRST_ROWS + 6 * t * C1
        flat[base : base + 3 * C1] = g_down[:, :C1]
        flat[base + 3 * C1 : base + 6 * C1] = g_down[:, C1:]
    here = g4[0:16].reshape(256, 2 * C2)
    below = g4[1:17].reshape(256, 2 * C2)
    g_h = [dot_nt(here, rdt[1]), dot_nt(here, rdt[2]) + dot_nt(below, rdt[0])]
    g_t = []
    for a in range(2):
        g_pre = (gs[a].reshape(256, 2 * C1) + g_h[a]) * slope_h[a]
        gv[1 - a, a : a + 16] = spread(g_pre).reshape(16, 16, 4 * C1)
        g_t.append(g_pre.T.astype(BF16))
    for t in range(3):
        g_first = dot(g_t[0], window(xv, 0, t)) + dot(g_t[1], window(xv, 1, t))
        for ct in range(3):
            block = (
                g_first[:C1, ct * C1 : (ct + 1) * C1] + g_first[C1:, (ct + 1) * C1 : (ct + 2) * C1]
            )
            base = (3 * t + ct) * C1
            flat[base : base + C1] = block.T.astype(BF16)
    flat[FIRST_ROWS + DOWN_ROWS + UP_ROWS :] = jnp.zeros(
        (FLAT_ROWS - FIRST_ROWS - DOWN_ROWS - UP_ROWS, C1), BF16
    )
    for a in range(2):
        g_x = (
            dot_nt(window(gv, a, 0), rft[0])
            + dot_nt(window(gv, a, 1), rft[1])
            + dot_nt(window(gv, a, 2), rft[2])
        )
        gs[a] = g_x.reshape(16, 16, 2 * C1)

    def clear(r, carry):
        can_b[r] = jnp.zeros((48, C1), F32)
        can_g[r] = jnp.zeros((48, C1), F32)
        return carry

    lax.fori_loop(0, 48, clear, 0, unroll=4)

    def place(i, carry):
        for a in range(2):
            r = start_r + 2 * i + a
            for b in range(2):
                can_b[r, pl.ds(start_c + b, 16, 2), :] = bs[a, i, :, b * C1 : (b + 1) * C1]
                can_g[r, pl.ds(start_c + b, 16, 2), :] = gs[a, i, :, b * C1 : (b + 1) * C1]
        return carry

    lax.fori_loop(0, 16, place, 0, unroll=2)

    def give(r, carry):
        up_o[r, :, :C1] = can_b[r].astype(BF16)
        up_o[r, :, C1:] = can_g[r].astype(BF16)
        mid_o[r, :, :C1] = can_b[r + 16]
        mid_o[r, :, C1:] = can_g[r + 16]
        down_o[r, :, :C1] = can_b[r + 32].astype(BF16)
        down_o[r, :, C1:] = can_g[r + 32].astype(BF16)
        return carry

    lax.fori_loop(0, 16, give, 0, unroll=2)


VMEM = pl.BlockSpec(memory_space=pltpu.VMEM)
SMEM = pl.BlockSpec(memory_space=pltpu.SMEM)


def prepared(where, offsets, table, w_first, w_down, w_up):
    return pl.pallas_call(
        prepare_kernel,
        out_shape=(
            jax.ShapeDtypeStruct((2, 16, 16, 2 * C1), F32),
            jax.ShapeDtypeStruct((3, 4 * C1, 2 * C1), BF16),
            jax.ShapeDtypeStruct((3, 2 * C1, 4 * C1), BF16),
            jax.ShapeDtypeStruct((3, 2 * C1, 2 * C2), BF16),
            jax.ShapeDtypeStruct((2, C2, 2 * C1), BF16),
        ),
        in_specs=[SMEM, SMEM, VMEM, VMEM, VMEM, VMEM],
        out_specs=[VMEM] * 5,
        compiler_params=pltpu.CompilerParams(vmem_limit_bytes=16 * 2**20),
        cost_estimate=pl.CostEstimate(flops=5 * 10**6, bytes_accessed=10**7, transcendentals=0),
        name="prepare",
    )(where, offsets, table, w_first, w_down, w_up)


def patch_work(start, left, middle, right, fb, rf, rft, wd, rdt, ru):
    strip = jax.ShapeDtypeStruct((16, 48, 2 * C1), BF16)
    return pl.pallas_call(
        net_kernel,
        out_shape=(
            strip,
            jax.ShapeDtypeStruct((16, 48, 2 * C1), F32),
            strip,
            jax.ShapeDtypeStruct((FLAT_ROWS, C1), BF16),
        ),
        in_specs=[SMEM] + [VMEM] * 9,
        out_specs=[VMEM] * 4,
        scratch_shapes=[
            pltpu.VMEM((32, 64, C1), F32),
            pltpu.VMEM((32, 64, C1), F32),
            pltpu.VMEM((2, 17, 16, 4 * C1), BF16),
            pltpu.VMEM((2, 17, 16, 3 * C1), BF16),
            pltpu.VMEM((2, 17, 16, 4 * C1), BF16),
            pltpu.VMEM((17, 16, 2 * C2), BF16),
            pltpu.VMEM((2, 16, 16, 2 * C1), F32),
            pltpu.VMEM((2, 16, 16, 2 * C1), F32),
            pltpu.VMEM((48, 48, C1), F32),
            pltpu.VMEM((48, 48, C1), F32),
        ],
        compiler_params=pltpu.CompilerParams(vmem_limit_bytes=40 * 2**20),
        cost_estimate=pl.CostEstimate(flops=2 * 10**9, bytes_accessed=10**7, transcendentals=200000),
        name="patch_work",
    )(start, left, middle, right, fb, rf, rft, wd, rdt, ru)


def neighbours(axes, before, after):
    size = lax.axis_size(axes)
    ahead = [(i, i + 1) for i in range(size - 1)]
    back = [(i + 1, i) for i in range(size - 1)]
    return lax.ppermute(before, axes, ahead), lax.ppermute(after, axes, back)


def scattered(x, axes):
    size = lax.axis_size(axes)
    parts = x.reshape(size, x.shape[0] // size, x.shape[1])
    got = lax.all_to_all(parts, axes, 0, 0, tiled=True)
    return got.astype(F32).sum(0).astype(BF16)


def gathered(x, axes):
    size = lax.axis_size(axes)
    parts = jnp.broadcast_to(x[None], (size,) + x.shape)
    return lax.all_to_all(parts, axes, 0, 0, tiled=True)


def summed_over_mesh(part):
    part = scattered(part, "core")
    part = scattered(part, "x")
    part = scattered(part, "y")
    part = gathered(part, ("zl", "zh")).astype(F32).sum(0).astype(BF16)
    for axis in ("y", "x", "core"):
        part = gathered(part, axis).reshape(-1, part.shape[1])
    return part


def per_device(field, cotangent, w_first, w_down, w_up, offsets, blend_table):
    rows_n = lax.axis_size(ROW)
    cols_n = lax.axis_size(COL)
    row_at = lax.axis_index(ROW)
    col_at = lax.axis_index(COL)
    where = jnp.stack([row_at, col_at]).astype(jnp.int32)
    both = jnp.concatenate([field, cotangent], axis=2)
    fb, rf, rft, rdt, ru = prepared(
        where, offsets.reshape(rows_n, 2 * cols_n), blend_table, w_first, w_down, w_up
    )
    above, under = neighbours(ROW, both, both)
    middle = jnp.concatenate([above, both, under], axis=0)
    left, right = neighbours(COL, middle, middle)
    start = MARGIN + offsets[row_at, col_at]
    up, mid, down, flat = patch_work(
        start, left, middle, right, fb, rf, rft, w_down.reshape(3, 3 * C1, C2), rdt, ru
    )
    from_above, from_under = neighbours(ROW, down, up)
    total = summed_over_mesh(flat)
    mid = mid + from_above.astype(F32) + from_under.astype(F32)
    from_left, from_right = neighbours(
        COL, mid[:, 32:].astype(BF16), mid[:, :16].astype(BF16)
    )
    own = mid[:, 16:32] + from_left.astype(F32) + from_right.astype(F32)
    blended = own[:, :, :C1].astype(BF16)
    field_grad = own[:, :, C1:]
    scale = 1.0 / math.sqrt(TILE * rows_n * TILE * cols_n)
    total = total.astype(F32) * scale
    g_first = total[:FIRST_ROWS].reshape(w_first.shape)
    g_down = total[FIRST_ROWS : FIRST_ROWS + DOWN_ROWS].reshape(3, 2, 3 * C1, C1)
    g_down = g_down.transpose(0, 2, 1, 3).reshape(w_down.shape)
    g_up = total[FIRST_ROWS + DOWN_ROWS : FIRST_ROWS + DOWN_ROWS + UP_ROWS].reshape(w_up.shape)
    return (blended, field_grad, g_first, g_down, g_up)


def solution(mesh):
    fine = Mesh(mesh.devices.reshape(8, 4, 2, 4, 2), ("y", "zl", "core", "x", "zh"))
    tiles = P(ROW, COL, None)
    return jax.shard_map(
        per_device,
        mesh=fine,
        in_specs=(tiles, tiles, P(), P(), P(), P(), P()),
        out_specs=(tiles, tiles, P(), P(), P()),
        check_vma=False,
    )
```

time: 274 us -> 163 us (0.59); the launches traced: 270 us -> 162 us
  local copies, waits for them, and re-layouts: 68.9 us -> 11 us
  starting transfers between devices: 105 us -> 51.5 us
  blocking collectives: 12.9 us -> 64.1 us
  matrix products: 34.5 us -> 0 us
  between operations: 16.9 us -> 0.88 us
  other arithmetic: 12.6 us -> 3.76 us
  Pallas kernels: 0 us -> 6.06 us
  waiting for transfers between devices: 19.1 us -> 24.4 us
    ppermute x16 -> x8, starting transfers between devices: 68 us -> 31.7 us  [neighbours(): return (lax.ppermute(before, axes, ahead), lax.ppermute(after, axes, back))]
    dot_general x84 -> x0, matrix products: 34.5 us -> none  [the longest x27 12.1 us: conv_same(): jnp.dot(window, kernel[row_tap, col_tap], preferred_element_type=jnp.floa...]
    unnamed x102 -> x12, local copies, waits for them, and re-layouts: 35.2 us -> 2.49 us
    all_to_all x1 -> x2, blocking collectives: 8.43 us -> 38.9 us  [gathered(): return lax.all_to_all(parts, axes, 0, 0, tiled=True)]
    all_to_all x1 -> x2, blocking collectives: 4.5 us -> 25.2 us  [scattered(): got = lax.all_to_all(parts, axes, 0, 0, tiled=True)]
    pad x6 -> x0, local copies, waits for them, and re-layouts: 17.2 us -> none  [the longest x3 11.2 us: conv_down(): padded = jnp.pad(inputs, ((1, 1), (1, 1), (0, 0)))]
    all_to_all x2 -> x1, starting transfers between devices: 18.3 us -> 9.66 us  [scattered(): got = lax.all_to_all(parts, axes, 0, 0, tiled=True)]
    all_to_all x3 -> x2, starting transfers between devices: 18.7 us -> 10.1 us  [gathered(): return lax.all_to_all(parts, axes, 0, 0, tiled=True)]
  transfers between devices with their start and end apart: 21 -> 11, of which waited for: 4 -> 7; matrix products, arithmetic and copies ran while one was open for 13% -> 3% of each run, Pallas kernels for 0% -> 1%
where the time goes in v2:
time: 163 us; the launch traced here: 162 us
  blocking collectives  64.1 us (39%)
  starting transfers between devices  51.5 us (32%)
  waiting for transfers between devices  24.4 us (15%)
  local copies, waits for them, and re-layouts  11 us (7%)
  Pallas kernels  6.06 us (4%)
  other arithmetic  3.76 us (2%)
    all_to_all x2, blocking collectives, gathered(): return lax.all_to_all(parts, axes, 0, 0, tiled=True)  38.9 us
    ppermute x8, starting transfers between devices, neighbours(): return (lax.ppermute(before, axes, ahead), lax.ppermute(after, axes, back))  31.7 us
    all_to_all x2, blocking collectives, scattered(): got = lax.all_to_all(parts, axes, 0, 0, tiled=True)  25.2 us
    ppermute x8, waiting for transfers between devices, neighbours(): return (lax.ppermute(before, axes, ahead), lax.ppermute(after, axes, back))  13.9 us
    all_to_all x2, starting transfers between devices, gathered(): return lax.all_to_all(parts, axes, 0, 0, tiled=True)  10.1 us
    all_to_all x1, starting transfers between devices, scattered(): got = lax.all_to_all(parts, axes, 0, 0, tiled=True)  9.66 us
    all_to_all x2, waiting for transfers between devices, gathered(): return lax.all_to_all(parts, axes, 0, 0, tiled=True)  6.15 us
    pallas_call x1, Pallas kernels, patch_work(): pl.pallas_call(net_kernel, out_shape=(strip, jax.ShapeDtypeStruct((16, 48...  4.6 us
  transfers between devices with their start and end apart: 11, of which 7 were waited for; matrix products, arithmetic and copies ran while one was open for 3% of the time, Pallas kernels for 1%

profile of v2, /device:TPU:1, one launch (start us, length us, event | category | flops | bytes accessed | tf_op | source)
XLA Modules:
  0.0 161.7 jit_solution(6440161651520966289)
XLA Ops:
  0.7 0.9 constant_dynamic-update-slice_fusion.1
  1.6 0.9 constant_dynamic-update-slice_fusion
  2.5 1.3 collective-permute-start.1
  3.8 12.1 %collective-permute-start = (bf16[16,16,256]{2,1,0:T(8,128)(2,1)S(1)}, bf16[16,16,256]{2,1,0:T(8,128)(2,1)S(1)}, u32[]{:S(2)}, u32[]{:S(2)}) collective-permute-start(bf16[16,16,256]{2,1,0:T(8,128)(2,1)S(1)} %constant_dynamic-update-slice_fusion), channel_id=1, source_target_pairs={{0,1},{1,2},{2,3},{3,4},{4,5},{5,6},{6,7},{8,9},{9,10},{10,11},{11... | collective-permute-start | bytes 393224 | tf_op jit(solution)/shard_map/ppermute | solution.py:283
  15.9 0.5 collective-permute-done.1
  16.4 2.4 %collective-permute-done = bf16[16,16,256]{2,1,0:T(8,128)(2,1)S(1)} collective-permute-done((bf16[16,16,256]{2,1,0:T(8,128)(2,1)S(1)}, bf16[16,16,256]{2,1,0:T(8,128)(2,1)S(1)}, u32[]{:S(2)}, u32[]{:S(2)}) %collective-permute-start) | collective-permute-done | bytes 131104 | tf_op jit(solution)/shard_map/ppermute | solution.py:283
  18.9 4.7 %collective-permute-start.3 = (bf16[48,16,256]{2,1,0:T(8,128)(2,1)S(1)}, bf16[48,16,256]{2,1,0:T(8,128)(2,1)S(1)}, u32[]{:S(2)}, u32[]{:S(2)}) collective-permute-start(bf16[48,16,256]{2,1,0:T(8,128)(2,1)S(1)} %pad_maximum_fusion.middle), channel_id=1, source_target_pairs={{8,0},{16,8},{24,16},{32,24},{40,32},{48,40},{56,48},{64,56},{72,6... | collective-permute-start | bytes 1179656 | tf_op jit(solution)/shard_map/ppermute | solution.py:283
  23.6 2.7 %collective-permute-start.2 = (bf16[48,16,256]{2,1,0:T(8,128)(2,1)S(1)}, bf16[48,16,256]{2,1,0:T(8,128)(2,1)S(1)}, u32[]{:S(2)}, u32[]{:S(2)}) collective-permute-start(bf16[48,16,256]{2,1,0:T(8,128)(2,1)S(1)} %pad_maximum_fusion.middle), channel_id=1, source_target_pairs={{0,8},{8,16},{16,24},{24,32},{32,40},{40,48},{48,56},{56,64},{64,7... | collective-permute-start | bytes 1179656 | tf_op jit(solution)/shard_map/ppermute | solution.py:283
  26.3 0.8 copy.17
  27.1 0.9 add_reduce_fusion.start
  28.0 0.1 pad_add_fusion.where
  28.1 1.5 prepare.1
  29.6 0.2 collective-permute-done.3.right
  29.8 6.4 %collective-permute-done.2.left = bf16[48,16,256]{2,1,0:T(8,128)(2,1)S(1)} collective-permute-done((bf16[48,16,256]{2,1,0:T(8,128)(2,1)S(1)}, bf16[48,16,256]{2,1,0:T(8,128)(2,1)S(1)}, u32[]{:S(2)}, u32[]{:S(2)}) %collective-permute-start.2) | collective-permute-done | bytes 393248 | tf_op jit(solution)/shard_map/ppermute | solution.py:283
  36.2 4.6 %patch_work.1 = (bf16[16,48,256]{2,1,0:T(8,128)(2,1)S(1)}, f32[16,48,256]{2,1,0:T(8,128)S(1)}, bf16[16,48,256]{2,1,0:T(8,128)(2,1)S(1)}, bf16[4608,128]{1,0:T(8,128)(2,1)S(1)}) custom-call(s32[2]{0:T(128)S(1)} %add_reduce_fusion.start, bf16[48,16,256]{2,1,0:T(8,128)(2,1)S(1)} %collective-permute-done.2.left, ...), custom_call_target="tpu_custom_call" | custom-call | flops 2000000000 | bytes 10000000 | tf_op jit(solution)/shard_map/patch_work/pallas_call | solution.py:251
  40.8 4.3 %all_to_all.35 = bf16[2,2304,128]{2,1,0:T(8,128)(2,1)S(1)} all-to-all(bf16[2,2304,128]{2,1,0:T(8,128)(2,1)S(1)} %bitcast.16), channel_id=1, replica_groups=mesh['y'=8,'zl'=4,'core'=2,'x'=4,'zh'=2] {'core'}, dimensions={0} | all-to-all | bytes 2359296 | tf_op jit(solution)/shard_map/all_to_all | solution.py:289
  45.1 0.6 reduce_sum.48
  45.7 20.9 %all_to_all.36 = bf16[4,576,128]{2,1,0:T(8,128)(2,1)S(1)} all-to-all(bf16[4,576,128]{2,1,0:T(8,128)(2,1)S(1)} %bitcast.24), channel_id=1, replica_groups=mesh['y'=8,'zl'=4,'core'=2,'x'=4,'zh'=2] {'x'}, dimensions={0} | all-to-all | bytes 1179648 | tf_op jit(solution)/shard_map/all_to_all | solution.py:289
  66.6 0.8 reduce_sum.49
  67.4 9.7 %all-to-all-start.2 = ((bf16[8,72,128]{2,1,0:T(8,128)(2,1)}), bf16[8,72,128]{2,1,0:T(8,128)(2,1)S(1)}, u32[]{:S(2)}, u32[]{:S(2)}) async-start(bf16[8,72,128]{2,1,0:T(8,128)(2,1)} %bitcast.6), calls=%async_computation.2 | async-start | bytes 294912 | tf_op jit(solution)/shard_map/all_to_all | solution.py:289
  77.0 2.4 %collective-permute-start.4 = (bf16[16,48,256]{2,1,0:T(8,128)(2,1)S(1)}, bf16[16,48,256]{2,1,0:T(8,128)(2,1)S(1)}, u32[]{:S(2)}, u32[]{:S(2)}) collective-permute-start(bf16[16,48,256]{2,1,0:T(8,128)(2,1)S(1)} %get-tuple-element.20), channel_id=1, source_target_pairs={{0,1},{1,2},{2,3},{3,4},{4,5},{5,6},{6,7},{8,9},{9,10},{10,11},{11... | collective-permute-start | bytes 1179656 | tf_op jit(solution)/shard_map/ppermute | solution.py:283
  79.5 1.3 collective-permute-start.5
  80.8 4.4 %all-to-all-done.2 = bf16[8,72,128]{2,1,0:T(8,128)(2,1)S(1)} async-done(((bf16[8,72,128]{2,1,0:T(8,128)(2,1)}), bf16[8,72,128]{2,1,0:T(8,128)(2,1)S(1)}, u32[]{:S(2)}, u32[]{:S(2)}) %all-to-all-start.2) | async-done | bytes 147488 | tf_op jit(solution)/shard_map/all_to_all | solution.py:289
  85.2 34.6 %all_to_all.37 = bf16[8,72,128]{2,1,0:T(8,128)(2,1)S(1)} all-to-all(bf16[8,72,128]{2,1,0:T(8,128)(2,1)S(1)} %broadcast_in_dim.12), channel_id=1, replica_groups=mesh['y'=8,'zl'=4,'core'=2,'x'=4,'zh'=2] {'zl','zh'}, dimensions={0} | all-to-all | bytes 294912 | tf_op jit(solution)/shard_map/all_to_all | solution.py:296
  119.8 0.7 broadcast_in_dim.13
  120.5 6.6 %all-to-all-start.4 = ((bf16[8,72,128]{2,1,0:T(8,128)(2,1)}), bf16[8,72,128]{2,1,0:T(8,128)(2,1)S(1)}, u32[]{:S(2)}, u32[]{:S(2)}) async-start(bf16[8,72,128]{2,1,0:T(8,128)(2,1)} %broadcast_in_dim.13), calls=%async_computation.4 | async-start | bytes 294912 | tf_op jit(solution)/shard_map/all_to_all | solution.py:296
  127.1 0.0 collective-permute-done.4
  127.1 0.0 collective-permute-done.5
  127.1 0.0 copy-start.4
  127.2 0.7 copy-done.4
  127.9 1.1 fusion.1
  129.0 6.2 %all-to-all-done.4 = bf16[8,72,128]{2,1,0:T(8,128)(2,1)S(1)} async-done(((bf16[8,72,128]{2,1,0:T(8,128)(2,1)}), bf16[8,72,128]{2,1,0:T(8,128)(2,1)S(1)}, u32[]{:S(2)}, u32[]{:S(2)}) %all-to-all-start.4) | async-done | bytes 147488 | tf_op jit(solution)/shard_map/all_to_all | solution.py:296
  135.2 0.9 broadcast_in_dim.29
  136.1 3.5 %all-to-all-start.5 = ((bf16[4,576,128]{2,1,0:T(8,128)(2,1)}), bf16[4,576,128]{2,1,0:T(8,128)(2,1)S(1)}, u32[]{:S(2)}, u32[]{:S(2)}) async-start(bf16[4,576,128]{2,1,0:T(8,128)(2,1)} %broadcast_in_dim.29), calls=%async_computation.5 | async-start | bytes 1179648 | tf_op jit(solution)/shard_map/all_to_all | solution.py:296
  139.6 5.3 %collective-permute-start.6 = (bf16[16,16,256]{2,1,0:T(8,128)(2,1)S(1)}, bf16[16,16,256]{2,1,0:T(8,128)(2,1)S(1)}, u32[]{:S(2)}, u32[]{:S(2)}) collective-permute-start(bf16[16,16,256]{2,1,0:T(8,128)(2,1)S(1)} %get-tuple-element.25), channel_id=1, source_target_pairs={{0,8},{8,16},{16,24},{24,32},{32,40},{40,48},{48,56},{56,64},{64,7... | collective-permute-start | bytes 393224 | tf_op jit(solution)/shard_map/ppermute | solution.py:283
  144.9 1.9 %collective-permute-start.7 = (bf16[16,16,256]{2,1,0:T(8,128)(2,1)S(1)}, bf16[16,16,256]{2,1,0:T(8,128)(2,1)S(1)}, u32[]{:S(2)}, u32[]{:S(2)}) collective-permute-start(bf16[16,16,256]{2,1,0:T(8,128)(2,1)S(1)} %get-tuple-element.26), channel_id=1, source_target_pairs={{8,0},{16,8},{24,16},{32,24},{40,32},{48,40},{56,48},{64,56},{72,6... | collective-permute-start | bytes 393224 | tf_op jit(solution)/shard_map/ppermute | solution.py:283
  146.8 4.3 %collective-permute-done.7 = bf16[16,16,256]{2,1,0:T(8,128)(2,1)S(1)} collective-permute-done((bf16[16,16,256]{2,1,0:T(8,128)(2,1)S(1)}, bf16[16,16,256]{2,1,0:T(8,128)(2,1)S(1)}, u32[]{:S(2)}, u32[]{:S(2)}) %collective-permute-start.7) | collective-permute-done | bytes 131104 | tf_op jit(solution)/shard_map/ppermute | solution.py:283
  151.2 0.6 slice.47
  151.8 0.7 slice.39
  152.5 0.0 all-to-all-done.5
  152.5 0.1 broadcast_in_dim.31
  152.6 4.3 %all_to_all.38 = bf16[2,2304,128]{2,1,0:T(8,128)(2,1)S(1)} all-to-all(bf16[2,2304,128]{2,1,0:T(8,128)(2,1)S(1)} %broadcast_in_dim.31), channel_id=1, replica_groups=mesh['y'=8,'zl'=4,'core'=2,'x'=4,'zh'=2] {'core'}, dimensions={0} | all-to-all | bytes 2359296 | tf_op jit(solution)/shard_map/all_to_all | solution.py:296
  156.9 0.2 convert_multiply_fusion
  157.1 0.8 slice.42
  157.9 0.9 slice.40
  158.8 0.1 slice.41
  158.9 0.9 copy.21
  159.8 2.0 %reshape.54 = f32[3,3,128,256]{3,2,1,0:T(8,128)} reshape(f32[3,384,2,128]{3,2,1,0:T(2,128)S(1)} %bitcast.22) | data formatting | bytes 2359296 | tf_op jit(solution)/shard_map/reshape | solution.py:339
  (16 shorter events, 0.3 us)
Async XLA Ops:
  0.6 27.5 %copy-start = (bf16[3,3,128,256]{3,2,1,0:T(8,128)(2,1)S(1)}, bf16[3,3,128,256]{3,2,1,0:T(8,128)(2,1)}, u32[]{:S(2)}) copy-start(bf16[3,3,128,256]{3,2,1,0:T(8,128)(2,1)} %w_down.1) | copy-start | bytes 1769476
  0.6 27.5 %copy-start.3 = (s32[32,32]{1,0:T(8,128)S(1)}, s32[32,32]{1,0:T(8,128)}, u32[]{:S(2)}) copy-start(s32[32,32]{1,0:T(8,128)} %table.1) | copy-start | bytes 12292
  0.7 27.5 %copy-start.2 = (bf16[2,2,256,128]{3,2,1,0:T(8,128)(2,1)S(1)}, bf16[2,2,256,128]{3,2,1,0:T(8,128)(2,1)}, u32[]{:S(2)}) copy-start(bf16[2,2,256,128]{3,2,1,0:T(8,128)(2,1)} %w_up.1) | copy-start | bytes 786436
  0.7 27.5 %copy-start.1 = (bf16[3,3,128,128]{3,2,1,0:T(8,128)(2,1)S(1)}, bf16[3,3,128,128]{3,2,1,0:T(8,128)(2,1)}, u32[]{:S(2)}) copy-start(bf16[3,3,128,128]{3,2,1,0:T(8,128)(2,1)} %w_first.1) | copy-start | bytes 884740
  2.5 13.9 %collective-permute-start.1 = (bf16[16,16,256]{2,1,0:T(8,128)(2,1)S(1)}, bf16[16,16,256]{2,1,0:T(8,128)(2,1)S(1)}, u32[]{:S(2)}, u32[]{:S(2)}) collective-permute-start(bf16[16,16,256]{2,1,0:T(8,128)(2,1)S(1)} %constant_dynamic-update-slice_fusion), channel_id=1, source_target_pairs={{1,0},{2,1},{3,2},{4,3},{5,4},{6,5},{7,6},{9,8},{10,9},{11,10},{12... | collective-permute-start | bytes 393224 | tf_op jit(solution)/shard_map/ppermute | solution.py:283
  3.8 15.0 %collective-permute-start = (bf16[16,16,256]{2,1,0:T(8,128)(2,1)S(1)}, bf16[16,16,256]{2,1,0:T(8,128)(2,1)S(1)}, u32[]{:S(2)}, u32[]{:S(2)}) collective-permute-start(bf16[16,16,256]{2,1,0:T(8,128)(2,1)S(1)} %constant_dynamic-update-slice_fusion), channel_id=1, source_target_pairs={{0,1},{1,2},{2,3},{3,4},{4,5},{5,6},{6,7},{8,9},{9,10},{10,11},{11... | collective-permute-start | bytes 393224 | tf_op jit(solution)/shard_map/ppermute | solution.py:283
  18.9 10.9 %collective-permute-start.3 = (bf16[48,16,256]{2,1,0:T(8,128)(2,1)S(1)}, bf16[48,16,256]{2,1,0:T(8,128)(2,1)S(1)}, u32[]{:S(2)}, u32[]{:S(2)}) collective-permute-start(bf16[48,16,256]{2,1,0:T(8,128)(2,1)S(1)} %pad_maximum_fusion.middle), channel_id=1, source_target_pairs={{8,0},{16,8},{24,16},{32,24},{40,32},{48,40},{56,48},{64,56},{72,6... | collective-permute-start | bytes 1179656 | tf_op jit(solution)/shard_map/ppermute | solution.py:283
  23.6 12.6 %collective-permute-start.2 = (bf16[48,16,256]{2,1,0:T(8,128)(2,1)S(1)}, bf16[48,16,256]{2,1,0:T(8,128)(2,1)S(1)}, u32[]{:S(2)}, u32[]{:S(2)}) collective-permute-start(bf16[48,16,256]{2,1,0:T(8,128)(2,1)S(1)} %pad_maximum_fusion.middle), channel_id=1, source_target_pairs={{0,8},{8,16},{16,24},{24,32},{32,40},{40,48},{48,56},{56,64},{64,7... | collective-permute-start | bytes 1179656 | tf_op jit(solution)/shard_map/ppermute | solution.py:283
  67.4 17.8 %all-to-all-start.2 = ((bf16[8,72,128]{2,1,0:T(8,128)(2,1)}), bf16[8,72,128]{2,1,0:T(8,128)(2,1)S(1)}, u32[]{:S(2)}, u32[]{:S(2)}) async-start(bf16[8,72,128]{2,1,0:T(8,128)(2,1)} %bitcast.6), calls=%async_computation.2 | async-start | bytes 294912 | tf_op jit(solution)/shard_map/all_to_all | solution.py:289
  77.0 50.1 %collective-permute-start.4 = (bf16[16,48,256]{2,1,0:T(8,128)(2,1)S(1)}, bf16[16,48,256]{2,1,0:T(8,128)(2,1)S(1)}, u32[]{:S(2)}, u32[]{:S(2)}) collective-permute-start(bf16[16,48,256]{2,1,0:T(8,128)(2,1)S(1)} %get-tuple-element.20), channel_id=1, source_target_pairs={{0,1},{1,2},{2,3},{3,4},{4,5},{5,6},{6,7},{8,9},{9,10},{10,11},{11... | collective-permute-start | bytes 1179656 | tf_op jit(solution)/shard_map/ppermute | solution.py:283
  79.5 47.7 %collective-permute-start.5 = (bf16[16,48,256]{2,1,0:T(8,128)(2,1)S(1)}, bf16[16,48,256]{2,1,0:T(8,128)(2,1)S(1)}, u32[]{:S(2)}, u32[]{:S(2)}) collective-permute-start(bf16[16,48,256]{2,1,0:T(8,128)(2,1)S(1)} %get-tuple-element.21), channel_id=1, source_target_pairs={{1,0},{2,1},{3,2},{4,3},{5,4},{6,5},{7,6},{9,8},{10,9},{11,10},{12... | collective-permute-start | bytes 1179656 | tf_op jit(solution)/shard_map/ppermute | solution.py:283
  120.5 14.7 %all-to-all-start.4 = ((bf16[8,72,128]{2,1,0:T(8,128)(2,1)}), bf16[8,72,128]{2,1,0:T(8,128)(2,1)S(1)}, u32[]{:S(2)}, u32[]{:S(2)}) async-start(bf16[8,72,128]{2,1,0:T(8,128)(2,1)} %broadcast_in_dim.13), calls=%async_computation.4 | async-start | bytes 294912 | tf_op jit(solution)/shard_map/all_to_all | solution.py:296
  127.1 0.7 copy-start.4
  136.1 16.4 %all-to-all-start.5 = ((bf16[4,576,128]{2,1,0:T(8,128)(2,1)}), bf16[4,576,128]{2,1,0:T(8,128)(2,1)S(1)}, u32[]{:S(2)}, u32[]{:S(2)}) async-start(bf16[4,576,128]{2,1,0:T(8,128)(2,1)} %broadcast_in_dim.29), calls=%async_computation.5 | async-start | bytes 1179648 | tf_op jit(solution)/shard_map/all_to_all | solution.py:296
  139.6 7.2 %collective-permute-start.6 = (bf16[16,16,256]{2,1,0:T(8,128)(2,1)S(1)}, bf16[16,16,256]{2,1,0:T(8,128)(2,1)S(1)}, u32[]{:S(2)}, u32[]{:S(2)}) collective-permute-start(bf16[16,16,256]{2,1,0:T(8,128)(2,1)S(1)} %get-tuple-element.25), channel_id=1, source_target_pairs={{0,8},{8,16},{16,24},{24,32},{32,40},{40,48},{48,56},{56,64},{64,7... | collective-permute-start | bytes 393224 | tf_op jit(solution)/shard_map/ppermute | solution.py:283
  144.9 6.3 %collective-permute-start.7 = (bf16[16,16,256]{2,1,0:T(8,128)(2,1)S(1)}, bf16[16,16,256]{2,1,0:T(8,128)(2,1)S(1)}, u32[]{:S(2)}, u32[]{:S(2)}) collective-permute-start(bf16[16,16,256]{2,1,0:T(8,128)(2,1)S(1)} %get-tuple-element.26), channel_id=1, source_target_pairs={{8,0},{16,8},{24,16},{32,24},{40,32},{48,40},{56,48},{64,56},{72,6... | collective-permute-start | bytes 393224 | tf_op jit(solution)/shard_map/ppermute | solution.py:283

commit v3 on v2

--- a/solution.py
+++ b/solution.py
@@ -1,3 +1,4 @@
+import functools
 import math
 
 import jax
@@ -78,6 +79,45 @@
             ru[a, :, pl.ds(b * C1, C1)] = w_up[a, b]
 
 
+def assemble_kernel(starts, above, both, under, to_left, own, to_right, grown):
+    grown[:, 0:16] = above[...]
+    grown[:, 16:32] = both[...]
+    grown[:, 32:48] = under[...]
+    for side, out in enumerate((to_left, own, to_right)):
+        out[...] = grown[:, pl.ds(starts[side], 32)]
+
+
+def combine_kernel(starts, from_left, own, from_right, up, mid, down, canvas):
+    canvas[...] = jnp.zeros_like(canvas)
+    canvas[:, pl.ds(starts[1], 32)] = own[...]
+    for side, part in ((0, from_left), (2, from_right)):
+        spot = (slice(None), pl.ds(starts[side], 32))
+        canvas[spot] = canvas[spot] + part[...].astype(F32)
+    up[...] = canvas[:, 0:16].astype(BF16)
+    mid[...] = canvas[:, 16:32]
+    down[...] = canvas[:, 32:48].astype(BF16)
+
+
+def finish_kernel(own, from_above, from_under, blended, field_grad):
+    total = own[...] + from_above[...].astype(F32) + from_under[...].astype(F32)
+    blended[...] = total[0].astype(BF16)
+    field_grad[...] = total[1]
+
+
+def unpack_kernel(scale, halves, g_first, g_down, g_up):
+    def rows(base, count):
+        return halves[base : base + count].astype(F32) * scale
+
+    for t in range(9):
+        g_first[t] = rows(t * C1, C1)
+    for t in range(3):
+        base = FIRST_ROWS + 6 * t * C1
+        g_down[t, :, :C1] = rows(base, 3 * C1)
+        g_down[t, :, C1:] = rows(base + 3 * C1, 3 * C1)
+    for t in range(4):
+        g_up[t] = rows(FIRST_ROWS + DOWN_ROWS + t * C2, C2)
+
+
 def shifted(x, by):
     j = lax.broadcasted_iota(jnp.int32, x.shape, 0) % 16
     moved = pltpu.roll(x, by % x.shape[0], 0)
@@ -97,10 +137,10 @@
 
 def net_kernel(
     start, left, middle, right, fb, rf, rft, wd, rdt, ru,
-    up_o, mid_o, down_o, flat,
+    left_o, mid_o, right_o, flat,
     fs, cs, xv, hv, gv, g4, gs, bs, can_b, can_g,
 ):
-    start_r, start_c = start[0], start[1]
+    start_c = start[0]
     for ref in (xv, hv, gv):
         edge = jnp.zeros((16, ref.shape[-1]), BF16)
         ref[0, 0] = edge
@@ -109,9 +149,8 @@
 
     def stage(r, carry):
         for k, ref in enumerate((left, middle, right)):
-            cells = ref[start_r + r].astype(F32)
-            fs[r, 8 + 16 * k : 24 + 16 * k, :] = cells[:, :C1]
-            cs[r, 8 + 16 * k : 24 + 16 * k, :] = cells[:, C1:]
+            fs[r, 8 + 16 * k : 24 + 16 * k, :] = ref[0, r].astype(F32)
+            cs[r, 8 + 16 * k : 24 + 16 * k, :] = ref[1, r].astype(F32)
         return carry
 
     lax.fori_loop(0, 32, stage, 0, unroll=4)
@@ -200,11 +239,11 @@
         can_g[r] = jnp.zeros((48, C1), F32)
         return carry
 
-    lax.fori_loop(0, 48, clear, 0, unroll=4)
+    lax.fori_loop(0, 32, clear, 0, unroll=4)
 
     def place(i, carry):
         for a in range(2):
-            r = start_r + 2 * i + a
+            r = 2 * i + a
             for b in range(2):
                 can_b[r, pl.ds(start_c + b, 16, 2), :] = bs[a, i, :, b * C1 : (b + 1) * C1]
                 can_g[r, pl.ds(start_c + b, 16, 2), :] = gs[a, i, :, b * C1 : (b + 1) * C1]
@@ -213,15 +252,13 @@
     lax.fori_loop(0, 16, place, 0, unroll=2)
 
     def give(r, carry):
-        up_o[r, :, :C1] = can_b[r].astype(BF16)
-        up_o[r, :, C1:] = can_g[r].astype(BF16)
-        mid_o[r, :, :C1] = can_b[r + 16]
-        mid_o[r, :, C1:] = can_g[r + 16]
-        down_o[r, :, :C1] = can_b[r + 32].astype(BF16)
-        down_o[r, :, C1:] = can_g[r + 32].astype(BF16)
+        for k, canvas in enumerate((can_b, can_g)):
+            left_o[k, r] = canvas[r, 0:16].astype(BF16)
+            mid_o[k, r] = canvas[r, 16:32]
+            right_o[k, r] = canvas[r, 32:48].astype(BF16)
         return carry
 
-    lax.fori_loop(0, 16, give, 0, unroll=2)
+    lax.fori_loop(0, 32, give, 0, unroll=2)
 
 
 VMEM = pl.BlockSpec(memory_space=pltpu.VMEM)
@@ -247,12 +284,12 @@
 
 
 def patch_work(start, left, middle, right, fb, rf, rft, wd, rdt, ru):
-    strip = jax.ShapeDtypeStruct((16, 48, 2 * C1), BF16)
+    strip = jax.ShapeDtypeStruct((2, 32, 16, C1), BF16)
     return pl.pallas_call(
         net_kernel,
         out_shape=(
             strip,
-            jax.ShapeDtypeStruct((16, 48, 2 * C1), F32),
+            jax.ShapeDtypeStruct((2, 32, 16, C1), F32),
             strip,
             jax.ShapeDtypeStruct((FLAT_ROWS, C1), BF16),
         ),
@@ -267,8 +304,8 @@
             pltpu.VMEM((17, 16, 2 * C2), BF16),
             pltpu.VMEM((2, 16, 16, 2 * C1), F32),
             pltpu.VMEM((2, 16, 16, 2 * C1), F32),
-            pltpu.VMEM((48, 48, C1), F32),
-            pltpu.VMEM((48, 48, C1), F32),
+            pltpu.VMEM((32, 48, C1), F32),
+            pltpu.VMEM((32, 48, C1), F32),
         ],
         compiler_params=pltpu.CompilerParams(vmem_limit_bytes=40 * 2**20),
         cost_estimate=pl.CostEstimate(flops=2 * 10**9, bytes_accessed=10**7, transcendentals=200000),
@@ -276,6 +313,19 @@
     )(start, left, middle, right, fb, rf, rft, wd, rdt, ru)
 
 
+def small_call(body, name, outs, scratch, *args, smem=0):
+    return pl.pallas_call(
+        body,
+        out_shape=tuple(jax.ShapeDtypeStruct(shape, kind) for shape, kind in outs),
+        in_specs=[SMEM] * smem + [VMEM] * (len(args) - smem),
+        out_specs=[VMEM] * len(outs),
+        scratch_shapes=scratch,
+        compiler_params=pltpu.CompilerParams(vmem_limit_bytes=16 * 2**20),
+        cost_estimate=pl.CostEstimate(flops=10**6, bytes_accessed=2 * 10**6, transcendentals=0),
+        name=name,
+    )(*args)
+
+
 def neighbours(axes, before, after):
     size = lax.axis_size(axes)
     ahead = [(i, i + 1) for i in range(size - 1)]
@@ -296,11 +346,7 @@
     return lax.all_to_all(parts, axes, 0, 0, tiled=True)
 
 
-def summed_over_mesh(part):
-    part = scattered(part, "core")
-    part = scattered(part, "x")
-    part = scattered(part, "y")
-    part = gathered(part, ("zl", "zh")).astype(F32).sum(0).astype(BF16)
+def spread_back(part):
     for axis in ("y", "x", "core"):
         part = gathered(part, axis).reshape(-1, part.shape[1])
     return part
@@ -312,33 +358,76 @@
     row_at = lax.axis_index(ROW)
     col_at = lax.axis_index(COL)
     where = jnp.stack([row_at, col_at]).astype(jnp.int32)
-    both = jnp.concatenate([field, cotangent], axis=2)
+    both = jnp.stack([field, cotangent])
+    starts = jnp.stack(
+        [MARGIN + offsets[row_at, jnp.clip(col_at + step, 0, cols_n - 1), 0] for step in (-1, 0, 1)]
+    )
+    start_c = (MARGIN + offsets[row_at, col_at, 1])[None]
     fb, rf, rft, rdt, ru = prepared(
         where, offsets.reshape(rows_n, 2 * cols_n), blend_table, w_first, w_down, w_up
     )
     above, under = neighbours(ROW, both, both)
-    middle = jnp.concatenate([above, both, under], axis=0)
-    left, right = neighbours(COL, middle, middle)
-    start = MARGIN + offsets[row_at, col_at]
-    up, mid, down, flat = patch_work(
-        start, left, middle, right, fb, rf, rft, w_down.reshape(3, 3 * C1, C2), rdt, ru
+    window_shape = (2, 32, TILE, C1)
+    to_left, own, to_right = small_call(
+        assemble_kernel,
+        "assemble",
+        [(window_shape, BF16)] * 3,
+        [pltpu.VMEM((2, 48, TILE, C1), BF16)],
+        starts,
+        above,
+        both,
+        under,
+        smem=1,
+    )
+    left, right = neighbours(COL, to_right, to_left)
+    to_left, own, to_right, flat = patch_work(
+        start_c, left, own, right, fb, rf, rft, w_down.reshape(3, 3 * C1, C2), rdt, ru
+    )
+    from_left, from_right = neighbours(COL, to_right, to_left)
+    part = scattered(flat, "core")
+    part, from_left, from_right = lax.optimization_barrier((part, from_left, from_right))
+    part = scattered(part, "x")
+    tile_shape = (2, TILE, TILE, C1)
+    up, own, down = small_call(
+        combine_kernel,
+        "combine",
+        [(tile_shape, BF16), (tile_shape, F32), (tile_shape, BF16)],
+        [pltpu.VMEM((2, 48, TILE, C1), F32)],
+        starts,
+        from_left,
+        own,
+        from_right,
+        smem=1,
     )
     from_above, from_under = neighbours(ROW, down, up)
-    total = summed_over_mesh(flat)
-    mid = mid + from_above.astype(F32) + from_under.astype(F32)
-    from_left, from_right = neighbours(
-        COL, mid[:, 32:].astype(BF16), mid[:, :16].astype(BF16)
-    )
-    own = mid[:, 16:32] + from_left.astype(F32) + from_right.astype(F32)
-    blended = own[:, :, :C1].astype(BF16)
-    field_grad = own[:, :, C1:]
+    part, from_above, from_under = lax.optimization_barrier((part, from_above, from_under))
+    part = scattered(part, "y")
+    part = gathered(part, ("zl", "zh")).astype(F32).sum(0).astype(BF16)
+    blended, field_grad = small_call(
+        finish_kernel,
+        "finish",
+        [(field.shape, BF16), (field.shape, F32)],
+        [],
+        own,
+        from_above,
+        from_under,
+    )
+    total = spread_back(part)
     scale = 1.0 / math.sqrt(TILE * rows_n * TILE * cols_n)
-    total = total.astype(F32) * scale
-    g_first = total[:FIRST_ROWS].reshape(w_first.shape)
-    g_down = total[FIRST_ROWS : FIRST_ROWS + DOWN_ROWS].reshape(3, 2, 3 * C1, C1)
-    g_down = g_down.transpose(0, 2, 1, 3).reshape(w_down.shape)
-    g_up = total[FIRST_ROWS + DOWN_ROWS : FIRST_ROWS + DOWN_ROWS + UP_ROWS].reshape(w_up.shape)
-    return (blended, field_grad, g_first, g_down, g_up)
+    g_first, g_down, g_up = small_call(
+        functools.partial(unpack_kernel, scale),
+        "unpack",
+        [((9, C1, C1), F32), ((3, 3 * C1, C2), F32), ((4, C2, C1), F32)],
+        [],
+        total,
+    )
+    return (
+        blended,
+        field_grad,
+        g_first.reshape(w_first.shape),
+        g_down.reshape(w_down.shape),
+        g_up.reshape(w_up.shape),
+    )
 
 
 def solution(mesh):

time: 163 us -> 151 us (0.926)
  waiting for transfers between devices: 24.4 us -> 18.4 us
  local copies, waits for them, and re-layouts: 11 us -> 6.01 us
  starting transfers between devices: 51.5 us -> 47.6 us
  Pallas kernels: 6.06 us -> 8.98 us
  between operations: 0.88 us -> 3.39 us
  blocking collectives: 64.1 us -> 62 us
    all_to_all x2 -> x1, starting transfers between devices: 10.1 us -> 3.75 us  [gathered(): return lax.all_to_all(parts, axes, 0, 0, tiled=True)]
    ppermute x8, waiting for transfers between devices: 13.9 us -> 8.46 us  [neighbours(): return (lax.ppermute(before, axes, ahead), lax.ppermute(after, axes, back))]
    all_to_all x2 -> x3, blocking collectives: 38.9 us -> 35.1 us  [gathered(): return lax.all_to_all(parts, axes, 0, 0, tiled=True)]
    slice x6 -> x0, local copies, waits for them, and re-layouts: 3.08 us -> none  [the longest x1 0.85 us: per_device(): g_first = total[:FIRST_ROWS].reshape(w_first.shape)]
    all_to_all x1, starting transfers between devices: 9.66 us -> 12.6 us  [scattered(): got = lax.all_to_all(parts, axes, 0, 0, tiled=True)]
    pallas_call x1 -> x5, Pallas kernels: 4.6 us -> 7.53 us  [the longest x1 3.94 us: patch_work(): pl.pallas_call(net_kernel, out_shape=(strip, jax.ShapeDtypeStruct((2, 32,...]
    reshape x2 -> x0, local copies, waits for them, and re-layouts: 2.87 us -> none  [the longest x1 1.96 us: per_device(): g_down = g_down.transpose(0, 2, 1, 3).reshape(w_down.shape)]
    all_to_all x2, blocking collectives: 25.2 us -> 26.9 us  [scattered(): got = lax.all_to_all(parts, axes, 0, 0, tiled=True)]
  transfers between devices with their start and end apart: 11 -> 10, of which waited for: 7 -> 3; matrix products, arithmetic and copies ran while one was open for 3% -> 3% of each run, Pallas kernels for 1% -> 2%
where the time goes in v3:
time: 151 us; the launch traced here: 150 us
  blocking collectives  62 us (41%)
  starting transfers between devices  47.6 us (32%)
  waiting for transfers between devices  18.4 us (12%)
  Pallas kernels  8.98 us (6%)
  local copies, waits for them, and re-layouts  6.01 us (4%)
  other arithmetic  3.71 us (2%)
  between operations  3.39 us (2%)
    all_to_all x3, blocking collectives, gathered(): return lax.all_to_all(parts, axes, 0, 0, tiled=True)  35.1 us
    ppermute x8, starting transfers between devices, neighbours(): return (lax.ppermute(before, axes, ahead), lax.ppermute(after, axes, back))  31.2 us
    all_to_all x2, blocking collectives, scattered(): got = lax.all_to_all(parts, axes, 0, 0, tiled=True)  26.9 us
    all_to_all x1, starting transfers between devices, scattered(): got = lax.all_to_all(parts, axes, 0, 0, tiled=True)  12.6 us
    ppermute x8, waiting for transfers between devices, neighbours(): return (lax.ppermute(before, axes, ahead), lax.ppermute(after, axes, back))  8.46 us
    all_to_all x1, waiting for transfers between devices, gathered(): return lax.all_to_all(parts, axes, 0, 0, tiled=True)  6.58 us
    pallas_call x1, Pallas kernels, patch_work(): pl.pallas_call(net_kernel, out_shape=(strip, jax.ShapeDtypeStruct((2, 32,...  3.94 us
    all_to_all x1, starting transfers between devices, gathered(): return lax.all_to_all(parts, axes, 0, 0, tiled=True)  3.75 us
  transfers between devices with their start and end apart: 10, of which 3 were waited for; matrix products, arithmetic and copies ran while one was open for 3% of the time, Pallas kernels for 2%

profile of v3, /device:TPU:1, one launch (start us, length us, event | category | flops | bytes accessed | tf_op | source)
XLA Modules:
  0.0 150.1 jit_solution(3139904091611599040)
XLA Ops:
  0.6 0.0 copy-start
  0.6 0.9 pad_maximum_fusion.both
  1.6 1.3 collective-permute-start.1
  2.9 12.1 %collective-permute-start = (bf16[2,16,16,128]{3,2,1,0:T(8,128)(2,1)S(1)}, bf16[2,16,16,128]{3,2,1,0:T(8,128)(2,1)S(1)}, u32[]{:S(2)}, u32[]{:S(2)}) collective-permute-start(bf16[2,16,16,128]{3,2,1,0:T(8,128)(2,1)S(1)} %pad_maximum_fusion.both), channel_id=1, source_target_pairs={{0,1},{1,2},{2,3},{3,4},{4,5},{5,6},{6,7},{8,9},{9,10},{10,11},{11... | collective-permute-start | bytes 393224 | tf_op jit(solution)/shard_map/ppermute | solution.py:333
  15.0 1.5 constant_dynamic-slice_fusion.3
  18.4 0.1 pad_add_fusion.starts
  18.5 0.0 collective-permute-done.1.under
  18.5 0.0 collective-permute-done.above
  18.5 0.6 assemble.1
  19.1 4.9 %collective-permute-start.2 = (bf16[2,32,16,128]{3,2,1,0:T(8,128)(2,1)S(1)}, bf16[2,32,16,128]{3,2,1,0:T(8,128)(2,1)S(1)}, u32[]{:S(2)}, u32[]{:S(2)}) collective-permute-start(bf16[2,32,16,128]{3,2,1,0:T(8,128)(2,1)S(1)} %get-tuple-element.31), channel_id=1, source_target_pairs={{0,8},{8,16},{16,24},{24,32},{32,40},{40,48},{48,56},{56,64},{64,7... | collective-permute-start | bytes 786440 | tf_op jit(solution)/shard_map/ppermute | solution.py:333
  24.0 1.9 %collective-permute-start.3 = (bf16[2,32,16,128]{3,2,1,0:T(8,128)(2,1)S(1)}, bf16[2,32,16,128]{3,2,1,0:T(8,128)(2,1)S(1)}, u32[]{:S(2)}, u32[]{:S(2)}) collective-permute-start(bf16[2,32,16,128]{3,2,1,0:T(8,128)(2,1)S(1)} %get-tuple-element.33), channel_id=1, source_target_pairs={{8,0},{16,8},{24,16},{32,24},{40,32},{48,40},{56,48},{64,56},{72,6... | collective-permute-start | bytes 786440 | tf_op jit(solution)/shard_map/ppermute | solution.py:333
  26.0 0.8 copy.15
  27.5 0.1 pad_add_fusion.1.where
  27.6 0.0 copy-done
  27.6 0.0 copy-start.1
  27.6 1.0 copy-done.1
  28.5 0.0 copy-start.2
  28.5 0.9 copy-done.2
  29.5 0.0 copy-start.3
  29.5 0.7 copy-done.3
  30.2 1.5 prepare.1
  31.7 0.0 collective-permute-done.2.left
  31.7 0.0 collective-permute-done.3.right
  31.7 3.9 %patch_work.1 = (bf16[2,32,16,128]{3,2,1,0:T(8,128)(2,1)S(1)}, f32[2,32,16,128]{3,2,1,0:T(8,128)S(1)}, bf16[2,32,16,128]{3,2,1,0:T(8,128)(2,1)S(1)}, bf16[4608,128]{1,0:T(8,128)(2,1)S(1)}) custom-call(s32[1]{0:T(128)} %bitcast.3.start, bf16[2,32,16,128]{3,2,1,0:T(8,128)(2,1)S(1)} %collective-permute-done.2.left, ...), custom_call_target="tpu_custom_call" | custom-call | flops 2000000000 | bytes 10000000 | tf_op jit(solution)/shard_map/patch_work/pallas_call | solution.py:288
  35.7 3.6 %collective-permute-start.4 = (bf16[2,32,16,128]{3,2,1,0:T(8,128)(2,1)S(1)}, bf16[2,32,16,128]{3,2,1,0:T(8,128)(2,1)S(1)}, u32[]{:S(2)}, u32[]{:S(2)}) collective-permute-start(bf16[2,32,16,128]{3,2,1,0:T(8,128)(2,1)S(1)} %get-tuple-element.40), channel_id=1, source_target_pairs={{0,8},{8,16},{16,24},{24,32},{32,40},{40,48},{48,56},{56,64},{64,7... | collective-permute-start | bytes 786440 | tf_op jit(solution)/shard_map/ppermute | solution.py:333
  39.3 1.9 %collective-permute-start.5 = (bf16[2,32,16,128]{3,2,1,0:T(8,128)(2,1)S(1)}, bf16[2,32,16,128]{3,2,1,0:T(8,128)(2,1)S(1)}, u32[]{:S(2)}, u32[]{:S(2)}) collective-permute-start(bf16[2,32,16,128]{3,2,1,0:T(8,128)(2,1)S(1)} %get-tuple-element.41), channel_id=1, source_target_pairs={{8,0},{16,8},{24,16},{32,24},{40,32},{48,40},{56,48},{64,56},{72,6... | collective-permute-start | bytes 786440 | tf_op jit(solution)/shard_map/ppermute | solution.py:333
  41.2 5.1 %all_to_all.35 = bf16[2,2304,128]{2,1,0:T(8,128)(2,1)} all-to-all(bf16[2,2304,128]{2,1,0:T(8,128)(2,1)S(1)} %bitcast.20), channel_id=1, replica_groups=mesh['y'=8,'zl'=4,'core'=2,'x'=4,'zh'=2] {'core'}, dimensions={0} | all-to-all | bytes 2359296 | tf_op jit(solution)/shard_map/all_to_all | solution.py:339
  46.3 2.5 %reduce_sum.48 = bf16[2304,128]{1,0:T(8,128)(2,1)} reduce(bf16[2,2304,128]{2,1,0:T(8,128)(2,1)} %all_to_all.35, bf16[]{:T(256)} %constant.47.clone.1), dimensions={0}, to_apply=%region_0.1 | reduce | flops 294912 | bytes 1769474 | tf_op jit(solution)/shard_map/reduce_sum | solution.py:340
  48.8 0.0 collective-permute-done.4.from_left
  48.8 0.0 collective-permute-done.5.from_right
  48.8 12.6 %all-to-all-start.1 = ((bf16[4,576,128]{2,1,0:T(8,128)(2,1)}), bf16[4,576,128]{2,1,0:T(8,128)(2,1)S(1)}, u32[]{:S(2)}, u32[]{:S(2)}) async-start(bf16[4,576,128]{2,1,0:T(8,128)(2,1)} %bitcast.11), calls=%async_computation.1 | async-start | bytes 1179648 | tf_op jit(solution)/shard_map/all_to_all | solution.py:339
  61.4 0.8 combine.1
  62.2 4.2 %collective-permute-start.6 = (bf16[2,16,16,128]{3,2,1,0:T(8,128)(2,1)S(1)}, bf16[2,16,16,128]{3,2,1,0:T(8,128)(2,1)S(1)}, u32[]{:S(2)}, u32[]{:S(2)}) collective-permute-start(bf16[2,16,16,128]{3,2,1,0:T(8,128)(2,1)S(1)} %get-tuple-element.47), channel_id=1, source_target_pairs={{0,1},{1,2},{2,3},{3,4},{4,5},{5,6},{6,7},{8,9},{9,10},{10,11},{11... | collective-permute-start | bytes 393224 | tf_op jit(solution)/shard_map/ppermute | solution.py:333
  66.4 1.3 collective-permute-start.7
  67.7 3.4 %all-to-all-done.1 = bf16[4,576,128]{2,1,0:T(8,128)(2,1)S(1)} async-done(((bf16[4,576,128]{2,1,0:T(8,128)(2,1)}), bf16[4,576,128]{2,1,0:T(8,128)(2,1)S(1)}, u32[]{:S(2)}, u32[]{:S(2)}) %all-to-all-start.1) | async-done | bytes 589856 | tf_op jit(solution)/shard_map/all_to_all | solution.py:339
  71.1 0.1 reduce_sum.49
  71.2 0.0 collective-permute-done.6.from_above
  71.2 8.4 %collective-permute-done.7.from_under = bf16[2,16,16,128]{3,2,1,0:T(8,128)(2,1)S(1)} collective-permute-done((bf16[2,16,16,128]{3,2,1,0:T(8,128)(2,1)S(1)}, bf16[2,16,16,128]{3,2,1,0:T(8,128)(2,1)S(1)}, u32[]{:S(2)}, u32[]{:S(2)}) %collective-permute-start.7) | collective-permute-done | bytes 131104 | tf_op jit(solution)/shard_map/ppermute | solution.py:333
  79.6 21.8 %all_to_all.36 = bf16[8,72,128]{2,1,0:T(8,128)(2,1)S(1)} all-to-all(bf16[8,72,128]{2,1,0:T(8,128)(2,1)S(1)} %bitcast.23), channel_id=1, replica_groups=mesh['y'=8,'zl'=4,'core'=2,'x'=4,'zh'=2] {'y'}, dimensions={0} | all-to-all | bytes 294912 | tf_op jit(solution)/shard_map/all_to_all | solution.py:339
  101.4 12.5 %all_to_all.37 = bf16[8,72,128]{2,1,0:T(8,128)(2,1)S(1)} all-to-all(bf16[8,72,128]{2,1,0:T(8,128)(2,1)S(1)} %broadcast_in_dim.30), channel_id=1, replica_groups=mesh['y'=8,'zl'=4,'core'=2,'x'=4,'zh'=2] {'zl','zh'}, dimensions={0} | all-to-all | bytes 294912 | tf_op jit(solution)/shard_map/all_to_all | solution.py:346
  114.0 10.5 %all_to_all.38 = bf16[8,72,128]{2,1,0:T(8,128)(2,1)S(1)} all-to-all(bf16[8,72,128]{2,1,0:T(8,128)(2,1)S(1)} %broadcast_in_dim.31), channel_id=1, replica_groups=mesh['y'=8,'zl'=4,'core'=2,'x'=4,'zh'=2] {'y'}, dimensions={0} | all-to-all | bytes 294912 | tf_op jit(solution)/shard_map/all_to_all | solution.py:346
  124.5 0.9 broadcast_in_dim.33
  125.4 3.8 %all-to-all-start.5 = ((bf16[4,576,128]{2,1,0:T(8,128)(2,1)}), bf16[4,576,128]{2,1,0:T(8,128)(2,1)S(1)}, u32[]{:S(2)}, u32[]{:S(2)}) async-start(bf16[4,576,128]{2,1,0:T(8,128)(2,1)} %broadcast_in_dim.33), calls=%async_computation.5 | async-start | bytes 1179648 | tf_op jit(solution)/shard_map/all_to_all | solution.py:346
  129.1 0.7 finish.1
  129.8 6.6 %all-to-all-done.5 = bf16[4,576,128]{2,1,0:T(8,128)(2,1)S(1)} async-done(((bf16[4,576,128]{2,1,0:T(8,128)(2,1)}), bf16[4,576,128]{2,1,0:T(8,128)(2,1)S(1)}, u32[]{:S(2)}, u32[]{:S(2)}) %all-to-all-start.5) | async-done | bytes 589856 | tf_op jit(solution)/shard_map/all_to_all | solution.py:346
  136.4 0.1 broadcast_in_dim.35
  136.5 12.1 %all_to_all.39 = bf16[2,2304,128]{2,1,0:T(8,128)(2,1)S(1)} all-to-all(bf16[2,2304,128]{2,1,0:T(8,128)(2,1)S(1)} %broadcast_in_dim.35), channel_id=1, replica_groups=mesh['y'=8,'zl'=4,'core'=2,'x'=4,'zh'=2] {'core'}, dimensions={0} | all-to-all | bytes 2359296 | tf_op jit(solution)/shard_map/all_to_all | solution.py:346
  148.6 1.5 unpack.1
  (5 shorter events, 0.1 us)
Async XLA Ops:
  0.6 26.9 %copy-start = (bf16[3,3,128,256]{3,2,1,0:T(8,128)(2,1)S(1)}, bf16[3,3,128,256]{3,2,1,0:T(8,128)(2,1)}, u32[]{:S(2)}) copy-start(bf16[3,3,128,256]{3,2,1,0:T(8,128)(2,1)} %w_down.1) | copy-start | bytes 1769476
  1.6 16.9 %collective-permute-start.1 = (bf16[2,16,16,128]{3,2,1,0:T(8,128)(2,1)S(1)}, bf16[2,16,16,128]{3,2,1,0:T(8,128)(2,1)S(1)}, u32[]{:S(2)}, u32[]{:S(2)}) collective-permute-start(bf16[2,16,16,128]{3,2,1,0:T(8,128)(2,1)S(1)} %pad_maximum_fusion.both), channel_id=1, source_target_pairs={{1,0},{2,1},{3,2},{4,3},{5,4},{6,5},{7,6},{9,8},{10,9},{11,10},{12... | collective-permute-start | bytes 393224 | tf_op jit(solution)/shard_map/ppermute | solution.py:333
  2.9 15.6 %collective-permute-start = (bf16[2,16,16,128]{3,2,1,0:T(8,128)(2,1)S(1)}, bf16[2,16,16,128]{3,2,1,0:T(8,128)(2,1)S(1)}, u32[]{:S(2)}, u32[]{:S(2)}) collective-permute-start(bf16[2,16,16,128]{3,2,1,0:T(8,128)(2,1)S(1)} %pad_maximum_fusion.both), channel_id=1, source_target_pairs={{0,1},{1,2},{2,3},{3,4},{4,5},{5,6},{6,7},{8,9},{9,10},{10,11},{11... | collective-permute-start | bytes 393224 | tf_op jit(solution)/shard_map/ppermute | solution.py:333
  19.1 12.5 %collective-permute-start.2 = (bf16[2,32,16,128]{3,2,1,0:T(8,128)(2,1)S(1)}, bf16[2,32,16,128]{3,2,1,0:T(8,128)(2,1)S(1)}, u32[]{:S(2)}, u32[]{:S(2)}) collective-permute-start(bf16[2,32,16,128]{3,2,1,0:T(8,128)(2,1)S(1)} %get-tuple-element.31), channel_id=1, source_target_pairs={{0,8},{8,16},{16,24},{24,32},{32,40},{40,48},{48,56},{56,64},{64,7... | collective-permute-start | bytes 786440 | tf_op jit(solution)/shard_map/ppermute | solution.py:333
  24.0 7.7 %collective-permute-start.3 = (bf16[2,32,16,128]{3,2,1,0:T(8,128)(2,1)S(1)}, bf16[2,32,16,128]{3,2,1,0:T(8,128)(2,1)S(1)}, u32[]{:S(2)}, u32[]{:S(2)}) collective-permute-start(bf16[2,32,16,128]{3,2,1,0:T(8,128)(2,1)S(1)} %get-tuple-element.33), channel_id=1, source_target_pairs={{8,0},{16,8},{24,16},{32,24},{40,32},{48,40},{56,48},{64,56},{72,6... | collective-permute-start | bytes 786440 | tf_op jit(solution)/shard_map/ppermute | solution.py:333
  27.6 1.0 copy-start.1
  28.5 0.9 copy-start.2
  29.5 0.7 copy-start.3
  35.7 13.1 %collective-permute-start.4 = (bf16[2,32,16,128]{3,2,1,0:T(8,128)(2,1)S(1)}, bf16[2,32,16,128]{3,2,1,0:T(8,128)(2,1)S(1)}, u32[]{:S(2)}, u32[]{:S(2)}) collective-permute-start(bf16[2,32,16,128]{3,2,1,0:T(8,128)(2,1)S(1)} %get-tuple-element.40), channel_id=1, source_target_pairs={{0,8},{8,16},{16,24},{24,32},{32,40},{40,48},{48,56},{56,64},{64,7... | collective-permute-start | bytes 786440 | tf_op jit(solution)/shard_map/ppermute | solution.py:333
  39.3 9.5 %collective-permute-start.5 = (bf16[2,32,16,128]{3,2,1,0:T(8,128)(2,1)S(1)}, bf16[2,32,16,128]{3,2,1,0:T(8,128)(2,1)S(1)}, u32[]{:S(2)}, u32[]{:S(2)}) collective-permute-start(bf16[2,32,16,128]{3,2,1,0:T(8,128)(2,1)S(1)} %get-tuple-element.41), channel_id=1, source_target_pairs={{8,0},{16,8},{24,16},{32,24},{40,32},{48,40},{56,48},{64,56},{72,6... | collective-permute-start | bytes 786440 | tf_op jit(solution)/shard_map/ppermute | solution.py:333
  48.8 22.2 %all-to-all-start.1 = ((bf16[4,576,128]{2,1,0:T(8,128)(2,1)}), bf16[4,576,128]{2,1,0:T(8,128)(2,1)S(1)}, u32[]{:S(2)}, u32[]{:S(2)}) async-start(bf16[4,576,128]{2,1,0:T(8,128)(2,1)} %bitcast.11), calls=%async_computation.1 | async-start | bytes 1179648 | tf_op jit(solution)/shard_map/all_to_all | solution.py:339
  62.2 8.9 %collective-permute-start.6 = (bf16[2,16,16,128]{3,2,1,0:T(8,128)(2,1)S(1)}, bf16[2,16,16,128]{3,2,1,0:T(8,128)(2,1)S(1)}, u32[]{:S(2)}, u32[]{:S(2)}) collective-permute-start(bf16[2,16,16,128]{3,2,1,0:T(8,128)(2,1)S(1)} %get-tuple-element.47), channel_id=1, source_target_pairs={{0,1},{1,2},{2,3},{3,4},{4,5},{5,6},{6,7},{8,9},{9,10},{10,11},{11... | collective-permute-start | bytes 393224 | tf_op jit(solution)/shard_map/ppermute | solution.py:333
  66.4 13.2 %collective-permute-start.7 = (bf16[2,16,16,128]{3,2,1,0:T(8,128)(2,1)S(1)}, bf16[2,16,16,128]{3,2,1,0:T(8,128)(2,1)S(1)}, u32[]{:S(2)}, u32[]{:S(2)}) collective-permute-start(bf16[2,16,16,128]{3,2,1,0:T(8,128)(2,1)S(1)} %get-tuple-element.48), channel_id=1, source_target_pairs={{1,0},{2,1},{3,2},{4,3},{5,4},{6,5},{7,6},{9,8},{10,9},{11,10},{12... | collective-permute-start | bytes 393224 | tf_op jit(solution)/shard_map/ppermute | solution.py:333
  125.4 11.0 %all-to-all-start.5 = ((bf16[4,576,128]{2,1,0:T(8,128)(2,1)}), bf16[4,576,128]{2,1,0:T(8,128)(2,1)S(1)}, u32[]{:S(2)}, u32[]{:S(2)}) async-start(bf16[4,576,128]{2,1,0:T(8,128)(2,1)} %broadcast_in_dim.33), calls=%async_computation.5 | async-start | bytes 1179648 | tf_op jit(solution)/shard_map/all_to_all | solution.py:346

commit v4 on v3

--- a/solution.py
+++ b/solution.py
@@ -277,7 +277,7 @@
         ),
         in_specs=[SMEM, SMEM, VMEM, VMEM, VMEM, VMEM],
         out_specs=[VMEM] * 5,
-        compiler_params=pltpu.CompilerParams(vmem_limit_bytes=16 * 2**20),
+        compiler_params=pltpu.CompilerParams(vmem_limit_bytes=10 * 2**20),
         cost_estimate=pl.CostEstimate(flops=5 * 10**6, bytes_accessed=10**7, transcendentals=0),
         name="prepare",
     )(where, offsets, table, w_first, w_down, w_up)
@@ -307,7 +307,7 @@
             pltpu.VMEM((32, 48, C1), F32),
             pltpu.VMEM((32, 48, C1), F32),
         ],
-        compiler_params=pltpu.CompilerParams(vmem_limit_bytes=40 * 2**20),
+        compiler_params=pltpu.CompilerParams(vmem_limit_bytes=24 * 2**20),
         cost_estimate=pl.CostEstimate(flops=2 * 10**9, bytes_accessed=10**7, transcendentals=200000),
         name="patch_work",
     )(start, left, middle, right, fb, rf, rft, wd, rdt, ru)
@@ -320,17 +320,18 @@
         in_specs=[SMEM] * smem + [VMEM] * (len(args) - smem),
         out_specs=[VMEM] * len(outs),
         scratch_shapes=scratch,
-        compiler_params=pltpu.CompilerParams(vmem_limit_bytes=16 * 2**20),
+        compiler_params=pltpu.CompilerParams(vmem_limit_bytes=10 * 2**20),
         cost_estimate=pl.CostEstimate(flops=10**6, bytes_accessed=2 * 10**6, transcendentals=0),
         name=name,
     )(*args)
 
 
-def neighbours(axes, before, after):
-    size = lax.axis_size(axes)
-    ahead = [(i, i + 1) for i in range(size - 1)]
-    back = [(i + 1, i) for i in range(size - 1)]
-    return lax.ppermute(before, axes, ahead), lax.ppermute(after, axes, back)
+def from_before(axes, x):
+    return lax.ppermute(x, axes, [(i, i + 1) for i in range(lax.axis_size(axes) - 1)])
+
+
+def from_after(axes, x):
+    return lax.ppermute(x, axes, [(i + 1, i) for i in range(lax.axis_size(axes) - 1)])
 
 
 def scattered(x, axes):
@@ -344,12 +345,6 @@
     size = lax.axis_size(axes)
     parts = jnp.broadcast_to(x[None], (size,) + x.shape)
     return lax.all_to_all(parts, axes, 0, 0, tiled=True)
-
-
-def spread_back(part):
-    for axis in ("y", "x", "core"):
-        part = gathered(part, axis).reshape(-1, part.shape[1])
-    return part
 
 
 def per_device(field, cotangent, w_first, w_down, w_up, offsets, blend_table):
@@ -366,7 +361,7 @@
     fb, rf, rft, rdt, ru = prepared(
         where, offsets.reshape(rows_n, 2 * cols_n), blend_table, w_first, w_down, w_up
     )
-    above, under = neighbours(ROW, both, both)
+    above, under = from_before(ROW, both), from_after(ROW, both)
     window_shape = (2, 32, TILE, C1)
     to_left, own, to_right = small_call(
         assemble_kernel,
@@ -379,14 +374,18 @@
         under,
         smem=1,
     )
-    left, right = neighbours(COL, to_right, to_left)
+    left, right = from_before(COL, to_right), from_after(COL, to_left)
     to_left, own, to_right, flat = patch_work(
         start_c, left, own, right, fb, rf, rft, w_down.reshape(3, 3 * C1, C2), rdt, ru
     )
-    from_left, from_right = neighbours(COL, to_right, to_left)
+    from_left = from_before(COL, to_right)
     part = scattered(flat, "core")
+    part = scattered(part, "x")
+    part, from_left, to_left = lax.optimization_barrier((part, from_left, to_left))
+    from_right = from_after(COL, to_left)
+    part = scattered(part, "y")
     part, from_left, from_right = lax.optimization_barrier((part, from_left, from_right))
-    part = scattered(part, "x")
+    part = gathered(part, ("zl", "zh")).astype(F32).sum(0).astype(BF16)
     tile_shape = (2, TILE, TILE, C1)
     up, own, down = small_call(
         combine_kernel,
@@ -399,10 +398,14 @@
         from_right,
         smem=1,
     )
-    from_above, from_under = neighbours(ROW, down, up)
+    part, up, own, down = lax.optimization_barrier((part, up, own, down))
+    from_above = from_before(ROW, down)
+    part = gathered(part, "y").reshape(-1, C1)
+    part, from_above, up = lax.optimization_barrier((part, from_above, up))
+    from_under = from_after(ROW, up)
+    part = gathered(part, "x").reshape(-1, C1)
     part, from_above, from_under = lax.optimization_barrier((part, from_above, from_under))
-    part = scattered(part, "y")
-    part = gathered(part, ("zl", "zh")).astype(F32).sum(0).astype(BF16)
+    total = gathered(part, "core").reshape(-1, C1)
     blended, field_grad = small_call(
         finish_kernel,
         "finish",
@@ -412,7 +415,6 @@
         from_above,
         from_under,
     )
-    total = spread_back(part)
     scale = 1.0 / math.sqrt(TILE * rows_n * TILE * cols_n)
     g_first, g_down, g_up = small_call(
         functools.partial(unpack_kernel, scale),

time: 151 us -> 146 us (0.967)
  blocking collectives: 62 us -> 36.1 us
  starting transfers between devices: 47.6 us -> 60.1 us
  waiting for transfers between devices: 18.4 us -> 24.8 us
    all_to_all x3 -> x1, blocking collectives: 35.1 us -> 9.54 us  [gathered(): return lax.all_to_all(parts, axes, 0, 0, tiled=True)]
    all_to_all x1 -> x3, starting transfers between devices: 3.75 us -> 15 us  [gathered(): return lax.all_to_all(parts, axes, 0, 0, tiled=True)]
    all_to_all x1, waiting for transfers between devices: 3.36 us -> 5.83 us  [scattered(): got = lax.all_to_all(parts, axes, 0, 0, tiled=True)]
    all_to_all x1 -> x3, waiting for transfers between devices: 6.58 us -> 8.57 us  [gathered(): return lax.all_to_all(parts, axes, 0, 0, tiled=True)]
    ppermute x8, waiting for transfers between devices: 8.46 us -> 10.3 us  [the longest x4 8.42 us: from_after(): lax.ppermute(x, axes, [(i + 1, i) for i in range(lax.axis_size(axes) - 1)])]
  transfers between devices with their start and end apart: 10 -> 12, of which waited for: 3 -> 5; matrix products, arithmetic and copies ran while one was open for 3% -> 2% of each run, Pallas kernels for 2% -> 2%
where the time goes in v4:
time: 146 us; the launch traced here: 144 us
  starting transfers between devices  60.1 us (41%)
  blocking collectives  36.1 us (25%)
  waiting for transfers between devices  24.8 us (17%)
  Pallas kernels  8.98 us (6%)
  local copies, waits for them, and re-layouts  7.32 us (5%)
  other arithmetic  3.71 us (3%)
  between operations  3.4 us (2%)
    all_to_all x2, blocking collectives, scattered(): got = lax.all_to_all(parts, axes, 0, 0, tiled=True)  26.5 us
    ppermute x4, starting transfers between devices, from_before(): lax.ppermute(x, axes, [(i, i + 1) for i in range(lax.axis_size(axes) - 1)])  24.1 us
    all_to_all x3, starting transfers between devices, gathered(): return lax.all_to_all(parts, axes, 0, 0, tiled=True)  15 us
    all_to_all x1, starting transfers between devices, scattered(): got = lax.all_to_all(parts, axes, 0, 0, tiled=True)  13.1 us
    all_to_all x1, blocking collectives, gathered(): return lax.all_to_all(parts, axes, 0, 0, tiled=True)  9.54 us
    all_to_all x3, waiting for transfers between devices, gathered(): return lax.all_to_all(parts, axes, 0, 0, tiled=True)  8.57 us
    ppermute x4, waiting for transfers between devices, from_after(): lax.ppermute(x, axes, [(i + 1, i) for i in range(lax.axis_size(axes) - 1)])  8.42 us
    ppermute x4, starting transfers between devices, from_after(): lax.ppermute(x, axes, [(i + 1, i) for i in range(lax.axis_size(axes) - 1)])  7.93 us
  transfers between devices with their start and end apart: 12, of which 5 were waited for; matrix products, arithmetic and copies ran while one was open for 2% of the time, Pallas kernels for 2%

profile of v4, /device:TPU:1, one launch (start us, length us, event | category | flops | bytes accessed | tf_op | source)
XLA Modules:
  0.0 144.3 jit_solution(4939571521933858486)
XLA Ops:
  0.6 0.0 copy-start
  0.6 0.9 pad_maximum_fusion.both
  1.6 1.3 collective-permute-start.1
  2.9 12.1 %collective-permute-start = (bf16[2,16,16,128]{3,2,1,0:T(8,128)(2,1)S(1)}, bf16[2,16,16,128]{3,2,1,0:T(8,128)(2,1)S(1)}, u32[]{:S(2)}, u32[]{:S(2)}) collective-permute-start(bf16[2,16,16,128]{3,2,1,0:T(8,128)(2,1)S(1)} %pad_maximum_fusion.both), channel_id=1, source_target_pairs={{0,1},{1,2},{2,3},{3,4},{4,5},{5,6},{6,7},{8,9},{9,10},{10,11},{11... | collective-permute-start | bytes 393224 | tf_op jit(solution)/shard_map/ppermute | solution.py:330
  15.0 1.5 %constant_dynamic-slice_fusion.2 = (s32[1,1,1]{1,2,0:T(1,128)}, s32[1,1,1]{1,2,0:T(1,128)}, s32[1,1,1]{1,2,0:T(1,128)}, s32[1,1,1]{1,2,0:T(1,128)}) fusion(s32[8,64,2]{1,2,0:T(2,128)} %param.12, s32[]{:T(128)S(6)} %select_n.4, s32[]{:T(128)S(6)} %min.10, s32[]{:T(128)S(6)} %min.11, s32[]{:T(128)S(6)} %select_n.5, s32[]{:T(128)S(6)} %min.12), kind=kLoop, calls=%fused_computation.3 | loop fusion | bytes 52 | tf_op jit(solution)/shard_map/dynamic_slice | solution.py:358
  18.4 0.1 pad_add_fusion.starts
  18.5 0.0 collective-permute-done.1.under
  18.5 0.0 collective-permute-done.above
  18.5 0.6 assemble.1
  19.1 4.9 %collective-permute-start.2 = (bf16[2,32,16,128]{3,2,1,0:T(8,128)(2,1)S(1)}, bf16[2,32,16,128]{3,2,1,0:T(8,128)(2,1)S(1)}, u32[]{:S(2)}, u32[]{:S(2)}) collective-permute-start(bf16[2,32,16,128]{3,2,1,0:T(8,128)(2,1)S(1)} %get-tuple-element.41), channel_id=1, source_target_pairs={{0,8},{8,16},{16,24},{24,32},{32,40},{40,48},{48,56},{56,64},{64,7... | collective-permute-start | bytes 786440 | tf_op jit(solution)/shard_map/ppermute | solution.py:330
  24.0 1.9 %collective-permute-start.3 = (bf16[2,32,16,128]{3,2,1,0:T(8,128)(2,1)S(1)}, bf16[2,32,16,128]{3,2,1,0:T(8,128)(2,1)S(1)}, u32[]{:S(2)}, u32[]{:S(2)}) collective-permute-start(bf16[2,32,16,128]{3,2,1,0:T(8,128)(2,1)S(1)} %get-tuple-element.43), channel_id=1, source_target_pairs={{8,0},{16,8},{24,16},{32,24},{40,32},{48,40},{56,48},{64,56},{72,6... | collective-permute-start | bytes 786440 | tf_op jit(solution)/shard_map/ppermute | solution.py:334
  26.0 0.8 copy.15
  27.5 0.1 pad_add_fusion.1.where
  27.6 1.0 copy-done.1
  28.5 0.9 copy-done.2
  29.5 0.7 copy-done.3
  30.2 1.5 %prepare.1 = (f32[2,16,16,256]{3,2,1,0:T(8,128)S(1)}, bf16[3,512,256]{2,1,0:T(8,128)(2,1)S(1)}, bf16[3,256,512]{2,1,0:T(8,128)(2,1)S(1)}, bf16[3,256,512]{2,1,0:T(8,128)(2,1)S(1)}, bf16[2,256,256]{2,1,0:T(8,128)(2,1)S(1)}) custom-call(s32[2]{0:T(128)S(1)} %pad_add_fusion.1.where, s32[8,128]{1,0:T(8,128)S(1)} %copy.16.offsets, s32[32,32]{1,0:T(8,128)S(1)} %copy-done.3, ...), custom_call_target="tpu_custom_call" | custom-call | flops 5000000 | bytes 10000000 | tf_op jit(solution)/shard_map/prepare/pallas_call | solution.py:269
  31.7 0.0 collective-permute-done.2.left
  31.7 0.0 collective-permute-done.3.right
  31.7 3.9 %patch_work.1 = (bf16[2,32,16,128]{3,2,1,0:T(8,128)(2,1)S(1)}, f32[2,32,16,128]{3,2,1,0:T(8,128)S(1)}, bf16[2,32,16,128]{3,2,1,0:T(8,128)(2,1)S(1)}, bf16[4608,128]{1,0:T(8,128)(2,1)S(1)}) custom-call(s32[1]{0:T(128)} %bitcast.start, bf16[2,32,16,128]{3,2,1,0:T(8,128)(2,1)S(1)} %collective-permute-done.2.left, ...), custom_call_target="tpu_custom_call" | custom-call | flops 2000000000 | bytes 10000000 | tf_op jit(solution)/shard_map/patch_work/pallas_call | solution.py:288
  35.7 5.1 %all_to_all.35 = bf16[2,2304,128]{2,1,0:T(8,128)(2,1)} all-to-all(bf16[2,2304,128]{2,1,0:T(8,128)(2,1)S(1)} %bitcast.20), channel_id=1, replica_groups=mesh['y'=8,'zl'=4,'core'=2,'x'=4,'zh'=2] {'core'}, dimensions={0} | all-to-all | bytes 2359296 | tf_op jit(solution)/shard_map/all_to_all | solution.py:340
  40.8 2.5 %reduce_sum.48 = bf16[2304,128]{1,0:T(8,128)(2,1)} reduce(bf16[2,2304,128]{2,1,0:T(8,128)(2,1)} %all_to_all.35, bf16[]{:T(256)} %constant.47.clone.1), dimensions={0}, to_apply=%region_0.1 | reduce | flops 294912 | bytes 1769474 | tf_op jit(solution)/shard_map/reduce_sum | solution.py:341
  43.2 13.1 %all-to-all-start.1 = ((bf16[4,576,128]{2,1,0:T(8,128)(2,1)}), bf16[4,576,128]{2,1,0:T(8,128)(2,1)S(1)}, u32[]{:S(2)}, u32[]{:S(2)}) async-start(bf16[4,576,128]{2,1,0:T(8,128)(2,1)} %bitcast.11), calls=%async_computation.1 | async-start | bytes 1179648 | tf_op jit(solution)/shard_map/all_to_all | solution.py:340
  56.4 3.8 %collective-permute-start.4 = (bf16[2,32,16,128]{3,2,1,0:T(8,128)(2,1)S(1)}, bf16[2,32,16,128]{3,2,1,0:T(8,128)(2,1)S(1)}, u32[]{:S(2)}, u32[]{:S(2)}) collective-permute-start(bf16[2,32,16,128]{3,2,1,0:T(8,128)(2,1)S(1)} %get-tuple-element.50), channel_id=1, source_target_pairs={{0,8},{8,16},{16,24},{24,32},{32,40},{40,48},{48,56},{56,64},{64,7... | collective-permute-start | bytes 786440 | tf_op jit(solution)/shard_map/ppermute | solution.py:330
  60.1 5.8 %all-to-all-done.1 = bf16[4,576,128]{2,1,0:T(8,128)(2,1)S(1)} async-done(((bf16[4,576,128]{2,1,0:T(8,128)(2,1)}), bf16[4,576,128]{2,1,0:T(8,128)(2,1)S(1)}, u32[]{:S(2)}, u32[]{:S(2)}) %all-to-all-start.1) | async-done | bytes 589856 | tf_op jit(solution)/shard_map/all_to_all | solution.py:340
  66.0 0.1 reduce_sum.49
  66.1 0.0 collective-permute-done.4.from_left
  66.1 3.4 %collective-permute-start.5 = (bf16[2,32,16,128]{3,2,1,0:T(8,128)(2,1)S(1)}, bf16[2,32,16,128]{3,2,1,0:T(8,128)(2,1)S(1)}, u32[]{:S(2)}, u32[]{:S(2)}) collective-permute-start(bf16[2,32,16,128]{3,2,1,0:T(8,128)(2,1)S(1)} %get-tuple-element.54), channel_id=1, source_target_pairs={{8,0},{16,8},{24,16},{32,24},{40,32},{48,40},{56,48},{64,56},{72,6... | collective-permute-start | bytes 786440 | tf_op jit(solution)/shard_map/ppermute | solution.py:334
  69.5 21.4 %all_to_all.36 = bf16[8,72,128]{2,1,0:T(8,128)(2,1)S(1)} all-to-all(bf16[8,72,128]{2,1,0:T(8,128)(2,1)S(1)} %bitcast.23), channel_id=1, replica_groups=mesh['y'=8,'zl'=4,'core'=2,'x'=4,'zh'=2] {'y'}, dimensions={0} | all-to-all | bytes 294912 | tf_op jit(solution)/shard_map/all_to_all | solution.py:340
  91.0 0.0 collective-permute-done.5.from_right
  91.0 0.7 broadcast_in_dim.11
  91.6 3.4 %all-to-all-start.3 = ((bf16[8,72,128]{2,1,0:T(8,128)(2,1)}), bf16[8,72,128]{2,1,0:T(8,128)(2,1)S(1)}, u32[]{:S(2)}, u32[]{:S(2)}) async-start(bf16[8,72,128]{2,1,0:T(8,128)(2,1)} %broadcast_in_dim.11), calls=%async_computation.3 | async-start | bytes 294912 | tf_op jit(solution)/shard_map/all_to_all | solution.py:347
  95.0 0.8 combine.1
  95.8 5.9 %all-to-all-done.3 = bf16[8,72,128]{2,1,0:T(8,128)(2,1)S(1)} async-done(((bf16[8,72,128]{2,1,0:T(8,128)(2,1)}), bf16[8,72,128]{2,1,0:T(8,128)(2,1)S(1)}, u32[]{:S(2)}, u32[]{:S(2)}) %all-to-all-start.3) | async-done | bytes 147488 | tf_op jit(solution)/shard_map/all_to_all | solution.py:347
  101.7 0.7 broadcast_in_dim.12
  102.4 3.4 %all-to-all-start.4 = ((bf16[8,72,128]{2,1,0:T(8,128)(2,1)}), bf16[8,72,128]{2,1,0:T(8,128)(2,1)S(1)}, u32[]{:S(2)}, u32[]{:S(2)}) async-start(bf16[8,72,128]{2,1,0:T(8,128)(2,1)} %broadcast_in_dim.12), calls=%async_computation.4 | async-start | bytes 294912 | tf_op jit(solution)/shard_map/all_to_all | solution.py:347
  105.8 3.4 %collective-permute-start.6 = (bf16[2,16,16,128]{3,2,1,0:T(8,128)(2,1)S(1)}, bf16[2,16,16,128]{3,2,1,0:T(8,128)(2,1)S(1)}, u32[]{:S(2)}, u32[]{:S(2)}) collective-permute-start(bf16[2,16,16,128]{3,2,1,0:T(8,128)(2,1)S(1)} %get-tuple-element.64), channel_id=1, source_target_pairs={{0,1},{1,2},{2,3},{3,4},{4,5},{5,6},{6,7},{8,9},{9,10},{10,11},{11... | collective-permute-start | bytes 393224 | tf_op jit(solution)/shard_map/ppermute | solution.py:330
  109.1 1.9 %collective-permute-done.6.from_above = bf16[2,16,16,128]{3,2,1,0:T(8,128)(2,1)S(1)} collective-permute-done((bf16[2,16,16,128]{3,2,1,0:T(8,128)(2,1)S(1)}, bf16[2,16,16,128]{3,2,1,0:T(8,128)(2,1)S(1)}, u32[]{:S(2)}, u32[]{:S(2)}) %collective-permute-start.6) | collective-permute-done | bytes 131104 | tf_op jit(solution)/shard_map/ppermute | solution.py:330
  111.1 2.7 %all-to-all-done.4 = bf16[8,72,128]{2,1,0:T(8,128)(2,1)S(1)} async-done(((bf16[8,72,128]{2,1,0:T(8,128)(2,1)}), bf16[8,72,128]{2,1,0:T(8,128)(2,1)S(1)}, u32[]{:S(2)}, u32[]{:S(2)}) %all-to-all-start.4) | async-done | bytes 147488 | tf_op jit(solution)/shard_map/all_to_all | solution.py:347
  113.8 0.9 broadcast_in_dim.13
  114.7 8.2 %all-to-all-start.5 = ((bf16[4,576,128]{2,1,0:T(8,128)(2,1)}), bf16[4,576,128]{2,1,0:T(8,128)(2,1)S(1)}, u32[]{:S(2)}, u32[]{:S(2)}) async-start(bf16[4,576,128]{2,1,0:T(8,128)(2,1)} %broadcast_in_dim.13), calls=%async_computation.5 | async-start | bytes 1179648 | tf_op jit(solution)/shard_map/all_to_all | solution.py:347
  122.9 1.3 collective-permute-start.7
  124.2 8.4 %collective-permute-done.7.from_under = bf16[2,16,16,128]{3,2,1,0:T(8,128)(2,1)S(1)} collective-permute-done((bf16[2,16,16,128]{3,2,1,0:T(8,128)(2,1)S(1)}, bf16[2,16,16,128]{3,2,1,0:T(8,128)(2,1)S(1)}, u32[]{:S(2)}, u32[]{:S(2)}) %collective-permute-start.7) | collective-permute-done | bytes 131104 | tf_op jit(solution)/shard_map/ppermute | solution.py:334
  132.5 0.0 all-to-all-done.5
  132.5 0.1 broadcast_in_dim.14
  132.6 9.5 %all_to_all.37 = bf16[2,2304,128]{2,1,0:T(8,128)(2,1)S(1)} all-to-all(bf16[2,2304,128]{2,1,0:T(8,128)(2,1)S(1)} %broadcast_in_dim.14), channel_id=1, replica_groups=mesh['y'=8,'zl'=4,'core'=2,'x'=4,'zh'=2] {'core'}, dimensions={0} | all-to-all | bytes 2359296 | tf_op jit(solution)/shard_map/all_to_all | solution.py:347
  142.2 1.5 %unpack.1 = (f32[9,128,128]{2,1,0:T(8,128)}, f32[3,384,256]{2,1,0:T(8,128)}, f32[4,256,128]{2,1,0:T(8,128)}) custom-call(bf16[4608,128]{1,0:T(8,128)(2,1)S(1)} %bitcast.19), custom_call_target="tpu_custom_call" | custom-call | flops 1000000 | bytes 2000000 | tf_op jit(solution)/shard_map/unpack/pallas_call | solution.py:317
  143.6 0.7 finish.1
  (7 shorter events, 0.1 us)
Async XLA Ops:
  0.6 26.9 %copy-start = (bf16[3,3,128,256]{3,2,1,0:T(8,128)(2,1)S(1)}, bf16[3,3,128,256]{3,2,1,0:T(8,128)(2,1)}, u32[]{:S(2)}) copy-start(bf16[3,3,128,256]{3,2,1,0:T(8,128)(2,1)} %w_down.1) | copy-start | bytes 1769476
  1.6 16.9 %collective-permute-start.1 = (bf16[2,16,16,128]{3,2,1,0:T(8,128)(2,1)S(1)}, bf16[2,16,16,128]{3,2,1,0:T(8,128)(2,1)S(1)}, u32[]{:S(2)}, u32[]{:S(2)}) collective-permute-start(bf16[2,16,16,128]{3,2,1,0:T(8,128)(2,1)S(1)} %pad_maximum_fusion.both), channel_id=1, source_target_pairs={{1,0},{2,1},{3,2},{4,3},{5,4},{6,5},{7,6},{9,8},{10,9},{11,10},{12... | collective-permute-start | bytes 393224 | tf_op jit(solution)/shard_map/ppermute | solution.py:334
  2.9 15.6 %collective-permute-start = (bf16[2,16,16,128]{3,2,1,0:T(8,128)(2,1)S(1)}, bf16[2,16,16,128]{3,2,1,0:T(8,128)(2,1)S(1)}, u32[]{:S(2)}, u32[]{:S(2)}) collective-permute-start(bf16[2,16,16,128]{3,2,1,0:T(8,128)(2,1)S(1)} %pad_maximum_fusion.both), channel_id=1, source_target_pairs={{0,1},{1,2},{2,3},{3,4},{4,5},{5,6},{6,7},{8,9},{9,10},{10,11},{11... | collective-permute-start | bytes 393224 | tf_op jit(solution)/shard_map/ppermute | solution.py:330
  19.1 12.5 %collective-permute-start.2 = (bf16[2,32,16,128]{3,2,1,0:T(8,128)(2,1)S(1)}, bf16[2,32,16,128]{3,2,1,0:T(8,128)(2,1)S(1)}, u32[]{:S(2)}, u32[]{:S(2)}) collective-permute-start(bf16[2,32,16,128]{3,2,1,0:T(8,128)(2,1)S(1)} %get-tuple-element.41), channel_id=1, source_target_pairs={{0,8},{8,16},{16,24},{24,32},{32,40},{40,48},{48,56},{56,64},{64,7... | collective-permute-start | bytes 786440 | tf_op jit(solution)/shard_map/ppermute | solution.py:330
  24.0 7.7 %collective-permute-start.3 = (bf16[2,32,16,128]{3,2,1,0:T(8,128)(2,1)S(1)}, bf16[2,32,16,128]{3,2,1,0:T(8,128)(2,1)S(1)}, u32[]{:S(2)}, u32[]{:S(2)}) collective-permute-start(bf16[2,32,16,128]{3,2,1,0:T(8,128)(2,1)S(1)} %get-tuple-element.43), channel_id=1, source_target_pairs={{8,0},{16,8},{24,16},{32,24},{40,32},{48,40},{56,48},{64,56},{72,6... | collective-permute-start | bytes 786440 | tf_op jit(solution)/shard_map/ppermute | solution.py:334
  27.6 1.0 copy-start.1
  28.5 0.9 copy-start.2
  29.5 0.7 copy-start.3
  43.2 22.7 %all-to-all-start.1 = ((bf16[4,576,128]{2,1,0:T(8,128)(2,1)}), bf16[4,576,128]{2,1,0:T(8,128)(2,1)S(1)}, u32[]{:S(2)}, u32[]{:S(2)}) async-start(bf16[4,576,128]{2,1,0:T(8,128)(2,1)} %bitcast.11), calls=%async_computation.1 | async-start | bytes 1179648 | tf_op jit(solution)/shard_map/all_to_all | solution.py:340
  56.4 9.7 %collective-permute-start.4 = (bf16[2,32,16,128]{3,2,1,0:T(8,128)(2,1)S(1)}, bf16[2,32,16,128]{3,2,1,0:T(8,128)(2,1)S(1)}, u32[]{:S(2)}, u32[]{:S(2)}) collective-permute-start(bf16[2,32,16,128]{3,2,1,0:T(8,128)(2,1)S(1)} %get-tuple-element.50), channel_id=1, source_target_pairs={{0,8},{8,16},{16,24},{24,32},{32,40},{40,48},{48,56},{56,64},{64,7... | collective-permute-start | bytes 786440 | tf_op jit(solution)/shard_map/ppermute | solution.py:330
  66.1 24.9 %collective-permute-start.5 = (bf16[2,32,16,128]{3,2,1,0:T(8,128)(2,1)S(1)}, bf16[2,32,16,128]{3,2,1,0:T(8,128)(2,1)S(1)}, u32[]{:S(2)}, u32[]{:S(2)}) collective-permute-start(bf16[2,32,16,128]{3,2,1,0:T(8,128)(2,1)S(1)} %get-tuple-element.54), channel_id=1, source_target_pairs={{8,0},{16,8},{24,16},{32,24},{40,32},{48,40},{56,48},{64,56},{72,6... | collective-permute-start | bytes 786440 | tf_op jit(solution)/shard_map/ppermute | solution.py:334
  91.6 10.0 %all-to-all-start.3 = ((bf16[8,72,128]{2,1,0:T(8,128)(2,1)}), bf16[8,72,128]{2,1,0:T(8,128)(2,1)S(1)}, u32[]{:S(2)}, u32[]{:S(2)}) async-start(bf16[8,72,128]{2,1,0:T(8,128)(2,1)} %broadcast_in_dim.11), calls=%async_computation.3 | async-start | bytes 294912 | tf_op jit(solution)/shard_map/all_to_all | solution.py:347
  102.4 11.4 %all-to-all-start.4 = ((bf16[8,72,128]{2,1,0:T(8,128)(2,1)}), bf16[8,72,128]{2,1,0:T(8,128)(2,1)S(1)}, u32[]{:S(2)}, u32[]{:S(2)}) async-start(bf16[8,72,128]{2,1,0:T(8,128)(2,1)} %broadcast_in_dim.12), calls=%async_computation.4 | async-start | bytes 294912 | tf_op jit(solution)/shard_map/all_to_all | solution.py:347
  105.8 5.3 %collective-permute-start.6 = (bf16[2,16,16,128]{3,2,1,0:T(8,128)(2,1)S(1)}, bf16[2,16,16,128]{3,2,1,0:T(8,128)(2,1)S(1)}, u32[]{:S(2)}, u32[]{:S(2)}) collective-permute-start(bf16[2,16,16,128]{3,2,1,0:T(8,128)(2,1)S(1)} %get-tuple-element.64), channel_id=1, source_target_pairs={{0,1},{1,2},{2,3},{3,4},{4,5},{5,6},{6,7},{8,9},{9,10},{10,11},{11... | collective-permute-start | bytes 393224 | tf_op jit(solution)/shard_map/ppermute | solution.py:330
  114.7 17.9 %all-to-all-start.5 = ((bf16[4,576,128]{2,1,0:T(8,128)(2,1)}), bf16[4,576,128]{2,1,0:T(8,128)(2,1)S(1)}, u32[]{:S(2)}, u32[]{:S(2)}) async-start(bf16[4,576,128]{2,1,0:T(8,128)(2,1)} %broadcast_in_dim.13), calls=%async_computation.5 | async-start | bytes 1179648 | tf_op jit(solution)/shard_map/all_to_all | solution.py:347
  122.9 9.7 %collective-permute-start.7 = (bf16[2,16,16,128]{3,2,1,0:T(8,128)(2,1)S(1)}, bf16[2,16,16,128]{3,2,1,0:T(8,128)(2,1)S(1)}, u32[]{:S(2)}, u32[]{:S(2)}) collective-permute-start(bf16[2,16,16,128]{3,2,1,0:T(8,128)(2,1)S(1)} %get-tuple-element.68), channel_id=1, source_target_pairs={{1,0},{2,1},{3,2},{4,3},{5,4},{6,5},{7,6},{9,8},{10,9},{11,10},{12... | collective-permute-start | bytes 393224 | tf_op jit(solution)/shard_map/ppermute | solution.py:334

commit v5 on v4

--- a/solution.py
+++ b/solution.py
@@ -21,7 +21,8 @@
 FIRST_ROWS = 9 * C1
 DOWN_ROWS = 18 * C1
 UP_ROWS = 4 * C2
-FLAT_ROWS = 4608
+USED_ROWS = FIRST_ROWS + DOWN_ROWS + UP_ROWS
+HALF_ROWS = 2304
 
 
 def dot(a, b):
@@ -87,12 +88,17 @@
         out[...] = grown[:, pl.ds(starts[side], 32)]
 
 
-def combine_kernel(starts, from_left, own, from_right, up, mid, down, canvas):
+def add_left_kernel(starts, from_left, own, canvas):
     canvas[...] = jnp.zeros_like(canvas)
     canvas[:, pl.ds(starts[1], 32)] = own[...]
-    for side, part in ((0, from_left), (2, from_right)):
-        spot = (slice(None), pl.ds(starts[side], 32))
-        canvas[spot] = canvas[spot] + part[...].astype(F32)
+    spot = (slice(None), pl.ds(starts[0], 32))
+    canvas[spot] = canvas[spot] + from_left[...].astype(F32)
+
+
+def add_right_kernel(starts, given, from_right, up, mid, down, canvas):
+    canvas[...] = given[...]
+    spot = (slice(None), pl.ds(starts[2], 32))
+    canvas[spot] = canvas[spot] + from_right[...].astype(F32)
     up[...] = canvas[:, 0:16].astype(BF16)
     mid[...] = canvas[:, 16:32]
     down[...] = canvas[:, 32:48].astype(BF16)
@@ -104,9 +110,13 @@
     field_grad[...] = total[1]
 
 
-def unpack_kernel(scale, halves, g_first, g_down, g_up):
+def unpack_kernel(scale, core, own, other, g_first, g_down, g_up, halves):
+    halves[core[0]] = own[...]
+    halves[1 - core[0]] = other[...]
+
     def rows(base, count):
-        return halves[base : base + count].astype(F32) * scale
+        half, at = base // HALF_ROWS, base % HALF_ROWS
+        return halves[half, at : at + count].astype(F32) * scale
 
     for t in range(9):
         g_first[t] = rows(t * C1, C1)
@@ -137,10 +147,15 @@
 
 def net_kernel(
     start, left, middle, right, fb, rf, rft, wd, rdt, ru,
-    left_o, mid_o, right_o, flat,
-    fs, cs, xv, hv, gv, g4, gs, bs, can_b, can_g,
+    left_o, mid_o, right_o, keep, send,
+    fs, cs, xv, hv, gv, g4, gs, bs, can_b, can_g, halves,
 ):
-    start_c = start[0]
+    start_c, core = start[0], start[1]
+
+    def put(base, value):
+        half, at = base // HALF_ROWS, base % HALF_ROWS
+        halves[core if half == 0 else 1 - core, at : at + value.shape[0]] = value.astype(BF16)
+
     for ref in (xv, hv, gv):
         edge = jnp.zeros((16, ref.shape[-1]), BF16)
         ref[0, 0] = edge
@@ -193,20 +208,20 @@
         bs[a] = (fb[a].reshape(256, 2 * C1) * out).reshape(16, 16, 2 * C1)
         g = gs[a].reshape(256, 2 * C1).astype(BF16)
         g_d = g_d + dot_nt(g, ru[a])
-        g_up = dot(d_t, g).astype(BF16)
+        g_up = dot(d_t, g)
         base = FIRST_ROWS + DOWN_ROWS + 2 * a * C2
-        flat[base : base + C2] = g_up[:, :C1]
-        flat[base + C2 : base + 2 * C2] = g_up[:, C1:]
+        put(base, g_up[:, :C1])
+        put(base + C2, g_up[:, C1:])
     g_pre = g_d.astype(BF16).astype(F32) * slope_d
     g4[0:16] = jnp.concatenate([g_pre.astype(BF16), shifted(g_pre, -1).astype(BF16)], axis=1).reshape(
         16, 16, 2 * C2
     )
     g_pre_t = g_pre.T.astype(BF16)
     for t in range(3):
-        g_down = dot(g_pre_t, window(hv, 0, t)).T.astype(BF16)
+        g_down = dot(g_pre_t, window(hv, 0, t)).T
         base = FIRST_ROWS + 6 * t * C1
-        flat[base : base + 3 * C1] = g_down[:, :C1]
-        flat[base + 3 * C1 : base + 6 * C1] = g_down[:, C1:]
+        put(base, g_down[:, :C1])
+        put(base + 3 * C1, g_down[:, C1:])
     here = g4[0:16].reshape(256, 2 * C2)
     below = g4[1:17].reshape(256, 2 * C2)
     g_h = [dot_nt(here, rdt[1]), dot_nt(here, rdt[2]) + dot_nt(below, rdt[0])]
@@ -221,11 +236,10 @@
             block = (
                 g_first[:C1, ct * C1 : (ct + 1) * C1] + g_first[C1:, (ct + 1) * C1 : (ct + 2) * C1]
             )
-            base = (3 * t + ct) * C1
-            flat[base : base + C1] = block.T.astype(BF16)
-    flat[FIRST_ROWS + DOWN_ROWS + UP_ROWS :] = jnp.zeros(
-        (FLAT_ROWS - FIRST_ROWS - DOWN_ROWS - UP_ROWS, C1), BF16
-    )
+            put((3 * t + ct) * C1, block.T)
+    put(USED_ROWS, jnp.zeros((2 * HALF_ROWS - USED_ROWS, C1), F32))
+    keep[...] = halves[0]
+    send[...] = halves[1]
     for a in range(2):
         g_x = (
             dot_nt(window(gv, a, 0), rft[0])
@@ -291,10 +305,11 @@
             strip,
             jax.ShapeDtypeStruct((2, 32, 16, C1), F32),
             strip,
-            jax.ShapeDtypeStruct((FLAT_ROWS, C1), BF16),
+            jax.ShapeDtypeStruct((HALF_ROWS, C1), BF16),
+            jax.ShapeDtypeStruct((HALF_ROWS, C1), BF16),
         ),
         in_specs=[SMEM] + [VMEM] * 9,
-        out_specs=[VMEM] * 4,
+        out_specs=[VMEM] * 5,
         scratch_shapes=[
             pltpu.VMEM((32, 64, C1), F32),
             pltpu.VMEM((32, 64, C1), F32),
@@ -306,6 +321,7 @@
             pltpu.VMEM((2, 16, 16, 2 * C1), F32),
             pltpu.VMEM((32, 48, C1), F32),
             pltpu.VMEM((32, 48, C1), F32),
+            pltpu.VMEM((2, HALF_ROWS, C1), BF16),
         ],
         compiler_params=pltpu.CompilerParams(vmem_limit_bytes=24 * 2**20),
         cost_estimate=pl.CostEstimate(flops=2 * 10**9, bytes_accessed=10**7, transcendentals=200000),
@@ -334,6 +350,14 @@
     return lax.ppermute(x, axes, [(i + 1, i) for i in range(lax.axis_size(axes) - 1)])
 
 
+def swapped(x):
+    return lax.ppermute(x, "core", [(0, 1), (1, 0)])
+
+
+def added(x, y):
+    return (x.astype(F32) + y.astype(F32)).astype(BF16)
+
+
 def scattered(x, axes):
     size = lax.axis_size(axes)
     parts = x.reshape(size, x.shape[0] // size, x.shape[1])
@@ -357,11 +381,13 @@
     starts = jnp.stack(
         [MARGIN + offsets[row_at, jnp.clip(col_at + step, 0, cols_n - 1), 0] for step in (-1, 0, 1)]
     )
-    start_c = (MARGIN + offsets[row_at, col_at, 1])[None]
+    core = lax.axis_index("core").astype(jnp.int32)
+    start = jnp.stack([MARGIN + offsets[row_at, col_at, 1], core])
     fb, rf, rft, rdt, ru = prepared(
         where, offsets.reshape(rows_n, 2 * cols_n), blend_table, w_first, w_down, w_up
     )
     above, under = from_before(ROW, both), from_after(ROW, both)
+    above, under, fb, rf, rft, rdt, ru = lax.optimization_barrier((above, under, fb, rf, rft, rdt, ru))
     window_shape = (2, 32, TILE, C1)
     to_left, own, to_right = small_call(
         assemble_kernel,
@@ -375,37 +401,36 @@
         smem=1,
     )
     left, right = from_before(COL, to_right), from_after(COL, to_left)
-    to_left, own, to_right, flat = patch_work(
-        start_c, left, own, right, fb, rf, rft, w_down.reshape(3, 3 * C1, C2), rdt, ru
+    to_left, own, to_right, keep, send = patch_work(
+        start, left, own, right, fb, rf, rft, w_down.reshape(3, 3 * C1, C2), rdt, ru
     )
     from_left = from_before(COL, to_right)
-    part = scattered(flat, "core")
+    part = added(keep, swapped(send))
     part = scattered(part, "x")
     part, from_left, to_left = lax.optimization_barrier((part, from_left, to_left))
     from_right = from_after(COL, to_left)
     part = scattered(part, "y")
-    part, from_left, from_right = lax.optimization_barrier((part, from_left, from_right))
+    canvas = small_call(
+        add_left_kernel, "add_left", [((2, 48, TILE, C1), F32)], [], starts, from_left, own, smem=1
+    )[0]
+    part, canvas, from_right = lax.optimization_barrier((part, canvas, from_right))
     part = gathered(part, ("zl", "zh")).astype(F32).sum(0).astype(BF16)
     tile_shape = (2, TILE, TILE, C1)
     up, own, down = small_call(
-        combine_kernel,
-        "combine",
+        add_right_kernel,
+        "add_right",
         [(tile_shape, BF16), (tile_shape, F32), (tile_shape, BF16)],
         [pltpu.VMEM((2, 48, TILE, C1), F32)],
         starts,
-        from_left,
-        own,
+        canvas,
         from_right,
         smem=1,
     )
     part, up, own, down = lax.optimization_barrier((part, up, own, down))
-    from_above = from_before(ROW, down)
+    from_above, from_under = from_before(ROW, down), from_after(ROW, up)
     part = gathered(part, "y").reshape(-1, C1)
-    part, from_above, up = lax.optimization_barrier((part, from_above, up))
-    from_under = from_after(ROW, up)
+    part, own, from_above, from_under = lax.optimization_barrier((part, own, from_above, from_under))
     part = gathered(part, "x").reshape(-1, C1)
-    part, from_above, from_under = lax.optimization_barrier((part, from_above, from_under))
-    total = gathered(part, "core").reshape(-1, C1)
     blended, field_grad = small_call(
         finish_kernel,
         "finish",
@@ -415,13 +440,18 @@
         from_above,
         from_under,
     )
+    part, blended, field_grad = lax.optimization_barrier((part, blended, field_grad))
+    other = swapped(part)
     scale = 1.0 / math.sqrt(TILE * rows_n * TILE * cols_n)
     g_first, g_down, g_up = small_call(
         functools.partial(unpack_kernel, scale),
         "unpack",
         [((9, C1, C1), F32), ((3, 3 * C1, C2), F32), ((4, C2, C1), F32)],
-        [],
-        total,
+        [pltpu.VMEM((2, HALF_ROWS, C1), BF16)],
+        core[None],
+        part,
+        other,
+        smem=1,
     )
     return (
         blended,

time: 146 us -> 143 us (0.979)
  blocking collectives: 36.1 us -> 0 us
  waiting for transfers between devices: 24.8 us -> 44.3 us
  starting transfers between devices: 60.1 us -> 72.8 us
    all_to_all x3 -> x0, blocking collectives: 36.1 us -> none  [the longest x2 26.5 us: scattered(): got = lax.all_to_all(parts, axes, 0, 0, tiled=True)]
    ppermute x0 -> x2, starting transfers between devices: none -> 11.6 us  [swapped(): return lax.ppermute(x, 'core', [(0, 1), (1, 0)])]
    all_to_all x1 -> x2, waiting for transfers between devices: 5.83 us -> 14.5 us  [scattered(): got = lax.all_to_all(parts, axes, 0, 0, tiled=True)]
    all_to_all x1 -> x2, starting transfers between devices: 13.1 us -> 18.6 us  [scattered(): got = lax.all_to_all(parts, axes, 0, 0, tiled=True)]
    ppermute x4, waiting for transfers between devices: 8.42 us -> 12.9 us  [from_after(): lax.ppermute(x, axes, [(i + 1, i) for i in range(lax.axis_size(axes) - 1)])]
    all_to_all x3, waiting for transfers between devices: 8.57 us -> 12.6 us  [gathered(): return lax.all_to_all(parts, axes, 0, 0, tiled=True)]
    ppermute x0 -> x2, waiting for transfers between devices: none -> 3.58 us  [swapped(): return lax.ppermute(x, 'core', [(0, 1), (1, 0)])]
    all_to_all x3, starting transfers between devices: 15 us -> 12.2 us  [gathered(): return lax.all_to_all(parts, axes, 0, 0, tiled=True)]
  transfers between devices with their start and end apart: 12 -> 15, of which waited for: 5 -> 9; matrix products, arithmetic and copies ran while one was open for 2% -> 2% of each run, Pallas kernels for 2% -> 2%
where the time goes in v5:
time: 143 us; the launch traced here: 142 us
  starting transfers between devices  72.8 us (51%)
  waiting for transfers between devices  44.3 us (31%)
  Pallas kernels  10.2 us (7%)
  local copies, waits for them, and re-layouts  8.25 us (6%)
  between operations  3.42 us (2%)
  other arithmetic  2.9 us (2%)
    ppermute x4, starting transfers between devices, from_before(): lax.ppermute(x, axes, [(i, i + 1) for i in range(lax.axis_size(axes) - 1)])  22.1 us
    all_to_all x2, starting transfers between devices, scattered(): got = lax.all_to_all(parts, axes, 0, 0, tiled=True)  18.6 us
    all_to_all x2, waiting for transfers between devices, scattered(): got = lax.all_to_all(parts, axes, 0, 0, tiled=True)  14.5 us
    ppermute x4, waiting for transfers between devices, from_after(): lax.ppermute(x, axes, [(i + 1, i) for i in range(lax.axis_size(axes) - 1)])  12.9 us
    all_to_all x3, waiting for transfers between devices, gathered(): return lax.all_to_all(parts, axes, 0, 0, tiled=True)  12.6 us
    all_to_all x3, starting transfers between devices, gathered(): return lax.all_to_all(parts, axes, 0, 0, tiled=True)  12.2 us
    ppermute x2, starting transfers between devices, swapped(): return lax.ppermute(x, 'core', [(0, 1), (1, 0)])  11.6 us
    ppermute x4, starting transfers between devices, from_after(): lax.ppermute(x, axes, [(i + 1, i) for i in range(lax.axis_size(axes) - 1)])  8.27 us
  transfers between devices with their start and end apart: 15, of which 9 were waited for; matrix products, arithmetic and copies ran while one was open for 2% of the time, Pallas kernels for 2%

profile of v5, /device:TPU:1, one launch (start us, length us, event | category | flops | bytes accessed | tf_op | source)
XLA Modules:
  0.0 141.9 jit_solution(6315714425526803991)
XLA Ops:
  0.6 0.9 pad_maximum_fusion.both
  1.5 1.3 collective-permute-start.1
  2.8 12.1 %collective-permute-start = (bf16[2,16,16,128]{3,2,1,0:T(8,128)(2,1)S(1)}, bf16[2,16,16,128]{3,2,1,0:T(8,128)(2,1)S(1)}, u32[]{:S(2)}, u32[]{:S(2)}) collective-permute-start(bf16[2,16,16,128]{3,2,1,0:T(8,128)(2,1)S(1)} %pad_maximum_fusion.both), channel_id=1, source_target_pairs={{0,1},{1,2},{2,3},{3,4},{4,5},{5,6},{6,7},{8,9},{9,10},{10,11},{11... | collective-permute-start | bytes 393224 | tf_op jit(solution)/shard_map/ppermute | solution.py:346
  14.9 0.1 pad_add_fusion.2.where
  15.0 0.8 copy.15
  15.8 1.4 %constant_dynamic-slice_fusion.2 = (s32[1,1,1]{1,2,0:T(1,128)}, s32[1,1,1]{1,2,0:T(1,128)}, s32[1,1,1]{1,2,0:T(1,128)}, s32[1,1,1]{1,2,0:T(1,128)}) fusion(s32[8,64,2]{1,2,0:T(2,128)} %param.12, s32[]{:T(128)S(6)} %select_n.4, s32[]{:T(128)S(6)} %min.10, s32[]{:T(128)S(6)} %min.11, s32[]{:T(128)S(6)} %select_n.5, s32[]{:T(128)S(6)} %min.12), kind=kLoop, calls=%fused_computation.4 | loop fusion | bytes 52 | tf_op jit(solution)/shard_map/dynamic_slice | solution.py:382
  19.2 1.1 copy-done
  20.3 1.0 copy-done.2
  21.3 0.9 copy-done.3
  22.2 0.7 copy-done.4
  23.0 1.5 %prepare.1 = (f32[2,16,16,256]{3,2,1,0:T(8,128)S(1)}, bf16[3,512,256]{2,1,0:T(8,128)(2,1)S(1)}, bf16[3,256,512]{2,1,0:T(8,128)(2,1)S(1)}, bf16[3,256,512]{2,1,0:T(8,128)(2,1)S(1)}, bf16[2,256,256]{2,1,0:T(8,128)(2,1)S(1)}) custom-call(s32[2]{0:T(128)S(1)} %pad_add_fusion.2.where, s32[8,128]{1,0:T(8,128)S(1)} %copy.16.offsets, s32[32,32]{1,0:T(8,128)S(1)} %copy-done.4, ...), custom_call_target="tpu_custom_call" | custom-call | flops 5000000 | bytes 10000000 | tf_op jit(solution)/shard_map/prepare/pallas_call | solution.py:283
  24.4 0.1 pad_add_fusion.1.starts
  24.5 0.0 collective-permute-done.above
  24.5 0.6 assemble.1
  25.1 3.9 %collective-permute-start.2 = (bf16[2,32,16,128]{3,2,1,0:T(8,128)(2,1)S(1)}, bf16[2,32,16,128]{3,2,1,0:T(8,128)(2,1)S(1)}, u32[]{:S(2)}, u32[]{:S(2)}) collective-permute-start(bf16[2,32,16,128]{3,2,1,0:T(8,128)(2,1)S(1)} %get-tuple-element.57), channel_id=1, source_target_pairs={{0,8},{8,16},{16,24},{24,32},{32,40},{40,48},{48,56},{56,64},{64,7... | collective-permute-start | bytes 786440 | tf_op jit(solution)/shard_map/ppermute | solution.py:346
  29.1 2.5 %collective-permute-start.3 = (bf16[2,32,16,128]{3,2,1,0:T(8,128)(2,1)S(1)}, bf16[2,32,16,128]{3,2,1,0:T(8,128)(2,1)S(1)}, u32[]{:S(2)}, u32[]{:S(2)}) collective-permute-start(bf16[2,32,16,128]{3,2,1,0:T(8,128)(2,1)S(1)} %get-tuple-element.59), channel_id=1, source_target_pairs={{8,0},{16,8},{24,16},{32,24},{40,32},{48,40},{56,48},{64,56},{72,6... | collective-permute-start | bytes 786440 | tf_op jit(solution)/shard_map/ppermute | solution.py:350
  32.3 0.1 pad_add_fusion.start
  32.3 0.0 collective-permute-done.2.left
  32.4 4.4 %collective-permute-done.3.right = bf16[2,32,16,128]{3,2,1,0:T(8,128)(2,1)S(1)} collective-permute-done((bf16[2,32,16,128]{3,2,1,0:T(8,128)(2,1)S(1)}, bf16[2,32,16,128]{3,2,1,0:T(8,128)(2,1)S(1)}, u32[]{:S(2)}, u32[]{:S(2)}) %collective-permute-start.3) | collective-permute-done | bytes 262176 | tf_op jit(solution)/shard_map/ppermute | solution.py:350
  36.8 4.5 %patch_work.1 = (bf16[2,32,16,128]{3,2,1,0:T(8,128)(2,1)S(1)}, f32[2,32,16,128]{3,2,1,0:T(8,128)S(1)}, bf16[2,32,16,128]{3,2,1,0:T(8,128)(2,1)S(1)}, bf16[2304,128]{1,0:T(8,128)(2,1)S(1)}, bf16[2304,128]{1,0:T(8,128)(2,1)S(1)}) custom-call(s32[2]{0:T(128)S(1)} %pad_add_fusion.start, bf16[2,32,16,128]{3,2,1,0:T(8,128)(2,1)S(1)} %collective-permute-done.2.left, ...), custom_call_target="tpu_custom_call" | custom-call | flops 2000000000 | bytes 10000000 | tf_op jit(solution)/shard_map/patch_work/pallas_call | solution.py:302
  41.3 1.9 %collective-permute-start.4 = (bf16[2304,128]{1,0:T(8,128)(2,1)S(1)}, bf16[2304,128]{1,0:T(8,128)(2,1)S(1)}, u32[]{:S(2)}, u32[]{:S(2)}) collective-permute-start(bf16[2304,128]{1,0:T(8,128)(2,1)S(1)} %get-tuple-element.66), channel_id=1, source_target_pairs={{0,8},{8,0},{1,9},{9,1},{2,10},{10,2},{3,11},{11,3},{4,12},{12,4},... | collective-permute-start | bytes 1769480 | tf_op jit(solution)/shard_map/ppermute | solution.py:354
  43.2 2.0 %collective-permute-done.4 = bf16[2304,128]{1,0:T(8,128)(2,1)S(1)} collective-permute-done((bf16[2304,128]{1,0:T(8,128)(2,1)S(1)}, bf16[2304,128]{1,0:T(8,128)(2,1)S(1)}, u32[]{:S(2)}, u32[]{:S(2)}) %collective-permute-start.4) | collective-permute-done | bytes 589856 | tf_op jit(solution)/shard_map/ppermute | solution.py:354
  45.2 1.0 add_convert_fusion
  46.2 7.5 %all-to-all-start = ((bf16[4,576,128]{2,1,0:T(8,128)(2,1)}), bf16[4,576,128]{2,1,0:T(8,128)(2,1)S(1)}, u32[]{:S(2)}, u32[]{:S(2)}) async-start(bf16[4,576,128]{2,1,0:T(8,128)(2,1)} %bitcast.11), calls=%async_computation | async-start | bytes 1179648 | tf_op jit(solution)/shard_map/all_to_all | solution.py:364
  53.7 2.7 %collective-permute-start.5 = (bf16[2,32,16,128]{3,2,1,0:T(8,128)(2,1)S(1)}, bf16[2,32,16,128]{3,2,1,0:T(8,128)(2,1)S(1)}, u32[]{:S(2)}, u32[]{:S(2)}) collective-permute-start(bf16[2,32,16,128]{3,2,1,0:T(8,128)(2,1)S(1)} %get-tuple-element.67), channel_id=1, source_target_pairs={{0,8},{8,16},{16,24},{24,32},{32,40},{40,48},{48,56},{56,64},{64,7... | collective-permute-start | bytes 786440 | tf_op jit(solution)/shard_map/ppermute | solution.py:346
  56.4 7.1 %all-to-all-done = bf16[4,576,128]{2,1,0:T(8,128)(2,1)S(1)} async-done(((bf16[4,576,128]{2,1,0:T(8,128)(2,1)}), bf16[4,576,128]{2,1,0:T(8,128)(2,1)S(1)}, u32[]{:S(2)}, u32[]{:S(2)}) %all-to-all-start) | async-done | bytes 589856 | tf_op jit(solution)/shard_map/all_to_all | solution.py:364
  63.5 0.8 reduce_sum.36
  64.3 3.2 %collective-permute-start.6 = (bf16[2,32,16,128]{3,2,1,0:T(8,128)(2,1)S(1)}, bf16[2,32,16,128]{3,2,1,0:T(8,128)(2,1)S(1)}, u32[]{:S(2)}, u32[]{:S(2)}) collective-permute-start(bf16[2,32,16,128]{3,2,1,0:T(8,128)(2,1)S(1)} %get-tuple-element.72), channel_id=1, source_target_pairs={{8,0},{16,8},{24,16},{32,24},{40,32},{48,40},{56,48},{64,56},{72,6... | collective-permute-start | bytes 786440 | tf_op jit(solution)/shard_map/ppermute | solution.py:350
  67.5 11.1 %all-to-all-start.1 = ((bf16[8,72,128]{2,1,0:T(8,128)(2,1)}), bf16[8,72,128]{2,1,0:T(8,128)(2,1)S(1)}, u32[]{:S(2)}, u32[]{:S(2)}) async-start(bf16[8,72,128]{2,1,0:T(8,128)(2,1)} %bitcast.12), calls=%async_computation.1 | async-start | bytes 294912 | tf_op jit(solution)/shard_map/all_to_all | solution.py:364
  78.6 0.7 add_left.1.given
  79.2 7.4 %all-to-all-done.1 = bf16[8,72,128]{2,1,0:T(8,128)(2,1)S(1)} async-done(((bf16[8,72,128]{2,1,0:T(8,128)(2,1)}), bf16[8,72,128]{2,1,0:T(8,128)(2,1)S(1)}, u32[]{:S(2)}, u32[]{:S(2)}) %all-to-all-start.1) | async-done | bytes 147488 | tf_op jit(solution)/shard_map/all_to_all | solution.py:364
  86.7 0.7 broadcast_in_dim.6
  87.4 5.4 %all-to-all-start.2 = ((bf16[8,72,128]{2,1,0:T(8,128)(2,1)}), bf16[8,72,128]{2,1,0:T(8,128)(2,1)S(1)}, u32[]{:S(2)}, u32[]{:S(2)}) async-start(bf16[8,72,128]{2,1,0:T(8,128)(2,1)} %broadcast_in_dim.6), calls=%async_computation.2 | async-start | bytes 294912 | tf_op jit(solution)/shard_map/all_to_all | solution.py:371
  92.8 0.7 add_right.1
  93.5 6.1 %all-to-all-done.2 = bf16[8,72,128]{2,1,0:T(8,128)(2,1)S(1)} async-done(((bf16[8,72,128]{2,1,0:T(8,128)(2,1)}), bf16[8,72,128]{2,1,0:T(8,128)(2,1)S(1)}, u32[]{:S(2)}, u32[]{:S(2)}) %all-to-all-start.2) | async-done | bytes 147488 | tf_op jit(solution)/shard_map/all_to_all | solution.py:371
  99.5 0.7 broadcast_in_dim.7
  100.2 3.4 %all-to-all-start.3 = ((bf16[8,72,128]{2,1,0:T(8,128)(2,1)}), bf16[8,72,128]{2,1,0:T(8,128)(2,1)S(1)}, u32[]{:S(2)}, u32[]{:S(2)}) async-start(bf16[8,72,128]{2,1,0:T(8,128)(2,1)} %broadcast_in_dim.7), calls=%async_computation.3 | async-start | bytes 294912 | tf_op jit(solution)/shard_map/all_to_all | solution.py:371
  103.6 3.3 %collective-permute-start.7 = (bf16[2,16,16,128]{3,2,1,0:T(8,128)(2,1)S(1)}, bf16[2,16,16,128]{3,2,1,0:T(8,128)(2,1)S(1)}, u32[]{:S(2)}, u32[]{:S(2)}) collective-permute-start(bf16[2,16,16,128]{3,2,1,0:T(8,128)(2,1)S(1)} %get-tuple-element.81), channel_id=1, source_target_pairs={{0,1},{1,2},{2,3},{3,4},{4,5},{5,6},{6,7},{8,9},{9,10},{10,11},{11... | collective-permute-start | bytes 393224 | tf_op jit(solution)/shard_map/ppermute | solution.py:346
  107.0 1.3 collective-permute-start.8
  108.3 0.6 collective-permute-done.7.from_above
  108.9 8.5 %collective-permute-done.8.from_under = bf16[2,16,16,128]{3,2,1,0:T(8,128)(2,1)S(1)} collective-permute-done((bf16[2,16,16,128]{3,2,1,0:T(8,128)(2,1)S(1)}, bf16[2,16,16,128]{3,2,1,0:T(8,128)(2,1)S(1)}, u32[]{:S(2)}, u32[]{:S(2)}) %collective-permute-start.8) | collective-permute-done | bytes 131104 | tf_op jit(solution)/shard_map/ppermute | solution.py:350
  117.4 0.9 broadcast_in_dim.8
  118.3 3.5 %all-to-all-start.4 = ((bf16[4,576,128]{2,1,0:T(8,128)(2,1)}), bf16[4,576,128]{2,1,0:T(8,128)(2,1)S(1)}, u32[]{:S(2)}, u32[]{:S(2)}) async-start(bf16[4,576,128]{2,1,0:T(8,128)(2,1)} %broadcast_in_dim.8), calls=%async_computation.4 | async-start | bytes 1179648 | tf_op jit(solution)/shard_map/all_to_all | solution.py:371
  121.8 0.7 finish.1
  122.5 6.5 %all-to-all-done.4 = bf16[4,576,128]{2,1,0:T(8,128)(2,1)S(1)} async-done(((bf16[4,576,128]{2,1,0:T(8,128)(2,1)}), bf16[4,576,128]{2,1,0:T(8,128)(2,1)S(1)}, u32[]{:S(2)}, u32[]{:S(2)}) %all-to-all-start.4) | async-done | bytes 589856 | tf_op jit(solution)/shard_map/all_to_all | solution.py:371
  129.1 9.7 %collective-permute-start.9 = (bf16[2304,128]{1,0:T(8,128)(2,1)S(1)}, bf16[2304,128]{1,0:T(8,128)(2,1)S(1)}, u32[]{:S(2)}, u32[]{:S(2)}) collective-permute-start(bf16[2304,128]{1,0:T(8,128)(2,1)S(1)} %bitcast.18), channel_id=1, source_target_pairs={{0,8},{8,0},{1,9},{9,1},{2,10},{10,2},{3,11},{11,3},{4,12},{12,4},... | collective-permute-start | bytes 1769480 | tf_op jit(solution)/shard_map/ppermute | solution.py:354
  138.7 1.6 %collective-permute-done.9.other = bf16[2304,128]{1,0:T(8,128)(2,1)S(1)} collective-permute-done((bf16[2304,128]{1,0:T(8,128)(2,1)S(1)}, bf16[2304,128]{1,0:T(8,128)(2,1)S(1)}, u32[]{:S(2)}, u32[]{:S(2)}) %collective-permute-start.9) | collective-permute-done | bytes 589856 | tf_op jit(solution)/shard_map/ppermute | solution.py:354
  140.4 1.6 %unpack.1 = (f32[9,128,128]{2,1,0:T(8,128)}, f32[3,384,256]{2,1,0:T(8,128)}, f32[4,256,128]{2,1,0:T(8,128)}) custom-call(s32[1]{0:T(128)} %bitcast.1.core, bf16[2304,128]{1,0:T(8,128)(2,1)S(1)} %bitcast.19, bf16[2304,128]{1,0:T(8,128)(2,1)S(1)} %collective-permute-done.9.other), custom_call_target="tpu_custom_call" | custom-call | flops 1000000 | bytes 2000000 | tf_op jit(solution)/shard_map/unpack/pallas_call | solution.py:333
  (13 shorter events, 0.1 us)
Async XLA Ops:
  1.5 23.0 %collective-permute-start.1 = (bf16[2,16,16,128]{3,2,1,0:T(8,128)(2,1)S(1)}, bf16[2,16,16,128]{3,2,1,0:T(8,128)(2,1)S(1)}, u32[]{:S(2)}, u32[]{:S(2)}) collective-permute-start(bf16[2,16,16,128]{3,2,1,0:T(8,128)(2,1)S(1)} %pad_maximum_fusion.both), channel_id=1, source_target_pairs={{1,0},{2,1},{3,2},{4,3},{5,4},{6,5},{7,6},{9,8},{10,9},{11,10},{12... | collective-permute-start | bytes 393224 | tf_op jit(solution)/shard_map/ppermute | solution.py:350
  2.8 21.7 %collective-permute-start = (bf16[2,16,16,128]{3,2,1,0:T(8,128)(2,1)S(1)}, bf16[2,16,16,128]{3,2,1,0:T(8,128)(2,1)S(1)}, u32[]{:S(2)}, u32[]{:S(2)}) collective-permute-start(bf16[2,16,16,128]{3,2,1,0:T(8,128)(2,1)S(1)} %pad_maximum_fusion.both), channel_id=1, source_target_pairs={{0,1},{1,2},{2,3},{3,4},{4,5},{5,6},{6,7},{8,9},{9,10},{10,11},{11... | collective-permute-start | bytes 393224 | tf_op jit(solution)/shard_map/ppermute | solution.py:346
  19.2 1.1 copy-start
  20.3 1.0 copy-start.2
  21.3 0.9 copy-start.3
  22.2 0.7 copy-start.4
  23.0 13.8 %copy-start.1 = (bf16[3,3,128,256]{3,2,1,0:T(8,128)(2,1)S(1)}, bf16[3,3,128,256]{3,2,1,0:T(8,128)(2,1)}, u32[]{:S(2)}) copy-start(bf16[3,3,128,256]{3,2,1,0:T(8,128)(2,1)} %w_down.1) | copy-start | bytes 1769476
  25.1 7.2 %collective-permute-start.2 = (bf16[2,32,16,128]{3,2,1,0:T(8,128)(2,1)S(1)}, bf16[2,32,16,128]{3,2,1,0:T(8,128)(2,1)S(1)}, u32[]{:S(2)}, u32[]{:S(2)}) collective-permute-start(bf16[2,32,16,128]{3,2,1,0:T(8,128)(2,1)S(1)} %get-tuple-element.57), channel_id=1, source_target_pairs={{0,8},{8,16},{16,24},{24,32},{32,40},{40,48},{48,56},{56,64},{64,7... | collective-permute-start | bytes 786440 | tf_op jit(solution)/shard_map/ppermute | solution.py:346
  29.1 7.7 %collective-permute-start.3 = (bf16[2,32,16,128]{3,2,1,0:T(8,128)(2,1)S(1)}, bf16[2,32,16,128]{3,2,1,0:T(8,128)(2,1)S(1)}, u32[]{:S(2)}, u32[]{:S(2)}) collective-permute-start(bf16[2,32,16,128]{3,2,1,0:T(8,128)(2,1)S(1)} %get-tuple-element.59), channel_id=1, source_target_pairs={{8,0},{16,8},{24,16},{32,24},{40,32},{48,40},{56,48},{64,56},{72,6... | collective-permute-start | bytes 786440 | tf_op jit(solution)/shard_map/ppermute | solution.py:350
  41.3 3.9 %collective-permute-start.4 = (bf16[2304,128]{1,0:T(8,128)(2,1)S(1)}, bf16[2304,128]{1,0:T(8,128)(2,1)S(1)}, u32[]{:S(2)}, u32[]{:S(2)}) collective-permute-start(bf16[2304,128]{1,0:T(8,128)(2,1)S(1)} %get-tuple-element.66), channel_id=1, source_target_pairs={{0,8},{8,0},{1,9},{9,1},{2,10},{10,2},{3,11},{11,3},{4,12},{12,4},... | collective-permute-start | bytes 1769480 | tf_op jit(solution)/shard_map/ppermute | solution.py:354
  46.2 17.4 %all-to-all-start = ((bf16[4,576,128]{2,1,0:T(8,128)(2,1)}), bf16[4,576,128]{2,1,0:T(8,128)(2,1)S(1)}, u32[]{:S(2)}, u32[]{:S(2)}) async-start(bf16[4,576,128]{2,1,0:T(8,128)(2,1)} %bitcast.11), calls=%async_computation | async-start | bytes 1179648 | tf_op jit(solution)/shard_map/all_to_all | solution.py:364
  53.7 10.6 %collective-permute-start.5 = (bf16[2,32,16,128]{3,2,1,0:T(8,128)(2,1)S(1)}, bf16[2,32,16,128]{3,2,1,0:T(8,128)(2,1)S(1)}, u32[]{:S(2)}, u32[]{:S(2)}) collective-permute-start(bf16[2,32,16,128]{3,2,1,0:T(8,128)(2,1)S(1)} %get-tuple-element.67), channel_id=1, source_target_pairs={{0,8},{8,16},{16,24},{24,32},{32,40},{40,48},{48,56},{56,64},{64,7... | collective-permute-start | bytes 786440 | tf_op jit(solution)/shard_map/ppermute | solution.py:346
  64.3 22.4 %collective-permute-start.6 = (bf16[2,32,16,128]{3,2,1,0:T(8,128)(2,1)S(1)}, bf16[2,32,16,128]{3,2,1,0:T(8,128)(2,1)S(1)}, u32[]{:S(2)}, u32[]{:S(2)}) collective-permute-start(bf16[2,32,16,128]{3,2,1,0:T(8,128)(2,1)S(1)} %get-tuple-element.72), channel_id=1, source_target_pairs={{8,0},{16,8},{24,16},{32,24},{40,32},{48,40},{56,48},{64,56},{72,6... | collective-permute-start | bytes 786440 | tf_op jit(solution)/shard_map/ppermute | solution.py:350
  67.5 19.2 %all-to-all-start.1 = ((bf16[8,72,128]{2,1,0:T(8,128)(2,1)}), bf16[8,72,128]{2,1,0:T(8,128)(2,1)S(1)}, u32[]{:S(2)}, u32[]{:S(2)}) async-start(bf16[8,72,128]{2,1,0:T(8,128)(2,1)} %bitcast.12), calls=%async_computation.1 | async-start | bytes 294912 | tf_op jit(solution)/shard_map/all_to_all | solution.py:364
  87.4 12.1 %all-to-all-start.2 = ((bf16[8,72,128]{2,1,0:T(8,128)(2,1)}), bf16[8,72,128]{2,1,0:T(8,128)(2,1)S(1)}, u32[]{:S(2)}, u32[]{:S(2)}) async-start(bf16[8,72,128]{2,1,0:T(8,128)(2,1)} %broadcast_in_dim.6), calls=%async_computation.2 | async-start | bytes 294912 | tf_op jit(solution)/shard_map/all_to_all | solution.py:371
  100.2 17.2 %all-to-all-start.3 = ((bf16[8,72,128]{2,1,0:T(8,128)(2,1)}), bf16[8,72,128]{2,1,0:T(8,128)(2,1)S(1)}, u32[]{:S(2)}, u32[]{:S(2)}) async-start(bf16[8,72,128]{2,1,0:T(8,128)(2,1)} %broadcast_in_dim.7), calls=%async_computation.3 | async-start | bytes 294912 | tf_op jit(solution)/shard_map/all_to_all | solution.py:371
  103.6 5.3 %collective-permute-start.7 = (bf16[2,16,16,128]{3,2,1,0:T(8,128)(2,1)S(1)}, bf16[2,16,16,128]{3,2,1,0:T(8,128)(2,1)S(1)}, u32[]{:S(2)}, u32[]{:S(2)}) collective-permute-start(bf16[2,16,16,128]{3,2,1,0:T(8,128)(2,1)S(1)} %get-tuple-element.81), channel_id=1, source_target_pairs={{0,1},{1,2},{2,3},{3,4},{4,5},{5,6},{6,7},{8,9},{9,10},{10,11},{11... | collective-permute-start | bytes 393224 | tf_op jit(solution)/shard_map/ppermute | solution.py:346
  107.0 10.5 %collective-permute-start.8 = (bf16[2,16,16,128]{3,2,1,0:T(8,128)(2,1)S(1)}, bf16[2,16,16,128]{3,2,1,0:T(8,128)(2,1)S(1)}, u32[]{:S(2)}, u32[]{:S(2)}) collective-permute-start(bf16[2,16,16,128]{3,2,1,0:T(8,128)(2,1)S(1)} %get-tuple-element.82), channel_id=1, source_target_pairs={{1,0},{2,1},{3,2},{4,3},{5,4},{6,5},{7,6},{9,8},{10,9},{11,10},{12... | collective-permute-start | bytes 393224 | tf_op jit(solution)/shard_map/ppermute | solution.py:350
  118.3 10.7 %all-to-all-start.4 = ((bf16[4,576,128]{2,1,0:T(8,128)(2,1)}), bf16[4,576,128]{2,1,0:T(8,128)(2,1)S(1)}, u32[]{:S(2)}, u32[]{:S(2)}) async-start(bf16[4,576,128]{2,1,0:T(8,128)(2,1)} %broadcast_in_dim.8), calls=%async_computation.4 | async-start | bytes 1179648 | tf_op jit(solution)/shard_map/all_to_all | solution.py:371
  129.1 11.3 %collective-permute-start.9 = (bf16[2304,128]{1,0:T(8,128)(2,1)S(1)}, bf16[2304,128]{1,0:T(8,128)(2,1)S(1)}, u32[]{:S(2)}, u32[]{:S(2)}) collective-permute-start(bf16[2304,128]{1,0:T(8,128)(2,1)S(1)} %bitcast.18), channel_id=1, source_target_pairs={{0,8},{8,0},{1,9},{9,1},{2,10},{10,2},{3,11},{11,3},{4,12},{12,4},... | collective-permute-start | bytes 1769480 | tf_op jit(solution)/shard_map/ppermute | solution.py:354

commit v6 on v5

--- a/solution.py
+++ b/solution.py
@@ -80,32 +80,33 @@
             ru[a, :, pl.ds(b * C1, C1)] = w_up[a, b]
 
 
-def assemble_kernel(starts, above, both, under, to_left, own, to_right, grown):
-    grown[:, 0:16] = above[...]
+def assemble_kernel(places, from_a, both, from_b, to_a, own, to_b, grown):
+    grown[:, pl.ds(places[3], 16)] = from_a[...]
     grown[:, 16:32] = both[...]
-    grown[:, 32:48] = under[...]
-    for side, out in enumerate((to_left, own, to_right)):
-        out[...] = grown[:, pl.ds(starts[side], 32)]
-
-
-def add_left_kernel(starts, from_left, own, canvas):
+    grown[:, pl.ds(places[4], 16)] = from_b[...]
+    for side, out in enumerate((to_a, own, to_b)):
+        out[...] = grown[:, pl.ds(places[side], 32)]
+
+
+def add_a_kernel(places, from_a, own, canvas):
     canvas[...] = jnp.zeros_like(canvas)
-    canvas[:, pl.ds(starts[1], 32)] = own[...]
-    spot = (slice(None), pl.ds(starts[0], 32))
-    canvas[spot] = canvas[spot] + from_left[...].astype(F32)
-
-
-def add_right_kernel(starts, given, from_right, up, mid, down, canvas):
+    canvas[:, pl.ds(places[1], 32)] = own[...]
+    spot = (slice(None), pl.ds(places[0], 32))
+    strip = from_a[HALF_ROWS:].reshape(2, 32, 16, C1)
+    canvas[spot] = canvas[spot] + strip.astype(F32)
+
+
+def add_b_kernel(places, given, from_b, to_a, mid, to_b, canvas):
     canvas[...] = given[...]
-    spot = (slice(None), pl.ds(starts[2], 32))
-    canvas[spot] = canvas[spot] + from_right[...].astype(F32)
-    up[...] = canvas[:, 0:16].astype(BF16)
+    spot = (slice(None), pl.ds(places[2], 32))
+    canvas[spot] = canvas[spot] + from_b[...].astype(F32)
+    to_a[...] = canvas[:, pl.ds(places[3], 16)].astype(BF16)
     mid[...] = canvas[:, 16:32]
-    down[...] = canvas[:, 32:48].astype(BF16)
-
-
-def finish_kernel(own, from_above, from_under, blended, field_grad):
-    total = own[...] + from_above[...].astype(F32) + from_under[...].astype(F32)
+    to_b[...] = canvas[:, pl.ds(places[4], 16)].astype(BF16)
+
+
+def finish_kernel(own, from_a, from_b, blended, field_grad):
+    total = own[...] + from_a[...].astype(F32) + from_b[...].astype(F32)
     blended[...] = total[0].astype(BF16)
     field_grad[...] = total[1]
 
@@ -146,11 +147,12 @@
 
 
 def net_kernel(
-    start, left, middle, right, fb, rf, rft, wd, rdt, ru,
-    left_o, mid_o, right_o, keep, send,
+    start, side_a, middle, side_b, fb, rf, rft, wd, rdt, ru,
+    mid_o, strip_b, keep, send,
     fs, cs, xv, hv, gv, g4, gs, bs, can_b, can_g, halves,
 ):
     start_c, core = start[0], start[1]
+    at_a, at_b = 32 * (1 - core), 32 * core
 
     def put(base, value):
         half, at = base // HALF_ROWS, base % HALF_ROWS
@@ -163,9 +165,10 @@
     g4[16] = jnp.zeros((16, 2 * C2), BF16)
 
     def stage(r, carry):
-        for k, ref in enumerate((left, middle, right)):
-            fs[r, 8 + 16 * k : 24 + 16 * k, :] = ref[0, r].astype(F32)
-            cs[r, 8 + 16 * k : 24 + 16 * k, :] = ref[1, r].astype(F32)
+        for at, ref in ((at_a, side_a), (16, middle), (at_b, side_b)):
+            spot = pl.ds(pl.multiple_of(at + 8, 8), 16)
+            fs[r, spot, :] = ref[0, r].astype(F32)
+            cs[r, spot, :] = ref[1, r].astype(F32)
         return carry
 
     lax.fori_loop(0, 32, stage, 0, unroll=4)
@@ -239,7 +242,7 @@
             put((3 * t + ct) * C1, block.T)
     put(USED_ROWS, jnp.zeros((2 * HALF_ROWS - USED_ROWS, C1), F32))
     keep[...] = halves[0]
-    send[...] = halves[1]
+    send[:HALF_ROWS] = halves[1]
     for a in range(2):
         g_x = (
             dot_nt(window(gv, a, 0), rft[0])
@@ -267,9 +270,10 @@
 
     def give(r, carry):
         for k, canvas in enumerate((can_b, can_g)):
-            left_o[k, r] = canvas[r, 0:16].astype(BF16)
             mid_o[k, r] = canvas[r, 16:32]
-            right_o[k, r] = canvas[r, 32:48].astype(BF16)
+            strip = canvas[r, pl.ds(pl.multiple_of(at_a, 16), 16), :].astype(BF16)
+            send[pl.ds(pl.multiple_of(HALF_ROWS + (32 * k + r) * 16, 16), 16)] = strip
+            strip_b[k, r] = canvas[r, pl.ds(pl.multiple_of(at_b, 16), 16), :].astype(BF16)
         return carry
 
     lax.fori_loop(0, 32, give, 0, unroll=2)
@@ -297,19 +301,17 @@
     )(where, offsets, table, w_first, w_down, w_up)
 
 
-def patch_work(start, left, middle, right, fb, rf, rft, wd, rdt, ru):
-    strip = jax.ShapeDtypeStruct((2, 32, 16, C1), BF16)
+def patch_work(start, side_a, middle, side_b, fb, rf, rft, wd, rdt, ru):
     return pl.pallas_call(
         net_kernel,
         out_shape=(
-            strip,
             jax.ShapeDtypeStruct((2, 32, 16, C1), F32),
-            strip,
+            jax.ShapeDtypeStruct((2, 32, 16, C1), BF16),
             jax.ShapeDtypeStruct((HALF_ROWS, C1), BF16),
-            jax.ShapeDtypeStruct((HALF_ROWS, C1), BF16),
+            jax.ShapeDtypeStruct((HALF_ROWS + 2 * 32 * 16, C1), BF16),
         ),
         in_specs=[SMEM] + [VMEM] * 9,
-        out_specs=[VMEM] * 5,
+        out_specs=[VMEM] * 4,
         scratch_shapes=[
             pltpu.VMEM((32, 64, C1), F32),
             pltpu.VMEM((32, 64, C1), F32),
@@ -326,7 +328,7 @@
         compiler_params=pltpu.CompilerParams(vmem_limit_bytes=24 * 2**20),
         cost_estimate=pl.CostEstimate(flops=2 * 10**9, bytes_accessed=10**7, transcendentals=200000),
         name="patch_work",
-    )(start, left, middle, right, fb, rf, rft, wd, rdt, ru)
+    )(start, side_a, middle, side_b, fb, rf, rft, wd, rdt, ru)
 
 
 def small_call(body, name, outs, scratch, *args, smem=0):
@@ -342,16 +344,14 @@
     )(*args)
 
 
-def from_before(axes, x):
-    return lax.ppermute(x, axes, [(i, i + 1) for i in range(lax.axis_size(axes) - 1)])
-
-
-def from_after(axes, x):
-    return lax.ppermute(x, axes, [(i + 1, i) for i in range(lax.axis_size(axes) - 1)])
-
-
-def swapped(x):
-    return lax.ppermute(x, "core", [(0, 1), (1, 0)])
+def swapped_b(x, axes):
+    size = lax.axis_size(axes)
+    pairs = [(i, i + 1) for i in range(1, size - 1, 2)]
+    return lax.ppermute(x, axes, pairs + [(j, i) for i, j in pairs])
+
+
+def swapped_a(x, axis):
+    return lax.ppermute(x, axis, [(0, 1), (1, 0)])
 
 
 def added(x, y):
@@ -378,58 +378,60 @@
     col_at = lax.axis_index(COL)
     where = jnp.stack([row_at, col_at]).astype(jnp.int32)
     both = jnp.stack([field, cotangent])
-    starts = jnp.stack(
-        [MARGIN + offsets[row_at, jnp.clip(col_at + step, 0, cols_n - 1), 0] for step in (-1, 0, 1)]
-    )
     core = lax.axis_index("core").astype(jnp.int32)
+    zh = lax.axis_index("zh").astype(jnp.int32)
+    col_a = col_at + 1 - 2 * core
+    col_b = jnp.clip(col_at - 1 + 2 * core, 0, cols_n - 1)
+    firsts = [MARGIN + offsets[row_at, col, 0] for col in (col_a, col_at, col_b)]
+    places = jnp.stack(firsts + [32 * (1 - zh), 32 * zh]).astype(jnp.int32)
     start = jnp.stack([MARGIN + offsets[row_at, col_at, 1], core])
     fb, rf, rft, rdt, ru = prepared(
         where, offsets.reshape(rows_n, 2 * cols_n), blend_table, w_first, w_down, w_up
     )
-    above, under = from_before(ROW, both), from_after(ROW, both)
-    above, under, fb, rf, rft, rdt, ru = lax.optimization_barrier((above, under, fb, rf, rft, rdt, ru))
+    row_a, row_b = swapped_a(both, "zh"), swapped_b(both, ROW)
+    row_a, row_b, fb, rf, rft, rdt, ru = lax.optimization_barrier((row_a, row_b, fb, rf, rft, rdt, ru))
     window_shape = (2, 32, TILE, C1)
-    to_left, own, to_right = small_call(
+    to_a, own, to_b = small_call(
         assemble_kernel,
         "assemble",
         [(window_shape, BF16)] * 3,
         [pltpu.VMEM((2, 48, TILE, C1), BF16)],
-        starts,
-        above,
+        places,
+        row_a,
         both,
-        under,
+        row_b,
         smem=1,
     )
-    left, right = from_before(COL, to_right), from_after(COL, to_left)
-    to_left, own, to_right, keep, send = patch_work(
-        start, left, own, right, fb, rf, rft, w_down.reshape(3, 3 * C1, C2), rdt, ru
-    )
-    from_left = from_before(COL, to_right)
-    part = added(keep, swapped(send))
+    side_b, side_a = swapped_b(to_b, COL), swapped_a(to_a, "core")
+    own, strip_b, keep, send = patch_work(
+        start, side_a, own, side_b, fb, rf, rft, w_down.reshape(3, 3 * C1, C2), rdt, ru
+    )
+    got = swapped_a(send, "core")
+    from_b = swapped_b(strip_b, COL)
+    part = added(keep, got[:HALF_ROWS])
     part = scattered(part, "x")
-    part, from_left, to_left = lax.optimization_barrier((part, from_left, to_left))
-    from_right = from_after(COL, to_left)
+    part, from_b = lax.optimization_barrier((part, from_b))
     part = scattered(part, "y")
     canvas = small_call(
-        add_left_kernel, "add_left", [((2, 48, TILE, C1), F32)], [], starts, from_left, own, smem=1
+        add_a_kernel, "add_a", [((2, 48, TILE, C1), F32)], [], places, got, own, smem=1
     )[0]
-    part, canvas, from_right = lax.optimization_barrier((part, canvas, from_right))
+    part, canvas = lax.optimization_barrier((part, canvas))
     part = gathered(part, ("zl", "zh")).astype(F32).sum(0).astype(BF16)
     tile_shape = (2, TILE, TILE, C1)
-    up, own, down = small_call(
-        add_right_kernel,
-        "add_right",
+    to_a, own, to_b = small_call(
+        add_b_kernel,
+        "add_b",
         [(tile_shape, BF16), (tile_shape, F32), (tile_shape, BF16)],
         [pltpu.VMEM((2, 48, TILE, C1), F32)],
-        starts,
+        places,
         canvas,
-        from_right,
+        from_b,
         smem=1,
     )
-    part, up, own, down = lax.optimization_barrier((part, up, own, down))
-    from_above, from_under = from_before(ROW, down), from_after(ROW, up)
+    part, to_a, own, to_b = lax.optimization_barrier((part, to_a, own, to_b))
+    row_a, row_b = swapped_a(to_a, "zh"), swapped_b(to_b, ROW)
     part = gathered(part, "y").reshape(-1, C1)
-    part, own, from_above, from_under = lax.optimization_barrier((part, own, from_above, from_under))
+    part, own, row_a, row_b = lax.optimization_barrier((part, own, row_a, row_b))
     part = gathered(part, "x").reshape(-1, C1)
     blended, field_grad = small_call(
         finish_kernel,
@@ -437,11 +439,11 @@
         [(field.shape, BF16), (field.shape, F32)],
         [],
         own,
-        from_above,
-        from_under,
+        row_a,
+        row_b,
     )
     part, blended, field_grad = lax.optimization_barrier((part, blended, field_grad))
-    other = swapped(part)
+    other = swapped_a(part, "core")
     scale = 1.0 / math.sqrt(TILE * rows_n * TILE * cols_n)
     g_first, g_down, g_up = small_call(
         functools.partial(unpack_kernel, scale),

time: 143 us -> 141 us (0.986)
  waiting for transfers between devices: 44.3 us -> 38.8 us
  starting transfers between devices: 72.8 us -> 76.1 us
    all_to_all x3, starting transfers between devices: 12.2 us -> 19.6 us  [gathered(): return lax.all_to_all(parts, axes, 0, 0, tiled=True)]
    ppermute x10 -> x9, waiting for transfers between devices: 17.2 us -> 13.4 us  [the longest x5 9.7 us: swapped_a(): return lax.ppermute(x, axis, [(0, 1), (1, 0)])]
    all_to_all x2, starting transfers between devices: 18.6 us -> 16.2 us  [scattered(): got = lax.all_to_all(parts, axes, 0, 0, tiled=True)]
    all_to_all x2, waiting for transfers between devices: 14.5 us -> 12.8 us  [scattered(): got = lax.all_to_all(parts, axes, 0, 0, tiled=True)]
    ppermute x10 -> x9, starting transfers between devices: 42 us -> 40.3 us  [the longest x5 31 us: swapped_a(): return lax.ppermute(x, axis, [(0, 1), (1, 0)])]
  transfers between devices with their start and end apart: 15 -> 14, of which waited for: 9 -> 8; matrix products, arithmetic and copies ran while one was open for 2% -> 2% of each run, Pallas kernels for 2% -> 3%
where the time goes in v6:
time: 141 us; the launch traced here: 140 us
  starting transfers between devices  76.1 us (54%)
  waiting for transfers between devices  38.8 us (28%)
  Pallas kernels  10.3 us (7%)
  local copies, waits for them, and re-layouts  8.38 us (6%)
  between operations  3.4 us (2%)
  other arithmetic  2.84 us (2%)
    ppermute x5, starting transfers between devices, swapped_a(): return lax.ppermute(x, axis, [(0, 1), (1, 0)])  31 us
    all_to_all x3, starting transfers between devices, gathered(): return lax.all_to_all(parts, axes, 0, 0, tiled=True)  19.6 us
    all_to_all x2, starting transfers between devices, scattered(): got = lax.all_to_all(parts, axes, 0, 0, tiled=True)  16.2 us
    all_to_all x2, waiting for transfers between devices, scattered(): got = lax.all_to_all(parts, axes, 0, 0, tiled=True)  12.8 us
    all_to_all x3, waiting for transfers between devices, gathered(): return lax.all_to_all(parts, axes, 0, 0, tiled=True)  12.6 us
    ppermute x5, waiting for transfers between devices, swapped_a(): return lax.ppermute(x, axis, [(0, 1), (1, 0)])  9.7 us
    ppermute x4, starting transfers between devices, swapped_b(): return lax.ppermute(x, axes, pairs + [(j, i) for i, j in pairs])  9.24 us
    pallas_call x1, Pallas kernels, patch_work(): pl.pallas_call(net_kernel, out_shape=(jax.ShapeDtypeStruct((2, 32, 16, C1...  4.6 us
  transfers between devices with their start and end apart: 14, of which 8 were waited for; matrix products, arithmetic and copies ran while one was open for 2% of the time, Pallas kernels for 3%

profile of v6, /device:TPU:1, one launch (start us, length us, event | category | flops | bytes accessed | tf_op | source)
XLA Modules:
  0.0 139.8 jit_solution(15299957967277255987)
XLA Ops:
  0.6 0.9 pad_maximum_fusion.both
  1.5 0.7 collective-permute-start.1
  2.2 12.7 %collective-permute-start = (bf16[2,16,16,128]{3,2,1,0:T(8,128)(2,1)S(1)}, bf16[2,16,16,128]{3,2,1,0:T(8,128)(2,1)S(1)}, u32[]{:S(2)}, u32[]{:S(2)}) collective-permute-start(bf16[2,16,16,128]{3,2,1,0:T(8,128)(2,1)S(1)} %pad_maximum_fusion.both), channel_id=1, source_target_pairs={{0,1},{1,0},{2,3},{3,2},{4,5},{5,4},{6,7},{7,6},{8,9},{9,8},{10,11... | collective-permute-start | bytes 393224 | tf_op jit(solution)/shard_map/ppermute | solution.py:354
  14.9 0.8 copy.15
  15.8 1.5 %constant_dynamic-slice_fusion = (s32[1,1,1]{1,2,0:T(1,128)}, s32[1,1,1]{1,2,0:T(1,128)}, s32[1,1,1]{1,2,0:T(1,128)}, s32[1,1,1]{1,2,0:T(1,128)}) fusion(s32[8,64,2]{1,2,0:T(2,128)} %param.12, s32[]{:T(128)S(6)} %select_n.6, s32[]{:T(128)S(6)} %min.4, s32[]{:T(128)S(6)} %select_n.7, s32[]{:T(128)S(6)} %select_n.16), kind=kLoop, calls=%fused_computation.2 | loop fusion | bytes 48 | tf_op jit(solution)/shard_map/dynamic_slice | solution.py:385
  19.3 0.1 stack.53.places
  19.3 0.1 pad_add_fusion.1.where
  19.4 1.1 copy-done
  20.5 1.0 copy-done.2
  21.5 0.9 copy-done.3
  22.4 0.7 copy-done.4
  23.1 1.5 %prepare.1 = (f32[2,16,16,256]{3,2,1,0:T(8,128)S(1)}, bf16[3,512,256]{2,1,0:T(8,128)(2,1)S(1)}, bf16[3,256,512]{2,1,0:T(8,128)(2,1)S(1)}, bf16[3,256,512]{2,1,0:T(8,128)(2,1)S(1)}, bf16[2,256,256]{2,1,0:T(8,128)(2,1)S(1)}) custom-call(s32[2]{0:T(128)S(1)} %pad_add_fusion.1.where, s32[8,128]{1,0:T(8,128)S(1)} %copy.16.offsets, s32[32,32]{1,0:T(8,128)S(1)} %copy-done.4, ...), custom_call_target="tpu_custom_call" | custom-call | flops 5000000 | bytes 10000000 | tf_op jit(solution)/shard_map/prepare/pallas_call | solution.py:287
  24.6 0.0 collective-permute-done.from_a
  24.6 0.6 assemble.1
  25.2 2.9 %collective-permute-start.2 = (bf16[2,32,16,128]{3,2,1,0:T(8,128)(2,1)S(1)}, bf16[2,32,16,128]{3,2,1,0:T(8,128)(2,1)S(1)}, u32[]{:S(2)}, u32[]{:S(2)}) collective-permute-start(bf16[2,32,16,128]{3,2,1,0:T(8,128)(2,1)S(1)} %get-tuple-element.54), channel_id=1, source_target_pairs={{0,8},{8,0},{1,9},{9,1},{2,10},{10,2},{3,11},{11,3},{4,12},{12,4},... | collective-permute-start | bytes 786440 | tf_op jit(solution)/shard_map/ppermute | solution.py:354
  28.1 3.3 %collective-permute-start.3 = (bf16[2,32,16,128]{3,2,1,0:T(8,128)(2,1)S(1)}, bf16[2,32,16,128]{3,2,1,0:T(8,128)(2,1)S(1)}, u32[]{:S(2)}, u32[]{:S(2)}) collective-permute-start(bf16[2,32,16,128]{3,2,1,0:T(8,128)(2,1)S(1)} %get-tuple-element.56), channel_id=1, source_target_pairs={{8,16},{24,32},{40,48},{56,64},{72,80},{88,96},{104,112},{120,128}... | collective-permute-start | bytes 786440 | tf_op jit(solution)/shard_map/ppermute | solution.py:350
  32.0 0.1 pad_add_fusion.start
  32.1 0.0 collective-permute-done.2.side_a
  32.1 3.7 %collective-permute-done.3.side_b = bf16[2,32,16,128]{3,2,1,0:T(8,128)(2,1)S(1)} collective-permute-done((bf16[2,32,16,128]{3,2,1,0:T(8,128)(2,1)S(1)}, bf16[2,32,16,128]{3,2,1,0:T(8,128)(2,1)S(1)}, u32[]{:S(2)}, u32[]{:S(2)}) %collective-permute-start.3) | collective-permute-done | bytes 262176 | tf_op jit(solution)/shard_map/ppermute | solution.py:350
  35.8 4.6 %patch_work.1 = (f32[2,32,16,128]{3,2,1,0:T(8,128)S(1)}, bf16[2,32,16,128]{3,2,1,0:T(8,128)(2,1)S(1)}, bf16[2304,128]{1,0:T(8,128)(2,1)S(1)}, bf16[3328,128]{1,0:T(8,128)(2,1)S(1)}) custom-call(s32[2]{0:T(128)S(1)} %pad_add_fusion.start, bf16[2,32,16,128]{3,2,1,0:T(8,128)(2,1)S(1)} %collective-permute-done.2.side_a, ...), custom_call_target="tpu_custom_call" | custom-call | flops 2000000000 | bytes 10000000 | tf_op jit(solution)/shard_map/patch_work/pallas_call | solution.py:305
  40.4 1.9 %collective-permute-start.4 = (bf16[3328,128]{1,0:T(8,128)(2,1)S(1)}, bf16[3328,128]{1,0:T(8,128)(2,1)S(1)}, u32[]{:S(2)}, u32[]{:S(2)}) collective-permute-start(bf16[3328,128]{1,0:T(8,128)(2,1)S(1)} %get-tuple-element.63), channel_id=1, source_target_pairs={{0,8},{8,0},{1,9},{9,1},{2,10},{10,2},{3,11},{11,3},{4,12},{12,4},... | collective-permute-start | bytes 2555912 | tf_op jit(solution)/shard_map/ppermute | solution.py:354
  42.3 2.3 %collective-permute-done.4.from_a = bf16[3328,128]{1,0:T(8,128)(2,1)S(1)} collective-permute-done((bf16[3328,128]{1,0:T(8,128)(2,1)S(1)}, bf16[3328,128]{1,0:T(8,128)(2,1)S(1)}, u32[]{:S(2)}, u32[]{:S(2)}) %collective-permute-start.4) | collective-permute-done | bytes 852000 | tf_op jit(solution)/shard_map/ppermute | solution.py:354
  44.7 1.0 add_convert_fusion
  45.7 7.4 %all-to-all-start = ((bf16[4,576,128]{2,1,0:T(8,128)(2,1)}), bf16[4,576,128]{2,1,0:T(8,128)(2,1)S(1)}, u32[]{:S(2)}, u32[]{:S(2)}) async-start(bf16[4,576,128]{2,1,0:T(8,128)(2,1)} %bitcast.13), calls=%async_computation | async-start | bytes 1179648 | tf_op jit(solution)/shard_map/all_to_all | solution.py:364
  53.0 4.6 %collective-permute-start.5 = (bf16[2,32,16,128]{3,2,1,0:T(8,128)(2,1)S(1)}, bf16[2,32,16,128]{3,2,1,0:T(8,128)(2,1)S(1)}, u32[]{:S(2)}, u32[]{:S(2)}) collective-permute-start(bf16[2,32,16,128]{3,2,1,0:T(8,128)(2,1)S(1)} %get-tuple-element.64), channel_id=1, source_target_pairs={{8,16},{24,32},{40,48},{56,64},{72,80},{88,96},{104,112},{120,128}... | collective-permute-start | bytes 786440 | tf_op jit(solution)/shard_map/ppermute | solution.py:350
  57.7 5.2 %all-to-all-done = bf16[4,576,128]{2,1,0:T(8,128)(2,1)S(1)} async-done(((bf16[4,576,128]{2,1,0:T(8,128)(2,1)}), bf16[4,576,128]{2,1,0:T(8,128)(2,1)S(1)}, u32[]{:S(2)}, u32[]{:S(2)}) %all-to-all-start) | async-done | bytes 589856 | tf_op jit(solution)/shard_map/all_to_all | solution.py:364
  62.9 0.8 reduce_sum.36
  63.7 8.8 %all-to-all-start.1 = ((bf16[8,72,128]{2,1,0:T(8,128)(2,1)}), bf16[8,72,128]{2,1,0:T(8,128)(2,1)S(1)}, u32[]{:S(2)}, u32[]{:S(2)}) async-start(bf16[8,72,128]{2,1,0:T(8,128)(2,1)} %bitcast.14), calls=%async_computation.1 | async-start | bytes 294912 | tf_op jit(solution)/shard_map/all_to_all | solution.py:364
  72.5 0.7 add_a.1.given
  73.2 7.5 %all-to-all-done.1 = bf16[8,72,128]{2,1,0:T(8,128)(2,1)S(1)} async-done(((bf16[8,72,128]{2,1,0:T(8,128)(2,1)}), bf16[8,72,128]{2,1,0:T(8,128)(2,1)S(1)}, u32[]{:S(2)}, u32[]{:S(2)}) %all-to-all-start.1) | async-done | bytes 147488 | tf_op jit(solution)/shard_map/all_to_all | solution.py:364
  80.7 0.7 broadcast_in_dim.6
  81.4 5.0 %all-to-all-start.2 = ((bf16[8,72,128]{2,1,0:T(8,128)(2,1)}), bf16[8,72,128]{2,1,0:T(8,128)(2,1)S(1)}, u32[]{:S(2)}, u32[]{:S(2)}) async-start(bf16[8,72,128]{2,1,0:T(8,128)(2,1)} %broadcast_in_dim.6), calls=%async_computation.2 | async-start | bytes 294912 | tf_op jit(solution)/shard_map/all_to_all | solution.py:371
  86.4 0.7 add_b.1
  87.1 6.1 %all-to-all-done.2 = bf16[8,72,128]{2,1,0:T(8,128)(2,1)S(1)} async-done(((bf16[8,72,128]{2,1,0:T(8,128)(2,1)}), bf16[8,72,128]{2,1,0:T(8,128)(2,1)S(1)}, u32[]{:S(2)}, u32[]{:S(2)}) %all-to-all-start.2) | async-done | bytes 147488 | tf_op jit(solution)/shard_map/all_to_all | solution.py:371
  93.2 0.7 broadcast_in_dim.7
  93.9 3.4 %all-to-all-start.3 = ((bf16[8,72,128]{2,1,0:T(8,128)(2,1)}), bf16[8,72,128]{2,1,0:T(8,128)(2,1)S(1)}, u32[]{:S(2)}, u32[]{:S(2)}) async-start(bf16[8,72,128]{2,1,0:T(8,128)(2,1)} %broadcast_in_dim.7), calls=%async_computation.3 | async-start | bytes 294912 | tf_op jit(solution)/shard_map/all_to_all | solution.py:371
  97.3 3.3 %collective-permute-start.6 = (bf16[2,16,16,128]{3,2,1,0:T(8,128)(2,1)S(1)}, bf16[2,16,16,128]{3,2,1,0:T(8,128)(2,1)S(1)}, u32[]{:S(2)}, u32[]{:S(2)}) collective-permute-start(bf16[2,16,16,128]{3,2,1,0:T(8,128)(2,1)S(1)} %get-tuple-element.75), channel_id=1, source_target_pairs={{0,1},{1,0},{2,3},{3,2},{4,5},{5,4},{6,7},{7,6},{8,9},{9,8},{10,11... | collective-permute-start | bytes 393224 | tf_op jit(solution)/shard_map/ppermute | solution.py:354
  100.6 0.7 collective-permute-start.7
  101.3 5.7 %collective-permute-done.6.from_a = bf16[2,16,16,128]{3,2,1,0:T(8,128)(2,1)S(1)} collective-permute-done((bf16[2,16,16,128]{3,2,1,0:T(8,128)(2,1)S(1)}, bf16[2,16,16,128]{3,2,1,0:T(8,128)(2,1)S(1)}, u32[]{:S(2)}, u32[]{:S(2)}) %collective-permute-start.6) | collective-permute-done | bytes 131104 | tf_op jit(solution)/shard_map/ppermute | solution.py:354
  107.1 0.0 collective-permute-done.7.from_b
  107.1 0.0 all-to-all-done.3
  107.1 0.9 broadcast_in_dim.8
  108.0 11.2 %all-to-all-start.4 = ((bf16[4,576,128]{2,1,0:T(8,128)(2,1)}), bf16[4,576,128]{2,1,0:T(8,128)(2,1)S(1)}, u32[]{:S(2)}, u32[]{:S(2)}) async-start(bf16[4,576,128]{2,1,0:T(8,128)(2,1)} %broadcast_in_dim.8), calls=%async_computation.4 | async-start | bytes 1179648 | tf_op jit(solution)/shard_map/all_to_all | solution.py:371
  119.2 0.7 finish.1
  119.9 6.6 %all-to-all-done.4 = bf16[4,576,128]{2,1,0:T(8,128)(2,1)S(1)} async-done(((bf16[4,576,128]{2,1,0:T(8,128)(2,1)}), bf16[4,576,128]{2,1,0:T(8,128)(2,1)S(1)}, u32[]{:S(2)}, u32[]{:S(2)}) %all-to-all-start.4) | async-done | bytes 589856 | tf_op jit(solution)/shard_map/all_to_all | solution.py:371
  126.4 10.2 %collective-permute-start.8 = (bf16[2304,128]{1,0:T(8,128)(2,1)S(1)}, bf16[2304,128]{1,0:T(8,128)(2,1)S(1)}, u32[]{:S(2)}, u32[]{:S(2)}) collective-permute-start(bf16[2304,128]{1,0:T(8,128)(2,1)S(1)} %bitcast.20), channel_id=1, source_target_pairs={{0,8},{8,0},{1,9},{9,1},{2,10},{10,2},{3,11},{11,3},{4,12},{12,4},... | collective-permute-start | bytes 1769480 | tf_op jit(solution)/shard_map/ppermute | solution.py:354
  136.6 1.6 %collective-permute-done.8.other = bf16[2304,128]{1,0:T(8,128)(2,1)S(1)} collective-permute-done((bf16[2304,128]{1,0:T(8,128)(2,1)S(1)}, bf16[2304,128]{1,0:T(8,128)(2,1)S(1)}, u32[]{:S(2)}, u32[]{:S(2)}) %collective-permute-start.8) | collective-permute-done | bytes 589856 | tf_op jit(solution)/shard_map/ppermute | solution.py:354
  138.3 1.6 %unpack.1 = (f32[9,128,128]{2,1,0:T(8,128)}, f32[3,384,256]{2,1,0:T(8,128)}, f32[4,256,128]{2,1,0:T(8,128)}) custom-call(s32[1]{0:T(128)} %bitcast.1.core, bf16[2304,128]{1,0:T(8,128)(2,1)S(1)} %bitcast.21, bf16[2304,128]{1,0:T(8,128)(2,1)S(1)} %collective-permute-done.8.other), custom_call_target="tpu_custom_call" | custom-call | flops 1000000 | bytes 2000000 | tf_op jit(solution)/shard_map/unpack/pallas_call | solution.py:335
  (11 shorter events, 0.1 us)
Async XLA Ops:
  1.5 23.1 %collective-permute-start.1 = (bf16[2,16,16,128]{3,2,1,0:T(8,128)(2,1)S(1)}, bf16[2,16,16,128]{3,2,1,0:T(8,128)(2,1)S(1)}, u32[]{:S(2)}, u32[]{:S(2)}) collective-permute-start(bf16[2,16,16,128]{3,2,1,0:T(8,128)(2,1)S(1)} %pad_maximum_fusion.both), channel_id=1, source_target_pairs={{1,2},{3,4},{5,6},{2,1},{4,3},{6,5},{9,10},{11,12},{13,14},{10,9},... | collective-permute-start | bytes 393224 | tf_op jit(solution)/shard_map/ppermute | solution.py:350
  2.2 22.4 %collective-permute-start = (bf16[2,16,16,128]{3,2,1,0:T(8,128)(2,1)S(1)}, bf16[2,16,16,128]{3,2,1,0:T(8,128)(2,1)S(1)}, u32[]{:S(2)}, u32[]{:S(2)}) collective-permute-start(bf16[2,16,16,128]{3,2,1,0:T(8,128)(2,1)S(1)} %pad_maximum_fusion.both), channel_id=1, source_target_pairs={{0,1},{1,0},{2,3},{3,2},{4,5},{5,4},{6,7},{7,6},{8,9},{9,8},{10,11... | collective-permute-start | bytes 393224 | tf_op jit(solution)/shard_map/ppermute | solution.py:354
  19.4 1.1 copy-start
  20.5 1.0 copy-start.2
  21.5 0.9 copy-start.3
  22.4 0.7 copy-start.4
  23.1 12.7 %copy-start.1 = (bf16[3,3,128,256]{3,2,1,0:T(8,128)(2,1)S(1)}, bf16[3,3,128,256]{3,2,1,0:T(8,128)(2,1)}, u32[]{:S(2)}) copy-start(bf16[3,3,128,256]{3,2,1,0:T(8,128)(2,1)} %w_down.1) | copy-start | bytes 1769476
  25.2 6.9 %collective-permute-start.2 = (bf16[2,32,16,128]{3,2,1,0:T(8,128)(2,1)S(1)}, bf16[2,32,16,128]{3,2,1,0:T(8,128)(2,1)S(1)}, u32[]{:S(2)}, u32[]{:S(2)}) collective-permute-start(bf16[2,32,16,128]{3,2,1,0:T(8,128)(2,1)S(1)} %get-tuple-element.54), channel_id=1, source_target_pairs={{0,8},{8,0},{1,9},{9,1},{2,10},{10,2},{3,11},{11,3},{4,12},{12,4},... | collective-permute-start | bytes 786440 | tf_op jit(solution)/shard_map/ppermute | solution.py:354
  28.1 7.7 %collective-permute-start.3 = (bf16[2,32,16,128]{3,2,1,0:T(8,128)(2,1)S(1)}, bf16[2,32,16,128]{3,2,1,0:T(8,128)(2,1)S(1)}, u32[]{:S(2)}, u32[]{:S(2)}) collective-permute-start(bf16[2,32,16,128]{3,2,1,0:T(8,128)(2,1)S(1)} %get-tuple-element.56), channel_id=1, source_target_pairs={{8,16},{24,32},{40,48},{56,64},{72,80},{88,96},{104,112},{120,128}... | collective-permute-start | bytes 786440 | tf_op jit(solution)/shard_map/ppermute | solution.py:350
  40.4 4.3 %collective-permute-start.4 = (bf16[3328,128]{1,0:T(8,128)(2,1)S(1)}, bf16[3328,128]{1,0:T(8,128)(2,1)S(1)}, u32[]{:S(2)}, u32[]{:S(2)}) collective-permute-start(bf16[3328,128]{1,0:T(8,128)(2,1)S(1)} %get-tuple-element.63), channel_id=1, source_target_pairs={{0,8},{8,0},{1,9},{9,1},{2,10},{10,2},{3,11},{11,3},{4,12},{12,4},... | collective-permute-start | bytes 2555912 | tf_op jit(solution)/shard_map/ppermute | solution.py:354
  45.7 17.2 %all-to-all-start = ((bf16[4,576,128]{2,1,0:T(8,128)(2,1)}), bf16[4,576,128]{2,1,0:T(8,128)(2,1)S(1)}, u32[]{:S(2)}, u32[]{:S(2)}) async-start(bf16[4,576,128]{2,1,0:T(8,128)(2,1)} %bitcast.13), calls=%async_computation | async-start | bytes 1179648 | tf_op jit(solution)/shard_map/all_to_all | solution.py:364
  53.0 10.6 %collective-permute-start.5 = (bf16[2,32,16,128]{3,2,1,0:T(8,128)(2,1)S(1)}, bf16[2,32,16,128]{3,2,1,0:T(8,128)(2,1)S(1)}, u32[]{:S(2)}, u32[]{:S(2)}) collective-permute-start(bf16[2,32,16,128]{3,2,1,0:T(8,128)(2,1)S(1)} %get-tuple-element.64), channel_id=1, source_target_pairs={{8,16},{24,32},{40,48},{56,64},{72,80},{88,96},{104,112},{120,128}... | collective-permute-start | bytes 786440 | tf_op jit(solution)/shard_map/ppermute | solution.py:350
  63.7 17.0 %all-to-all-start.1 = ((bf16[8,72,128]{2,1,0:T(8,128)(2,1)}), bf16[8,72,128]{2,1,0:T(8,128)(2,1)S(1)}, u32[]{:S(2)}, u32[]{:S(2)}) async-start(bf16[8,72,128]{2,1,0:T(8,128)(2,1)} %bitcast.14), calls=%async_computation.1 | async-start | bytes 294912 | tf_op jit(solution)/shard_map/all_to_all | solution.py:364
  81.4 11.8 %all-to-all-start.2 = ((bf16[8,72,128]{2,1,0:T(8,128)(2,1)}), bf16[8,72,128]{2,1,0:T(8,128)(2,1)S(1)}, u32[]{:S(2)}, u32[]{:S(2)}) async-start(bf16[8,72,128]{2,1,0:T(8,128)(2,1)} %broadcast_in_dim.6), calls=%async_computation.2 | async-start | bytes 294912 | tf_op jit(solution)/shard_map/all_to_all | solution.py:371
  93.9 13.2 %all-to-all-start.3 = ((bf16[8,72,128]{2,1,0:T(8,128)(2,1)}), bf16[8,72,128]{2,1,0:T(8,128)(2,1)S(1)}, u32[]{:S(2)}, u32[]{:S(2)}) async-start(bf16[8,72,128]{2,1,0:T(8,128)(2,1)} %broadcast_in_dim.7), calls=%async_computation.3 | async-start | bytes 294912 | tf_op jit(solution)/shard_map/all_to_all | solution.py:371
  97.3 9.8 %collective-permute-start.6 = (bf16[2,16,16,128]{3,2,1,0:T(8,128)(2,1)S(1)}, bf16[2,16,16,128]{3,2,1,0:T(8,128)(2,1)S(1)}, u32[]{:S(2)}, u32[]{:S(2)}) collective-permute-start(bf16[2,16,16,128]{3,2,1,0:T(8,128)(2,1)S(1)} %get-tuple-element.75), channel_id=1, source_target_pairs={{0,1},{1,0},{2,3},{3,2},{4,5},{5,4},{6,7},{7,6},{8,9},{9,8},{10,11... | collective-permute-start | bytes 393224 | tf_op jit(solution)/shard_map/ppermute | solution.py:354
  100.6 6.4 %collective-permute-start.7 = (bf16[2,16,16,128]{3,2,1,0:T(8,128)(2,1)S(1)}, bf16[2,16,16,128]{3,2,1,0:T(8,128)(2,1)S(1)}, u32[]{:S(2)}, u32[]{:S(2)}) collective-permute-start(bf16[2,16,16,128]{3,2,1,0:T(8,128)(2,1)S(1)} %get-tuple-element.76), channel_id=1, source_target_pairs={{1,2},{3,4},{5,6},{2,1},{4,3},{6,5},{9,10},{11,12},{13,14},{10,9},... | collective-permute-start | bytes 393224 | tf_op jit(solution)/shard_map/ppermute | solution.py:350
  108.0 18.5 %all-to-all-start.4 = ((bf16[4,576,128]{2,1,0:T(8,128)(2,1)}), bf16[4,576,128]{2,1,0:T(8,128)(2,1)S(1)}, u32[]{:S(2)}, u32[]{:S(2)}) async-start(bf16[4,576,128]{2,1,0:T(8,128)(2,1)} %broadcast_in_dim.8), calls=%async_computation.4 | async-start | bytes 1179648 | tf_op jit(solution)/shard_map/all_to_all | solution.py:371
  126.4 11.8 %collective-permute-start.8 = (bf16[2304,128]{1,0:T(8,128)(2,1)S(1)}, bf16[2304,128]{1,0:T(8,128)(2,1)S(1)}, u32[]{:S(2)}, u32[]{:S(2)}) collective-permute-start(bf16[2304,128]{1,0:T(8,128)(2,1)S(1)} %bitcast.20), channel_id=1, source_target_pairs={{0,8},{8,0},{1,9},{9,1},{2,10},{10,2},{3,11},{11,3},{4,12},{12,4},... | collective-permute-start | bytes 1769480 | tf_op jit(solution)/shard_map/ppermute | solution.py:354

commit v7 on v6

--- a/solution.py
+++ b/solution.py
@@ -33,15 +33,27 @@
     return lax.dot_general(a, b, (((1,), (1,)), ((), ())), preferred_element_type=F32)
 
 
-def prepare_kernel(where, offsets, table, w_first, w_down, w_up, fb, rf, rft, rdt, ru):
+def prepare_kernel(
+    where, offsets, table, w_first, w_down, w_up,
+    places, fb, rf, rft, rdt, ru,
+):
     row_at, col_at = where[0], where[1]
-    rows_n, cols_n = offsets.shape[0], offsets.shape[1] // 2
+    rows_n, cols_n = offsets.shape[0], offsets.shape[2]
+    core, zh = lax.rem(col_at, 2), lax.rem(row_at, 2)
+    col_b = jnp.clip(col_at - 1 + 2 * core, 0, cols_n - 1)
+    for k, col in enumerate((col_at + 1 - 2 * core, col_at, col_b)):
+        places[k] = MARGIN + offsets[row_at, 0, col]
+    places[3] = 32 * (1 - zh)
+    places[4] = 32 * zh
+    places[5] = MARGIN + offsets[row_at, 1, col_at]
+    places[6] = core
+    places[7] = 0
     sub = lax.broadcasted_iota(jnp.int32, (32, 32), 0)
     lane = lax.broadcasted_iota(jnp.int32, (32, 32), 1)
     column = jnp.where(sub < 16, 2 * sub, 2 * (sub - 16) + 1)
     table_t = table[...].astype(F32).T.astype(BF16)
-    own_r = offsets[row_at, 2 * col_at]
-    own_c = offsets[row_at, 2 * col_at + 1]
+    own_r = offsets[row_at, 0, col_at]
+    own_c = offsets[row_at, 1, col_at]
     total = jnp.zeros((32, 32), F32)
     own = jnp.zeros((32, 32), F32)
     for row_step in range(-REACH, REACH + 1):
@@ -50,8 +62,8 @@
             inside = (near_r >= 0) & (near_r < rows_n) & (near_c >= 0) & (near_c < cols_n)
             at_r = jnp.clip(near_r, 0, rows_n - 1)
             at_c = jnp.clip(near_c, 0, cols_n - 1)
-            down_by = row_step * TILE + offsets[at_r, 2 * at_c] - own_r
-            right_by = col_step * TILE + offsets[at_r, 2 * at_c + 1] - own_c
+            down_by = row_step * TILE + offsets[at_r, 0, at_c] - own_r
+            right_by = col_step * TILE + offsets[at_r, 1, at_c] - own_c
             down_by = jnp.where(inside, down_by, FAR)
             pick_c = (column - right_by == lane).astype(F32).astype(BF16)
             pick_r = (lane - down_by == sub).astype(F32).astype(BF16)
@@ -88,32 +100,25 @@
         out[...] = grown[:, pl.ds(places[side], 32)]
 
 
-def add_a_kernel(places, from_a, own, canvas):
+def add_kernel(places, from_a, own, from_b, to_a, mid, to_b, canvas):
     canvas[...] = jnp.zeros_like(canvas)
     canvas[:, pl.ds(places[1], 32)] = own[...]
-    spot = (slice(None), pl.ds(places[0], 32))
-    strip = from_a[HALF_ROWS:].reshape(2, 32, 16, C1)
-    canvas[spot] = canvas[spot] + strip.astype(F32)
-
-
-def add_b_kernel(places, given, from_b, to_a, mid, to_b, canvas):
-    canvas[...] = given[...]
-    spot = (slice(None), pl.ds(places[2], 32))
-    canvas[spot] = canvas[spot] + from_b[...].astype(F32)
+    for side, strip in ((0, from_a[HALF_ROWS:].reshape(2, 32, 16, C1)), (2, from_b[...])):
+        spot = (slice(None), pl.ds(places[side], 32))
+        canvas[spot] = canvas[spot] + strip.astype(F32)
     to_a[...] = canvas[:, pl.ds(places[3], 16)].astype(BF16)
     mid[...] = canvas[:, 16:32]
     to_b[...] = canvas[:, pl.ds(places[4], 16)].astype(BF16)
 
 
-def finish_kernel(own, from_a, from_b, blended, field_grad):
-    total = own[...] + from_a[...].astype(F32) + from_b[...].astype(F32)
-    blended[...] = total[0].astype(BF16)
-    field_grad[...] = total[1]
-
-
-def unpack_kernel(scale, core, own, other, g_first, g_down, g_up, halves):
-    halves[core[0]] = own[...]
-    halves[1 - core[0]] = other[...]
+def finish_kernel(which, own, from_a, from_b, out):
+    total = own[which] + from_a[which].astype(F32) + from_b[which].astype(F32)
+    out[...] = total.astype(out.dtype)
+
+
+def unpack_kernel(scale, places, own, other, g_first, g_down, g_up, halves):
+    halves[places[6]] = own[...]
+    halves[1 - places[6]] = other[...]
 
     def rows(base, count):
         half, at = base // HALF_ROWS, base % HALF_ROWS
@@ -147,11 +152,11 @@
 
 
 def net_kernel(
-    start, side_a, middle, side_b, fb, rf, rft, wd, rdt, ru,
+    places, side_a, middle, side_b, fb, rf, rft, wd, rdt, ru,
     mid_o, strip_b, keep, send,
     fs, cs, xv, hv, gv, g4, gs, bs, can_b, can_g, halves,
 ):
-    start_c, core = start[0], start[1]
+    start_c, core = places[5], places[6]
     at_a, at_b = 32 * (1 - core), 32 * core
 
     def put(base, value):
@@ -287,6 +292,7 @@
     return pl.pallas_call(
         prepare_kernel,
         out_shape=(
+            jax.ShapeDtypeStruct((8,), jnp.int32),
             jax.ShapeDtypeStruct((2, 16, 16, 2 * C1), F32),
             jax.ShapeDtypeStruct((3, 4 * C1, 2 * C1), BF16),
             jax.ShapeDtypeStruct((3, 2 * C1, 4 * C1), BF16),
@@ -294,14 +300,14 @@
             jax.ShapeDtypeStruct((2, C2, 2 * C1), BF16),
         ),
         in_specs=[SMEM, SMEM, VMEM, VMEM, VMEM, VMEM],
-        out_specs=[VMEM] * 5,
+        out_specs=[SMEM] + [VMEM] * 5,
         compiler_params=pltpu.CompilerParams(vmem_limit_bytes=10 * 2**20),
         cost_estimate=pl.CostEstimate(flops=5 * 10**6, bytes_accessed=10**7, transcendentals=0),
         name="prepare",
     )(where, offsets, table, w_first, w_down, w_up)
 
 
-def patch_work(start, side_a, middle, side_b, fb, rf, rft, wd, rdt, ru):
+def patch_work(places, side_a, middle, side_b, fb, rf, rft, wd, rdt, ru):
     return pl.pallas_call(
         net_kernel,
         out_shape=(
@@ -328,7 +334,7 @@
         compiler_params=pltpu.CompilerParams(vmem_limit_bytes=24 * 2**20),
         cost_estimate=pl.CostEstimate(flops=2 * 10**9, bytes_accessed=10**7, transcendentals=200000),
         name="patch_work",
-    )(start, side_a, middle, side_b, fb, rf, rft, wd, rdt, ru)
+    )(places, side_a, middle, side_b, fb, rf, rft, wd, rdt, ru)
 
 
 def small_call(body, name, outs, scratch, *args, smem=0):
@@ -378,18 +384,13 @@
     col_at = lax.axis_index(COL)
     where = jnp.stack([row_at, col_at]).astype(jnp.int32)
     both = jnp.stack([field, cotangent])
-    core = lax.axis_index("core").astype(jnp.int32)
-    zh = lax.axis_index("zh").astype(jnp.int32)
-    col_a = col_at + 1 - 2 * core
-    col_b = jnp.clip(col_at - 1 + 2 * core, 0, cols_n - 1)
-    firsts = [MARGIN + offsets[row_at, col, 0] for col in (col_a, col_at, col_b)]
-    places = jnp.stack(firsts + [32 * (1 - zh), 32 * zh]).astype(jnp.int32)
-    start = jnp.stack([MARGIN + offsets[row_at, col_at, 1], core])
-    fb, rf, rft, rdt, ru = prepared(
-        where, offsets.reshape(rows_n, 2 * cols_n), blend_table, w_first, w_down, w_up
+    places, fb, rf, rft, rdt, ru = prepared(
+        where, offsets.transpose(0, 2, 1), blend_table, w_first, w_down, w_up
     )
     row_a, row_b = swapped_a(both, "zh"), swapped_b(both, ROW)
-    row_a, row_b, fb, rf, rft, rdt, ru = lax.optimization_barrier((row_a, row_b, fb, rf, rft, rdt, ru))
+    row_a, row_b, places, fb, rf, rft, rdt, ru = lax.optimization_barrier(
+        (row_a, row_b, places, fb, rf, rft, rdt, ru)
+    )
     window_shape = (2, 32, TILE, C1)
     to_a, own, to_b = small_call(
         assemble_kernel,
@@ -402,9 +403,9 @@
         row_b,
         smem=1,
     )
-    side_b, side_a = swapped_b(to_b, COL), swapped_a(to_a, "core")
+    side_a, side_b = swapped_a(to_a, "core"), swapped_b(to_b, COL)
     own, strip_b, keep, send = patch_work(
-        start, side_a, own, side_b, fb, rf, rft, w_down.reshape(3, 3 * C1, C2), rdt, ru
+        places, side_a, own, side_b, fb, rf, rft, w_down.reshape(3, 3 * C1, C2), rdt, ru
     )
     got = swapped_a(send, "core")
     from_b = swapped_b(strip_b, COL)
@@ -412,37 +413,33 @@
     part = scattered(part, "x")
     part, from_b = lax.optimization_barrier((part, from_b))
     part = scattered(part, "y")
-    canvas = small_call(
-        add_a_kernel, "add_a", [((2, 48, TILE, C1), F32)], [], places, got, own, smem=1
-    )[0]
-    part, canvas = lax.optimization_barrier((part, canvas))
-    part = gathered(part, ("zl", "zh")).astype(F32).sum(0).astype(BF16)
     tile_shape = (2, TILE, TILE, C1)
     to_a, own, to_b = small_call(
-        add_b_kernel,
-        "add_b",
+        add_kernel,
+        "add",
         [(tile_shape, BF16), (tile_shape, F32), (tile_shape, BF16)],
         [pltpu.VMEM((2, 48, TILE, C1), F32)],
         places,
-        canvas,
+        got,
+        own,
         from_b,
         smem=1,
     )
-    part, to_a, own, to_b = lax.optimization_barrier((part, to_a, own, to_b))
-    row_a, row_b = swapped_a(to_a, "zh"), swapped_b(to_b, ROW)
+    row_a = swapped_a(to_a, "zh")
+    part, own, row_a, to_b = lax.optimization_barrier((part, own, row_a, to_b))
+    row_b = swapped_b(to_b, ROW)
+    part = gathered(part, ("zl", "zh")).astype(F32).sum(0).astype(BF16)
+    part, row_b = lax.optimization_barrier((part, row_b))
     part = gathered(part, "y").reshape(-1, C1)
-    part, own, row_a, row_b = lax.optimization_barrier((part, own, row_a, row_b))
+    blended = small_call(
+        functools.partial(finish_kernel, 0), "blend", [(field.shape, BF16)], [], own, row_a, row_b
+    )[0]
+    part, blended, own, row_a, row_b = lax.optimization_barrier((part, blended, own, row_a, row_b))
     part = gathered(part, "x").reshape(-1, C1)
-    blended, field_grad = small_call(
-        finish_kernel,
-        "finish",
-        [(field.shape, BF16), (field.shape, F32)],
-        [],
-        own,
-        row_a,
-        row_b,
-    )
-    part, blended, field_grad = lax.optimization_barrier((part, blended, field_grad))
+    field_grad = small_call(
+        functools.partial(finish_kernel, 1), "grad", [(field.shape, F32)], [], own, row_a, row_b
+    )[0]
+    part, field_grad = lax.optimization_barrier((part, field_grad))
     other = swapped_a(part, "core")
     scale = 1.0 / math.sqrt(TILE * rows_n * TILE * cols_n)
     g_first, g_down, g_up = small_call(
@@ -450,7 +447,7 @@
         "unpack",
         [((9, C1, C1), F32), ((3, 3 * C1, C2), F32), ((4, C2, C1), F32)],
         [pltpu.VMEM((2, HALF_ROWS, C1), BF16)],
-        core[None],
+        places,
         part,
         other,
         smem=1,

time: 141 us -> 144 us (1.021)
  starting transfers between devices: 76.1 us -> 81.9 us
  between operations: 3.4 us -> 0.8 us
  local copies, waits for them, and re-layouts: 8.38 us -> 6.64 us
    all_to_all x3, waiting for transfers between devices: 12.6 us -> 20.2 us  [gathered(): return lax.all_to_all(parts, axes, 0, 0, tiled=True)]
    all_to_all x2, waiting for transfers between devices: 12.8 us -> 7.01 us  [scattered(): got = lax.all_to_all(parts, axes, 0, 0, tiled=True)]
    all_to_all x3, starting transfers between devices: 19.6 us -> 24.8 us  [gathered(): return lax.all_to_all(parts, axes, 0, 0, tiled=True)]
    ppermute x4, starting transfers between devices: 9.24 us -> 12.9 us  [swapped_b(): return lax.ppermute(x, axes, pairs + [(j, i) for i, j in pairs])]
    ppermute x5, waiting for transfers between devices: 9.7 us -> 6.42 us  [swapped_a(): return lax.ppermute(x, axis, [(0, 1), (1, 0)])]
    ppermute x4, waiting for transfers between devices: 3.71 us -> 6.1 us  [swapped_b(): return lax.ppermute(x, axes, pairs + [(j, i) for i, j in pairs])]
    all_to_all x2, starting transfers between devices: 16.2 us -> 14.5 us  [scattered(): got = lax.all_to_all(parts, axes, 0, 0, tiled=True)]
    dynamic_slice x1 -> x0, local copies, waits for them, and re-layouts: 1.49 us -> none  [per_device(): offsets[row_at, col, 0]]
  transfers between devices with their start and end apart: 14 -> 14, of which waited for: 8 -> 9; matrix products, arithmetic and copies ran while one was open for 2% -> 1% of each run, Pallas kernels for 3% -> 3%
where the time goes in v7:
time: 144 us; the launch traced here: 143 us
  starting transfers between devices  81.9 us (57%)
  waiting for transfers between devices  39.7 us (28%)
  Pallas kernels  11 us (8%)
  local copies, waits for them, and re-layouts  6.64 us (5%)
  other arithmetic  2.75 us (2%)
    ppermute x5, starting transfers between devices, swapped_a(): return lax.ppermute(x, axis, [(0, 1), (1, 0)])  29.8 us
    all_to_all x3, starting transfers between devices, gathered(): return lax.all_to_all(parts, axes, 0, 0, tiled=True)  24.8 us
    all_to_all x3, waiting for transfers between devices, gathered(): return lax.all_to_all(parts, axes, 0, 0, tiled=True)  20.2 us
    all_to_all x2, starting transfers between devices, scattered(): got = lax.all_to_all(parts, axes, 0, 0, tiled=True)  14.5 us
    ppermute x4, starting transfers between devices, swapped_b(): return lax.ppermute(x, axes, pairs + [(j, i) for i, j in pairs])  12.9 us
    all_to_all x2, waiting for transfers between devices, scattered(): got = lax.all_to_all(parts, axes, 0, 0, tiled=True)  7.01 us
    ppermute x5, waiting for transfers between devices, swapped_a(): return lax.ppermute(x, axis, [(0, 1), (1, 0)])  6.42 us
    ppermute x4, waiting for transfers between devices, swapped_b(): return lax.ppermute(x, axes, pairs + [(j, i) for i, j in pairs])  6.1 us
  transfers between devices with their start and end apart: 14, of which 9 were waited for; matrix products, arithmetic and copies ran while one was open for 1% of the time, Pallas kernels for 3%

profile of v7, /device:TPU:1, one launch (start us, length us, event | category | flops | bytes accessed | tf_op | source)
XLA Modules:
  0.0 142.8 jit_solution(4070024187305184246)
XLA Ops:
  0.6 0.9 pad_maximum_fusion.both
  1.5 0.7 collective-permute-start.1
  2.2 12.7 %collective-permute-start = (bf16[2,16,16,128]{3,2,1,0:T(8,128)(2,1)S(1)}, bf16[2,16,16,128]{3,2,1,0:T(8,128)(2,1)S(1)}, u32[]{:S(2)}, u32[]{:S(2)}) collective-permute-start(bf16[2,16,16,128]{3,2,1,0:T(8,128)(2,1)S(1)} %pad_maximum_fusion.both), channel_id=1, source_target_pairs={{0,1},{1,0},{2,3},{3,2},{4,5},{5,4},{6,7},{7,6},{8,9},{9,8},{10,11... | collective-permute-start | bytes 393224 | tf_op jit(solution)/shard_map/ppermute | solution.py:360
  14.9 0.1 pad_add_fusion.where
  15.0 1.1 copy-done
  16.1 1.0 copy-done.2
  17.0 0.9 copy-done.3
  18.0 0.7 copy-done.4
  18.7 0.7 copy-done.5
  19.4 1.6 %prepare.1 = (s32[8]{0:T(128)S(1)}, f32[2,16,16,256]{3,2,1,0:T(8,128)S(1)}, bf16[3,512,256]{2,1,0:T(8,128)(2,1)S(1)}, bf16[3,256,512]{2,1,0:T(8,128)(2,1)S(1)}, ...) custom-call(s32[2]{0:T(128)S(1)} %pad_add_fusion.where, s32[8,2,64]{2,1,0:T(2,128)S(1)} %bitcast.16, ...), custom_call_target="tpu_custom_call" | custom-call | flops 5000000 | bytes 10000000 | tf_op jit(solution)/shard_map/prepare/pallas_call | solution.py:292
  21.0 0.0 collective-permute-done.1.from_b
  21.0 0.0 collective-permute-done.from_a
  21.0 0.6 assemble.1
  21.6 2.9 %collective-permute-start.2 = (bf16[2,32,16,128]{3,2,1,0:T(8,128)(2,1)S(1)}, bf16[2,32,16,128]{3,2,1,0:T(8,128)(2,1)S(1)}, u32[]{:S(2)}, u32[]{:S(2)}) collective-permute-start(bf16[2,32,16,128]{3,2,1,0:T(8,128)(2,1)S(1)} %get-tuple-element.56), channel_id=1, source_target_pairs={{0,8},{8,0},{1,9},{9,1},{2,10},{10,2},{3,11},{11,3},{4,12},{12,4},... | collective-permute-start | bytes 786440 | tf_op jit(solution)/shard_map/ppermute | solution.py:360
  24.5 6.9 %collective-permute-start.3 = (bf16[2,32,16,128]{3,2,1,0:T(8,128)(2,1)S(1)}, bf16[2,32,16,128]{3,2,1,0:T(8,128)(2,1)S(1)}, u32[]{:S(2)}, u32[]{:S(2)}) collective-permute-start(bf16[2,32,16,128]{3,2,1,0:T(8,128)(2,1)S(1)} %get-tuple-element.58), channel_id=1, source_target_pairs={{8,16},{24,32},{40,48},{56,64},{72,80},{88,96},{104,112},{120,128}... | collective-permute-start | bytes 786440 | tf_op jit(solution)/shard_map/ppermute | solution.py:356
  31.4 0.0 collective-permute-done.2.side_a
  31.4 6.1 %collective-permute-done.3.side_b = bf16[2,32,16,128]{3,2,1,0:T(8,128)(2,1)S(1)} collective-permute-done((bf16[2,32,16,128]{3,2,1,0:T(8,128)(2,1)S(1)}, bf16[2,32,16,128]{3,2,1,0:T(8,128)(2,1)S(1)}, u32[]{:S(2)}, u32[]{:S(2)}) %collective-permute-start.3) | collective-permute-done | bytes 262176 | tf_op jit(solution)/shard_map/ppermute | solution.py:356
  37.5 0.0 copy-done.1
  37.5 4.6 %patch_work.1 = (f32[2,32,16,128]{3,2,1,0:T(8,128)S(1)}, bf16[2,32,16,128]{3,2,1,0:T(8,128)(2,1)S(1)}, bf16[2304,128]{1,0:T(8,128)(2,1)S(1)}, bf16[3328,128]{1,0:T(8,128)(2,1)S(1)}) custom-call(s32[8]{0:T(128)S(1)} %get-tuple-element.53.places, bf16[2,32,16,128]{3,2,1,0:T(8,128)(2,1)S(1)} %collective-permute-done.2.side_a, ...), custom_call_target="tpu_custom_call" | custom-call | flops 2000000000 | bytes 10000000 | tf_op jit(solution)/shard_map/patch_work/pallas_call | solution.py:311
  42.1 1.9 %collective-permute-start.4 = (bf16[3328,128]{1,0:T(8,128)(2,1)S(1)}, bf16[3328,128]{1,0:T(8,128)(2,1)S(1)}, u32[]{:S(2)}, u32[]{:S(2)}) collective-permute-start(bf16[3328,128]{1,0:T(8,128)(2,1)S(1)} %get-tuple-element.65), channel_id=1, source_target_pairs={{0,8},{8,0},{1,9},{9,1},{2,10},{10,2},{3,11},{11,3},{4,12},{12,4},... | collective-permute-start | bytes 2555912 | tf_op jit(solution)/shard_map/ppermute | solution.py:360
  44.1 2.3 %collective-permute-done.4.from_a = bf16[3328,128]{1,0:T(8,128)(2,1)S(1)} collective-permute-done((bf16[3328,128]{1,0:T(8,128)(2,1)S(1)}, bf16[3328,128]{1,0:T(8,128)(2,1)S(1)}, u32[]{:S(2)}, u32[]{:S(2)}) %collective-permute-start.4) | collective-permute-done | bytes 852000 | tf_op jit(solution)/shard_map/ppermute | solution.py:360
  46.4 1.0 add_convert_fusion
  47.4 5.7 %all-to-all-start = ((bf16[4,576,128]{2,1,0:T(8,128)(2,1)}), bf16[4,576,128]{2,1,0:T(8,128)(2,1)S(1)}, u32[]{:S(2)}, u32[]{:S(2)}) async-start(bf16[4,576,128]{2,1,0:T(8,128)(2,1)} %bitcast.6), calls=%async_computation | async-start | bytes 1179648 | tf_op jit(solution)/shard_map/all_to_all | solution.py:370
  53.1 4.7 %collective-permute-start.5 = (bf16[2,32,16,128]{3,2,1,0:T(8,128)(2,1)S(1)}, bf16[2,32,16,128]{3,2,1,0:T(8,128)(2,1)S(1)}, u32[]{:S(2)}, u32[]{:S(2)}) collective-permute-start(bf16[2,32,16,128]{3,2,1,0:T(8,128)(2,1)S(1)} %get-tuple-element.66), channel_id=1, source_target_pairs={{8,16},{24,32},{40,48},{56,64},{72,80},{88,96},{104,112},{120,128}... | collective-permute-start | bytes 786440 | tf_op jit(solution)/shard_map/ppermute | solution.py:356
  57.7 5.2 %all-to-all-done = bf16[4,576,128]{2,1,0:T(8,128)(2,1)S(1)} async-done(((bf16[4,576,128]{2,1,0:T(8,128)(2,1)}), bf16[4,576,128]{2,1,0:T(8,128)(2,1)S(1)}, u32[]{:S(2)}, u32[]{:S(2)}) %all-to-all-start) | async-done | bytes 589856 | tf_op jit(solution)/shard_map/all_to_all | solution.py:370
  62.9 0.8 reduce_sum.36
  63.7 0.0 collective-permute-done.5.from_b
  63.7 8.8 %all-to-all-start.1 = ((bf16[8,72,128]{2,1,0:T(8,128)(2,1)}), bf16[8,72,128]{2,1,0:T(8,128)(2,1)S(1)}, u32[]{:S(2)}, u32[]{:S(2)}) async-start(bf16[8,72,128]{2,1,0:T(8,128)(2,1)} %bitcast.7), calls=%async_computation.1 | async-start | bytes 294912 | tf_op jit(solution)/shard_map/all_to_all | solution.py:370
  72.5 0.8 add.20
  73.3 5.6 %collective-permute-start.6 = (bf16[2,16,16,128]{3,2,1,0:T(8,128)(2,1)S(1)}, bf16[2,16,16,128]{3,2,1,0:T(8,128)(2,1)S(1)}, u32[]{:S(2)}, u32[]{:S(2)}) collective-permute-start(bf16[2,16,16,128]{3,2,1,0:T(8,128)(2,1)S(1)} %get-tuple-element.71), channel_id=1, source_target_pairs={{0,1},{1,0},{2,3},{3,2},{4,5},{5,4},{6,7},{7,6},{8,9},{9,8},{10,11... | collective-permute-start | bytes 393224 | tf_op jit(solution)/shard_map/ppermute | solution.py:360
  78.9 1.8 %all-to-all-done.1 = bf16[8,72,128]{2,1,0:T(8,128)(2,1)S(1)} async-done(((bf16[8,72,128]{2,1,0:T(8,128)(2,1)}), bf16[8,72,128]{2,1,0:T(8,128)(2,1)S(1)}, u32[]{:S(2)}, u32[]{:S(2)}) %all-to-all-start.1) | async-done | bytes 147488 | tf_op jit(solution)/shard_map/all_to_all | solution.py:370
  80.8 2.5 %collective-permute-done.6.from_a = bf16[2,16,16,128]{3,2,1,0:T(8,128)(2,1)S(1)} collective-permute-done((bf16[2,16,16,128]{3,2,1,0:T(8,128)(2,1)S(1)}, bf16[2,16,16,128]{3,2,1,0:T(8,128)(2,1)S(1)}, u32[]{:S(2)}, u32[]{:S(2)}) %collective-permute-start.6) | collective-permute-done | bytes 131104 | tf_op jit(solution)/shard_map/ppermute | solution.py:360
  83.2 0.7 broadcast_in_dim.6
  83.9 6.4 %all-to-all-start.2 = ((bf16[8,72,128]{2,1,0:T(8,128)(2,1)}), bf16[8,72,128]{2,1,0:T(8,128)(2,1)S(1)}, u32[]{:S(2)}, u32[]{:S(2)}) async-start(bf16[8,72,128]{2,1,0:T(8,128)(2,1)} %broadcast_in_dim.6), calls=%async_computation.2 | async-start | bytes 294912 | tf_op jit(solution)/shard_map/all_to_all | solution.py:377
  90.3 0.7 collective-permute-start.7
  90.9 6.1 %all-to-all-done.2 = bf16[8,72,128]{2,1,0:T(8,128)(2,1)S(1)} async-done(((bf16[8,72,128]{2,1,0:T(8,128)(2,1)}), bf16[8,72,128]{2,1,0:T(8,128)(2,1)S(1)}, u32[]{:S(2)}, u32[]{:S(2)}) %all-to-all-start.2) | async-done | bytes 147488 | tf_op jit(solution)/shard_map/all_to_all | solution.py:377
  97.1 0.0 collective-permute-done.7.from_b
  97.1 0.7 broadcast_in_dim.7
  97.8 6.4 %all-to-all-start.3 = ((bf16[8,72,128]{2,1,0:T(8,128)(2,1)}), bf16[8,72,128]{2,1,0:T(8,128)(2,1)S(1)}, u32[]{:S(2)}, u32[]{:S(2)}) async-start(bf16[8,72,128]{2,1,0:T(8,128)(2,1)} %broadcast_in_dim.7), calls=%async_computation.3 | async-start | bytes 294912 | tf_op jit(solution)/shard_map/all_to_all | solution.py:377
  104.1 0.7 blend.1
  104.8 7.5 %all-to-all-done.3 = bf16[8,72,128]{2,1,0:T(8,128)(2,1)S(1)} async-done(((bf16[8,72,128]{2,1,0:T(8,128)(2,1)}), bf16[8,72,128]{2,1,0:T(8,128)(2,1)S(1)}, u32[]{:S(2)}, u32[]{:S(2)}) %all-to-all-start.3) | async-done | bytes 147488 | tf_op jit(solution)/shard_map/all_to_all | solution.py:377
  112.2 0.9 broadcast_in_dim.8
  113.1 12.0 %all-to-all-start.4 = ((bf16[4,576,128]{2,1,0:T(8,128)(2,1)}), bf16[4,576,128]{2,1,0:T(8,128)(2,1)S(1)}, u32[]{:S(2)}, u32[]{:S(2)}) async-start(bf16[4,576,128]{2,1,0:T(8,128)(2,1)} %broadcast_in_dim.8), calls=%async_computation.4 | async-start | bytes 1179648 | tf_op jit(solution)/shard_map/all_to_all | solution.py:377
  125.1 0.7 grad.1
  125.8 6.6 %all-to-all-done.4 = bf16[4,576,128]{2,1,0:T(8,128)(2,1)S(1)} async-done(((bf16[4,576,128]{2,1,0:T(8,128)(2,1)}), bf16[4,576,128]{2,1,0:T(8,128)(2,1)S(1)}, u32[]{:S(2)}, u32[]{:S(2)}) %all-to-all-start.4) | async-done | bytes 589856 | tf_op jit(solution)/shard_map/all_to_all | solution.py:377
  132.4 6.7 %collective-permute-start.8 = (bf16[2304,128]{1,0:T(8,128)(2,1)S(1)}, bf16[2304,128]{1,0:T(8,128)(2,1)S(1)}, u32[]{:S(2)}, u32[]{:S(2)}) collective-permute-start(bf16[2304,128]{1,0:T(8,128)(2,1)S(1)} %bitcast.13), channel_id=1, source_target_pairs={{0,8},{8,0},{1,9},{9,1},{2,10},{10,2},{3,11},{11,3},{4,12},{12,4},... | collective-permute-start | bytes 1769480 | tf_op jit(solution)/shard_map/ppermute | solution.py:360
  139.1 1.6 %collective-permute-done.8.other = bf16[2304,128]{1,0:T(8,128)(2,1)S(1)} collective-permute-done((bf16[2304,128]{1,0:T(8,128)(2,1)S(1)}, bf16[2304,128]{1,0:T(8,128)(2,1)S(1)}, u32[]{:S(2)}, u32[]{:S(2)}) %collective-permute-start.8) | collective-permute-done | bytes 589856 | tf_op jit(solution)/shard_map/ppermute | solution.py:360
  140.7 2.1 %unpack.1 = (f32[9,128,128]{2,1,0:T(8,128)}, f32[3,384,256]{2,1,0:T(8,128)}, f32[4,256,128]{2,1,0:T(8,128)}) custom-call(s32[8]{0:T(128)S(1)} %get-tuple-element.53.places, bf16[2304,128]{1,0:T(8,128)(2,1)S(1)} %bitcast.14, bf16[2304,128]{1,0:T(8,128)(2,1)S(1)} %collective-permute-done.8.other), custom_call_target="tpu_custom_call" | custom-call | flops 1000000 | bytes 2000000 | tf_op jit(solution)/shard_map/unpack/pallas_call | solution.py:341
  (8 shorter events, 0.1 us)
Async XLA Ops:
  1.5 19.5 %collective-permute-start.1 = (bf16[2,16,16,128]{3,2,1,0:T(8,128)(2,1)S(1)}, bf16[2,16,16,128]{3,2,1,0:T(8,128)(2,1)S(1)}, u32[]{:S(2)}, u32[]{:S(2)}) collective-permute-start(bf16[2,16,16,128]{3,2,1,0:T(8,128)(2,1)S(1)} %pad_maximum_fusion.both), channel_id=1, source_target_pairs={{1,2},{3,4},{5,6},{2,1},{4,3},{6,5},{9,10},{11,12},{13,14},{10,9},... | collective-permute-start | bytes 393224 | tf_op jit(solution)/shard_map/ppermute | solution.py:356
  2.2 18.8 %collective-permute-start = (bf16[2,16,16,128]{3,2,1,0:T(8,128)(2,1)S(1)}, bf16[2,16,16,128]{3,2,1,0:T(8,128)(2,1)S(1)}, u32[]{:S(2)}, u32[]{:S(2)}) collective-permute-start(bf16[2,16,16,128]{3,2,1,0:T(8,128)(2,1)S(1)} %pad_maximum_fusion.both), channel_id=1, source_target_pairs={{0,1},{1,0},{2,3},{3,2},{4,5},{5,4},{6,7},{7,6},{8,9},{9,8},{10,11... | collective-permute-start | bytes 393224 | tf_op jit(solution)/shard_map/ppermute | solution.py:360
  15.0 1.1 copy-start
  16.1 1.0 copy-start.2
  17.0 0.9 copy-start.3
  18.0 0.7 copy-start.4
  18.7 0.7 copy-start.5
  19.4 18.1 %copy-start.1 = (bf16[3,3,128,256]{3,2,1,0:T(8,128)(2,1)S(1)}, bf16[3,3,128,256]{3,2,1,0:T(8,128)(2,1)}, u32[]{:S(2)}) copy-start(bf16[3,3,128,256]{3,2,1,0:T(8,128)(2,1)} %w_down.1) | copy-start | bytes 1769476
  21.6 9.8 %collective-permute-start.2 = (bf16[2,32,16,128]{3,2,1,0:T(8,128)(2,1)S(1)}, bf16[2,32,16,128]{3,2,1,0:T(8,128)(2,1)S(1)}, u32[]{:S(2)}, u32[]{:S(2)}) collective-permute-start(bf16[2,32,16,128]{3,2,1,0:T(8,128)(2,1)S(1)} %get-tuple-element.56), channel_id=1, source_target_pairs={{0,8},{8,0},{1,9},{9,1},{2,10},{10,2},{3,11},{11,3},{4,12},{12,4},... | collective-permute-start | bytes 786440 | tf_op jit(solution)/shard_map/ppermute | solution.py:360
  24.5 13.0 %collective-permute-start.3 = (bf16[2,32,16,128]{3,2,1,0:T(8,128)(2,1)S(1)}, bf16[2,32,16,128]{3,2,1,0:T(8,128)(2,1)S(1)}, u32[]{:S(2)}, u32[]{:S(2)}) collective-permute-start(bf16[2,32,16,128]{3,2,1,0:T(8,128)(2,1)S(1)} %get-tuple-element.58), channel_id=1, source_target_pairs={{8,16},{24,32},{40,48},{56,64},{72,80},{88,96},{104,112},{120,128}... | collective-permute-start | bytes 786440 | tf_op jit(solution)/shard_map/ppermute | solution.py:356
  42.1 4.3 %collective-permute-start.4 = (bf16[3328,128]{1,0:T(8,128)(2,1)S(1)}, bf16[3328,128]{1,0:T(8,128)(2,1)S(1)}, u32[]{:S(2)}, u32[]{:S(2)}) collective-permute-start(bf16[3328,128]{1,0:T(8,128)(2,1)S(1)} %get-tuple-element.65), channel_id=1, source_target_pairs={{0,8},{8,0},{1,9},{9,1},{2,10},{10,2},{3,11},{11,3},{4,12},{12,4},... | collective-permute-start | bytes 2555912 | tf_op jit(solution)/shard_map/ppermute | solution.py:360
  47.4 15.6 %all-to-all-start = ((bf16[4,576,128]{2,1,0:T(8,128)(2,1)}), bf16[4,576,128]{2,1,0:T(8,128)(2,1)S(1)}, u32[]{:S(2)}, u32[]{:S(2)}) async-start(bf16[4,576,128]{2,1,0:T(8,128)(2,1)} %bitcast.6), calls=%async_computation | async-start | bytes 1179648 | tf_op jit(solution)/shard_map/all_to_all | solution.py:370
  53.1 10.6 %collective-permute-start.5 = (bf16[2,32,16,128]{3,2,1,0:T(8,128)(2,1)S(1)}, bf16[2,32,16,128]{3,2,1,0:T(8,128)(2,1)S(1)}, u32[]{:S(2)}, u32[]{:S(2)}) collective-permute-start(bf16[2,32,16,128]{3,2,1,0:T(8,128)(2,1)S(1)} %get-tuple-element.66), channel_id=1, source_target_pairs={{8,16},{24,32},{40,48},{56,64},{72,80},{88,96},{104,112},{120,128}... | collective-permute-start | bytes 786440 | tf_op jit(solution)/shard_map/ppermute | solution.py:356
  63.7 17.0 %all-to-all-start.1 = ((bf16[8,72,128]{2,1,0:T(8,128)(2,1)}), bf16[8,72,128]{2,1,0:T(8,128)(2,1)S(1)}, u32[]{:S(2)}, u32[]{:S(2)}) async-start(bf16[8,72,128]{2,1,0:T(8,128)(2,1)} %bitcast.7), calls=%async_computation.1 | async-start | bytes 294912 | tf_op jit(solution)/shard_map/all_to_all | solution.py:370
  73.3 9.9 %collective-permute-start.6 = (bf16[2,16,16,128]{3,2,1,0:T(8,128)(2,1)S(1)}, bf16[2,16,16,128]{3,2,1,0:T(8,128)(2,1)S(1)}, u32[]{:S(2)}, u32[]{:S(2)}) collective-permute-start(bf16[2,16,16,128]{3,2,1,0:T(8,128)(2,1)S(1)} %get-tuple-element.71), channel_id=1, source_target_pairs={{0,1},{1,0},{2,3},{3,2},{4,5},{5,4},{6,7},{7,6},{8,9},{9,8},{10,11... | collective-permute-start | bytes 393224 | tf_op jit(solution)/shard_map/ppermute | solution.py:360
  83.9 13.1 %all-to-all-start.2 = ((bf16[8,72,128]{2,1,0:T(8,128)(2,1)}), bf16[8,72,128]{2,1,0:T(8,128)(2,1)S(1)}, u32[]{:S(2)}, u32[]{:S(2)}) async-start(bf16[8,72,128]{2,1,0:T(8,128)(2,1)} %broadcast_in_dim.6), calls=%async_computation.2 | async-start | bytes 294912 | tf_op jit(solution)/shard_map/all_to_all | solution.py:377
  90.3 6.8 %collective-permute-start.7 = (bf16[2,16,16,128]{3,2,1,0:T(8,128)(2,1)S(1)}, bf16[2,16,16,128]{3,2,1,0:T(8,128)(2,1)S(1)}, u32[]{:S(2)}, u32[]{:S(2)}) collective-permute-start(bf16[2,16,16,128]{3,2,1,0:T(8,128)(2,1)S(1)} %get-tuple-element.74), channel_id=1, source_target_pairs={{1,2},{3,4},{5,6},{2,1},{4,3},{6,5},{9,10},{11,12},{13,14},{10,9},... | collective-permute-start | bytes 393224 | tf_op jit(solution)/shard_map/ppermute | solution.py:356
  97.8 14.5 %all-to-all-start.3 = ((bf16[8,72,128]{2,1,0:T(8,128)(2,1)}), bf16[8,72,128]{2,1,0:T(8,128)(2,1)S(1)}, u32[]{:S(2)}, u32[]{:S(2)}) async-start(bf16[8,72,128]{2,1,0:T(8,128)(2,1)} %broadcast_in_dim.7), calls=%async_computation.3 | async-start | bytes 294912 | tf_op jit(solution)/shard_map/all_to_all | solution.py:377
  113.1 19.3 %all-to-all-start.4 = ((bf16[4,576,128]{2,1,0:T(8,128)(2,1)}), bf16[4,576,128]{2,1,0:T(8,128)(2,1)S(1)}, u32[]{:S(2)}, u32[]{:S(2)}) async-start(bf16[4,576,128]{2,1,0:T(8,128)(2,1)} %broadcast_in_dim.8), calls=%async_computation.4 | async-start | bytes 1179648 | tf_op jit(solution)/shard_map/all_to_all | solution.py:377
  132.4 8.3 %collective-permute-start.8 = (bf16[2304,128]{1,0:T(8,128)(2,1)S(1)}, bf16[2304,128]{1,0:T(8,128)(2,1)S(1)}, u32[]{:S(2)}, u32[]{:S(2)}) collective-permute-start(bf16[2304,128]{1,0:T(8,128)(2,1)S(1)} %bitcast.13), channel_id=1, source_target_pairs={{0,8},{8,0},{1,9},{9,1},{2,10},{10,2},{3,11},{11,3},{4,12},{12,4},... | collective-permute-start | bytes 1769480 | tf_op jit(solution)/shard_map/ppermute | solution.py:360

commit v8 on v7

--- a/solution.py
+++ b/solution.py
@@ -111,9 +111,10 @@
     to_b[...] = canvas[:, pl.ds(places[4], 16)].astype(BF16)
 
 
-def finish_kernel(which, own, from_a, from_b, out):
-    total = own[which] + from_a[which].astype(F32) + from_b[which].astype(F32)
-    out[...] = total.astype(out.dtype)
+def finish_kernel(own, from_a, from_b, blended, field_grad):
+    total = own[...] + from_a[...].astype(F32) + from_b[...].astype(F32)
+    blended[...] = total[0].astype(BF16)
+    field_grad[...] = total[1]
 
 
 def unpack_kernel(scale, places, own, other, g_first, g_down, g_up, halves):
@@ -410,9 +411,9 @@
     got = swapped_a(send, "core")
     from_b = swapped_b(strip_b, COL)
     part = added(keep, got[:HALF_ROWS])
-    part = scattered(part, "x")
+    part = scattered(part, ("x", "y"))
     part, from_b = lax.optimization_barrier((part, from_b))
-    part = scattered(part, "y")
+    part = gathered(part, ("zl", "zh")).astype(F32).sum(0).astype(BF16)
     tile_shape = (2, TILE, TILE, C1)
     to_a, own, to_b = small_call(
         add_kernel,
@@ -425,22 +426,20 @@
         from_b,
         smem=1,
     )
-    row_a = swapped_a(to_a, "zh")
-    part, own, row_a, to_b = lax.optimization_barrier((part, own, row_a, to_b))
-    row_b = swapped_b(to_b, ROW)
-    part = gathered(part, ("zl", "zh")).astype(F32).sum(0).astype(BF16)
-    part, row_b = lax.optimization_barrier((part, row_b))
-    part = gathered(part, "y").reshape(-1, C1)
-    blended = small_call(
-        functools.partial(finish_kernel, 0), "blend", [(field.shape, BF16)], [], own, row_a, row_b
-    )[0]
-    part, blended, own, row_a, row_b = lax.optimization_barrier((part, blended, own, row_a, row_b))
-    part = gathered(part, "x").reshape(-1, C1)
-    field_grad = small_call(
-        functools.partial(finish_kernel, 1), "grad", [(field.shape, F32)], [], own, row_a, row_b
-    )[0]
-    part, field_grad = lax.optimization_barrier((part, field_grad))
+    part, own, to_a, to_b = lax.optimization_barrier((part, own, to_a, to_b))
+    row_a, row_b = swapped_a(to_a, "zh"), swapped_b(to_b, ROW)
+    part = gathered(part, ("x", "y")).reshape(-1, C1)
+    part, own, row_a, row_b = lax.optimization_barrier((part, own, row_a, row_b))
     other = swapped_a(part, "core")
+    blended, field_grad = small_call(
+        finish_kernel,
+        "finish",
+        [(field.shape, BF16), (field.shape, F32)],
+        [],
+        own,
+        row_a,
+        row_b,
+    )
     scale = 1.0 / math.sqrt(TILE * rows_n * TILE * cols_n)
     g_first, g_down, g_up = small_call(
         functools.partial(unpack_kernel, scale),

time: 144 us -> 129 us (0.90)
  the two profiles are of different devices: /device:TPU:1 before, /device:TPU:7 now
where the time goes in v8:
time: 129 us; the launch traced here: 128 us
  starting transfers between devices  69.2 us (54%)
  waiting for transfers between devices  39.4 us (31%)
  Pallas kernels  10.4 us (8%)
  local copies, waits for them, and re-layouts  5.96 us (5%)
  other arithmetic  2.05 us (2%)
    ppermute x4, starting transfers between devices, swapped_b(): return lax.ppermute(x, axes, pairs + [(j, i) for i, j in pairs])  24.8 us
    all_to_all x2, starting transfers between devices, gathered(): return lax.all_to_all(parts, axes, 0, 0, tiled=True)  16.5 us
    ppermute x5, starting transfers between devices, swapped_a(): return lax.ppermute(x, axis, [(0, 1), (1, 0)])  16.2 us
    ppermute x4, waiting for transfers between devices, swapped_b(): return lax.ppermute(x, axes, pairs + [(j, i) for i, j in pairs])  15.7 us
    all_to_all x1, waiting for transfers between devices, scattered(): got = lax.all_to_all(parts, axes, 0, 0, tiled=True)  12.1 us
    all_to_all x1, starting transfers between devices, scattered(): got = lax.all_to_all(parts, axes, 0, 0, tiled=True)  11.7 us
    all_to_all x2, waiting for transfers between devices, gathered(): return lax.all_to_all(parts, axes, 0, 0, tiled=True)  6.06 us
    ppermute x5, waiting for transfers between devices, swapped_a(): return lax.ppermute(x, axis, [(0, 1), (1, 0)])  5.43 us
  transfers between devices with their start and end apart: 12, of which 8 were waited for; matrix products, arithmetic and copies ran while one was open for 0% of the time, Pallas kernels for 2%

profile of v8, /device:TPU:7, one launch (start us, length us, event | category | flops | bytes accessed | tf_op | source)
XLA Modules:
  0.0 127.8 jit_solution(14499003960431820027)
XLA Ops:
  0.6 0.9 pad_maximum_fusion.both
  1.5 10.9 %collective-permute-start.1 = (bf16[2,16,16,128]{3,2,1,0:T(8,128)(2,1)S(1)}, bf16[2,16,16,128]{3,2,1,0:T(8,128)(2,1)S(1)}, u32[]{:S(2)}, u32[]{:S(2)}) collective-permute-start(bf16[2,16,16,128]{3,2,1,0:T(8,128)(2,1)S(1)} %pad_maximum_fusion.both), channel_id=1, source_target_pairs={{1,2},{3,4},{5,6},{2,1},{4,3},{6,5},{9,10},{11,12},{13,14},{10,9},... | collective-permute-start | bytes 393224 | tf_op jit(solution)/shard_map/ppermute | solution.py:357
  12.4 1.9 %collective-permute-start = (bf16[2,16,16,128]{3,2,1,0:T(8,128)(2,1)S(1)}, bf16[2,16,16,128]{3,2,1,0:T(8,128)(2,1)S(1)}, u32[]{:S(2)}, u32[]{:S(2)}) collective-permute-start(bf16[2,16,16,128]{3,2,1,0:T(8,128)(2,1)S(1)} %pad_maximum_fusion.both), channel_id=1, source_target_pairs={{0,1},{1,0},{2,3},{3,2},{4,5},{5,4},{6,7},{7,6},{8,9},{9,8},{10,11... | collective-permute-start | bytes 393224 | tf_op jit(solution)/shard_map/ppermute | solution.py:361
  14.4 0.1 pad_add_fusion.where
  14.4 0.0 copy-start
  14.4 1.1 copy-done
  15.5 0.0 copy-start.2
  15.5 1.0 copy-done.2
  16.5 0.0 copy-start.3
  16.5 0.9 copy-done.3
  17.4 0.0 copy-start.4
  17.4 0.7 copy-done.4
  18.1 0.0 copy-start.5
  18.1 0.7 copy-done.5
  18.8 0.0 copy-start.1
  18.8 1.6 %prepare.1 = (s32[8]{0:T(128)S(1)}, f32[2,16,16,256]{3,2,1,0:T(8,128)S(1)}, bf16[3,512,256]{2,1,0:T(8,128)(2,1)S(1)}, bf16[3,256,512]{2,1,0:T(8,128)(2,1)S(1)}, ...) custom-call(s32[2]{0:T(128)S(1)} %pad_add_fusion.where, s32[8,2,64]{2,1,0:T(2,128)S(1)} %bitcast.14, ...), custom_call_target="tpu_custom_call" | custom-call | flops 5000000 | bytes 10000000 | tf_op jit(solution)/shard_map/prepare/pallas_call | solution.py:293
  20.4 0.0 collective-permute-done.1.from_b
  20.4 1.7 %collective-permute-done.from_a = bf16[2,16,16,128]{3,2,1,0:T(8,128)(2,1)S(1)} collective-permute-done((bf16[2,16,16,128]{3,2,1,0:T(8,128)(2,1)S(1)}, bf16[2,16,16,128]{3,2,1,0:T(8,128)(2,1)S(1)}, u32[]{:S(2)}, u32[]{:S(2)}) %collective-permute-start) | collective-permute-done | bytes 131104 | tf_op jit(solution)/shard_map/ppermute | solution.py:361
  22.1 0.6 assemble.1
  22.8 4.0 %collective-permute-start.2 = (bf16[2,32,16,128]{3,2,1,0:T(8,128)(2,1)S(1)}, bf16[2,32,16,128]{3,2,1,0:T(8,128)(2,1)S(1)}, u32[]{:S(2)}, u32[]{:S(2)}) collective-permute-start(bf16[2,32,16,128]{3,2,1,0:T(8,128)(2,1)S(1)} %get-tuple-element.53), channel_id=1, source_target_pairs={{0,8},{8,0},{1,9},{9,1},{2,10},{10,2},{3,11},{11,3},{4,12},{12,4},... | collective-permute-start | bytes 786440 | tf_op jit(solution)/shard_map/ppermute | solution.py:361
  26.8 5.7 %collective-permute-start.3 = (bf16[2,32,16,128]{3,2,1,0:T(8,128)(2,1)S(1)}, bf16[2,32,16,128]{3,2,1,0:T(8,128)(2,1)S(1)}, u32[]{:S(2)}, u32[]{:S(2)}) collective-permute-start(bf16[2,32,16,128]{3,2,1,0:T(8,128)(2,1)S(1)} %get-tuple-element.55), channel_id=1, source_target_pairs={{8,16},{24,32},{40,48},{56,64},{72,80},{88,96},{104,112},{120,128}... | collective-permute-start | bytes 786440 | tf_op jit(solution)/shard_map/ppermute | solution.py:357
  32.5 0.0 collective-permute-done.2.side_a
  32.5 6.1 %collective-permute-done.3.side_b = bf16[2,32,16,128]{3,2,1,0:T(8,128)(2,1)S(1)} collective-permute-done((bf16[2,32,16,128]{3,2,1,0:T(8,128)(2,1)S(1)}, bf16[2,32,16,128]{3,2,1,0:T(8,128)(2,1)S(1)}, u32[]{:S(2)}, u32[]{:S(2)}) %collective-permute-start.3) | collective-permute-done | bytes 262176 | tf_op jit(solution)/shard_map/ppermute | solution.py:357
  38.6 0.0 copy-done.1
  38.6 4.6 %patch_work.1 = (f32[2,32,16,128]{3,2,1,0:T(8,128)S(1)}, bf16[2,32,16,128]{3,2,1,0:T(8,128)(2,1)S(1)}, bf16[2304,128]{1,0:T(8,128)(2,1)S(1)}, bf16[3328,128]{1,0:T(8,128)(2,1)S(1)}) custom-call(s32[8]{0:T(128)S(1)} %get-tuple-element.50.places, bf16[2,32,16,128]{3,2,1,0:T(8,128)(2,1)S(1)} %collective-permute-done.2.side_a, ...), custom_call_target="tpu_custom_call" | custom-call | flops 2000000000 | bytes 10000000 | tf_op jit(solution)/shard_map/patch_work/pallas_call | solution.py:312
  43.3 1.9 %collective-permute-start.4 = (bf16[3328,128]{1,0:T(8,128)(2,1)S(1)}, bf16[3328,128]{1,0:T(8,128)(2,1)S(1)}, u32[]{:S(2)}, u32[]{:S(2)}) collective-permute-start(bf16[3328,128]{1,0:T(8,128)(2,1)S(1)} %get-tuple-element.62), channel_id=1, source_target_pairs={{0,8},{8,0},{1,9},{9,1},{2,10},{10,2},{3,11},{11,3},{4,12},{12,4},... | collective-permute-start | bytes 2555912 | tf_op jit(solution)/shard_map/ppermute | solution.py:361
  45.2 2.3 %collective-permute-done.4.from_a = bf16[3328,128]{1,0:T(8,128)(2,1)S(1)} collective-permute-done((bf16[3328,128]{1,0:T(8,128)(2,1)S(1)}, bf16[3328,128]{1,0:T(8,128)(2,1)S(1)}, u32[]{:S(2)}, u32[]{:S(2)}) %collective-permute-start.4) | collective-permute-done | bytes 852000 | tf_op jit(solution)/shard_map/ppermute | solution.py:361
  47.5 1.0 add_convert_fusion
  48.5 11.7 %all-to-all-start = ((bf16[32,72,128]{2,1,0:T(8,128)(2,1)}), bf16[32,72,128]{2,1,0:T(8,128)(2,1)S(1)}, u32[]{:S(2)}, u32[]{:S(2)}) async-start(bf16[32,72,128]{2,1,0:T(8,128)(2,1)} %bitcast.6), calls=%async_computation | async-start | bytes 1179648 | tf_op jit(solution)/shard_map/all_to_all | solution.py:371
  60.2 2.7 %collective-permute-start.5 = (bf16[2,32,16,128]{3,2,1,0:T(8,128)(2,1)S(1)}, bf16[2,32,16,128]{3,2,1,0:T(8,128)(2,1)S(1)}, u32[]{:S(2)}, u32[]{:S(2)}) collective-permute-start(bf16[2,32,16,128]{3,2,1,0:T(8,128)(2,1)S(1)} %get-tuple-element.63), channel_id=1, source_target_pairs={{8,16},{24,32},{40,48},{56,64},{72,80},{88,96},{104,112},{120,128}... | collective-permute-start | bytes 786440 | tf_op jit(solution)/shard_map/ppermute | solution.py:357
  62.9 12.1 %all-to-all-done = bf16[32,72,128]{2,1,0:T(8,128)(2,1)S(1)} async-done(((bf16[32,72,128]{2,1,0:T(8,128)(2,1)}), bf16[32,72,128]{2,1,0:T(8,128)(2,1)S(1)}, u32[]{:S(2)}, u32[]{:S(2)}) %all-to-all-start) | async-done | bytes 589856 | tf_op jit(solution)/shard_map/all_to_all | solution.py:371
  75.0 0.1 reduce_sum.24
  75.1 0.0 collective-permute-done.5.from_b
  75.1 0.7 broadcast_in_dim.4
  75.8 7.8 %all-to-all-start.1 = ((bf16[8,72,128]{2,1,0:T(8,128)(2,1)}), bf16[8,72,128]{2,1,0:T(8,128)(2,1)S(1)}, u32[]{:S(2)}, u32[]{:S(2)}) async-start(bf16[8,72,128]{2,1,0:T(8,128)(2,1)} %broadcast_in_dim.4), calls=%async_computation.1 | async-start | bytes 294912 | tf_op jit(solution)/shard_map/all_to_all | solution.py:378
  83.6 0.8 add.20
  84.3 6.1 %all-to-all-done.1 = bf16[8,72,128]{2,1,0:T(8,128)(2,1)S(1)} async-done(((bf16[8,72,128]{2,1,0:T(8,128)(2,1)}), bf16[8,72,128]{2,1,0:T(8,128)(2,1)S(1)}, u32[]{:S(2)}, u32[]{:S(2)}) %all-to-all-start.1) | async-done | bytes 147488 | tf_op jit(solution)/shard_map/all_to_all | solution.py:378
  90.4 0.9 broadcast_in_dim.5
  91.3 8.8 %all-to-all-start.2 = ((bf16[32,72,128]{2,1,0:T(8,128)(2,1)}), bf16[32,72,128]{2,1,0:T(8,128)(2,1)S(1)}, u32[]{:S(2)}, u32[]{:S(2)}) async-start(bf16[32,72,128]{2,1,0:T(8,128)(2,1)} %broadcast_in_dim.5), calls=%async_computation.2 | async-start | bytes 1179648 | tf_op jit(solution)/shard_map/all_to_all | solution.py:378
  100.1 4.0 %collective-permute-start.6 = (bf16[2,16,16,128]{3,2,1,0:T(8,128)(2,1)S(1)}, bf16[2,16,16,128]{3,2,1,0:T(8,128)(2,1)S(1)}, u32[]{:S(2)}, u32[]{:S(2)}) collective-permute-start(bf16[2,16,16,128]{3,2,1,0:T(8,128)(2,1)S(1)} %get-tuple-element.72), channel_id=1, source_target_pairs={{0,1},{1,0},{2,3},{3,2},{4,5},{5,4},{6,7},{7,6},{8,9},{9,8},{10,11... | collective-permute-start | bytes 393224 | tf_op jit(solution)/shard_map/ppermute | solution.py:361
  104.1 5.5 %collective-permute-start.7 = (bf16[2,16,16,128]{3,2,1,0:T(8,128)(2,1)S(1)}, bf16[2,16,16,128]{3,2,1,0:T(8,128)(2,1)S(1)}, u32[]{:S(2)}, u32[]{:S(2)}) collective-permute-start(bf16[2,16,16,128]{3,2,1,0:T(8,128)(2,1)S(1)} %get-tuple-element.73), channel_id=1, source_target_pairs={{1,2},{3,4},{5,6},{2,1},{4,3},{6,5},{9,10},{11,12},{13,14},{10,9},... | collective-permute-start | bytes 393224 | tf_op jit(solution)/shard_map/ppermute | solution.py:357
  109.6 0.5 collective-permute-done.6.from_a
  110.0 9.6 %collective-permute-done.7.from_b = bf16[2,16,16,128]{3,2,1,0:T(8,128)(2,1)S(1)} collective-permute-done((bf16[2,16,16,128]{3,2,1,0:T(8,128)(2,1)S(1)}, bf16[2,16,16,128]{3,2,1,0:T(8,128)(2,1)S(1)}, u32[]{:S(2)}, u32[]{:S(2)}) %collective-permute-start.7) | collective-permute-done | bytes 131104 | tf_op jit(solution)/shard_map/ppermute | solution.py:357
  119.7 0.0 all-to-all-done.2
  119.7 4.4 %collective-permute-start.8 = (bf16[2304,128]{1,0:T(8,128)(2,1)S(1)}, bf16[2304,128]{1,0:T(8,128)(2,1)S(1)}, u32[]{:S(2)}, u32[]{:S(2)}) collective-permute-start(bf16[2304,128]{1,0:T(8,128)(2,1)S(1)} %bitcast.11), channel_id=1, source_target_pairs={{0,8},{8,0},{1,9},{9,1},{2,10},{10,2},{3,11},{11,3},{4,12},{12,4},... | collective-permute-start | bytes 1769480 | tf_op jit(solution)/shard_map/ppermute | solution.py:361
  124.1 0.7 finish.1
  124.8 0.9 collective-permute-done.8.other
  125.7 2.1 %unpack.1 = (f32[9,128,128]{2,1,0:T(8,128)}, f32[3,384,256]{2,1,0:T(8,128)}, f32[4,256,128]{2,1,0:T(8,128)}) custom-call(s32[8]{0:T(128)S(1)} %get-tuple-element.50.places, bf16[2304,128]{1,0:T(8,128)(2,1)S(1)} %bitcast.12, bf16[2304,128]{1,0:T(8,128)(2,1)S(1)} %collective-permute-done.8.other), custom_call_target="tpu_custom_call" | custom-call | flops 1000000 | bytes 2000000 | tf_op jit(solution)/shard_map/unpack/pallas_call | solution.py:342
  (1 shorter events, 0.0 us)
Async XLA Ops:
  1.5 18.9 %collective-permute-start.1 = (bf16[2,16,16,128]{3,2,1,0:T(8,128)(2,1)S(1)}, bf16[2,16,16,128]{3,2,1,0:T(8,128)(2,1)S(1)}, u32[]{:S(2)}, u32[]{:S(2)}) collective-permute-start(bf16[2,16,16,128]{3,2,1,0:T(8,128)(2,1)S(1)} %pad_maximum_fusion.both), channel_id=1, source_target_pairs={{1,2},{3,4},{5,6},{2,1},{4,3},{6,5},{9,10},{11,12},{13,14},{10,9},... | collective-permute-start | bytes 393224 | tf_op jit(solution)/shard_map/ppermute | solution.py:357
  12.4 9.7 %collective-permute-start = (bf16[2,16,16,128]{3,2,1,0:T(8,128)(2,1)S(1)}, bf16[2,16,16,128]{3,2,1,0:T(8,128)(2,1)S(1)}, u32[]{:S(2)}, u32[]{:S(2)}) collective-permute-start(bf16[2,16,16,128]{3,2,1,0:T(8,128)(2,1)S(1)} %pad_maximum_fusion.both), channel_id=1, source_target_pairs={{0,1},{1,0},{2,3},{3,2},{4,5},{5,4},{6,7},{7,6},{8,9},{9,8},{10,11... | collective-permute-start | bytes 393224 | tf_op jit(solution)/shard_map/ppermute | solution.py:361
  14.4 1.1 copy-start
  15.5 1.0 copy-start.2
  16.5 0.9 copy-start.3
  17.4 0.7 copy-start.4
  18.1 0.7 copy-start.5
  18.8 19.8 %copy-start.1 = (bf16[3,3,128,256]{3,2,1,0:T(8,128)(2,1)S(1)}, bf16[3,3,128,256]{3,2,1,0:T(8,128)(2,1)}, u32[]{:S(2)}) copy-start(bf16[3,3,128,256]{3,2,1,0:T(8,128)(2,1)} %w_down.1) | copy-start | bytes 1769476
  22.8 9.7 %collective-permute-start.2 = (bf16[2,32,16,128]{3,2,1,0:T(8,128)(2,1)S(1)}, bf16[2,32,16,128]{3,2,1,0:T(8,128)(2,1)S(1)}, u32[]{:S(2)}, u32[]{:S(2)}) collective-permute-start(bf16[2,32,16,128]{3,2,1,0:T(8,128)(2,1)S(1)} %get-tuple-element.53), channel_id=1, source_target_pairs={{0,8},{8,0},{1,9},{9,1},{2,10},{10,2},{3,11},{11,3},{4,12},{12,4},... | collective-permute-start | bytes 786440 | tf_op jit(solution)/shard_map/ppermute | solution.py:361
  26.8 11.8 %collective-permute-start.3 = (bf16[2,32,16,128]{3,2,1,0:T(8,128)(2,1)S(1)}, bf16[2,32,16,128]{3,2,1,0:T(8,128)(2,1)S(1)}, u32[]{:S(2)}, u32[]{:S(2)}) collective-permute-start(bf16[2,32,16,128]{3,2,1,0:T(8,128)(2,1)S(1)} %get-tuple-element.55), channel_id=1, source_target_pairs={{8,16},{24,32},{40,48},{56,64},{72,80},{88,96},{104,112},{120,128}... | collective-permute-start | bytes 786440 | tf_op jit(solution)/shard_map/ppermute | solution.py:357
  43.3 4.3 %collective-permute-start.4 = (bf16[3328,128]{1,0:T(8,128)(2,1)S(1)}, bf16[3328,128]{1,0:T(8,128)(2,1)S(1)}, u32[]{:S(2)}, u32[]{:S(2)}) collective-permute-start(bf16[3328,128]{1,0:T(8,128)(2,1)S(1)} %get-tuple-element.62), channel_id=1, source_target_pairs={{0,8},{8,0},{1,9},{9,1},{2,10},{10,2},{3,11},{11,3},{4,12},{12,4},... | collective-permute-start | bytes 2555912 | tf_op jit(solution)/shard_map/ppermute | solution.py:361
  48.5 26.5 %all-to-all-start = ((bf16[32,72,128]{2,1,0:T(8,128)(2,1)}), bf16[32,72,128]{2,1,0:T(8,128)(2,1)S(1)}, u32[]{:S(2)}, u32[]{:S(2)}) async-start(bf16[32,72,128]{2,1,0:T(8,128)(2,1)} %bitcast.6), calls=%async_computation | async-start | bytes 1179648 | tf_op jit(solution)/shard_map/all_to_all | solution.py:371
  60.2 14.9 %collective-permute-start.5 = (bf16[2,32,16,128]{3,2,1,0:T(8,128)(2,1)S(1)}, bf16[2,32,16,128]{3,2,1,0:T(8,128)(2,1)S(1)}, u32[]{:S(2)}, u32[]{:S(2)}) collective-permute-start(bf16[2,32,16,128]{3,2,1,0:T(8,128)(2,1)S(1)} %get-tuple-element.63), channel_id=1, source_target_pairs={{8,16},{24,32},{40,48},{56,64},{72,80},{88,96},{104,112},{120,128}... | collective-permute-start | bytes 786440 | tf_op jit(solution)/shard_map/ppermute | solution.py:357
  75.8 14.6 %all-to-all-start.1 = ((bf16[8,72,128]{2,1,0:T(8,128)(2,1)}), bf16[8,72,128]{2,1,0:T(8,128)(2,1)S(1)}, u32[]{:S(2)}, u32[]{:S(2)}) async-start(bf16[8,72,128]{2,1,0:T(8,128)(2,1)} %broadcast_in_dim.4), calls=%async_computation.1 | async-start | bytes 294912 | tf_op jit(solution)/shard_map/all_to_all | solution.py:378
  91.3 28.3 %all-to-all-start.2 = ((bf16[32,72,128]{2,1,0:T(8,128)(2,1)}), bf16[32,72,128]{2,1,0:T(8,128)(2,1)S(1)}, u32[]{:S(2)}, u32[]{:S(2)}) async-start(bf16[32,72,128]{2,1,0:T(8,128)(2,1)} %broadcast_in_dim.5), calls=%async_computation.2 | async-start | bytes 1179648 | tf_op jit(solution)/shard_map/all_to_all | solution.py:378
  100.1 9.9 %collective-permute-start.6 = (bf16[2,16,16,128]{3,2,1,0:T(8,128)(2,1)S(1)}, bf16[2,16,16,128]{3,2,1,0:T(8,128)(2,1)S(1)}, u32[]{:S(2)}, u32[]{:S(2)}) collective-permute-start(bf16[2,16,16,128]{3,2,1,0:T(8,128)(2,1)S(1)} %get-tuple-element.72), channel_id=1, source_target_pairs={{0,1},{1,0},{2,3},{3,2},{4,5},{5,4},{6,7},{7,6},{8,9},{9,8},{10,11... | collective-permute-start | bytes 393224 | tf_op jit(solution)/shard_map/ppermute | solution.py:361
  104.1 15.6 %collective-permute-start.7 = (bf16[2,16,16,128]{3,2,1,0:T(8,128)(2,1)S(1)}, bf16[2,16,16,128]{3,2,1,0:T(8,128)(2,1)S(1)}, u32[]{:S(2)}, u32[]{:S(2)}) collective-permute-start(bf16[2,16,16,128]{3,2,1,0:T(8,128)(2,1)S(1)} %get-tuple-element.73), channel_id=1, source_target_pairs={{1,2},{3,4},{5,6},{2,1},{4,3},{6,5},{9,10},{11,12},{13,14},{10,9},... | collective-permute-start | bytes 393224 | tf_op jit(solution)/shard_map/ppermute | solution.py:357
  119.7 6.0 %collective-permute-start.8 = (bf16[2304,128]{1,0:T(8,128)(2,1)S(1)}, bf16[2304,128]{1,0:T(8,128)(2,1)S(1)}, u32[]{:S(2)}, u32[]{:S(2)}) collective-permute-start(bf16[2304,128]{1,0:T(8,128)(2,1)S(1)} %bitcast.11), channel_id=1, source_target_pairs={{0,8},{8,0},{1,9},{9,1},{2,10},{10,2},{3,11},{11,3},{4,12},{12,4},... | collective-permute-start | bytes 1769480 | tf_op jit(solution)/shard_map/ppermute | solution.py:361

commit v9 on v8

--- a/solution.py
+++ b/solution.py
@@ -153,7 +153,7 @@
 
 
 def net_kernel(
-    places, side_a, middle, side_b, fb, rf, rft, wd, rdt, ru,
+    places, side_b, middle, side_a, fb, rf, rft, wd, rdt, ru,
     mid_o, strip_b, keep, send,
     fs, cs, xv, hv, gv, g4, gs, bs, can_b, can_g, halves,
 ):
@@ -335,7 +335,7 @@
         compiler_params=pltpu.CompilerParams(vmem_limit_bytes=24 * 2**20),
         cost_estimate=pl.CostEstimate(flops=2 * 10**9, bytes_accessed=10**7, transcendentals=200000),
         name="patch_work",
-    )(places, side_a, middle, side_b, fb, rf, rft, wd, rdt, ru)
+    )(places, side_b, middle, side_a, fb, rf, rft, wd, rdt, ru)
 
 
 def small_call(body, name, outs, scratch, *args, smem=0):
@@ -426,8 +426,9 @@
         from_b,
         smem=1,
     )
-    part, own, to_a, to_b = lax.optimization_barrier((part, own, to_a, to_b))
-    row_a, row_b = swapped_a(to_a, "zh"), swapped_b(to_b, ROW)
+    row_a = swapped_a(to_a, "zh")
+    part, own, row_a, to_b = lax.optimization_barrier((part, own, row_a, to_b))
+    row_b = swapped_b(to_b, ROW)
     part = gathered(part, ("x", "y")).reshape(-1, C1)
     part, own, row_a, row_b = lax.optimization_barrier((part, own, row_a, row_b))
     other = swapped_a(part, "core")

time: 129 us -> 132 us (1.023)
  the two profiles are of different devices: /device:TPU:7 before, /device:TPU:1 now
where the time goes in v9:
time: 132 us; the launch traced here: 131 us
  starting transfers between devices  72.8 us (55%)
  waiting for transfers between devices  38.7 us (29%)
  Pallas kernels  10.4 us (8%)
  local copies, waits for them, and re-layouts  5.96 us (5%)
  other arithmetic  2.05 us (2%)
    ppermute x5, starting transfers between devices, swapped_a(): return lax.ppermute(x, axis, [(0, 1), (1, 0)])  30.6 us
    all_to_all x2, starting transfers between devices, gathered(): return lax.all_to_all(parts, axes, 0, 0, tiled=True)  16.4 us
    all_to_all x1, starting transfers between devices, scattered(): got = lax.all_to_all(parts, axes, 0, 0, tiled=True)  14.8 us
    all_to_all x2, waiting for transfers between devices, gathered(): return lax.all_to_all(parts, axes, 0, 0, tiled=True)  14.4 us
    all_to_all x1, waiting for transfers between devices, scattered(): got = lax.all_to_all(parts, axes, 0, 0, tiled=True)  13.6 us
    ppermute x4, starting transfers between devices, swapped_b(): return lax.ppermute(x, axes, pairs + [(j, i) for i, j in pairs])  11.1 us
    ppermute x5, waiting for transfers between devices, swapped_a(): return lax.ppermute(x, axis, [(0, 1), (1, 0)])  7.7 us
    pallas_call x1, Pallas kernels, patch_work(): pl.pallas_call(net_kernel, out_shape=(jax.ShapeDtypeStruct((2, 32, 16, C1...  4.63 us
  transfers between devices with their start and end apart: 12, of which 6 were waited for; matrix products, arithmetic and copies ran while one was open for 0% of the time, Pallas kernels for 2%

profile of v9, /device:TPU:1, one launch (start us, length us, event | category | flops | bytes accessed | tf_op | source)
XLA Modules:
  0.0 130.8 jit_solution(607923354820783772)
XLA Ops:
  0.6 0.9 pad_maximum_fusion.both
  1.5 0.7 collective-permute-start.1
  2.2 12.7 %collective-permute-start = (bf16[2,16,16,128]{3,2,1,0:T(8,128)(2,1)S(1)}, bf16[2,16,16,128]{3,2,1,0:T(8,128)(2,1)S(1)}, u32[]{:S(2)}, u32[]{:S(2)}) collective-permute-start(bf16[2,16,16,128]{3,2,1,0:T(8,128)(2,1)S(1)} %pad_maximum_fusion.both), channel_id=1, source_target_pairs={{0,1},{1,0},{2,3},{3,2},{4,5},{5,4},{6,7},{7,6},{8,9},{9,8},{10,11... | collective-permute-start | bytes 393224 | tf_op jit(solution)/shard_map/ppermute | solution.py:361
  14.9 0.1 pad_add_fusion.where
  15.0 0.0 copy-start
  15.0 1.1 copy-done
  16.1 0.0 copy-start.2
  16.1 1.0 copy-done.2
  17.0 0.0 copy-start.3
  17.0 0.9 copy-done.3
  18.0 0.0 copy-start.4
  18.0 0.7 copy-done.4
  18.7 0.0 copy-start.5
  18.7 0.7 copy-done.5
  19.4 0.0 copy-start.1
  19.4 1.6 %prepare.1 = (s32[8]{0:T(128)S(1)}, f32[2,16,16,256]{3,2,1,0:T(8,128)S(1)}, bf16[3,512,256]{2,1,0:T(8,128)(2,1)S(1)}, bf16[3,256,512]{2,1,0:T(8,128)(2,1)S(1)}, ...) custom-call(s32[2]{0:T(128)S(1)} %pad_add_fusion.where, s32[8,2,64]{2,1,0:T(2,128)S(1)} %bitcast.14, ...), custom_call_target="tpu_custom_call" | custom-call | flops 5000000 | bytes 10000000 | tf_op jit(solution)/shard_map/prepare/pallas_call | solution.py:293
  21.0 0.0 collective-permute-done.1.from_b
  21.0 0.0 collective-permute-done.from_a
  21.0 0.6 assemble.1
  21.6 7.8 %collective-permute-start.2 = (bf16[2,32,16,128]{3,2,1,0:T(8,128)(2,1)S(1)}, bf16[2,32,16,128]{3,2,1,0:T(8,128)(2,1)S(1)}, u32[]{:S(2)}, u32[]{:S(2)}) collective-permute-start(bf16[2,32,16,128]{3,2,1,0:T(8,128)(2,1)S(1)} %get-tuple-element.53), channel_id=1, source_target_pairs={{8,16},{24,32},{40,48},{56,64},{72,80},{88,96},{104,112},{120,128}... | collective-permute-start | bytes 786440 | tf_op jit(solution)/shard_map/ppermute | solution.py:357
  29.5 1.9 %collective-permute-start.3 = (bf16[2,32,16,128]{3,2,1,0:T(8,128)(2,1)S(1)}, bf16[2,32,16,128]{3,2,1,0:T(8,128)(2,1)S(1)}, u32[]{:S(2)}, u32[]{:S(2)}) collective-permute-start(bf16[2,32,16,128]{3,2,1,0:T(8,128)(2,1)S(1)} %get-tuple-element.55), channel_id=1, source_target_pairs={{0,8},{8,0},{1,9},{9,1},{2,10},{10,2},{3,11},{11,3},{4,12},{12,4},... | collective-permute-start | bytes 786440 | tf_op jit(solution)/shard_map/ppermute | solution.py:361
  31.4 3.0 %collective-permute-done.2.side_b = bf16[2,32,16,128]{3,2,1,0:T(8,128)(2,1)S(1)} collective-permute-done((bf16[2,32,16,128]{3,2,1,0:T(8,128)(2,1)S(1)}, bf16[2,32,16,128]{3,2,1,0:T(8,128)(2,1)S(1)}, u32[]{:S(2)}, u32[]{:S(2)}) %collective-permute-start.2) | collective-permute-done | bytes 262176 | tf_op jit(solution)/shard_map/ppermute | solution.py:357
  34.4 0.0 collective-permute-done.3.side_a
  34.4 0.0 copy-done.1
  34.4 4.6 %patch_work.1 = (f32[2,32,16,128]{3,2,1,0:T(8,128)S(1)}, bf16[2,32,16,128]{3,2,1,0:T(8,128)(2,1)S(1)}, bf16[2304,128]{1,0:T(8,128)(2,1)S(1)}, bf16[3328,128]{1,0:T(8,128)(2,1)S(1)}) custom-call(s32[8]{0:T(128)S(1)} %get-tuple-element.50.places, bf16[2,32,16,128]{3,2,1,0:T(8,128)(2,1)S(1)} %collective-permute-done.2.side_b, ...), custom_call_target="tpu_custom_call" | custom-call | flops 2000000000 | bytes 10000000 | tf_op jit(solution)/shard_map/patch_work/pallas_call | solution.py:312
  39.0 1.9 %collective-permute-start.4 = (bf16[3328,128]{1,0:T(8,128)(2,1)S(1)}, bf16[3328,128]{1,0:T(8,128)(2,1)S(1)}, u32[]{:S(2)}, u32[]{:S(2)}) collective-permute-start(bf16[3328,128]{1,0:T(8,128)(2,1)S(1)} %get-tuple-element.62), channel_id=1, source_target_pairs={{0,8},{8,0},{1,9},{9,1},{2,10},{10,2},{3,11},{11,3},{4,12},{12,4},... | collective-permute-start | bytes 2555912 | tf_op jit(solution)/shard_map/ppermute | solution.py:361
  41.0 2.3 %collective-permute-done.4.from_a = bf16[3328,128]{1,0:T(8,128)(2,1)S(1)} collective-permute-done((bf16[3328,128]{1,0:T(8,128)(2,1)S(1)}, bf16[3328,128]{1,0:T(8,128)(2,1)S(1)}, u32[]{:S(2)}, u32[]{:S(2)}) %collective-permute-start.4) | collective-permute-done | bytes 852000 | tf_op jit(solution)/shard_map/ppermute | solution.py:361
  43.3 1.0 add_convert_fusion
  44.3 14.8 %all-to-all-start = ((bf16[32,72,128]{2,1,0:T(8,128)(2,1)}), bf16[32,72,128]{2,1,0:T(8,128)(2,1)S(1)}, u32[]{:S(2)}, u32[]{:S(2)}) async-start(bf16[32,72,128]{2,1,0:T(8,128)(2,1)} %bitcast.6), calls=%async_computation | async-start | bytes 1179648 | tf_op jit(solution)/shard_map/all_to_all | solution.py:371
  59.1 1.9 %collective-permute-start.5 = (bf16[2,32,16,128]{3,2,1,0:T(8,128)(2,1)S(1)}, bf16[2,32,16,128]{3,2,1,0:T(8,128)(2,1)S(1)}, u32[]{:S(2)}, u32[]{:S(2)}) collective-permute-start(bf16[2,32,16,128]{3,2,1,0:T(8,128)(2,1)S(1)} %get-tuple-element.63), channel_id=1, source_target_pairs={{8,16},{24,32},{40,48},{56,64},{72,80},{88,96},{104,112},{120,128}... | collective-permute-start | bytes 786440 | tf_op jit(solution)/shard_map/ppermute | solution.py:357
  61.0 13.6 %all-to-all-done = bf16[32,72,128]{2,1,0:T(8,128)(2,1)S(1)} async-done(((bf16[32,72,128]{2,1,0:T(8,128)(2,1)}), bf16[32,72,128]{2,1,0:T(8,128)(2,1)S(1)}, u32[]{:S(2)}, u32[]{:S(2)}) %all-to-all-start) | async-done | bytes 589856 | tf_op jit(solution)/shard_map/all_to_all | solution.py:371
  74.6 0.1 reduce_sum.24
  74.7 0.0 collective-permute-done.5.from_b
  74.7 0.7 broadcast_in_dim.4
  75.4 7.4 %all-to-all-start.1 = ((bf16[8,72,128]{2,1,0:T(8,128)(2,1)}), bf16[8,72,128]{2,1,0:T(8,128)(2,1)S(1)}, u32[]{:S(2)}, u32[]{:S(2)}) async-start(bf16[8,72,128]{2,1,0:T(8,128)(2,1)} %broadcast_in_dim.4), calls=%async_computation.1 | async-start | bytes 294912 | tf_op jit(solution)/shard_map/all_to_all | solution.py:378
  82.8 0.8 add.20
  83.6 7.3 %collective-permute-start.6 = (bf16[2,16,16,128]{3,2,1,0:T(8,128)(2,1)S(1)}, bf16[2,16,16,128]{3,2,1,0:T(8,128)(2,1)S(1)}, u32[]{:S(2)}, u32[]{:S(2)}) collective-permute-start(bf16[2,16,16,128]{3,2,1,0:T(8,128)(2,1)S(1)} %get-tuple-element.68), channel_id=1, source_target_pairs={{0,1},{1,0},{2,3},{3,2},{4,5},{5,4},{6,7},{7,6},{8,9},{9,8},{10,11... | collective-permute-start | bytes 393224 | tf_op jit(solution)/shard_map/ppermute | solution.py:361
  90.8 0.0 all-to-all-done.1
  90.9 4.4 %collective-permute-done.6.from_a = bf16[2,16,16,128]{3,2,1,0:T(8,128)(2,1)S(1)} collective-permute-done((bf16[2,16,16,128]{3,2,1,0:T(8,128)(2,1)S(1)}, bf16[2,16,16,128]{3,2,1,0:T(8,128)(2,1)S(1)}, u32[]{:S(2)}, u32[]{:S(2)}) %collective-permute-start.6) | collective-permute-done | bytes 131104 | tf_op jit(solution)/shard_map/ppermute | solution.py:361
  95.3 0.9 broadcast_in_dim.5
  96.2 9.0 %all-to-all-start.2 = ((bf16[32,72,128]{2,1,0:T(8,128)(2,1)}), bf16[32,72,128]{2,1,0:T(8,128)(2,1)S(1)}, u32[]{:S(2)}, u32[]{:S(2)}) async-start(bf16[32,72,128]{2,1,0:T(8,128)(2,1)} %broadcast_in_dim.5), calls=%async_computation.2 | async-start | bytes 1179648 | tf_op jit(solution)/shard_map/all_to_all | solution.py:378
  105.2 0.7 collective-permute-start.7
  105.9 0.0 collective-permute-done.7.from_b
  105.9 14.4 %all-to-all-done.2 = bf16[32,72,128]{2,1,0:T(8,128)(2,1)S(1)} async-done(((bf16[32,72,128]{2,1,0:T(8,128)(2,1)}), bf16[32,72,128]{2,1,0:T(8,128)(2,1)S(1)}, u32[]{:S(2)}, u32[]{:S(2)}) %all-to-all-start.2) | async-done | bytes 589856 | tf_op jit(solution)/shard_map/all_to_all | solution.py:378
  120.3 6.8 %collective-permute-start.8 = (bf16[2304,128]{1,0:T(8,128)(2,1)S(1)}, bf16[2304,128]{1,0:T(8,128)(2,1)S(1)}, u32[]{:S(2)}, u32[]{:S(2)}) collective-permute-start(bf16[2304,128]{1,0:T(8,128)(2,1)S(1)} %bitcast.11), channel_id=1, source_target_pairs={{0,8},{8,0},{1,9},{9,1},{2,10},{10,2},{3,11},{11,3},{4,12},{12,4},... | collective-permute-start | bytes 1769480 | tf_op jit(solution)/shard_map/ppermute | solution.py:361
  127.1 0.7 finish.1
  127.8 0.9 collective-permute-done.8.other
  128.7 2.1 %unpack.1 = (f32[9,128,128]{2,1,0:T(8,128)}, f32[3,384,256]{2,1,0:T(8,128)}, f32[4,256,128]{2,1,0:T(8,128)}) custom-call(s32[8]{0:T(128)S(1)} %get-tuple-element.50.places, bf16[2304,128]{1,0:T(8,128)(2,1)S(1)} %bitcast.12, bf16[2304,128]{1,0:T(8,128)(2,1)S(1)} %collective-permute-done.8.other), custom_call_target="tpu_custom_call" | custom-call | flops 1000000 | bytes 2000000 | tf_op jit(solution)/shard_map/unpack/pallas_call | solution.py:342
  (1 shorter events, 0.0 us)
Async XLA Ops:
  1.5 19.5 %collective-permute-start.1 = (bf16[2,16,16,128]{3,2,1,0:T(8,128)(2,1)S(1)}, bf16[2,16,16,128]{3,2,1,0:T(8,128)(2,1)S(1)}, u32[]{:S(2)}, u32[]{:S(2)}) collective-permute-start(bf16[2,16,16,128]{3,2,1,0:T(8,128)(2,1)S(1)} %pad_maximum_fusion.both), channel_id=1, source_target_pairs={{1,2},{3,4},{5,6},{2,1},{4,3},{6,5},{9,10},{11,12},{13,14},{10,9},... | collective-permute-start | bytes 393224 | tf_op jit(solution)/shard_map/ppermute | solution.py:357
  2.2 18.8 %collective-permute-start = (bf16[2,16,16,128]{3,2,1,0:T(8,128)(2,1)S(1)}, bf16[2,16,16,128]{3,2,1,0:T(8,128)(2,1)S(1)}, u32[]{:S(2)}, u32[]{:S(2)}) collective-permute-start(bf16[2,16,16,128]{3,2,1,0:T(8,128)(2,1)S(1)} %pad_maximum_fusion.both), channel_id=1, source_target_pairs={{0,1},{1,0},{2,3},{3,2},{4,5},{5,4},{6,7},{7,6},{8,9},{9,8},{10,11... | collective-permute-start | bytes 393224 | tf_op jit(solution)/shard_map/ppermute | solution.py:361
  15.0 1.1 copy-start
  16.1 1.0 copy-start.2
  17.0 0.9 copy-start.3
  18.0 0.7 copy-start.4
  18.7 0.7 copy-start.5
  19.4 15.0 %copy-start.1 = (bf16[3,3,128,256]{3,2,1,0:T(8,128)(2,1)S(1)}, bf16[3,3,128,256]{3,2,1,0:T(8,128)(2,1)}, u32[]{:S(2)}) copy-start(bf16[3,3,128,256]{3,2,1,0:T(8,128)(2,1)} %w_down.1) | copy-start | bytes 1769476
  21.6 12.8 %collective-permute-start.2 = (bf16[2,32,16,128]{3,2,1,0:T(8,128)(2,1)S(1)}, bf16[2,32,16,128]{3,2,1,0:T(8,128)(2,1)S(1)}, u32[]{:S(2)}, u32[]{:S(2)}) collective-permute-start(bf16[2,32,16,128]{3,2,1,0:T(8,128)(2,1)S(1)} %get-tuple-element.53), channel_id=1, source_target_pairs={{8,16},{24,32},{40,48},{56,64},{72,80},{88,96},{104,112},{120,128}... | collective-permute-start | bytes 786440 | tf_op jit(solution)/shard_map/ppermute | solution.py:357
  29.5 4.9 %collective-permute-start.3 = (bf16[2,32,16,128]{3,2,1,0:T(8,128)(2,1)S(1)}, bf16[2,32,16,128]{3,2,1,0:T(8,128)(2,1)S(1)}, u32[]{:S(2)}, u32[]{:S(2)}) collective-permute-start(bf16[2,32,16,128]{3,2,1,0:T(8,128)(2,1)S(1)} %get-tuple-element.55), channel_id=1, source_target_pairs={{0,8},{8,0},{1,9},{9,1},{2,10},{10,2},{3,11},{11,3},{4,12},{12,4},... | collective-permute-start | bytes 786440 | tf_op jit(solution)/shard_map/ppermute | solution.py:361
  39.0 4.3 %collective-permute-start.4 = (bf16[3328,128]{1,0:T(8,128)(2,1)S(1)}, bf16[3328,128]{1,0:T(8,128)(2,1)S(1)}, u32[]{:S(2)}, u32[]{:S(2)}) collective-permute-start(bf16[3328,128]{1,0:T(8,128)(2,1)S(1)} %get-tuple-element.62), channel_id=1, source_target_pairs={{0,8},{8,0},{1,9},{9,1},{2,10},{10,2},{3,11},{11,3},{4,12},{12,4},... | collective-permute-start | bytes 2555912 | tf_op jit(solution)/shard_map/ppermute | solution.py:361
  44.3 30.3 %all-to-all-start = ((bf16[32,72,128]{2,1,0:T(8,128)(2,1)}), bf16[32,72,128]{2,1,0:T(8,128)(2,1)S(1)}, u32[]{:S(2)}, u32[]{:S(2)}) async-start(bf16[32,72,128]{2,1,0:T(8,128)(2,1)} %bitcast.6), calls=%async_computation | async-start | bytes 1179648 | tf_op jit(solution)/shard_map/all_to_all | solution.py:371
  59.1 15.6 %collective-permute-start.5 = (bf16[2,32,16,128]{3,2,1,0:T(8,128)(2,1)S(1)}, bf16[2,32,16,128]{3,2,1,0:T(8,128)(2,1)S(1)}, u32[]{:S(2)}, u32[]{:S(2)}) collective-permute-start(bf16[2,32,16,128]{3,2,1,0:T(8,128)(2,1)S(1)} %get-tuple-element.63), channel_id=1, source_target_pairs={{8,16},{24,32},{40,48},{56,64},{72,80},{88,96},{104,112},{120,128}... | collective-permute-start | bytes 786440 | tf_op jit(solution)/shard_map/ppermute | solution.py:357
  75.4 15.5 %all-to-all-start.1 = ((bf16[8,72,128]{2,1,0:T(8,128)(2,1)}), bf16[8,72,128]{2,1,0:T(8,128)(2,1)S(1)}, u32[]{:S(2)}, u32[]{:S(2)}) async-start(bf16[8,72,128]{2,1,0:T(8,128)(2,1)} %broadcast_in_dim.4), calls=%async_computation.1 | async-start | bytes 294912 | tf_op jit(solution)/shard_map/all_to_all | solution.py:378
  83.6 11.8 %collective-permute-start.6 = (bf16[2,16,16,128]{3,2,1,0:T(8,128)(2,1)S(1)}, bf16[2,16,16,128]{3,2,1,0:T(8,128)(2,1)S(1)}, u32[]{:S(2)}, u32[]{:S(2)}) collective-permute-start(bf16[2,16,16,128]{3,2,1,0:T(8,128)(2,1)S(1)} %get-tuple-element.68), channel_id=1, source_target_pairs={{0,1},{1,0},{2,3},{3,2},{4,5},{5,4},{6,7},{7,6},{8,9},{9,8},{10,11... | collective-permute-start | bytes 393224 | tf_op jit(solution)/shard_map/ppermute | solution.py:361
  96.2 24.1 %all-to-all-start.2 = ((bf16[32,72,128]{2,1,0:T(8,128)(2,1)}), bf16[32,72,128]{2,1,0:T(8,128)(2,1)S(1)}, u32[]{:S(2)}, u32[]{:S(2)}) async-start(bf16[32,72,128]{2,1,0:T(8,128)(2,1)} %broadcast_in_dim.5), calls=%async_computation.2 | async-start | bytes 1179648 | tf_op jit(solution)/shard_map/all_to_all | solution.py:378
  105.2 0.7 collective-permute-start.7
  120.3 8.4 %collective-permute-start.8 = (bf16[2304,128]{1,0:T(8,128)(2,1)S(1)}, bf16[2304,128]{1,0:T(8,128)(2,1)S(1)}, u32[]{:S(2)}, u32[]{:S(2)}) collective-permute-start(bf16[2304,128]{1,0:T(8,128)(2,1)S(1)} %bitcast.11), channel_id=1, source_target_pairs={{0,8},{8,0},{1,9},{9,1},{2,10},{10,2},{3,11},{11,3},{4,12},{12,4},... | collective-permute-start | bytes 1769480 | tf_op jit(solution)/shard_map/ppermute | solution.py:361

commit v10 on v8

--- a/solution.py
+++ b/solution.py
@@ -117,22 +117,23 @@
     field_grad[...] = total[1]
 
 
-def unpack_kernel(scale, places, own, other, g_first, g_down, g_up, halves):
-    halves[places[6]] = own[...]
-    halves[1 - places[6]] = other[...]
-
-    def rows(base, count):
-        half, at = base // HALF_ROWS, base % HALF_ROWS
-        return halves[half, at : at + count].astype(F32) * scale
-
-    for t in range(9):
-        g_first[t] = rows(t * C1, C1)
-    for t in range(3):
-        base = FIRST_ROWS + 6 * t * C1
-        g_down[t, :, :C1] = rows(base, 3 * C1)
-        g_down[t, :, C1:] = rows(base + 3 * C1, 3 * C1)
-    for t in range(4):
-        g_up[t] = rows(FIRST_ROWS + DOWN_ROWS + t * C2, C2)
+def unpack_kernel(scale, places, own, other, g_first, g_down, g_up):
+    def write(parts):
+        def rows(base, count):
+            at = base % HALF_ROWS
+            return parts[base // HALF_ROWS][at : at + count].astype(F32) * scale
+
+        for t in range(9):
+            g_first[t] = rows(t * C1, C1)
+        for t in range(3):
+            base = FIRST_ROWS + 6 * t * C1
+            g_down[t, :, :C1] = rows(base, 3 * C1)
+            g_down[t, :, C1:] = rows(base + 3 * C1, 3 * C1)
+        for t in range(4):
+            g_up[t] = rows(FIRST_ROWS + DOWN_ROWS + t * C2, C2)
+
+    pl.when(places[6] == 0)(lambda: write((own, other)))
+    pl.when(places[6] == 1)(lambda: write((other, own)))
 
 
 def shifted(x, by):
@@ -153,7 +154,7 @@
 
 
 def net_kernel(
-    places, side_a, middle, side_b, fb, rf, rft, wd, rdt, ru,
+    places, side_b, middle, side_a, fb, rf, rft, wd, rdt, ru,
     mid_o, strip_b, keep, send,
     fs, cs, xv, hv, gv, g4, gs, bs, can_b, can_g, halves,
 ):
@@ -335,7 +336,7 @@
         compiler_params=pltpu.CompilerParams(vmem_limit_bytes=24 * 2**20),
         cost_estimate=pl.CostEstimate(flops=2 * 10**9, bytes_accessed=10**7, transcendentals=200000),
         name="patch_work",
-    )(places, side_a, middle, side_b, fb, rf, rft, wd, rdt, ru)
+    )(places, side_b, middle, side_a, fb, rf, rft, wd, rdt, ru)
 
 
 def small_call(body, name, outs, scratch, *args, smem=0):
@@ -429,7 +430,7 @@
     part, own, to_a, to_b = lax.optimization_barrier((part, own, to_a, to_b))
     row_a, row_b = swapped_a(to_a, "zh"), swapped_b(to_b, ROW)
     part = gathered(part, ("x", "y")).reshape(-1, C1)
-    part, own, row_a, row_b = lax.optimization_barrier((part, own, row_a, row_b))
+    part, row_b, own, row_a = lax.optimization_barrier((part, row_b, own, row_a))
     other = swapped_a(part, "core")
     blended, field_grad = small_call(
         finish_kernel,
@@ -445,7 +446,7 @@
         functools.partial(unpack_kernel, scale),
         "unpack",
         [((9, C1, C1), F32), ((3, 3 * C1, C2), F32), ((4, C2, C1), F32)],
-        [pltpu.VMEM((2, HALF_ROWS, C1), BF16)],
+        [],
         places,
         part,
         other,

time: 129 us -> 127 us (0.984)
  the two profiles are of different devices: /device:TPU:7 before, /device:TPU:1 now
where the time goes in v10:
time: 127 us; the launch traced here: 125 us
  starting transfers between devices  75.9 us (60%)
  waiting for transfers between devices  29.9 us (24%)
  Pallas kernels  10.4 us (8%)
  local copies, waits for them, and re-layouts  5.96 us (5%)
  other arithmetic  2.05 us (2%)
    ppermute x5, starting transfers between devices, swapped_a(): return lax.ppermute(x, axis, [(0, 1), (1, 0)])  34.4 us
    all_to_all x2, starting transfers between devices, gathered(): return lax.all_to_all(parts, axes, 0, 0, tiled=True)  15.6 us
    all_to_all x1, starting transfers between devices, scattered(): got = lax.all_to_all(parts, axes, 0, 0, tiled=True)  14.8 us
    all_to_all x1, waiting for transfers between devices, scattered(): got = lax.all_to_all(parts, axes, 0, 0, tiled=True)  13.6 us
    ppermute x4, starting transfers between devices, swapped_b(): return lax.ppermute(x, axes, pairs + [(j, i) for i, j in pairs])  11.1 us
    all_to_all x2, waiting for transfers between devices, gathered(): return lax.all_to_all(parts, axes, 0, 0, tiled=True)  7.19 us
    ppermute x5, waiting for transfers between devices, swapped_a(): return lax.ppermute(x, axis, [(0, 1), (1, 0)])  6.11 us
    pallas_call x1, Pallas kernels, patch_work(): pl.pallas_call(net_kernel, out_shape=(jax.ShapeDtypeStruct((2, 32, 16, C1...  4.63 us
  transfers between devices with their start and end apart: 12, of which 7 were waited for; matrix products, arithmetic and copies ran while one was open for 0% of the time, Pallas kernels for 2%

profile of v10, /device:TPU:1, one launch (start us, length us, event | category | flops | bytes accessed | tf_op | source)
XLA Modules:
  0.0 125.0 jit_solution(11328273962977324006)
XLA Ops:
  0.6 0.9 pad_maximum_fusion.both
  1.5 0.7 collective-permute-start.1
  2.2 12.7 %collective-permute-start = (bf16[2,16,16,128]{3,2,1,0:T(8,128)(2,1)S(1)}, bf16[2,16,16,128]{3,2,1,0:T(8,128)(2,1)S(1)}, u32[]{:S(2)}, u32[]{:S(2)}) collective-permute-start(bf16[2,16,16,128]{3,2,1,0:T(8,128)(2,1)S(1)} %pad_maximum_fusion.both), channel_id=1, source_target_pairs={{0,1},{1,0},{2,3},{3,2},{4,5},{5,4},{6,7},{7,6},{8,9},{9,8},{10,11... | collective-permute-start | bytes 393224 | tf_op jit(solution)/shard_map/ppermute | solution.py:362
  14.9 0.1 pad_add_fusion.where
  15.0 0.0 copy-start
  15.0 1.1 copy-done
  16.1 0.0 copy-start.2
  16.1 1.0 copy-done.2
  17.0 0.0 copy-start.3
  17.0 0.9 copy-done.3
  18.0 0.0 copy-start.4
  18.0 0.7 copy-done.4
  18.7 0.0 copy-start.5
  18.7 0.7 copy-done.5
  19.4 0.0 copy-start.1
  19.4 1.6 %prepare.1 = (s32[8]{0:T(128)S(1)}, f32[2,16,16,256]{3,2,1,0:T(8,128)S(1)}, bf16[3,512,256]{2,1,0:T(8,128)(2,1)S(1)}, bf16[3,256,512]{2,1,0:T(8,128)(2,1)S(1)}, ...) custom-call(s32[2]{0:T(128)S(1)} %pad_add_fusion.where, s32[8,2,64]{2,1,0:T(2,128)S(1)} %bitcast.14, ...), custom_call_target="tpu_custom_call" | custom-call | flops 5000000 | bytes 10000000 | tf_op jit(solution)/shard_map/prepare/pallas_call | solution.py:294
  21.0 0.0 collective-permute-done.1.from_b
  21.0 0.0 collective-permute-done.from_a
  21.0 0.6 assemble.1
  21.6 7.8 %collective-permute-start.2 = (bf16[2,32,16,128]{3,2,1,0:T(8,128)(2,1)S(1)}, bf16[2,32,16,128]{3,2,1,0:T(8,128)(2,1)S(1)}, u32[]{:S(2)}, u32[]{:S(2)}) collective-permute-start(bf16[2,32,16,128]{3,2,1,0:T(8,128)(2,1)S(1)} %get-tuple-element.53), channel_id=1, source_target_pairs={{8,16},{24,32},{40,48},{56,64},{72,80},{88,96},{104,112},{120,128}... | collective-permute-start | bytes 786440 | tf_op jit(solution)/shard_map/ppermute | solution.py:358
  29.5 1.9 %collective-permute-start.3 = (bf16[2,32,16,128]{3,2,1,0:T(8,128)(2,1)S(1)}, bf16[2,32,16,128]{3,2,1,0:T(8,128)(2,1)S(1)}, u32[]{:S(2)}, u32[]{:S(2)}) collective-permute-start(bf16[2,32,16,128]{3,2,1,0:T(8,128)(2,1)S(1)} %get-tuple-element.55), channel_id=1, source_target_pairs={{0,8},{8,0},{1,9},{9,1},{2,10},{10,2},{3,11},{11,3},{4,12},{12,4},... | collective-permute-start | bytes 786440 | tf_op jit(solution)/shard_map/ppermute | solution.py:362
  31.4 3.0 %collective-permute-done.2.side_b = bf16[2,32,16,128]{3,2,1,0:T(8,128)(2,1)S(1)} collective-permute-done((bf16[2,32,16,128]{3,2,1,0:T(8,128)(2,1)S(1)}, bf16[2,32,16,128]{3,2,1,0:T(8,128)(2,1)S(1)}, u32[]{:S(2)}, u32[]{:S(2)}) %collective-permute-start.2) | collective-permute-done | bytes 262176 | tf_op jit(solution)/shard_map/ppermute | solution.py:358
  34.4 0.0 collective-permute-done.3.side_a
  34.4 0.0 copy-done.1
  34.4 4.6 %patch_work.1 = (f32[2,32,16,128]{3,2,1,0:T(8,128)S(1)}, bf16[2,32,16,128]{3,2,1,0:T(8,128)(2,1)S(1)}, bf16[2304,128]{1,0:T(8,128)(2,1)S(1)}, bf16[3328,128]{1,0:T(8,128)(2,1)S(1)}) custom-call(s32[8]{0:T(128)S(1)} %get-tuple-element.50.places, bf16[2,32,16,128]{3,2,1,0:T(8,128)(2,1)S(1)} %collective-permute-done.2.side_b, ...), custom_call_target="tpu_custom_call" | custom-call | flops 2000000000 | bytes 10000000 | tf_op jit(solution)/shard_map/patch_work/pallas_call | solution.py:313
  39.0 1.9 %collective-permute-start.4 = (bf16[3328,128]{1,0:T(8,128)(2,1)S(1)}, bf16[3328,128]{1,0:T(8,128)(2,1)S(1)}, u32[]{:S(2)}, u32[]{:S(2)}) collective-permute-start(bf16[3328,128]{1,0:T(8,128)(2,1)S(1)} %get-tuple-element.62), channel_id=1, source_target_pairs={{0,8},{8,0},{1,9},{9,1},{2,10},{10,2},{3,11},{11,3},{4,12},{12,4},... | collective-permute-start | bytes 2555912 | tf_op jit(solution)/shard_map/ppermute | solution.py:362
  41.0 2.3 %collective-permute-done.4.from_a = bf16[3328,128]{1,0:T(8,128)(2,1)S(1)} collective-permute-done((bf16[3328,128]{1,0:T(8,128)(2,1)S(1)}, bf16[3328,128]{1,0:T(8,128)(2,1)S(1)}, u32[]{:S(2)}, u32[]{:S(2)}) %collective-permute-start.4) | collective-permute-done | bytes 852000 | tf_op jit(solution)/shard_map/ppermute | solution.py:362
  43.3 1.0 add_convert_fusion
  44.3 14.8 %all-to-all-start = ((bf16[32,72,128]{2,1,0:T(8,128)(2,1)}), bf16[32,72,128]{2,1,0:T(8,128)(2,1)S(1)}, u32[]{:S(2)}, u32[]{:S(2)}) async-start(bf16[32,72,128]{2,1,0:T(8,128)(2,1)} %bitcast.6), calls=%async_computation | async-start | bytes 1179648 | tf_op jit(solution)/shard_map/all_to_all | solution.py:372
  59.1 1.9 %collective-permute-start.5 = (bf16[2,32,16,128]{3,2,1,0:T(8,128)(2,1)S(1)}, bf16[2,32,16,128]{3,2,1,0:T(8,128)(2,1)S(1)}, u32[]{:S(2)}, u32[]{:S(2)}) collective-permute-start(bf16[2,32,16,128]{3,2,1,0:T(8,128)(2,1)S(1)} %get-tuple-element.63), channel_id=1, source_target_pairs={{8,16},{24,32},{40,48},{56,64},{72,80},{88,96},{104,112},{120,128}... | collective-permute-start | bytes 786440 | tf_op jit(solution)/shard_map/ppermute | solution.py:358
  61.0 13.6 %all-to-all-done = bf16[32,72,128]{2,1,0:T(8,128)(2,1)S(1)} async-done(((bf16[32,72,128]{2,1,0:T(8,128)(2,1)}), bf16[32,72,128]{2,1,0:T(8,128)(2,1)S(1)}, u32[]{:S(2)}, u32[]{:S(2)}) %all-to-all-start) | async-done | bytes 589856 | tf_op jit(solution)/shard_map/all_to_all | solution.py:372
  74.6 0.1 reduce_sum.24
  74.7 0.0 collective-permute-done.5.from_b
  74.7 0.7 broadcast_in_dim.4
  75.4 7.4 %all-to-all-start.1 = ((bf16[8,72,128]{2,1,0:T(8,128)(2,1)}), bf16[8,72,128]{2,1,0:T(8,128)(2,1)S(1)}, u32[]{:S(2)}, u32[]{:S(2)}) async-start(bf16[8,72,128]{2,1,0:T(8,128)(2,1)} %broadcast_in_dim.4), calls=%async_computation.1 | async-start | bytes 294912 | tf_op jit(solution)/shard_map/all_to_all | solution.py:379
  82.8 0.8 add.20
  83.6 6.0 %all-to-all-done.1 = bf16[8,72,128]{2,1,0:T(8,128)(2,1)S(1)} async-done(((bf16[8,72,128]{2,1,0:T(8,128)(2,1)}), bf16[8,72,128]{2,1,0:T(8,128)(2,1)S(1)}, u32[]{:S(2)}, u32[]{:S(2)}) %all-to-all-start.1) | async-done | bytes 147488 | tf_op jit(solution)/shard_map/all_to_all | solution.py:379
  89.6 0.9 broadcast_in_dim.5
  90.5 8.2 %all-to-all-start.2 = ((bf16[32,72,128]{2,1,0:T(8,128)(2,1)}), bf16[32,72,128]{2,1,0:T(8,128)(2,1)S(1)}, u32[]{:S(2)}, u32[]{:S(2)}) async-start(bf16[32,72,128]{2,1,0:T(8,128)(2,1)} %broadcast_in_dim.5), calls=%async_computation.2 | async-start | bytes 1179648 | tf_op jit(solution)/shard_map/all_to_all | solution.py:379
  98.7 0.7 collective-permute-start.6
  99.4 9.5 %collective-permute-start.7 = (bf16[2,16,16,128]{3,2,1,0:T(8,128)(2,1)S(1)}, bf16[2,16,16,128]{3,2,1,0:T(8,128)(2,1)S(1)}, u32[]{:S(2)}, u32[]{:S(2)}) collective-permute-start(bf16[2,16,16,128]{3,2,1,0:T(8,128)(2,1)S(1)} %get-tuple-element.73), channel_id=1, source_target_pairs={{0,1},{1,0},{2,3},{3,2},{4,5},{5,4},{6,7},{7,6},{8,9},{9,8},{10,11... | collective-permute-start | bytes 393224 | tf_op jit(solution)/shard_map/ppermute | solution.py:362
  108.9 0.0 collective-permute-done.6.from_b
  108.9 2.9 %collective-permute-done.7.from_a = bf16[2,16,16,128]{3,2,1,0:T(8,128)(2,1)S(1)} collective-permute-done((bf16[2,16,16,128]{3,2,1,0:T(8,128)(2,1)S(1)}, bf16[2,16,16,128]{3,2,1,0:T(8,128)(2,1)S(1)}, u32[]{:S(2)}, u32[]{:S(2)}) %collective-permute-start.7) | collective-permute-done | bytes 131104 | tf_op jit(solution)/shard_map/ppermute | solution.py:362
  111.7 1.1 all-to-all-done.2
  112.9 8.4 %collective-permute-start.8 = (bf16[2304,128]{1,0:T(8,128)(2,1)S(1)}, bf16[2304,128]{1,0:T(8,128)(2,1)S(1)}, u32[]{:S(2)}, u32[]{:S(2)}) collective-permute-start(bf16[2304,128]{1,0:T(8,128)(2,1)S(1)} %bitcast.11), channel_id=1, source_target_pairs={{0,8},{8,0},{1,9},{9,1},{2,10},{10,2},{3,11},{11,3},{4,12},{12,4},... | collective-permute-start | bytes 1769480 | tf_op jit(solution)/shard_map/ppermute | solution.py:362
  121.3 0.7 finish.1
  122.0 0.9 collective-permute-done.8.other
  122.9 2.1 %unpack.1 = (f32[9,128,128]{2,1,0:T(8,128)}, f32[3,384,256]{2,1,0:T(8,128)}, f32[4,256,128]{2,1,0:T(8,128)}) custom-call(s32[8]{0:T(128)S(1)} %get-tuple-element.50.places, bf16[2304,128]{1,0:T(8,128)(2,1)S(1)} %bitcast.12, bf16[2304,128]{1,0:T(8,128)(2,1)S(1)} %collective-permute-done.8.other), custom_call_target="tpu_custom_call" | custom-call | flops 1000000 | bytes 2000000 | tf_op jit(solution)/shard_map/unpack/pallas_call | solution.py:343
  (1 shorter events, 0.0 us)
Async XLA Ops:
  1.5 19.5 %collective-permute-start.1 = (bf16[2,16,16,128]{3,2,1,0:T(8,128)(2,1)S(1)}, bf16[2,16,16,128]{3,2,1,0:T(8,128)(2,1)S(1)}, u32[]{:S(2)}, u32[]{:S(2)}) collective-permute-start(bf16[2,16,16,128]{3,2,1,0:T(8,128)(2,1)S(1)} %pad_maximum_fusion.both), channel_id=1, source_target_pairs={{1,2},{3,4},{5,6},{2,1},{4,3},{6,5},{9,10},{11,12},{13,14},{10,9},... | collective-permute-start | bytes 393224 | tf_op jit(solution)/shard_map/ppermute | solution.py:358
  2.2 18.8 %collective-permute-start = (bf16[2,16,16,128]{3,2,1,0:T(8,128)(2,1)S(1)}, bf16[2,16,16,128]{3,2,1,0:T(8,128)(2,1)S(1)}, u32[]{:S(2)}, u32[]{:S(2)}) collective-permute-start(bf16[2,16,16,128]{3,2,1,0:T(8,128)(2,1)S(1)} %pad_maximum_fusion.both), channel_id=1, source_target_pairs={{0,1},{1,0},{2,3},{3,2},{4,5},{5,4},{6,7},{7,6},{8,9},{9,8},{10,11... | collective-permute-start | bytes 393224 | tf_op jit(solution)/shard_map/ppermute | solution.py:362
  15.0 1.1 copy-start
  16.1 1.0 copy-start.2
  17.0 0.9 copy-start.3
  18.0 0.7 copy-start.4
  18.7 0.7 copy-start.5
  19.4 15.0 %copy-start.1 = (bf16[3,3,128,256]{3,2,1,0:T(8,128)(2,1)S(1)}, bf16[3,3,128,256]{3,2,1,0:T(8,128)(2,1)}, u32[]{:S(2)}) copy-start(bf16[3,3,128,256]{3,2,1,0:T(8,128)(2,1)} %w_down.1) | copy-start | bytes 1769476
  21.6 12.8 %collective-permute-start.2 = (bf16[2,32,16,128]{3,2,1,0:T(8,128)(2,1)S(1)}, bf16[2,32,16,128]{3,2,1,0:T(8,128)(2,1)S(1)}, u32[]{:S(2)}, u32[]{:S(2)}) collective-permute-start(bf16[2,32,16,128]{3,2,1,0:T(8,128)(2,1)S(1)} %get-tuple-element.53), channel_id=1, source_target_pairs={{8,16},{24,32},{40,48},{56,64},{72,80},{88,96},{104,112},{120,128}... | collective-permute-start | bytes 786440 | tf_op jit(solution)/shard_map/ppermute | solution.py:358
  29.5 4.9 %collective-permute-start.3 = (bf16[2,32,16,128]{3,2,1,0:T(8,128)(2,1)S(1)}, bf16[2,32,16,128]{3,2,1,0:T(8,128)(2,1)S(1)}, u32[]{:S(2)}, u32[]{:S(2)}) collective-permute-start(bf16[2,32,16,128]{3,2,1,0:T(8,128)(2,1)S(1)} %get-tuple-element.55), channel_id=1, source_target_pairs={{0,8},{8,0},{1,9},{9,1},{2,10},{10,2},{3,11},{11,3},{4,12},{12,4},... | collective-permute-start | bytes 786440 | tf_op jit(solution)/shard_map/ppermute | solution.py:362
  39.0 4.3 %collective-permute-start.4 = (bf16[3328,128]{1,0:T(8,128)(2,1)S(1)}, bf16[3328,128]{1,0:T(8,128)(2,1)S(1)}, u32[]{:S(2)}, u32[]{:S(2)}) collective-permute-start(bf16[3328,128]{1,0:T(8,128)(2,1)S(1)} %get-tuple-element.62), channel_id=1, source_target_pairs={{0,8},{8,0},{1,9},{9,1},{2,10},{10,2},{3,11},{11,3},{4,12},{12,4},... | collective-permute-start | bytes 2555912 | tf_op jit(solution)/shard_map/ppermute | solution.py:362
  44.3 30.3 %all-to-all-start = ((bf16[32,72,128]{2,1,0:T(8,128)(2,1)}), bf16[32,72,128]{2,1,0:T(8,128)(2,1)S(1)}, u32[]{:S(2)}, u32[]{:S(2)}) async-start(bf16[32,72,128]{2,1,0:T(8,128)(2,1)} %bitcast.6), calls=%async_computation | async-start | bytes 1179648 | tf_op jit(solution)/shard_map/all_to_all | solution.py:372
  59.1 15.6 %collective-permute-start.5 = (bf16[2,32,16,128]{3,2,1,0:T(8,128)(2,1)S(1)}, bf16[2,32,16,128]{3,2,1,0:T(8,128)(2,1)S(1)}, u32[]{:S(2)}, u32[]{:S(2)}) collective-permute-start(bf16[2,32,16,128]{3,2,1,0:T(8,128)(2,1)S(1)} %get-tuple-element.63), channel_id=1, source_target_pairs={{8,16},{24,32},{40,48},{56,64},{72,80},{88,96},{104,112},{120,128}... | collective-permute-start | bytes 786440 | tf_op jit(solution)/shard_map/ppermute | solution.py:358
  75.4 14.2 %all-to-all-start.1 = ((bf16[8,72,128]{2,1,0:T(8,128)(2,1)}), bf16[8,72,128]{2,1,0:T(8,128)(2,1)S(1)}, u32[]{:S(2)}, u32[]{:S(2)}) async-start(bf16[8,72,128]{2,1,0:T(8,128)(2,1)} %broadcast_in_dim.4), calls=%async_computation.1 | async-start | bytes 294912 | tf_op jit(solution)/shard_map/all_to_all | solution.py:379
  90.5 22.3 %all-to-all-start.2 = ((bf16[32,72,128]{2,1,0:T(8,128)(2,1)}), bf16[32,72,128]{2,1,0:T(8,128)(2,1)S(1)}, u32[]{:S(2)}, u32[]{:S(2)}) async-start(bf16[32,72,128]{2,1,0:T(8,128)(2,1)} %broadcast_in_dim.5), calls=%async_computation.2 | async-start | bytes 1179648 | tf_op jit(solution)/shard_map/all_to_all | solution.py:379
  98.7 10.2 %collective-permute-start.6 = (bf16[2,16,16,128]{3,2,1,0:T(8,128)(2,1)S(1)}, bf16[2,16,16,128]{3,2,1,0:T(8,128)(2,1)S(1)}, u32[]{:S(2)}, u32[]{:S(2)}) collective-permute-start(bf16[2,16,16,128]{3,2,1,0:T(8,128)(2,1)S(1)} %get-tuple-element.71), channel_id=1, source_target_pairs={{1,2},{3,4},{5,6},{2,1},{4,3},{6,5},{9,10},{11,12},{13,14},{10,9},... | collective-permute-start | bytes 393224 | tf_op jit(solution)/shard_map/ppermute | solution.py:358
  99.4 12.3 %collective-permute-start.7 = (bf16[2,16,16,128]{3,2,1,0:T(8,128)(2,1)S(1)}, bf16[2,16,16,128]{3,2,1,0:T(8,128)(2,1)S(1)}, u32[]{:S(2)}, u32[]{:S(2)}) collective-permute-start(bf16[2,16,16,128]{3,2,1,0:T(8,128)(2,1)S(1)} %get-tuple-element.73), channel_id=1, source_target_pairs={{0,1},{1,0},{2,3},{3,2},{4,5},{5,4},{6,7},{7,6},{8,9},{9,8},{10,11... | collective-permute-start | bytes 393224 | tf_op jit(solution)/shard_map/ppermute | solution.py:362
  112.9 10.0 %collective-permute-start.8 = (bf16[2304,128]{1,0:T(8,128)(2,1)S(1)}, bf16[2304,128]{1,0:T(8,128)(2,1)S(1)}, u32[]{:S(2)}, u32[]{:S(2)}) collective-permute-start(bf16[2304,128]{1,0:T(8,128)(2,1)S(1)} %bitcast.11), channel_id=1, source_target_pairs={{0,8},{8,0},{1,9},{9,1},{2,10},{10,2},{3,11},{11,3},{4,12},{12,4},... | collective-permute-start | bytes 1769480 | tf_op jit(solution)/shard_map/ppermute | solution.py:362

commit v11 on v10

--- a/solution.py
+++ b/solution.py
@@ -11,6 +11,8 @@
 MARGIN = 8
 ROW = ("x", "zh")
 COL = ("y", "zl", "core")
+PLANE = ("x", "y")
+DEPTH = ("zl", "zh")
 F32 = jnp.float32
 BF16 = jnp.bfloat16
 REACH = 2
@@ -117,7 +119,16 @@
     field_grad[...] = total[1]
 
 
-def unpack_kernel(scale, places, own, other, g_first, g_down, g_up):
+def sum_kernel(parts, copies):
+    total = parts[0].astype(F32)
+    for k in range(1, parts.shape[0]):
+        total = total + parts[k].astype(F32)
+    total = total.astype(BF16)
+    for k in range(copies.shape[0]):
+        copies[k] = total
+
+
+def unpack_kernel(scale, core, own, other, g_first, g_down, g_up):
     def write(parts):
         def rows(base, count):
             at = base % HALF_ROWS
@@ -132,8 +143,8 @@
         for t in range(4):
             g_up[t] = rows(FIRST_ROWS + DOWN_ROWS + t * C2, C2)
 
-    pl.when(places[6] == 0)(lambda: write((own, other)))
-    pl.when(places[6] == 1)(lambda: write((other, own)))
+    pl.when(core[0] == 0)(lambda: write((own, other)))
+    pl.when(core[0] == 1)(lambda: write((other, own)))
 
 
 def shifted(x, by):
@@ -366,17 +377,13 @@
     return (x.astype(F32) + y.astype(F32)).astype(BF16)
 
 
-def scattered(x, axes):
-    size = lax.axis_size(axes)
-    parts = x.reshape(size, x.shape[0] // size, x.shape[1])
-    got = lax.all_to_all(parts, axes, 0, 0, tiled=True)
-    return got.astype(F32).sum(0).astype(BF16)
-
-
-def gathered(x, axes):
-    size = lax.axis_size(axes)
-    parts = jnp.broadcast_to(x[None], (size,) + x.shape)
+def exchanged(parts, axes):
     return lax.all_to_all(parts, axes, 0, 0, tiled=True)
+
+
+def summed_for(axes, parts):
+    shape = (lax.axis_size(axes),) + parts.shape[1:]
+    return small_call(sum_kernel, "sum", [(shape, BF16)], [], parts)[0]
 
 
 def per_device(field, cotangent, w_first, w_down, w_up, offsets, blend_table):
@@ -412,9 +419,10 @@
     got = swapped_a(send, "core")
     from_b = swapped_b(strip_b, COL)
     part = added(keep, got[:HALF_ROWS])
-    part = scattered(part, ("x", "y"))
+    part = exchanged(part.reshape(lax.axis_size(PLANE), -1, C1), PLANE)
+    part = summed_for(DEPTH, part)
     part, from_b = lax.optimization_barrier((part, from_b))
-    part = gathered(part, ("zl", "zh")).astype(F32).sum(0).astype(BF16)
+    part = summed_for(PLANE, exchanged(part, DEPTH))
     tile_shape = (2, TILE, TILE, C1)
     to_a, own, to_b = small_call(
         add_kernel,
@@ -429,7 +437,7 @@
     )
     part, own, to_a, to_b = lax.optimization_barrier((part, own, to_a, to_b))
     row_a, row_b = swapped_a(to_a, "zh"), swapped_b(to_b, ROW)
-    part = gathered(part, ("x", "y")).reshape(-1, C1)
+    part = exchanged(part, PLANE).reshape(-1, C1)
     part, row_b, own, row_a = lax.optimization_barrier((part, row_b, own, row_a))
     other = swapped_a(part, "core")
     blended, field_grad = small_call(
@@ -447,7 +455,7 @@
         "unpack",
         [((9, C1, C1), F32), ((3, 3 * C1, C2), F32), ((4, C2, C1), F32)],
         [],
-        places,
+        lax.axis_index("core").astype(jnp.int32)[None],
         part,
         other,
         smem=1,

time: 127 us -> 126 us (level)
  the two profiles are of different devices: /device:TPU:1 before, /device:TPU:3 now
where the time goes in v11:
time: 126 us; the launch traced here: 125 us
  starting transfers between devices  65.6 us (52%)
  waiting for transfers between devices  40.9 us (32%)
  Pallas kernels  11.5 us (9%)
  local copies, waits for them, and re-layouts  4.39 us (3%)
  other arithmetic  1.93 us (2%)
    all_to_all x3, starting transfers between devices, exchanged(): return lax.all_to_all(parts, axes, 0, 0, tiled=True)  28.2 us
    ppermute x4, starting transfers between devices, swapped_b(): return lax.ppermute(x, axes, pairs + [(j, i) for i, j in pairs])  21.1 us
    all_to_all x3, waiting for transfers between devices, exchanged(): return lax.all_to_all(parts, axes, 0, 0, tiled=True)  18.7 us
    ppermute x5, waiting for transfers between devices, swapped_a(): return lax.ppermute(x, axis, [(0, 1), (1, 0)])  16.9 us
    ppermute x5, starting transfers between devices, swapped_a(): return lax.ppermute(x, axis, [(0, 1), (1, 0)])  16.4 us
    ppermute x4, waiting for transfers between devices, swapped_b(): return lax.ppermute(x, axes, pairs + [(j, i) for i, j in pairs])  5.36 us
    pallas_call x6, Pallas kernels, small_call(): pl.pallas_call(body, out_shape=tuple((jax.ShapeDtypeStruct(shape, kind) f...  5.27 us
    pallas_call x1, Pallas kernels, patch_work(): pl.pallas_call(net_kernel, out_shape=(jax.ShapeDtypeStruct((2, 32, 16, C1...  4.63 us
  transfers between devices with their start and end apart: 12, of which 8 were waited for; matrix products, arithmetic and copies ran while one was open for 0% of the time, Pallas kernels for 3%

profile of v11, /device:TPU:3, one launch (start us, length us, event | category | flops | bytes accessed | tf_op | source)
XLA Modules:
  0.0 125.1 jit_solution(1216979695173073223)
XLA Ops:
  0.6 0.9 pad_maximum_fusion.both
  1.5 10.6 %collective-permute-start.1 = (bf16[2,16,16,128]{3,2,1,0:T(8,128)(2,1)S(1)}, bf16[2,16,16,128]{3,2,1,0:T(8,128)(2,1)S(1)}, u32[]{:S(2)}, u32[]{:S(2)}) collective-permute-start(bf16[2,16,16,128]{3,2,1,0:T(8,128)(2,1)S(1)} %pad_maximum_fusion.both), channel_id=1, source_target_pairs={{1,2},{3,4},{5,6},{2,1},{4,3},{6,5},{9,10},{11,12},{13,14},{10,9},... | collective-permute-start | bytes 393224 | tf_op jit(solution)/shard_map/ppermute | solution.py:369
  12.1 1.9 %collective-permute-start = (bf16[2,16,16,128]{3,2,1,0:T(8,128)(2,1)S(1)}, bf16[2,16,16,128]{3,2,1,0:T(8,128)(2,1)S(1)}, u32[]{:S(2)}, u32[]{:S(2)}) collective-permute-start(bf16[2,16,16,128]{3,2,1,0:T(8,128)(2,1)S(1)} %pad_maximum_fusion.both), channel_id=1, source_target_pairs={{0,1},{1,0},{2,3},{3,2},{4,5},{5,4},{6,7},{7,6},{8,9},{9,8},{10,11... | collective-permute-start | bytes 393224 | tf_op jit(solution)/shard_map/ppermute | solution.py:373
  14.1 0.1 pad_add_fusion.where
  14.2 0.0 copy-start
  14.2 1.1 copy-done
  15.2 0.0 copy-start.2
  15.2 1.0 copy-done.2
  16.2 0.0 copy-start.3
  16.2 0.9 copy-done.3
  17.2 0.0 copy-start.4
  17.2 0.7 copy-done.4
  17.9 0.0 copy-start.5
  17.9 0.7 copy-done.5
  18.6 0.0 copy-start.1
  18.6 1.6 %prepare.1 = (s32[8]{0:T(128)S(1)}, f32[2,16,16,256]{3,2,1,0:T(8,128)S(1)}, bf16[3,512,256]{2,1,0:T(8,128)(2,1)S(1)}, bf16[3,256,512]{2,1,0:T(8,128)(2,1)S(1)}, ...) custom-call(s32[2]{0:T(128)S(1)} %pad_add_fusion.where, s32[8,2,64]{2,1,0:T(2,128)S(1)} %bitcast.15, ...), custom_call_target="tpu_custom_call" | custom-call | flops 5000000 | bytes 10000000 | tf_op jit(solution)/shard_map/prepare/pallas_call | solution.py:305
  20.1 0.0 collective-permute-done.1.from_b
  20.2 5.3 %collective-permute-done.from_a = bf16[2,16,16,128]{3,2,1,0:T(8,128)(2,1)S(1)} collective-permute-done((bf16[2,16,16,128]{3,2,1,0:T(8,128)(2,1)S(1)}, bf16[2,16,16,128]{3,2,1,0:T(8,128)(2,1)S(1)}, u32[]{:S(2)}, u32[]{:S(2)}) %collective-permute-start) | collective-permute-done | bytes 131104 | tf_op jit(solution)/shard_map/ppermute | solution.py:373
  25.5 0.6 assemble.1
  26.1 3.9 %collective-permute-start.2 = (bf16[2,32,16,128]{3,2,1,0:T(8,128)(2,1)S(1)}, bf16[2,32,16,128]{3,2,1,0:T(8,128)(2,1)S(1)}, u32[]{:S(2)}, u32[]{:S(2)}) collective-permute-start(bf16[2,32,16,128]{3,2,1,0:T(8,128)(2,1)S(1)} %get-tuple-element.53), channel_id=1, source_target_pairs={{8,16},{24,32},{40,48},{56,64},{72,80},{88,96},{104,112},{120,128}... | collective-permute-start | bytes 786440 | tf_op jit(solution)/shard_map/ppermute | solution.py:369
  30.0 1.9 %collective-permute-start.3 = (bf16[2,32,16,128]{3,2,1,0:T(8,128)(2,1)S(1)}, bf16[2,32,16,128]{3,2,1,0:T(8,128)(2,1)S(1)}, u32[]{:S(2)}, u32[]{:S(2)}) collective-permute-start(bf16[2,32,16,128]{3,2,1,0:T(8,128)(2,1)S(1)} %get-tuple-element.55), channel_id=1, source_target_pairs={{0,8},{8,0},{1,9},{9,1},{2,10},{10,2},{3,11},{11,3},{4,12},{12,4},... | collective-permute-start | bytes 786440 | tf_op jit(solution)/shard_map/ppermute | solution.py:373
  32.0 4.2 %collective-permute-done.2.side_b = bf16[2,32,16,128]{3,2,1,0:T(8,128)(2,1)S(1)} collective-permute-done((bf16[2,32,16,128]{3,2,1,0:T(8,128)(2,1)S(1)}, bf16[2,32,16,128]{3,2,1,0:T(8,128)(2,1)S(1)}, u32[]{:S(2)}, u32[]{:S(2)}) %collective-permute-start.2) | collective-permute-done | bytes 262176 | tf_op jit(solution)/shard_map/ppermute | solution.py:369
  36.2 0.0 collective-permute-done.3.side_a
  36.2 0.0 copy-done.1
  36.2 4.6 %patch_work.1 = (f32[2,32,16,128]{3,2,1,0:T(8,128)S(1)}, bf16[2,32,16,128]{3,2,1,0:T(8,128)(2,1)S(1)}, bf16[2304,128]{1,0:T(8,128)(2,1)S(1)}, bf16[3328,128]{1,0:T(8,128)(2,1)S(1)}) custom-call(s32[8]{0:T(128)S(1)} %get-tuple-element.50.places, bf16[2,32,16,128]{3,2,1,0:T(8,128)(2,1)S(1)} %collective-permute-done.2.side_b, ...), custom_call_target="tpu_custom_call" | custom-call | flops 2000000000 | bytes 10000000 | tf_op jit(solution)/shard_map/patch_work/pallas_call | solution.py:324
  40.8 1.9 %collective-permute-start.4 = (bf16[3328,128]{1,0:T(8,128)(2,1)S(1)}, bf16[3328,128]{1,0:T(8,128)(2,1)S(1)}, u32[]{:S(2)}, u32[]{:S(2)}) collective-permute-start(bf16[3328,128]{1,0:T(8,128)(2,1)S(1)} %get-tuple-element.62), channel_id=1, source_target_pairs={{0,8},{8,0},{1,9},{9,1},{2,10},{10,2},{3,11},{11,3},{4,12},{12,4},... | collective-permute-start | bytes 2555912 | tf_op jit(solution)/shard_map/ppermute | solution.py:373
  42.7 2.3 %collective-permute-done.4.from_a = bf16[3328,128]{1,0:T(8,128)(2,1)S(1)} collective-permute-done((bf16[3328,128]{1,0:T(8,128)(2,1)S(1)}, bf16[3328,128]{1,0:T(8,128)(2,1)S(1)}, u32[]{:S(2)}, u32[]{:S(2)}) %collective-permute-start.4) | collective-permute-done | bytes 852000 | tf_op jit(solution)/shard_map/ppermute | solution.py:373
  45.1 1.0 add_convert_fusion
  46.0 12.2 %all-to-all-start = ((bf16[32,72,128]{2,1,0:T(8,128)(2,1)}), bf16[32,72,128]{2,1,0:T(8,128)(2,1)S(1)}, u32[]{:S(2)}, u32[]{:S(2)}) async-start(bf16[32,72,128]{2,1,0:T(8,128)(2,1)} %bitcast.6), calls=%async_computation | async-start | bytes 1179648 | tf_op jit(solution)/shard_map/all_to_all | solution.py:381
  58.3 2.2 %collective-permute-start.5 = (bf16[2,32,16,128]{3,2,1,0:T(8,128)(2,1)S(1)}, bf16[2,32,16,128]{3,2,1,0:T(8,128)(2,1)S(1)}, u32[]{:S(2)}, u32[]{:S(2)}) collective-permute-start(bf16[2,32,16,128]{3,2,1,0:T(8,128)(2,1)S(1)} %get-tuple-element.63), channel_id=1, source_target_pairs={{8,16},{24,32},{40,48},{56,64},{72,80},{88,96},{104,112},{120,128}... | collective-permute-start | bytes 786440 | tf_op jit(solution)/shard_map/ppermute | solution.py:369
  60.4 12.7 %all-to-all-done.parts = bf16[32,72,128]{2,1,0:T(8,128)(2,1)S(1)} async-done(((bf16[32,72,128]{2,1,0:T(8,128)(2,1)}), bf16[32,72,128]{2,1,0:T(8,128)(2,1)S(1)}, u32[]{:S(2)}, u32[]{:S(2)}) %all-to-all-start) | async-done | bytes 589856 | tf_op jit(solution)/shard_map/all_to_all | solution.py:381
  73.1 0.8 sum.2
  73.9 0.0 collective-permute-done.5.from_b
  73.9 7.1 %all-to-all-start.1 = ((bf16[8,72,128]{2,1,0:T(8,128)(2,1)}), bf16[8,72,128]{2,1,0:T(8,128)(2,1)S(1)}, u32[]{:S(2)}, u32[]{:S(2)}) async-start(bf16[8,72,128]{2,1,0:T(8,128)(2,1)} %sum.2), calls=%async_computation.1 | async-start | bytes 294912 | tf_op jit(solution)/shard_map/all_to_all | solution.py:381
  81.0 0.8 add.20
  81.7 6.0 %all-to-all-done.1.parts = bf16[8,72,128]{2,1,0:T(8,128)(2,1)S(1)} async-done(((bf16[8,72,128]{2,1,0:T(8,128)(2,1)}), bf16[8,72,128]{2,1,0:T(8,128)(2,1)S(1)}, u32[]{:S(2)}, u32[]{:S(2)}) %all-to-all-start.1) | async-done | bytes 147488 | tf_op jit(solution)/shard_map/all_to_all | solution.py:381
  87.7 0.9 sum.3
  88.6 8.9 %all-to-all-start.2 = ((bf16[32,72,128]{2,1,0:T(8,128)(2,1)}), bf16[32,72,128]{2,1,0:T(8,128)(2,1)S(1)}, u32[]{:S(2)}, u32[]{:S(2)}) async-start(bf16[32,72,128]{2,1,0:T(8,128)(2,1)} %sum.3), calls=%async_computation.2 | async-start | bytes 1179648 | tf_op jit(solution)/shard_map/all_to_all | solution.py:381
  97.5 4.4 %collective-permute-start.6 = (bf16[2,16,16,128]{3,2,1,0:T(8,128)(2,1)S(1)}, bf16[2,16,16,128]{3,2,1,0:T(8,128)(2,1)S(1)}, u32[]{:S(2)}, u32[]{:S(2)}) collective-permute-start(bf16[2,16,16,128]{3,2,1,0:T(8,128)(2,1)S(1)} %get-tuple-element.71), channel_id=1, source_target_pairs={{1,2},{3,4},{5,6},{2,1},{4,3},{6,5},{9,10},{11,12},{13,14},{10,9},... | collective-permute-start | bytes 393224 | tf_op jit(solution)/shard_map/ppermute | solution.py:369
  101.8 5.7 %collective-permute-start.7 = (bf16[2,16,16,128]{3,2,1,0:T(8,128)(2,1)S(1)}, bf16[2,16,16,128]{3,2,1,0:T(8,128)(2,1)S(1)}, u32[]{:S(2)}, u32[]{:S(2)}) collective-permute-start(bf16[2,16,16,128]{3,2,1,0:T(8,128)(2,1)S(1)} %get-tuple-element.73), channel_id=1, source_target_pairs={{0,1},{1,0},{2,3},{3,2},{4,5},{5,4},{6,7},{7,6},{8,9},{9,8},{10,11... | collective-permute-start | bytes 393224 | tf_op jit(solution)/shard_map/ppermute | solution.py:373
  107.6 1.2 collective-permute-done.6.from_b
  108.7 8.3 %collective-permute-done.7.from_a = bf16[2,16,16,128]{3,2,1,0:T(8,128)(2,1)S(1)} collective-permute-done((bf16[2,16,16,128]{3,2,1,0:T(8,128)(2,1)S(1)}, bf16[2,16,16,128]{3,2,1,0:T(8,128)(2,1)S(1)}, u32[]{:S(2)}, u32[]{:S(2)}) %collective-permute-start.7) | collective-permute-done | bytes 131104 | tf_op jit(solution)/shard_map/ppermute | solution.py:373
  117.0 0.0 all-to-all-done.2
  117.0 4.9 %collective-permute-start.8 = (bf16[2304,128]{1,0:T(8,128)(2,1)S(1)}, bf16[2304,128]{1,0:T(8,128)(2,1)S(1)}, u32[]{:S(2)}, u32[]{:S(2)}) collective-permute-start(bf16[2304,128]{1,0:T(8,128)(2,1)S(1)} %bitcast.12), channel_id=1, source_target_pairs={{0,8},{8,0},{1,9},{9,1},{2,10},{10,2},{3,11},{11,3},{4,12},{12,4},... | collective-permute-start | bytes 1769480 | tf_op jit(solution)/shard_map/ppermute | solution.py:373
  121.9 0.7 finish.1
  122.6 0.9 collective-permute-done.8.other
  123.5 1.5 %unpack.1 = (f32[9,128,128]{2,1,0:T(8,128)}, f32[3,384,256]{2,1,0:T(8,128)}, f32[4,256,128]{2,1,0:T(8,128)}) custom-call(s32[1]{0:T(128)} %bitcast.8.core, bf16[2304,128]{1,0:T(8,128)(2,1)S(1)} %bitcast.13, bf16[2304,128]{1,0:T(8,128)(2,1)S(1)} %collective-permute-done.8.other), custom_call_target="tpu_custom_call" | custom-call | flops 1000000 | bytes 2000000 | tf_op jit(solution)/shard_map/unpack/pallas_call | solution.py:354
Async XLA Ops:
  1.5 18.6 %collective-permute-start.1 = (bf16[2,16,16,128]{3,2,1,0:T(8,128)(2,1)S(1)}, bf16[2,16,16,128]{3,2,1,0:T(8,128)(2,1)S(1)}, u32[]{:S(2)}, u32[]{:S(2)}) collective-permute-start(bf16[2,16,16,128]{3,2,1,0:T(8,128)(2,1)S(1)} %pad_maximum_fusion.both), channel_id=1, source_target_pairs={{1,2},{3,4},{5,6},{2,1},{4,3},{6,5},{9,10},{11,12},{13,14},{10,9},... | collective-permute-start | bytes 393224 | tf_op jit(solution)/shard_map/ppermute | solution.py:369
  12.1 13.4 %collective-permute-start = (bf16[2,16,16,128]{3,2,1,0:T(8,128)(2,1)S(1)}, bf16[2,16,16,128]{3,2,1,0:T(8,128)(2,1)S(1)}, u32[]{:S(2)}, u32[]{:S(2)}) collective-permute-start(bf16[2,16,16,128]{3,2,1,0:T(8,128)(2,1)S(1)} %pad_maximum_fusion.both), channel_id=1, source_target_pairs={{0,1},{1,0},{2,3},{3,2},{4,5},{5,4},{6,7},{7,6},{8,9},{9,8},{10,11... | collective-permute-start | bytes 393224 | tf_op jit(solution)/shard_map/ppermute | solution.py:373
  14.2 1.1 copy-start
  15.2 1.0 copy-start.2
  16.2 0.9 copy-start.3
  17.2 0.7 copy-start.4
  17.9 0.7 copy-start.5
  18.6 17.6 %copy-start.1 = (bf16[3,3,128,256]{3,2,1,0:T(8,128)(2,1)S(1)}, bf16[3,3,128,256]{3,2,1,0:T(8,128)(2,1)}, u32[]{:S(2)}) copy-start(bf16[3,3,128,256]{3,2,1,0:T(8,128)(2,1)} %w_down.1) | copy-start | bytes 1769476
  26.1 10.0 %collective-permute-start.2 = (bf16[2,32,16,128]{3,2,1,0:T(8,128)(2,1)S(1)}, bf16[2,32,16,128]{3,2,1,0:T(8,128)(2,1)S(1)}, u32[]{:S(2)}, u32[]{:S(2)}) collective-permute-start(bf16[2,32,16,128]{3,2,1,0:T(8,128)(2,1)S(1)} %get-tuple-element.53), channel_id=1, source_target_pairs={{8,16},{24,32},{40,48},{56,64},{72,80},{88,96},{104,112},{120,128}... | collective-permute-start | bytes 786440 | tf_op jit(solution)/shard_map/ppermute | solution.py:369
  30.0 6.1 %collective-permute-start.3 = (bf16[2,32,16,128]{3,2,1,0:T(8,128)(2,1)S(1)}, bf16[2,32,16,128]{3,2,1,0:T(8,128)(2,1)S(1)}, u32[]{:S(2)}, u32[]{:S(2)}) collective-permute-start(bf16[2,32,16,128]{3,2,1,0:T(8,128)(2,1)S(1)} %get-tuple-element.55), channel_id=1, source_target_pairs={{0,8},{8,0},{1,9},{9,1},{2,10},{10,2},{3,11},{11,3},{4,12},{12,4},... | collective-permute-start | bytes 786440 | tf_op jit(solution)/shard_map/ppermute | solution.py:373
  40.8 4.3 %collective-permute-start.4 = (bf16[3328,128]{1,0:T(8,128)(2,1)S(1)}, bf16[3328,128]{1,0:T(8,128)(2,1)S(1)}, u32[]{:S(2)}, u32[]{:S(2)}) collective-permute-start(bf16[3328,128]{1,0:T(8,128)(2,1)S(1)} %get-tuple-element.62), channel_id=1, source_target_pairs={{0,8},{8,0},{1,9},{9,1},{2,10},{10,2},{3,11},{11,3},{4,12},{12,4},... | collective-permute-start | bytes 2555912 | tf_op jit(solution)/shard_map/ppermute | solution.py:373
  46.0 27.1 %all-to-all-start = ((bf16[32,72,128]{2,1,0:T(8,128)(2,1)}), bf16[32,72,128]{2,1,0:T(8,128)(2,1)S(1)}, u32[]{:S(2)}, u32[]{:S(2)}) async-start(bf16[32,72,128]{2,1,0:T(8,128)(2,1)} %bitcast.6), calls=%async_computation | async-start | bytes 1179648 | tf_op jit(solution)/shard_map/all_to_all | solution.py:381
  58.3 15.6 %collective-permute-start.5 = (bf16[2,32,16,128]{3,2,1,0:T(8,128)(2,1)S(1)}, bf16[2,32,16,128]{3,2,1,0:T(8,128)(2,1)S(1)}, u32[]{:S(2)}, u32[]{:S(2)}) collective-permute-start(bf16[2,32,16,128]{3,2,1,0:T(8,128)(2,1)S(1)} %get-tuple-element.63), channel_id=1, source_target_pairs={{8,16},{24,32},{40,48},{56,64},{72,80},{88,96},{104,112},{120,128}... | collective-permute-start | bytes 786440 | tf_op jit(solution)/shard_map/ppermute | solution.py:369
  73.9 13.8 %all-to-all-start.1 = ((bf16[8,72,128]{2,1,0:T(8,128)(2,1)}), bf16[8,72,128]{2,1,0:T(8,128)(2,1)S(1)}, u32[]{:S(2)}, u32[]{:S(2)}) async-start(bf16[8,72,128]{2,1,0:T(8,128)(2,1)} %sum.2), calls=%async_computation.1 | async-start | bytes 294912 | tf_op jit(solution)/shard_map/all_to_all | solution.py:381
  88.6 28.5 %all-to-all-start.2 = ((bf16[32,72,128]{2,1,0:T(8,128)(2,1)}), bf16[32,72,128]{2,1,0:T(8,128)(2,1)S(1)}, u32[]{:S(2)}, u32[]{:S(2)}) async-start(bf16[32,72,128]{2,1,0:T(8,128)(2,1)} %sum.3), calls=%async_computation.2 | async-start | bytes 1179648 | tf_op jit(solution)/shard_map/all_to_all | solution.py:381
  97.5 11.3 %collective-permute-start.6 = (bf16[2,16,16,128]{3,2,1,0:T(8,128)(2,1)S(1)}, bf16[2,16,16,128]{3,2,1,0:T(8,128)(2,1)S(1)}, u32[]{:S(2)}, u32[]{:S(2)}) collective-permute-start(bf16[2,16,16,128]{3,2,1,0:T(8,128)(2,1)S(1)} %get-tuple-element.71), channel_id=1, source_target_pairs={{1,2},{3,4},{5,6},{2,1},{4,3},{6,5},{9,10},{11,12},{13,14},{10,9},... | collective-permute-start | bytes 393224 | tf_op jit(solution)/shard_map/ppermute | solution.py:369
  101.8 15.2 %collective-permute-start.7 = (bf16[2,16,16,128]{3,2,1,0:T(8,128)(2,1)S(1)}, bf16[2,16,16,128]{3,2,1,0:T(8,128)(2,1)S(1)}, u32[]{:S(2)}, u32[]{:S(2)}) collective-permute-start(bf16[2,16,16,128]{3,2,1,0:T(8,128)(2,1)S(1)} %get-tuple-element.73), channel_id=1, source_target_pairs={{0,1},{1,0},{2,3},{3,2},{4,5},{5,4},{6,7},{7,6},{8,9},{9,8},{10,11... | collective-permute-start | bytes 393224 | tf_op jit(solution)/shard_map/ppermute | solution.py:373
  117.0 6.5 %collective-permute-start.8 = (bf16[2304,128]{1,0:T(8,128)(2,1)S(1)}, bf16[2304,128]{1,0:T(8,128)(2,1)S(1)}, u32[]{:S(2)}, u32[]{:S(2)}) collective-permute-start(bf16[2304,128]{1,0:T(8,128)(2,1)S(1)} %bitcast.12), channel_id=1, source_target_pairs={{0,8},{8,0},{1,9},{9,1},{2,10},{10,2},{3,11},{11,3},{4,12},{12,4},... | collective-permute-start | bytes 1769480 | tf_op jit(solution)/shard_map/ppermute | solution.py:373

commit v12 on v11

--- a/solution.py
+++ b/solution.py
@@ -11,7 +11,7 @@
 MARGIN = 8
 ROW = ("x", "zh")
 COL = ("y", "zl", "core")
-PLANE = ("x", "y")
+PLANE = ("y", "x")
 DEPTH = ("zl", "zh")
 F32 = jnp.float32
 BF16 = jnp.bfloat16

time: 126 us -> 125 us (level)
  the two profiles are of different devices: /device:TPU:3 before, /device:TPU:1 now
where the time goes in v12:
time: 125 us; the launch traced here: 124 us
  starting transfers between devices  71.3 us (57%)
  waiting for transfers between devices  33.8 us (27%)
  Pallas kernels  11.5 us (9%)
  local copies, waits for them, and re-layouts  4.39 us (4%)
  other arithmetic  1.93 us (2%)
    ppermute x5, starting transfers between devices, swapped_a(): return lax.ppermute(x, axis, [(0, 1), (1, 0)])  32.5 us
    all_to_all x3, starting transfers between devices, exchanged(): return lax.all_to_all(parts, axes, 0, 0, tiled=True)  27.6 us
    all_to_all x3, waiting for transfers between devices, exchanged(): return lax.all_to_all(parts, axes, 0, 0, tiled=True)  24.5 us
    ppermute x4, starting transfers between devices, swapped_b(): return lax.ppermute(x, axes, pairs + [(j, i) for i, j in pairs])  11.1 us
    ppermute x5, waiting for transfers between devices, swapped_a(): return lax.ppermute(x, axis, [(0, 1), (1, 0)])  6.36 us
    pallas_call x6, Pallas kernels, small_call(): pl.pallas_call(body, out_shape=tuple((jax.ShapeDtypeStruct(shape, kind) f...  5.27 us
    pallas_call x1, Pallas kernels, patch_work(): pl.pallas_call(net_kernel, out_shape=(jax.ShapeDtypeStruct((2, 32, 16, C1...  4.64 us
    unnamed x12, local copies, waits for them, and re-layouts  4.39 us
  transfers between devices with their start and end apart: 12, of which 7 were waited for; matrix products, arithmetic and copies ran while one was open for 0% of the time, Pallas kernels for 3%

profile of v12, /device:TPU:1, one launch (start us, length us, event | category | flops | bytes accessed | tf_op | source)
XLA Modules:
  0.0 123.7 jit_solution(8261623808851815540)
XLA Ops:
  0.6 0.9 pad_maximum_fusion.both
  1.5 0.7 collective-permute-start.1
  2.2 12.7 %collective-permute-start = (bf16[2,16,16,128]{3,2,1,0:T(8,128)(2,1)S(1)}, bf16[2,16,16,128]{3,2,1,0:T(8,128)(2,1)S(1)}, u32[]{:S(2)}, u32[]{:S(2)}) collective-permute-start(bf16[2,16,16,128]{3,2,1,0:T(8,128)(2,1)S(1)} %pad_maximum_fusion.both), channel_id=1, source_target_pairs={{0,1},{1,0},{2,3},{3,2},{4,5},{5,4},{6,7},{7,6},{8,9},{9,8},{10,11... | collective-permute-start | bytes 393224 | tf_op jit(solution)/shard_map/ppermute | solution.py:373
  14.9 0.1 pad_add_fusion.where
  15.0 0.0 copy-start
  15.0 1.1 copy-done
  16.1 0.0 copy-start.2
  16.1 1.0 copy-done.2
  17.0 0.0 copy-start.3
  17.0 0.9 copy-done.3
  18.0 0.0 copy-start.4
  18.0 0.7 copy-done.4
  18.7 0.0 copy-start.5
  18.7 0.7 copy-done.5
  19.4 0.0 copy-start.1
  19.4 1.6 %prepare.1 = (s32[8]{0:T(128)S(1)}, f32[2,16,16,256]{3,2,1,0:T(8,128)S(1)}, bf16[3,512,256]{2,1,0:T(8,128)(2,1)S(1)}, bf16[3,256,512]{2,1,0:T(8,128)(2,1)S(1)}, ...) custom-call(s32[2]{0:T(128)S(1)} %pad_add_fusion.where, s32[8,2,64]{2,1,0:T(2,128)S(1)} %bitcast.15, ...), custom_call_target="tpu_custom_call" | custom-call | flops 5000000 | bytes 10000000 | tf_op jit(solution)/shard_map/prepare/pallas_call | solution.py:305
  21.0 0.0 collective-permute-done.1.from_b
  21.0 0.0 collective-permute-done.from_a
  21.0 0.6 assemble.1
  21.6 7.8 %collective-permute-start.2 = (bf16[2,32,16,128]{3,2,1,0:T(8,128)(2,1)S(1)}, bf16[2,32,16,128]{3,2,1,0:T(8,128)(2,1)S(1)}, u32[]{:S(2)}, u32[]{:S(2)}) collective-permute-start(bf16[2,32,16,128]{3,2,1,0:T(8,128)(2,1)S(1)} %get-tuple-element.53), channel_id=1, source_target_pairs={{8,16},{24,32},{40,48},{56,64},{72,80},{88,96},{104,112},{120,128}... | collective-permute-start | bytes 786440 | tf_op jit(solution)/shard_map/ppermute | solution.py:369
  29.5 1.9 %collective-permute-start.3 = (bf16[2,32,16,128]{3,2,1,0:T(8,128)(2,1)S(1)}, bf16[2,32,16,128]{3,2,1,0:T(8,128)(2,1)S(1)}, u32[]{:S(2)}, u32[]{:S(2)}) collective-permute-start(bf16[2,32,16,128]{3,2,1,0:T(8,128)(2,1)S(1)} %get-tuple-element.55), channel_id=1, source_target_pairs={{0,8},{8,0},{1,9},{9,1},{2,10},{10,2},{3,11},{11,3},{4,12},{12,4},... | collective-permute-start | bytes 786440 | tf_op jit(solution)/shard_map/ppermute | solution.py:373
  31.4 3.0 %collective-permute-done.2.side_b = bf16[2,32,16,128]{3,2,1,0:T(8,128)(2,1)S(1)} collective-permute-done((bf16[2,32,16,128]{3,2,1,0:T(8,128)(2,1)S(1)}, bf16[2,32,16,128]{3,2,1,0:T(8,128)(2,1)S(1)}, u32[]{:S(2)}, u32[]{:S(2)}) %collective-permute-start.2) | collective-permute-done | bytes 262176 | tf_op jit(solution)/shard_map/ppermute | solution.py:369
  34.4 0.0 collective-permute-done.3.side_a
  34.4 0.0 copy-done.1
  34.4 4.6 %patch_work.1 = (f32[2,32,16,128]{3,2,1,0:T(8,128)S(1)}, bf16[2,32,16,128]{3,2,1,0:T(8,128)(2,1)S(1)}, bf16[2304,128]{1,0:T(8,128)(2,1)S(1)}, bf16[3328,128]{1,0:T(8,128)(2,1)S(1)}) custom-call(s32[8]{0:T(128)S(1)} %get-tuple-element.50.places, bf16[2,32,16,128]{3,2,1,0:T(8,128)(2,1)S(1)} %collective-permute-done.2.side_b, ...), custom_call_target="tpu_custom_call" | custom-call | flops 2000000000 | bytes 10000000 | tf_op jit(solution)/shard_map/patch_work/pallas_call | solution.py:324
  39.0 1.9 %collective-permute-start.4 = (bf16[3328,128]{1,0:T(8,128)(2,1)S(1)}, bf16[3328,128]{1,0:T(8,128)(2,1)S(1)}, u32[]{:S(2)}, u32[]{:S(2)}) collective-permute-start(bf16[3328,128]{1,0:T(8,128)(2,1)S(1)} %get-tuple-element.62), channel_id=1, source_target_pairs={{0,8},{8,0},{1,9},{9,1},{2,10},{10,2},{3,11},{11,3},{4,12},{12,4},... | collective-permute-start | bytes 2555912 | tf_op jit(solution)/shard_map/ppermute | solution.py:373
  41.0 2.3 %collective-permute-done.4.from_a = bf16[3328,128]{1,0:T(8,128)(2,1)S(1)} collective-permute-done((bf16[3328,128]{1,0:T(8,128)(2,1)S(1)}, bf16[3328,128]{1,0:T(8,128)(2,1)S(1)}, u32[]{:S(2)}, u32[]{:S(2)}) %collective-permute-start.4) | collective-permute-done | bytes 852000 | tf_op jit(solution)/shard_map/ppermute | solution.py:373
  43.3 1.0 add_convert_fusion
  44.3 14.8 %all-to-all-start = ((bf16[32,72,128]{2,1,0:T(8,128)(2,1)}), bf16[32,72,128]{2,1,0:T(8,128)(2,1)S(1)}, u32[]{:S(2)}, u32[]{:S(2)}) async-start(bf16[32,72,128]{2,1,0:T(8,128)(2,1)} %bitcast.6), calls=%async_computation | async-start | bytes 1179648 | tf_op jit(solution)/shard_map/all_to_all | solution.py:381
  59.0 1.9 %collective-permute-start.5 = (bf16[2,32,16,128]{3,2,1,0:T(8,128)(2,1)S(1)}, bf16[2,32,16,128]{3,2,1,0:T(8,128)(2,1)S(1)}, u32[]{:S(2)}, u32[]{:S(2)}) collective-permute-start(bf16[2,32,16,128]{3,2,1,0:T(8,128)(2,1)S(1)} %get-tuple-element.63), channel_id=1, source_target_pairs={{8,16},{24,32},{40,48},{56,64},{72,80},{88,96},{104,112},{120,128}... | collective-permute-start | bytes 786440 | tf_op jit(solution)/shard_map/ppermute | solution.py:369
  61.0 15.7 %all-to-all-done.parts = bf16[32,72,128]{2,1,0:T(8,128)(2,1)S(1)} async-done(((bf16[32,72,128]{2,1,0:T(8,128)(2,1)}), bf16[32,72,128]{2,1,0:T(8,128)(2,1)S(1)}, u32[]{:S(2)}, u32[]{:S(2)}) %all-to-all-start) | async-done | bytes 589856 | tf_op jit(solution)/shard_map/all_to_all | solution.py:381
  76.7 0.8 sum.2
  77.4 0.0 collective-permute-done.5.from_b
  77.4 5.0 %all-to-all-start.1 = ((bf16[8,72,128]{2,1,0:T(8,128)(2,1)}), bf16[8,72,128]{2,1,0:T(8,128)(2,1)S(1)}, u32[]{:S(2)}, u32[]{:S(2)}) async-start(bf16[8,72,128]{2,1,0:T(8,128)(2,1)} %sum.2), calls=%async_computation.1 | async-start | bytes 294912 | tf_op jit(solution)/shard_map/all_to_all | solution.py:381
  82.4 0.8 add.20
  83.2 6.0 %all-to-all-done.1.parts = bf16[8,72,128]{2,1,0:T(8,128)(2,1)S(1)} async-done(((bf16[8,72,128]{2,1,0:T(8,128)(2,1)}), bf16[8,72,128]{2,1,0:T(8,128)(2,1)S(1)}, u32[]{:S(2)}, u32[]{:S(2)}) %all-to-all-start.1) | async-done | bytes 147488 | tf_op jit(solution)/shard_map/all_to_all | solution.py:381
  89.2 0.9 sum.3
  90.0 7.9 %all-to-all-start.2 = ((bf16[32,72,128]{2,1,0:T(8,128)(2,1)}), bf16[32,72,128]{2,1,0:T(8,128)(2,1)S(1)}, u32[]{:S(2)}, u32[]{:S(2)}) async-start(bf16[32,72,128]{2,1,0:T(8,128)(2,1)} %sum.3), calls=%async_computation.2 | async-start | bytes 1179648 | tf_op jit(solution)/shard_map/all_to_all | solution.py:381
  98.0 0.7 collective-permute-start.6
  98.6 9.5 %collective-permute-start.7 = (bf16[2,16,16,128]{3,2,1,0:T(8,128)(2,1)S(1)}, bf16[2,16,16,128]{3,2,1,0:T(8,128)(2,1)S(1)}, u32[]{:S(2)}, u32[]{:S(2)}) collective-permute-start(bf16[2,16,16,128]{3,2,1,0:T(8,128)(2,1)S(1)} %get-tuple-element.73), channel_id=1, source_target_pairs={{0,1},{1,0},{2,3},{3,2},{4,5},{5,4},{6,7},{7,6},{8,9},{9,8},{10,11... | collective-permute-start | bytes 393224 | tf_op jit(solution)/shard_map/ppermute | solution.py:373
  108.1 0.0 collective-permute-done.6.from_b
  108.1 3.1 %collective-permute-done.7.from_a = bf16[2,16,16,128]{3,2,1,0:T(8,128)(2,1)S(1)} collective-permute-done((bf16[2,16,16,128]{3,2,1,0:T(8,128)(2,1)S(1)}, bf16[2,16,16,128]{3,2,1,0:T(8,128)(2,1)S(1)}, u32[]{:S(2)}, u32[]{:S(2)}) %collective-permute-start.7) | collective-permute-done | bytes 131104 | tf_op jit(solution)/shard_map/ppermute | solution.py:373
  111.2 2.8 %all-to-all-done.2 = bf16[32,72,128]{2,1,0:T(8,128)(2,1)S(1)} async-done(((bf16[32,72,128]{2,1,0:T(8,128)(2,1)}), bf16[32,72,128]{2,1,0:T(8,128)(2,1)S(1)}, u32[]{:S(2)}, u32[]{:S(2)}) %all-to-all-start.2) | async-done | bytes 589856 | tf_op jit(solution)/shard_map/all_to_all | solution.py:381
  114.0 6.5 %collective-permute-start.8 = (bf16[2304,128]{1,0:T(8,128)(2,1)S(1)}, bf16[2304,128]{1,0:T(8,128)(2,1)S(1)}, u32[]{:S(2)}, u32[]{:S(2)}) collective-permute-start(bf16[2304,128]{1,0:T(8,128)(2,1)S(1)} %bitcast.12), channel_id=1, source_target_pairs={{0,8},{8,0},{1,9},{9,1},{2,10},{10,2},{3,11},{11,3},{4,12},{12,4},... | collective-permute-start | bytes 1769480 | tf_op jit(solution)/shard_map/ppermute | solution.py:373
  120.5 0.7 finish.1
  121.2 0.9 collective-permute-done.8.other
  122.1 1.5 %unpack.1 = (f32[9,128,128]{2,1,0:T(8,128)}, f32[3,384,256]{2,1,0:T(8,128)}, f32[4,256,128]{2,1,0:T(8,128)}) custom-call(s32[1]{0:T(128)} %bitcast.8.core, bf16[2304,128]{1,0:T(8,128)(2,1)S(1)} %bitcast.13, bf16[2304,128]{1,0:T(8,128)(2,1)S(1)} %collective-permute-done.8.other), custom_call_target="tpu_custom_call" | custom-call | flops 1000000 | bytes 2000000 | tf_op jit(solution)/shard_map/unpack/pallas_call | solution.py:354
Async XLA Ops:
  1.5 19.5 %collective-permute-start.1 = (bf16[2,16,16,128]{3,2,1,0:T(8,128)(2,1)S(1)}, bf16[2,16,16,128]{3,2,1,0:T(8,128)(2,1)S(1)}, u32[]{:S(2)}, u32[]{:S(2)}) collective-permute-start(bf16[2,16,16,128]{3,2,1,0:T(8,128)(2,1)S(1)} %pad_maximum_fusion.both), channel_id=1, source_target_pairs={{1,2},{3,4},{5,6},{2,1},{4,3},{6,5},{9,10},{11,12},{13,14},{10,9},... | collective-permute-start | bytes 393224 | tf_op jit(solution)/shard_map/ppermute | solution.py:369
  2.2 18.8 %collective-permute-start = (bf16[2,16,16,128]{3,2,1,0:T(8,128)(2,1)S(1)}, bf16[2,16,16,128]{3,2,1,0:T(8,128)(2,1)S(1)}, u32[]{:S(2)}, u32[]{:S(2)}) collective-permute-start(bf16[2,16,16,128]{3,2,1,0:T(8,128)(2,1)S(1)} %pad_maximum_fusion.both), channel_id=1, source_target_pairs={{0,1},{1,0},{2,3},{3,2},{4,5},{5,4},{6,7},{7,6},{8,9},{9,8},{10,11... | collective-permute-start | bytes 393224 | tf_op jit(solution)/shard_map/ppermute | solution.py:373
  15.0 1.1 copy-start
  16.1 1.0 copy-start.2
  17.0 0.9 copy-start.3
  18.0 0.7 copy-start.4
  18.7 0.7 copy-start.5
  19.4 15.0 %copy-start.1 = (bf16[3,3,128,256]{3,2,1,0:T(8,128)(2,1)S(1)}, bf16[3,3,128,256]{3,2,1,0:T(8,128)(2,1)}, u32[]{:S(2)}) copy-start(bf16[3,3,128,256]{3,2,1,0:T(8,128)(2,1)} %w_down.1) | copy-start | bytes 1769476
  21.6 12.8 %collective-permute-start.2 = (bf16[2,32,16,128]{3,2,1,0:T(8,128)(2,1)S(1)}, bf16[2,32,16,128]{3,2,1,0:T(8,128)(2,1)S(1)}, u32[]{:S(2)}, u32[]{:S(2)}) collective-permute-start(bf16[2,32,16,128]{3,2,1,0:T(8,128)(2,1)S(1)} %get-tuple-element.53), channel_id=1, source_target_pairs={{8,16},{24,32},{40,48},{56,64},{72,80},{88,96},{104,112},{120,128}... | collective-permute-start | bytes 786440 | tf_op jit(solution)/shard_map/ppermute | solution.py:369
  29.5 4.9 %collective-permute-start.3 = (bf16[2,32,16,128]{3,2,1,0:T(8,128)(2,1)S(1)}, bf16[2,32,16,128]{3,2,1,0:T(8,128)(2,1)S(1)}, u32[]{:S(2)}, u32[]{:S(2)}) collective-permute-start(bf16[2,32,16,128]{3,2,1,0:T(8,128)(2,1)S(1)} %get-tuple-element.55), channel_id=1, source_target_pairs={{0,8},{8,0},{1,9},{9,1},{2,10},{10,2},{3,11},{11,3},{4,12},{12,4},... | collective-permute-start | bytes 786440 | tf_op jit(solution)/shard_map/ppermute | solution.py:373
  39.0 4.3 %collective-permute-start.4 = (bf16[3328,128]{1,0:T(8,128)(2,1)S(1)}, bf16[3328,128]{1,0:T(8,128)(2,1)S(1)}, u32[]{:S(2)}, u32[]{:S(2)}) collective-permute-start(bf16[3328,128]{1,0:T(8,128)(2,1)S(1)} %get-tuple-element.62), channel_id=1, source_target_pairs={{0,8},{8,0},{1,9},{9,1},{2,10},{10,2},{3,11},{11,3},{4,12},{12,4},... | collective-permute-start | bytes 2555912 | tf_op jit(solution)/shard_map/ppermute | solution.py:373
  44.3 32.4 %all-to-all-start = ((bf16[32,72,128]{2,1,0:T(8,128)(2,1)}), bf16[32,72,128]{2,1,0:T(8,128)(2,1)S(1)}, u32[]{:S(2)}, u32[]{:S(2)}) async-start(bf16[32,72,128]{2,1,0:T(8,128)(2,1)} %bitcast.6), calls=%async_computation | async-start | bytes 1179648 | tf_op jit(solution)/shard_map/all_to_all | solution.py:381
  59.0 18.4 %collective-permute-start.5 = (bf16[2,32,16,128]{3,2,1,0:T(8,128)(2,1)S(1)}, bf16[2,32,16,128]{3,2,1,0:T(8,128)(2,1)S(1)}, u32[]{:S(2)}, u32[]{:S(2)}) collective-permute-start(bf16[2,32,16,128]{3,2,1,0:T(8,128)(2,1)S(1)} %get-tuple-element.63), channel_id=1, source_target_pairs={{8,16},{24,32},{40,48},{56,64},{72,80},{88,96},{104,112},{120,128}... | collective-permute-start | bytes 786440 | tf_op jit(solution)/shard_map/ppermute | solution.py:369
  77.4 11.7 %all-to-all-start.1 = ((bf16[8,72,128]{2,1,0:T(8,128)(2,1)}), bf16[8,72,128]{2,1,0:T(8,128)(2,1)S(1)}, u32[]{:S(2)}, u32[]{:S(2)}) async-start(bf16[8,72,128]{2,1,0:T(8,128)(2,1)} %sum.2), calls=%async_computation.1 | async-start | bytes 294912 | tf_op jit(solution)/shard_map/all_to_all | solution.py:381
  90.0 24.0 %all-to-all-start.2 = ((bf16[32,72,128]{2,1,0:T(8,128)(2,1)}), bf16[32,72,128]{2,1,0:T(8,128)(2,1)S(1)}, u32[]{:S(2)}, u32[]{:S(2)}) async-start(bf16[32,72,128]{2,1,0:T(8,128)(2,1)} %sum.3), calls=%async_computation.2 | async-start | bytes 1179648 | tf_op jit(solution)/shard_map/all_to_all | solution.py:381
  98.0 10.2 %collective-permute-start.6 = (bf16[2,16,16,128]{3,2,1,0:T(8,128)(2,1)S(1)}, bf16[2,16,16,128]{3,2,1,0:T(8,128)(2,1)S(1)}, u32[]{:S(2)}, u32[]{:S(2)}) collective-permute-start(bf16[2,16,16,128]{3,2,1,0:T(8,128)(2,1)S(1)} %get-tuple-element.71), channel_id=1, source_target_pairs={{1,2},{3,4},{5,6},{2,1},{4,3},{6,5},{9,10},{11,12},{13,14},{10,9},... | collective-permute-start | bytes 393224 | tf_op jit(solution)/shard_map/ppermute | solution.py:369
  98.6 12.6 %collective-permute-start.7 = (bf16[2,16,16,128]{3,2,1,0:T(8,128)(2,1)S(1)}, bf16[2,16,16,128]{3,2,1,0:T(8,128)(2,1)S(1)}, u32[]{:S(2)}, u32[]{:S(2)}) collective-permute-start(bf16[2,16,16,128]{3,2,1,0:T(8,128)(2,1)S(1)} %get-tuple-element.73), channel_id=1, source_target_pairs={{0,1},{1,0},{2,3},{3,2},{4,5},{5,4},{6,7},{7,6},{8,9},{9,8},{10,11... | collective-permute-start | bytes 393224 | tf_op jit(solution)/shard_map/ppermute | solution.py:373
  114.0 8.1 %collective-permute-start.8 = (bf16[2304,128]{1,0:T(8,128)(2,1)S(1)}, bf16[2304,128]{1,0:T(8,128)(2,1)S(1)}, u32[]{:S(2)}, u32[]{:S(2)}) collective-permute-start(bf16[2304,128]{1,0:T(8,128)(2,1)S(1)} %bitcast.12), channel_id=1, source_target_pairs={{0,8},{8,0},{1,9},{9,1},{2,10},{10,2},{3,11},{11,3},{4,12},{12,4},... | collective-permute-start | bytes 1769480 | tf_op jit(solution)/shard_map/ppermute | solution.py:373
